TPU v7x, 256 devices: a whole 4x4x8 slice. The times are simulated.
256 devices in a mesh: ctx: 64 (over x_lo, y, z), head: 4 (over x_hi, core).
Axes of the slice: x: 4 (x_hi: 2, x_lo: 2; x = x_hi * 2 + x_lo), y: 4, z: 8, core: 2. Of those that a mesh axis runs over, the one named last changes fastest.
Arguments:
- queries: bfloat16 [8192, 2048], P('ctx', 'head')
- keys: bfloat16 [8192, 1024], P('ctx', 'head')
- values: bfloat16 [8192, 1024], P('ctx', 'head'), may hold values from -6 to 6
- positions: int32 [8192], P('ctx'), may hold values from 0 to 12287, as said below
- query_gain: float32 [128], replicated, as said below
- key_gain: float32 [128], replicated, as said below
- out_weight: bfloat16 [2048, 5376], P('head'), may hold values from -0.125 to 0.125
Outputs:
- mixed_rows: bfloat16 [8192, 5376], P(('ctx', 'head'))
Inputs may be any that keep to these rules, and one draw needn't show every extreme that they name: `positions`: rise strictly along the document by 1 or 2 a token; the first is 0 and the last is 12287. `query_gain`: positive. `key_gain`: positive.
All inputs are finite; a program needn't handle non-finite values.
Results may differ from a plain program's by a relative error of at most 0.015.
Values may be sent and summed in bfloat16 or wider, within the bound.
No kernel may reach another device: no remote copies, remote signals or barrier semaphores. Data moves between devices by JAX's collectives and lax.ppermute only.
A program may use at most 128 MiB of HBM per device.

v0:
```python
import jax
import jax.numpy as jnp
from jax import lax
from jax.sharding import PartitionSpec as P

ROPE_BASE = 1000000.0
EPSILON = 1e-06
SCALE = 168.0 ** (-0.5)
NEGATIVE = -1e30


def normed(vectors, scaling):
    return (
        vectors * lax.rsqrt(jnp.mean(vectors * vectors, axis=-1, keepdims=True) + EPSILON) * scaling
    )


def rotated(vectors, token_positions):
    half_width = vectors.shape[-1] // 2
    frequency = ROPE_BASE ** (-2.0 * jnp.arange(half_width, dtype=jnp.float32) / vectors.shape[-1])
    angles = token_positions.astype(jnp.float32)[:, None] * frequency[None, :]
    cosines = jnp.cos(angles)[:, None, :]
    sines = jnp.sin(angles)[:, None, :]
    leading = vectors[..., :half_width]
    trailing = vectors[..., half_width:]
    return jnp.concatenate(
        [leading * cosines - trailing * sines, trailing * cosines + leading * sines], axis=-1
    )


def prepare(vectors, token_positions, scaling, head_width):
    row_total = vectors.shape[0]
    shaped = vectors.astype(jnp.float32).reshape(row_total, -1, head_width)
    return (
        rotated(normed(shaped, scaling), token_positions)
        .astype(jnp.bfloat16)
        .reshape(row_total, -1)
    )


def refold(stacked):
    ctx_count = lax.axis_size("ctx")
    ctx_place = lax.axis_index("ctx")
    half_rows = stacked.shape[0] // 2
    piece_rows = stacked.shape[0] // ctx_count
    spread = lax.all_to_all(stacked, "ctx", split_axis=0, concat_axis=0, tiled=True)
    parity = (ctx_place >= ctx_count // 2).astype(jnp.int32)
    targets = jnp.arange(ctx_count, dtype=jnp.int32)
    wanted = jnp.where(targets % 2 == parity, targets, 2 * ctx_count - 1 - targets)
    sources = wanted // 2
    arranged = jnp.take(spread.reshape(ctx_count, piece_rows, -1), sources, axis=0).reshape(
        stacked.shape
    )
    collected = lax.all_to_all(arranged, "ctx", split_axis=0, concat_axis=0, tiled=True)
    first_half = collected[:half_rows]
    second_half = collected[half_rows:]
    even_place = ctx_place % 2 == 0
    lower_rows = jnp.where(even_place, first_half, second_half)
    upper_rows = jnp.where(even_place, second_half, first_half)
    return jnp.concatenate([lower_rows, upper_rows], axis=0)


def token_index(row_marks, ctx_count, block_rows):
    owner_slot = row_marks // (2 * block_rows)
    within = row_marks % (2 * block_rows)
    block_id = jnp.where(within < block_rows, owner_slot, 2 * ctx_count - 1 - owner_slot)
    return block_id * block_rows + within % block_rows


def attend(running, query_half, query_marks, key_piece, value_piece, key_marks, head_width):
    highest, totals, summed = running
    row_total = query_half.shape[0]
    kv_heads = key_piece.shape[1] // head_width
    query_heads = query_half.reshape(row_total, kv_heads, -1, head_width)
    key_heads = key_piece.reshape(-1, kv_heads, head_width)
    value_heads = value_piece.reshape(-1, kv_heads, head_width)
    scores = (
        jnp.einsum("qgrd,kgd->grqk", query_heads, key_heads, preferred_element_type=jnp.float32)
        * SCALE
    )
    visible = key_marks[None, :] <= query_marks[:, None]
    scores = jnp.where(visible, scores, NEGATIVE)
    new_highest = jnp.maximum(highest, jnp.max(scores, axis=-1))
    weights = jnp.where(visible, jnp.exp(scores - new_highest[..., None]), 0.0)
    totals = jnp.sum(weights, axis=-1)
    update = jnp.einsum(
        "grqk,kgd->grqd",
        weights.astype(jnp.bfloat16),
        value_heads,
        preferred_element_type=jnp.float32,
    )
    summed = update
    return (new_highest, totals, summed)


def attention(query_rows, query_marks, key_rows, value_rows, ctx_count, block_rows, head_width):
    kv_heads = key_rows.shape[1] // head_width
    groups = query_rows.shape[1] // key_rows.shape[1]
    halves = (query_rows[:block_rows], query_rows[block_rows:])
    empty = (
        jnp.full((kv_heads, groups, block_rows), NEGATIVE, jnp.float32),
        jnp.zeros((kv_heads, groups, block_rows), jnp.float32),
        jnp.zeros((kv_heads, groups, block_rows, head_width), jnp.float32),
    )

    def absorb(states, arrived):
        key_piece, value_piece = arrived
        row_marks = jnp.arange(key_piece.shape[0], dtype=jnp.int32)
        key_marks = token_index(row_marks, ctx_count, block_rows)
        updated = []
        for which_half in range(2):

            def compute_half(running, which_half=which_half):
                return attend(
                    running,
                    halves[which_half],
                    query_marks[which_half],
                    key_piece,
                    value_piece,
                    key_marks,
                    head_width,
                )

            def keep_half(running):
                return running

            needed = jnp.min(key_marks) <= jnp.max(query_marks[which_half])
            updated.append(lax.cond(needed, compute_half, keep_half, states[which_half]))
        return (updated[0], updated[1])

    finished = absorb(
        (empty, empty),
        (
            lax.all_gather(key_rows, "ctx", axis=0, tiled=True),
            lax.all_gather(value_rows, "ctx", axis=0, tiled=True),
        ),
    )
    outputs = []
    for which_half in range(2):
        normal = finished[which_half][2] / finished[which_half][1][..., None]
        outputs.append(jnp.transpose(normal, (2, 0, 1, 3)).reshape(block_rows, -1))
    return jnp.concatenate(outputs, axis=0).astype(jnp.bfloat16)


def on_device(queries, keys, values, positions, query_gain, key_gain, out_weight):
    head_width = query_gain.shape[0]
    ctx_count = lax.axis_size("ctx")
    ctx_place = lax.axis_index("ctx")
    row_total = queries.shape[0]
    block_rows = row_total // 2
    query_rows = prepare(queries, positions, query_gain, head_width)
    key_rows = prepare(keys, positions, key_gain, head_width)
    query_cols = query_rows.shape[1]
    key_cols = key_rows.shape[1]
    offsets = jnp.arange(block_rows, dtype=jnp.int32)
    folded_marks = (
        ctx_place * block_rows + offsets,
        (2 * ctx_count - 1 - ctx_place) * block_rows + offsets,
    )
    refolded = refold(jnp.concatenate([query_rows, key_rows, values], axis=1))
    query_rows = refolded[:, :query_cols]
    key_rows = refolded[:, query_cols : query_cols + key_cols]
    value_rows = refolded[:, query_cols + key_cols :]
    attended = attention(
        query_rows, folded_marks, key_rows, value_rows, ctx_count, block_rows, head_width
    )
    return lax.psum_scatter(
        jnp.dot(attended, out_weight, preferred_element_type=jnp.float32).astype(jnp.bfloat16),
        "head",
        scatter_dimension=0,
        tiled=True,
    )


def solution(mesh):
    return jax.shard_map(
        on_device,
        mesh=mesh,
        in_specs=(
            P("ctx", "head"),
            P("ctx", "head"),
            P("ctx", "head"),
            P("ctx"),
            P(),
            P(),
            P("head", None),
        ),
        out_specs=P(("ctx", "head"), None),
        check_vma=False,
    )
```

profile of v0, /device:TPU:1, one launch (start us, length us, event | category | flops | bytes accessed | tf_op | source)
XLA Modules:
  0.0 775.7 jit_solution(2820541000050140139)
XLA Ops:
  6.5 1.0 reshape.252
  7.5 0.2 multiply_reduce_fusion
  7.8 0.7 convert_element_type.39
  8.4 0.9 multiply_multiply_fusion
  9.3 0.3 multiply_cosine_fusion
  9.6 0.3 subtract_convert_fusion
  9.9 0.2 pad_maximum_fusion.1
  10.2 0.9 reshape.254
  11.1 0.2 multiply_reduce_fusion.1
  11.3 0.9 multiply_multiply_fusion.1
  12.2 0.3 subtract_convert_fusion.1
  12.5 0.2 pad_maximum_fusion.2
  12.7 0.9 concatenate.23
  13.6 0.9 pad_maximum_fusion
  14.5 13.6 %all-to-all-start = ((bf16[64,2,1024]{2,1,0:T(2,128)(2,1)}), bf16[64,2,1024]{2,1,0:T(2,128)(2,1)S(1)}, u32[]{:S(2)}, u32[]{:S(2)}) async-start(bf16[64,2,1024]{2,1,0:T(2,128)(2,1)} %pad_maximum_fusion), calls=%async_computation | async-start | bytes 524288 | tf_op jit(solution)/shard_map/all_to_all | solution.py:46
  28.2 11.5 %all-to-all-done = bf16[64,2,1024]{2,1,0:T(2,128)(2,1)S(1)} async-done(((bf16[64,2,1024]{2,1,0:T(2,128)(2,1)}), bf16[64,2,1024]{2,1,0:T(2,128)(2,1)S(1)}, u32[]{:S(2)}, u32[]{:S(2)}) %all-to-all-start) | async-done | bytes 262176 | tf_op jit(solution)/shard_map/all_to_all | solution.py:46
  39.6 1.1 gather_fusion
  40.7 1.0 broadcast_select_fusion
  41.8 6.0 all-to-all-start.1
  47.8 10.9 %all-to-all-done.1 = bf16[64,2,1024]{2,1,0:T(2,128)(2,1)S(1)} async-done(((bf16[64,2,1024]{2,1,0:T(2,128)(2,1)}), bf16[64,2,1024]{2,1,0:T(2,128)(2,1)S(1)}, u32[]{:S(2)}, u32[]{:S(2)}) %all-to-all-start.1) | async-done | bytes 262176 | tf_op jit(solution)/shard_map/all_to_all | solution.py:54
  58.7 0.2 broadcast_select_fusion.1
  59.1 0.7 fusion.49
  59.8 0.7 all-gather.5.cloned.1.call-update
  60.6 0.7 fusion.45
  61.3 0.6 fusion.42
  64.4 254.4 %all-gather.3.cloned.1.call-done = bf16[8192,256]{1,0:T(8,128)(2,1)} async-done(((bf16[128,256]{1,0:T(8,128)(2,1)}), bf16[8192,256]{1,0:T(8,128)(2,1)}) %all-gather.3.cloned.1.call-update) | async-done | bytes 4194320 | tf_op jit(solution)/shard_map/all_gather | solution.py:134
  318.9 303.4 %all-gather.5.cloned.1.call-done = bf16[8192,256]{1,0:T(8,128)(2,1)} async-done(((bf16[128,256]{1,0:T(8,128)(2,1)}), bf16[8192,256]{1,0:T(8,128)(2,1)}) %all-gather.5.cloned.1.call-update) | async-done | bytes 4194320 | tf_op jit(solution)/shard_map/all_gather | solution.py:135
  622.2 31.0 %conditional.2 = (f32[2,2,64]{2,1,0:T(2,128)S(1)}, f32[2,2,64,128]{3,2,1,0:T(8,128)S(1)}) conditional(s32[]{:T(128)} %convert_element_type.37, () %tuple.21, (s32[8192]{0:T(1024)S(1)}, s32[64]{0:T(128)S(1)}, bf16[8192,256]{1,0:T(8,128)(2,1)}, bf16[64,1024]{1,0:T(8,128)(2,1)S(1)}, bf16[8192,256]{1,0:T(8,128)(2,1)}) %tuple.22), branch_computations={%region_4.5_spmd, %region_5.8_spmd} | conditional | flops 1093140224 | bytes 86481200 | solution.py:128
  622.2 0.3 broadcast_compare_fusion
  622.6 6.9 reshape.233
  629.5 7.8 fusion.47
  637.3 6.9 reshape.235
  644.2 6.8 fusion.4
  651.0 0.2 copy-done
  651.2 2.0 fusion.3
  653.2 0.1 fusion.33
  653.4 0.1 copy.40
  653.5 31.3 %conditional.3 = (f32[2,2,64]{2,1,0:T(2,128)S(1)}, f32[2,2,64,128]{3,2,1,0:T(8,128)S(1)}) conditional(s32[]{:T(128)} %convert_element_type.42, () %tuple.23, (s32[8192]{0:T(1024)S(1)}, s32[64]{0:T(128)S(1)}, bf16[8192,256]{1,0:T(8,128)(2,1)}, bf16[64,1024]{1,0:T(8,128)(2,1)S(1)}, bf16[8192,256]{1,0:T(8,128)(2,1)}) %tuple.24), branch_computations={%region_9.10_spmd, %region_10.13_spmd} | conditional | flops 1093140224 | bytes 86481200 | solution.py:128
  653.7 0.3 broadcast_compare_fusion.1
  654.1 6.9 reshape.236
  661.0 7.8 fusion.48
  668.8 6.9 reshape.238
  675.7 6.8 fusion.17
  682.5 0.2 copy-done.1
  682.7 2.0 fusion.16
  684.7 0.1 fusion.34
  685.0 4.5 convolution_convert_fusion
  689.5 79.7 %reduce-scatter.2.cloned.1.call-done = bf16[32,5376]{1,0:T(8,128)(2,1)} async-done(((bf16[128,5376]{1,0:T(8,128)(2,1)}), bf16[32,5376]{1,0:T(8,128)(2,1)}) %reduce-scatter.2.cloned.1.call-update) | async-done | bytes 344080 | tf_op jit(solution)/shard_map/reduce_scatter | solution.py:167
  (31 shorter events, 0.7 us)
Async XLA Ops:
  14.5 25.1 %all-to-all-start = ((bf16[64,2,1024]{2,1,0:T(2,128)(2,1)}), bf16[64,2,1024]{2,1,0:T(2,128)(2,1)S(1)}, u32[]{:S(2)}, u32[]{:S(2)}) async-start(bf16[64,2,1024]{2,1,0:T(2,128)(2,1)} %pad_maximum_fusion), calls=%async_computation | async-start | bytes 524288 | tf_op jit(solution)/shard_map/all_to_all | solution.py:46
  41.8 17.0 %all-to-all-start.1 = ((bf16[64,2,1024]{2,1,0:T(2,128)(2,1)}), bf16[64,2,1024]{2,1,0:T(2,128)(2,1)S(1)}, u32[]{:S(2)}, u32[]{:S(2)}) async-start(bf16[64,2,1024]{2,1,0:T(2,128)(2,1)} %broadcast_select_fusion), calls=%async_computation.1 | async-start | bytes 524288 | tf_op jit(solution)/shard_map/all_to_all | solution.py:54
  47.8 271.1 %all-gather.3.cloned.1.call-start = ((), (), s32[]{:S(2)}) async-start(), calls=%async_computation.3 | async-start | bytes 4259840 | tf_op jit(solution)/shard_map/all_gather | solution.py:134
  59.8 562.4 %all-gather.5.cloned.1.call-start = ((), (), s32[]{:S(2)}) async-start(), calls=%async_computation.4 | async-start | bytes 4259840 | tf_op jit(solution)/shard_map/all_gather | solution.py:135
  60.5 708.7 %reduce-scatter.2.cloned.1.call-start = ((), (), s32[]{:S(2)}) async-start(), calls=%async_computation.5 | async-start | bytes 1720320 | tf_op jit(solution)/shard_map/reduce_scatter | solution.py:167
  644.2 7.0 copy-start
  675.7 7.0 copy-start.1
Sparse Core Ops, SparseCore 0:
  59.9 258.9 all-gather.2
  320.6 301.5 all-gather.4
  689.7 79.4 reduce-scatter.1
where the time goes:
time: 777 us; the launch traced here: 776 us
  waiting for transfers between devices  661 us (85%)
  matrix products  33.6 us (4%)
  local copies, waits for them, and re-layouts  33.1 us (4%)
  starting transfers between devices  19.7 us (3%)
  between operations  15.8 us (2%)
  other arithmetic  12.7 us (2%)
    all_gather x1, waiting for transfers between devices, attention(): lax.all_gather(value_rows, 'ctx', axis=0, tiled=True)  303 us
    all_gather x1, waiting for transfers between devices, attention(): lax.all_gather(key_rows, 'ctx', axis=0, tiled=True)  254 us
    reduce_scatter x1, waiting for transfers between devices, on_device(): lax.psum_scatter(jnp.dot(attended, out_weight, preferred_element_type=jnp...  79.7 us
  transfers between devices with their start and end apart: 5, of which 5 were waited for; matrix products, arithmetic and copies ran while one was open for 0% of the time, Pallas kernels for 0%

commit v1 on v0

v1 whole, which is shorter than its diff:
```python
import functools

import jax
import jax.numpy as jnp
import numpy as np
from jax import lax
from jax.experimental import pallas as pl
from jax.experimental.pallas import tpu as pltpu
from jax.sharding import Mesh
from jax.sharding import PartitionSpec as P

EPSILON = 1e-06
HD = 128
PIECE = 128
NX, NY, NZ = 2, 4, 8
GROUP = NX * NY
QUERY_FACTOR = float(168.0**-0.5 / np.log(2.0))
NEGATIVE = -1e30
FREQUENCY = (1000000.0 ** (-2.0 * np.arange(64, dtype=np.float64) / 128)).astype(np.float32)
VMEM_LIMIT = 48 * 1024 * 1024
NT = (((1,), (1,)), ((), ()))


def pairs(count, partner):
    return [(i, partner(i)) for i in range(count)]


Z_PAIRS = (pairs(NZ, lambda i: i ^ 1), pairs(NZ, lambda i: (((i + 1) ^ 1) + 7) % 8))
Y_PAIRS = (pairs(NY, lambda i: i ^ 1), pairs(NY, lambda i: i ^ 3))
X_PAIRS = pairs(NX, lambda i: i ^ 1)


def prepare_kernel(q_ref, k_ref, pos_ref, freq_ref, qg_ref, kg_ref, q_out, k_out):
    lane = lax.broadcasted_iota(jnp.int32, (PIECE, HD), 1)
    angles = pos_ref[...].astype(jnp.float32) * freq_ref[...]
    cosines = jnp.cos(angles)
    sines = jnp.where(lane < HD // 2, -1.0, 1.0) * jnp.sin(angles)

    def rotate(vector, gain):
        vector = vector.astype(jnp.float32)
        normed = vector * lax.rsqrt(jnp.mean(vector * vector, axis=-1, keepdims=True) + EPSILON) * gain
        return normed * cosines + pltpu.roll(normed, HD // 2, 1) * sines

    for head in range(4):
        cols = slice(head * HD, (head + 1) * HD)
        q_out[:, cols] = (rotate(q_ref[:, cols], qg_ref[...]) * QUERY_FACTOR).astype(jnp.bfloat16)
    for head in range(2):
        cols = slice(head * HD, (head + 1) * HD)
        k_out[:, cols] = rotate(k_ref[:, cols], kg_ref[...]).astype(jnp.bfloat16)


def prepare(queries, keys, positions, query_gain, key_gain):
    freq = jnp.asarray(np.concatenate([FREQUENCY, FREQUENCY])[None, :])
    return pl.pallas_call(
        prepare_kernel,
        out_shape=(
            jax.ShapeDtypeStruct(queries.shape, jnp.bfloat16),
            jax.ShapeDtypeStruct(keys.shape, jnp.bfloat16),
        ),
    )(queries, keys, positions[:, None], freq, query_gain[None, :], key_gain[None, :])


def gather_z(own, first):
    here, there = Z_PAIRS[first], Z_PAIRS[1 - first]
    one = lax.ppermute(own, "z", here)
    two = lax.ppermute(jnp.concatenate([own, one], axis=0), "z", there)
    three = lax.ppermute(two, "z", here)
    four = lax.ppermute(three, "z", there)
    return [own, one, two, three, four]


def z_partner(which, z):
    return z ^ 1 if which == 0 else (((z + 1) ^ 1) + 7) & 7


def z_order(first, z):
    here = functools.partial(z_partner, first)
    there = functools.partial(z_partner, 1 - first)
    two = [there(z), here(there(z))]
    near = here(z)
    three = [there(near), here(there(near))]
    far = there(z)
    far_near = here(far)
    four = [there(far_near), here(there(far_near))]
    return [z, near] + two + three + four


def gather_xy(own):
    both = jnp.concatenate([own, lax.ppermute(own, "x", X_PAIRS)], axis=0)
    result = []
    for half in range(2):
        cols = both[:, half * 2 * HD : (half + 1) * 2 * HD]
        near = lax.ppermute(cols, "y", Y_PAIRS[half])
        far = lax.ppermute(jnp.concatenate([cols, near], axis=0), "y", Y_PAIRS[1 - half])
        result.append((near, far))
    return both, result


Y_STEPS = ((1, 3, 2), (3, 1, 2))


def attention_kernel(ids_ref, *refs):
    (q_both, near0, far0, near1, far1, k0, k1, k2, k3, k4, v0, v1, v2, v3, v4,
     out_ref, q_s, k_s, vt_s, v_s) = refs
    group = ids_ref[0]
    z = ids_ref[1]
    for half, (near, far) in enumerate(((near0, far0), (near1, far1))):
        first, second, third = Y_STEPS[half]
        for rel_y, ref, base, col in (
            (0, q_both, 0, half * 2 * HD),
            (first, near, 0, 0),
            (second, far, 0, 0),
            (third, far, 2 * PIECE, 0),
        ):
            for rel_x in range(NX):
                rows = slice(base + rel_x * PIECE, base + (rel_x + 1) * PIECE)
                for j in range(2):
                    q_s[half, rel_x * NY + rel_y, j * PIECE : (j + 1) * PIECE, :] = ref[
                        rows, col + j * HD : col + (j + 1) * HD
                    ]
    for first, pieces, dest in ((0, (k0, k1, k2, k3, k4), k_s), (1, (v0, v1, v2, v3, v4), v_s)):
        places = z_order(first, z)
        index = 0
        for piece in pieces:
            for part in range(piece.shape[0] // PIECE):
                start = pl.multiple_of(places[index] * PIECE, PIECE)
                dest[pl.ds(start, PIECE), :] = piece[part * PIECE : (part + 1) * PIECE, :]
                index += 1
    for half in range(2):
        vt_s[half] = jnp.transpose(v_s[:, half * HD : (half + 1) * HD])

    keys = NZ * PIECE

    def one(half, step, masked):
        query = q_s[half, step]
        scores = lax.dot_general(
            k_s[:, half * HD : (half + 1) * HD], query, NT, preferred_element_type=jnp.float32
        )
        if masked:
            key_row = lax.broadcasted_iota(jnp.int32, (keys, 2 * PIECE), 0)
            query_row = lax.broadcasted_iota(jnp.int32, (keys, 2 * PIECE), 1) % PIECE + z * PIECE
            scores = jnp.where(key_row <= query_row, scores, NEGATIVE)
        highest = jnp.max(scores, axis=0, keepdims=True)
        weights = jnp.exp2(scores - highest)
        total = jnp.sum(weights, axis=0, keepdims=True)
        summed = jnp.dot(vt_s[half], weights.astype(jnp.bfloat16), preferred_element_type=jnp.float32)
        normal = (summed / total).astype(jnp.bfloat16)
        level = highest + jnp.log2(total)
        top = level.astype(jnp.bfloat16)
        rest = level - top.astype(jnp.float32)
        middle = rest.astype(jnp.bfloat16)
        low = (rest - middle.astype(jnp.float32)).astype(jnp.bfloat16)
        for j in range(2):
            head = half * 2 + j
            lanes = slice(j * PIECE, (j + 1) * PIECE)
            out_ref[step, head * HD : (head + 1) * HD, :] = normal[:, lanes]
        return [part[:, j * PIECE : (j + 1) * PIECE] for j in range(2) for part in (top, middle, low)]

    def store_levels(step, rows):
        block = jnp.concatenate([r.astype(jnp.float32) for r in rows] + [jnp.zeros((4, PIECE), jnp.float32)], axis=0)
        out_ref[step, 4 * HD : 4 * HD + 16, :] = block.astype(jnp.bfloat16)

    store_levels(0, one(0, 0, True) + one(1, 0, True))

    def body(step, carry):
        seen = (group ^ step) > group

        @pl.when(seen)
        def _():
            store_levels(step, one(0, step, False) + one(1, step, False))

        @pl.when(jnp.logical_not(seen))
        def _():
            out_ref[step, 0 : 4 * HD, :] = jnp.zeros((4 * HD, PIECE), jnp.bfloat16)
            out_ref[step, 4 * HD : 4 * HD + 16, :] = jnp.full((16, PIECE), NEGATIVE, jnp.bfloat16)

        return carry

    lax.fori_loop(1, GROUP, body, 0)


def attention(ids, both, halves, keys, values):
    vmem = pl.BlockSpec(memory_space=pltpu.VMEM)
    smem = pl.BlockSpec(memory_space=pltpu.SMEM)
    (near0, far0), (near1, far1) = halves
    return pl.pallas_call(
        attention_kernel,
        out_shape=jax.ShapeDtypeStruct((GROUP, 4 * HD + 16, PIECE), jnp.bfloat16),
        in_specs=[smem] + [vmem] * 15,
        out_specs=vmem,
        scratch_shapes=[
            pltpu.VMEM((2, GROUP, 2 * PIECE, HD), jnp.bfloat16),
            pltpu.VMEM((NZ * PIECE, 2 * HD), jnp.bfloat16),
            pltpu.VMEM((2, HD, NZ * PIECE), jnp.bfloat16),
            pltpu.VMEM((NZ * PIECE, 2 * HD), jnp.bfloat16),
        ],
        compiler_params=pltpu.CompilerParams(vmem_limit_bytes=VMEM_LIMIT),
    )(ids, both, near0, far0, near1, far1, *keys, *values)


def combine_kernel(*refs):
    pieces, out_ref = refs[:-1], refs[-1]
    stats = [r[4 * HD : 4 * HD + 16, :].astype(jnp.float32) for r in pieces]
    for head in range(4):
        levels = [
            s[3 * head : 3 * head + 1] + s[3 * head + 1 : 3 * head + 2] + s[3 * head + 2 : 3 * head + 3]
            for s in stats
        ]
        highest = functools.reduce(jnp.maximum, levels)
        shares = [jnp.exp2(level - highest) for level in levels]
        scale = 1.0 / functools.reduce(jnp.add, shares)
        total = None
        for share, piece in zip(shares, pieces):
            term = piece[head * HD : (head + 1) * HD, :].astype(jnp.float32) * (share * scale)
            total = term if total is None else total + term
        out_ref[:, head * HD : (head + 1) * HD] = jnp.transpose(total).astype(jnp.bfloat16)


def combine(pieces):
    return pl.pallas_call(
        combine_kernel,
        out_shape=jax.ShapeDtypeStruct((PIECE, 4 * HD), jnp.bfloat16),
    )(*pieces)


def on_device(queries, keys, values, positions, query_gain, key_gain, out_weight):
    x, y, z = lax.axis_index("x"), lax.axis_index("y"), lax.axis_index("z")
    w, c = lax.axis_index("w"), lax.axis_index("c")
    ids = jnp.stack([x * NY + y, z]).astype(jnp.int32)
    query_rows, key_rows = prepare(queries, keys, positions, query_gain, key_gain)
    value_pieces = gather_z(values, 1)
    key_pieces = gather_z(key_rows, 0)
    both, halves = gather_xy(query_rows)
    partial = attention(ids, both, halves, key_pieces, value_pieces)
    received = [partial[0]] + [
        lax.ppermute(partial[step], ("x", "y"), pairs(GROUP, lambda i: i ^ step)) for step in range(1, GROUP)
    ]
    attended = combine(received)
    even = lax.ppermute(
        attended[: PIECE // 2], ("x", "y", "z"), pairs(64, lambda i: 2 * i if i < 32 else 127 - 2 * i)
    )
    odd = lax.ppermute(
        attended[PIECE // 2 :], ("x", "y", "z"), pairs(64, lambda i: 2 * i + 1 if i < 32 else 126 - 2 * i)
    )
    low = jnp.where(z % 2 == 0, even, odd)
    high = jnp.where(z % 2 == 0, odd, even)
    folded = jnp.stack([low, high]).reshape(2, 2, PIECE // 4, 4 * HD)
    mine = lax.dynamic_index_in_dim(folded, c, 1, keepdims=False)
    other = lax.dynamic_index_in_dim(folded, 1 - c, 1, keepdims=False)
    rows = jnp.concatenate([other, mine], axis=0).reshape(PIECE, 4 * HD)
    product = jnp.dot(rows, out_weight, preferred_element_type=jnp.float32).astype(jnp.bfloat16)
    product = product.reshape(2, 2, PIECE // 4, -1)
    got = lax.ppermute(product[0], "c", X_PAIRS)
    chip = product[1].astype(jnp.float32) + got.astype(jnp.float32)
    keep = lax.dynamic_index_in_dim(chip, w, 0, keepdims=False)
    give = lax.dynamic_index_in_dim(chip, 1 - w, 0, keepdims=False).astype(jnp.bfloat16)
    taken = lax.ppermute(give, "w", X_PAIRS)
    return (keep + taken.astype(jnp.float32)).astype(jnp.bfloat16)


def solution(mesh):
    inner = Mesh(mesh.devices.reshape(NX, NY, NZ, 2, 2), ("x", "y", "z", "w", "c"))
    ctx, head = ("x", "y", "z"), ("w", "c")
    return jax.shard_map(
        on_device,
        mesh=inner,
        in_specs=(P(ctx, head), P(ctx, head), P(ctx, head), P(ctx), P(), P(), P(head, None)),
        out_specs=P(ctx + head, None),
        check_vma=False,
    )
```

time: 777 us -> 103 us (0.13)
  the two profiles are of different devices: /device:TPU:1 before, /device:TPU:64 now
where the time goes in v1:
time: 103 us; the launch traced here: 102 us
  starting transfers between devices  38.9 us (38%)
  waiting for transfers between devices  35.1 us (34%)
  Pallas kernels  17.1 us (17%)
  local copies, waits for them, and re-layouts  4.69 us (5%)
  matrix products  3.46 us (3%)
  other arithmetic  2.78 us (3%)
    pallas_call x1, Pallas kernels, attention(): pl.pallas_call(attention_kernel, out_shape=jax.ShapeDtypeStruct((GROUP, 4...  12.4 us
    ppermute x7, starting transfers between devices, on_device(): lax.ppermute(partial[step], ('x', 'y'), pairs(GROUP, lambda i: i ^ step))  10.4 us
    ppermute x1, waiting for transfers between devices, on_device(): taken = lax.ppermute(give, 'w', X_PAIRS)  8.88 us
    ppermute x1, waiting for transfers between devices, on_device(): lax.ppermute(attended[PIECE // 2:], ('x', 'y', 'z'), pairs(64, lambda i:...  7.5 us
    ppermute x7, waiting for transfers between devices, on_device(): lax.ppermute(partial[step], ('x', 'y'), pairs(GROUP, lambda i: i ^ step))  5.79 us
    ppermute x1, starting transfers between devices, on_device(): lax.ppermute(attended[PIECE // 2:], ('x', 'y', 'z'), pairs(64, lambda i:...  5.54 us
    ppermute x2, starting transfers between devices, gather_z(): two = lax.ppermute(jnp.concatenate([own, one], axis=0), 'z', there)  4.64 us
    ppermute x2, waiting for transfers between devices, gather_xy(): near = lax.ppermute(cols, 'y', Y_PAIRS[half])  4.33 us
  transfers between devices with their start and end apart: 24, of which 15 were waited for; matrix products, arithmetic and copies ran while one was open for 3% of the time, Pallas kernels for 0%

profile of v1, /device:TPU:64, one launch (start us, length us, event | category | flops | bytes accessed | tf_op | source)
XLA Modules:
  0.0 102.2 jit_solution(14455738251465786232)
XLA Ops:
  0.0 1.4 %copy.9.pos_ref = s32[128,1]{1,0:T(8,128)} copy(s32[128,1]{0,1:T(1,128)} %bitcast.44) | data formatting | bytes 1024 | tf_op jit(solution)/shard_map/broadcast_in_dim | solution.py:60
  1.4 2.4 %shard_map.82 = (bf16[128,512]{1,0:T(8,128)(2,1)}, bf16[128,256]{1,0:T(8,128)(2,1)}) custom-call(bf16[128,512]{1,0:T(8,128)(2,1)} %q_ref.1, bf16[128,256]{1,0:T(8,128)(2,1)} %k_ref.1, s32[128,1]{1,0:T(8,128)} %copy.9.pos_ref, f32[1,128]{1,0:T(1,128)} %constant.56.clone.freq_ref, f32[1,128]{1,0:T(1,128)} %bitcast.45, f32[1,128]{1,0:T(1,128)} %bitcast.46), custom_call_target="tpu_custom_call" | custom-call | tf_op jit(solution)/shard_map/pallas_call | solution.py:54
  3.8 1.5 %collective-permute-start = (bf16[128,512]{1,0:T(8,128)(2,1)}, bf16[128,512]{1,0:T(8,128)(2,1)S(1)}, u32[]{:S(2)}, u32[]{:S(2)}) collective-permute-start(bf16[128,512]{1,0:T(8,128)(2,1)} %get-tuple-element.7), channel_id=1, source_target_pairs={{0,128},{128,0},{1,129},{129,1},{2,130},{130,2},{3,131},{131,3},{4... | collective-permute-start | bytes 393224 | tf_op jit(solution)/shard_map/ppermute | solution.py:89
  5.3 1.9 %collective-permute-start.5 = (bf16[128,256]{1,0:T(8,128)(2,1)}, bf16[128,256]{1,0:T(8,128)(2,1)S(1)}, u32[]{:S(2)}, u32[]{:S(2)}) collective-permute-start(bf16[128,256]{1,0:T(8,128)(2,1)} %get-tuple-element.8.refs_5_), channel_id=1, source_target_pairs={{0,4},{4,0},{8,12},{12,8},{16,20},{20,16},{24,28},{28,24},{1,5},{5... | collective-permute-start | bytes 196616 | tf_op jit(solution)/shard_map/ppermute | solution.py:65
  7.2 0.9 constant_dynamic-update-slice_fusion.1
  8.1 1.6 %collective-permute-done.5.refs_6_ = bf16[128,256]{1,0:T(8,128)(2,1)S(1)} collective-permute-done((bf16[128,256]{1,0:T(8,128)(2,1)}, bf16[128,256]{1,0:T(8,128)(2,1)S(1)}, u32[]{:S(2)}, u32[]{:S(2)}) %collective-permute-start.5) | collective-permute-done | bytes 65568 | tf_op jit(solution)/shard_map/ppermute | solution.py:65
  9.8 0.8 pad_maximum_fusion.2
  10.6 0.5 collective-permute-start.6
  11.1 0.6 collective-permute-done.9.refs_11_
  11.7 0.8 pad_maximum_fusion.3
  12.5 4.2 %collective-permute-start.10 = (bf16[256,256]{1,0:T(8,128)(2,1)S(1)}, bf16[256,256]{1,0:T(8,128)(2,1)S(1)}, u32[]{:S(2)}, u32[]{:S(2)}) collective-permute-start(bf16[256,256]{1,0:T(8,128)(2,1)S(1)} %pad_maximum_fusion.3), channel_id=1, source_target_pairs={{0,4},{4,0},{8,12},{12,8},{16,20},{20,16},{24,28},{28,24},{1,5},{5... | collective-permute-start | bytes 393224 | tf_op jit(solution)/shard_map/ppermute | solution.py:66
  16.8 3.1 %collective-permute-start.3 = (bf16[256,256]{1,0:T(8,128)(2,1)S(1)}, bf16[256,256]{1,0:T(8,128)(2,1)S(1)}, u32[]{:S(2)}, u32[]{:S(2)}) collective-permute-start(bf16[256,256]{1,0:T(8,128)(2,1)S(1)} %get-tuple-element.19), channel_id=1, source_target_pairs={{0,96},{32,64},{64,32},{96,0},{1,97},{33,65},{65,33},{97,1},{2,98}... | collective-permute-start | bytes 393224 | tf_op jit(solution)/shard_map/ppermute | solution.py:93
  19.9 0.1 collective-permute-start.1
  20.0 0.3 collective-permute-done.10.refs_12_
  20.3 1.0 %collective-permute-start.11 = (bf16[256,256]{1,0:T(8,128)(2,1)S(1)}, bf16[256,256]{1,0:T(8,128)(2,1)S(1)}, u32[]{:S(2)}, u32[]{:S(2)}) collective-permute-start(bf16[256,256]{1,0:T(8,128)(2,1)S(1)} %collective-permute-done.10.refs_12_), channel_id=1, source_target_pairs={{0,28},{4,8},{8,4},{12,16},{16,12},{20,24},{24,20},{28,0},{1,29},{... | collective-permute-start | bytes 393224 | tf_op jit(solution)/shard_map/ppermute | solution.py:67
  21.4 1.6 %collective-permute-done.3.refs_3_ = bf16[256,256]{1,0:T(8,128)(2,1)S(1)} collective-permute-done((bf16[256,256]{1,0:T(8,128)(2,1)S(1)}, bf16[256,256]{1,0:T(8,128)(2,1)S(1)}, u32[]{:S(2)}, u32[]{:S(2)}) %collective-permute-start.3) | collective-permute-done | bytes 131104 | tf_op jit(solution)/shard_map/ppermute | solution.py:93
  23.0 0.5 collective-permute-start.4
  23.5 2.7 %collective-permute-done.1.refs_1_ = bf16[256,256]{1,0:T(8,128)(2,1)S(1)} collective-permute-done((bf16[256,256]{1,0:T(8,128)(2,1)S(1)}, bf16[256,256]{1,0:T(8,128)(2,1)S(1)}, u32[]{:S(2)}, u32[]{:S(2)}) %collective-permute-start.1) | collective-permute-done | bytes 131104 | tf_op jit(solution)/shard_map/ppermute | solution.py:93
  26.2 0.1 collective-permute-start.2
  26.3 1.1 %collective-permute-start.8 = (bf16[256,256]{1,0:T(8,128)(2,1)S(1)}, bf16[256,256]{1,0:T(8,128)(2,1)S(1)}, u32[]{:S(2)}, u32[]{:S(2)}) collective-permute-start(bf16[256,256]{1,0:T(8,128)(2,1)S(1)} %collective-permute-done.7.refs_8_), channel_id=1, source_target_pairs={{0,28},{4,8},{8,4},{12,16},{16,12},{20,24},{24,20},{28,0},{1,29},{... | collective-permute-start | bytes 393224 | tf_op jit(solution)/shard_map/ppermute | solution.py:68
  27.4 2.5 %collective-permute-start.12 = (bf16[256,256]{1,0:T(8,128)(2,1)S(1)}, bf16[256,256]{1,0:T(8,128)(2,1)S(1)}, u32[]{:S(2)}, u32[]{:S(2)}) collective-permute-start(bf16[256,256]{1,0:T(8,128)(2,1)S(1)} %collective-permute-done.11.refs_13_), channel_id=1, source_target_pairs={{0,4},{4,0},{8,12},{12,8},{16,20},{20,16},{24,28},{28,24},{1,5},{5... | collective-permute-start | bytes 393224 | tf_op jit(solution)/shard_map/ppermute | solution.py:68
  30.0 1.4 %collective-permute-done.8.refs_9_ = bf16[256,256]{1,0:T(8,128)(2,1)S(1)} collective-permute-done((bf16[256,256]{1,0:T(8,128)(2,1)S(1)}, bf16[256,256]{1,0:T(8,128)(2,1)S(1)}, u32[]{:S(2)}, u32[]{:S(2)}) %collective-permute-start.8) | collective-permute-done | bytes 131104 | tf_op jit(solution)/shard_map/ppermute | solution.py:68
  31.4 1.5 %collective-permute-done.12.refs_14_ = bf16[256,256]{1,0:T(8,128)(2,1)S(1)} collective-permute-done((bf16[256,256]{1,0:T(8,128)(2,1)S(1)}, bf16[256,256]{1,0:T(8,128)(2,1)S(1)}, u32[]{:S(2)}, u32[]{:S(2)}) %collective-permute-start.12) | collective-permute-done | bytes 131104 | tf_op jit(solution)/shard_map/ppermute | solution.py:68
  32.9 1.0 collective-permute-done.2.refs_2_
  33.9 12.4 %shard_map.83 = bf16[8,528,128]{2,1,0:T(8,128)(2,1)S(1)} custom-call(s32[2]{0:T(128)S(1)} %pad_add_fusion.ids_ref, bf16[256,512]{1,0:T(8,128)(2,1)S(1)} %constant_dynamic-update-slice_fusion.refs_0_, bf16[256,256]{1,0:T(8,128)(2,1)S(1)} %collective-permute-done.1.refs_1_, bf16[512,256]{1,0:T(8,128)(2,1)S(1)} %collective-permute-done.2.refs_2_, ...), custom_call_target="tpu_custom_call" | custom-call | tf_op jit(solution)/shard_map/pallas_call | solution.py:186
  46.3 0.7 slice_bitcast_fusion
  47.0 4.7 %collective-permute-start.15 = (bf16[528,128]{1,0:T(8,128)(2,1)S(1)}, bf16[528,128]{1,0:T(8,128)(2,1)S(1)}, u32[]{:S(2)}, u32[]{:S(2)}) collective-permute-start(bf16[528,128]{1,0:T(8,128)(2,1)S(1)} %get-tuple-element.15), channel_id=1, source_target_pairs={{0,96},{32,64},{64,32},{96,0},{128,224},{160,192},{192,160},{224,1... | collective-permute-start | bytes 405512 | tf_op jit(solution)/shard_map/ppermute | solution.py:236
  51.7 0.3 collective-permute-start.17
  52.0 1.3 %collective-permute-done.13.refs_1_ = bf16[528,128]{1,0:T(8,128)(2,1)S(1)} collective-permute-done((bf16[528,128]{1,0:T(8,128)(2,1)S(1)}, bf16[528,128]{1,0:T(8,128)(2,1)S(1)}, u32[]{:S(2)}, u32[]{:S(2)}) %collective-permute-start.13) | collective-permute-done | bytes 135200 | tf_op jit(solution)/shard_map/ppermute | solution.py:236
  53.2 0.9 collective-permute-start.18
  54.1 0.2 collective-permute-done.14.refs_2_
  54.2 4.5 %collective-permute-start.19 = (bf16[528,128]{1,0:T(8,128)(2,1)S(1)}, bf16[528,128]{1,0:T(8,128)(2,1)S(1)}, u32[]{:S(2)}, u32[]{:S(2)}) collective-permute-start(bf16[528,128]{1,0:T(8,128)(2,1)S(1)} %get-tuple-element.11), channel_id=1, source_target_pairs={{0,224},{32,192},{64,160},{96,128},{128,96},{160,64},{192,32},{224... | collective-permute-start | bytes 405512 | tf_op jit(solution)/shard_map/ppermute | solution.py:236
  58.8 1.8 %collective-permute-done.18.refs_6_ = bf16[528,128]{1,0:T(8,128)(2,1)S(1)} collective-permute-done((bf16[528,128]{1,0:T(8,128)(2,1)S(1)}, bf16[528,128]{1,0:T(8,128)(2,1)S(1)}, u32[]{:S(2)}, u32[]{:S(2)}) %collective-permute-start.18) | collective-permute-done | bytes 135200 | tf_op jit(solution)/shard_map/ppermute | solution.py:236
  60.6 2.6 %collective-permute-done.19.refs_7_ = bf16[528,128]{1,0:T(8,128)(2,1)S(1)} collective-permute-done((bf16[528,128]{1,0:T(8,128)(2,1)S(1)}, bf16[528,128]{1,0:T(8,128)(2,1)S(1)}, u32[]{:S(2)}, u32[]{:S(2)}) %collective-permute-start.19) | collective-permute-done | bytes 135200 | tf_op jit(solution)/shard_map/ppermute | solution.py:236
  63.2 0.6 copy-done.8
  63.8 2.3 %shard_map.84 = bf16[128,512]{1,0:T(8,128)(2,1)} custom-call(bf16[528,128]{1,0:T(8,128)(2,1)} %get-tuple-element.18.refs_0_, bf16[528,128]{1,0:T(8,128)(2,1)} %copy-done.2, bf16[528,128]{1,0:T(8,128)(2,1)} %copy-done.3, bf16[528,128]{1,0:T(8,128)(2,1)} %copy-done.4, bf16[528,128]{1,0:T(8,128)(2,1)} %copy-done.5, bf16[528,128]{1,0:T(8,128)(2,1)} %copy-done.6, ...), custom_call_target="tpu_custom_call" | custom-call | tf_op jit(solution)/shard_map/pallas_call | solution.py:220
  66.1 0.9 fusion.8
  67.0 3.6 %collective-permute-start.20 = (bf16[64,512]{1,0:T(8,128)(2,1)S(1)}, bf16[64,512]{1,0:T(8,128)(2,1)S(1)}, u32[]{:S(2)}, u32[]{:S(2)}) collective-permute-start(bf16[64,512]{1,0:T(8,128)(2,1)S(1)} %get-tuple-element.26), channel_id=1, source_target_pairs={{0,0},{4,8},{8,16},{12,24},{16,32},{20,40},{24,48},{28,56},{32,64}... | collective-permute-start | bytes 196616 | tf_op jit(solution)/shard_map/ppermute | solution.py:239
  70.6 5.5 %collective-permute-start.21 = (bf16[64,512]{1,0:T(8,128)(2,1)S(1)}, bf16[64,512]{1,0:T(8,128)(2,1)S(1)}, u32[]{:S(2)}, u32[]{:S(2)}) collective-permute-start(bf16[64,512]{1,0:T(8,128)(2,1)S(1)} %get-tuple-element.25), channel_id=1, source_target_pairs={{0,4},{4,12},{8,20},{12,28},{16,36},{20,44},{24,52},{28,60},{32,68... | collective-permute-start | bytes 196616 | tf_op jit(solution)/shard_map/ppermute | solution.py:242
  76.2 7.5 %collective-permute-done.21 = bf16[64,512]{1,0:T(8,128)(2,1)S(1)} collective-permute-done((bf16[64,512]{1,0:T(8,128)(2,1)S(1)}, bf16[64,512]{1,0:T(8,128)(2,1)S(1)}, u32[]{:S(2)}, u32[]{:S(2)}) %collective-permute-start.21) | collective-permute-done | bytes 65568 | tf_op jit(solution)/shard_map/ppermute | solution.py:242
  83.8 3.5 %convolution_convert_fusion = bf16[128,5376]{1,0:T(8,128)(2,1)S(1)} fusion(bf16[128,512]{1,0:T(8,128)(2,1)S(1)} %bitcast.41, bf16[512,5376]{1,0:T(8,128)(2,1)} %param.14), kind=kOutput, calls=%fused_computation | convolution fusion | flops 705331200 | bytes 7012352 | tf_op jit(solution)/shard_map/dot_general | solution.py:251
  87.2 0.1 fusion.6
  87.3 0.1 collective-permute-start.22
  87.4 2.1 %collective-permute-done.22 = bf16[2,32,5376]{2,1,0:T(8,128)(2,1)S(1)} collective-permute-done((bf16[2,32,5376]{2,1,0:T(8,128)(2,1)S(1)}, bf16[2,32,5376]{2,1,0:T(8,128)(2,1)S(1)}, u32[]{:S(2)}, u32[]{:S(2)}) %collective-permute-start.22) | collective-permute-done | bytes 688160 | tf_op jit(solution)/shard_map/ppermute | solution.py:253
  89.6 0.1 convert_add_fusion
  89.7 2.8 %collective-permute-start.23 = (bf16[32,5376]{1,0:T(8,128)(2,1)S(1)}, bf16[32,5376]{1,0:T(8,128)(2,1)S(1)}, u32[]{:S(2)}, u32[]{:S(2)}) collective-permute-start(bf16[32,5376]{1,0:T(8,128)(2,1)S(1)} %fusion.1), channel_id=1, source_target_pairs={{0,2},{2,0},{1,3},{3,1},{4,6},{6,4},{5,7},{7,5},{8,10},{10,8},{9,1... | collective-permute-start | bytes 1032200 | tf_op jit(solution)/shard_map/ppermute | solution.py:257
  92.6 8.9 %collective-permute-done.23 = bf16[32,5376]{1,0:T(8,128)(2,1)S(1)} collective-permute-done((bf16[32,5376]{1,0:T(8,128)(2,1)S(1)}, bf16[32,5376]{1,0:T(8,128)(2,1)S(1)}, u32[]{:S(2)}, u32[]{:S(2)}) %collective-permute-start.23) | collective-permute-done | bytes 344096 | tf_op jit(solution)/shard_map/ppermute | solution.py:257
  101.4 0.8 fusion
  (40 shorter events, 0.3 us)
Async XLA Ops:
  3.8 30.1 %copy-start = (bf16[128,256]{1,0:T(8,128)(2,1)S(1)}, bf16[128,256]{1,0:T(8,128)(2,1)}, u32[]{:S(2)}) copy-start(bf16[128,256]{1,0:T(8,128)(2,1)} %refs_10_.1) | copy-start | bytes 196612
  3.8 30.1 %copy-start.1 = (bf16[128,256]{1,0:T(8,128)(2,1)S(1)}, bf16[128,256]{1,0:T(8,128)(2,1)}, u32[]{:S(2)}) copy-start(bf16[128,256]{1,0:T(8,128)(2,1)} %get-tuple-element.8.refs_5_) | copy-start | bytes 196612
  3.8 12.9 %collective-permute-start = (bf16[128,512]{1,0:T(8,128)(2,1)}, bf16[128,512]{1,0:T(8,128)(2,1)S(1)}, u32[]{:S(2)}, u32[]{:S(2)}) collective-permute-start(bf16[128,512]{1,0:T(8,128)(2,1)} %get-tuple-element.7), channel_id=1, source_target_pairs={{0,128},{128,0},{1,129},{129,1},{2,130},{130,2},{3,131},{131,3},{4... | collective-permute-start | bytes 393224 | tf_op jit(solution)/shard_map/ppermute | solution.py:89
  5.3 4.5 %collective-permute-start.5 = (bf16[128,256]{1,0:T(8,128)(2,1)}, bf16[128,256]{1,0:T(8,128)(2,1)S(1)}, u32[]{:S(2)}, u32[]{:S(2)}) collective-permute-start(bf16[128,256]{1,0:T(8,128)(2,1)} %get-tuple-element.8.refs_5_), channel_id=1, source_target_pairs={{0,4},{4,0},{8,12},{12,8},{16,20},{20,16},{24,28},{28,24},{1,5},{5... | collective-permute-start | bytes 196616 | tf_op jit(solution)/shard_map/ppermute | solution.py:65
  7.2 4.5 %collective-permute-start.9 = (bf16[128,256]{1,0:T(8,128)(2,1)}, bf16[128,256]{1,0:T(8,128)(2,1)S(1)}, u32[]{:S(2)}, u32[]{:S(2)}) collective-permute-start(bf16[128,256]{1,0:T(8,128)(2,1)} %refs_10_.1), channel_id=1, source_target_pairs={{0,28},{4,8},{8,4},{12,16},{16,12},{20,24},{24,20},{28,0},{1,29},{... | collective-permute-start | bytes 196616 | tf_op jit(solution)/shard_map/ppermute | solution.py:65
  10.6 9.4 %collective-permute-start.6 = (bf16[256,256]{1,0:T(8,128)(2,1)S(1)}, bf16[256,256]{1,0:T(8,128)(2,1)S(1)}, u32[]{:S(2)}, u32[]{:S(2)}) collective-permute-start(bf16[256,256]{1,0:T(8,128)(2,1)S(1)} %pad_maximum_fusion.2), channel_id=1, source_target_pairs={{0,28},{4,8},{8,4},{12,16},{16,12},{20,24},{24,20},{28,0},{1,29},{... | collective-permute-start | bytes 393224 | tf_op jit(solution)/shard_map/ppermute | solution.py:66
  12.5 7.8 %collective-permute-start.10 = (bf16[256,256]{1,0:T(8,128)(2,1)S(1)}, bf16[256,256]{1,0:T(8,128)(2,1)S(1)}, u32[]{:S(2)}, u32[]{:S(2)}) collective-permute-start(bf16[256,256]{1,0:T(8,128)(2,1)S(1)} %pad_maximum_fusion.3), channel_id=1, source_target_pairs={{0,4},{4,0},{8,12},{12,8},{16,20},{20,16},{24,28},{28,24},{1,5},{5... | collective-permute-start | bytes 393224 | tf_op jit(solution)/shard_map/ppermute | solution.py:66
  16.8 6.3 %collective-permute-start.3 = (bf16[256,256]{1,0:T(8,128)(2,1)S(1)}, bf16[256,256]{1,0:T(8,128)(2,1)S(1)}, u32[]{:S(2)}, u32[]{:S(2)}) collective-permute-start(bf16[256,256]{1,0:T(8,128)(2,1)S(1)} %get-tuple-element.19), channel_id=1, source_target_pairs={{0,96},{32,64},{64,32},{96,0},{1,97},{33,65},{65,33},{97,1},{2,98}... | collective-permute-start | bytes 393224 | tf_op jit(solution)/shard_map/ppermute | solution.py:93
  19.9 6.3 %collective-permute-start.1 = (bf16[256,256]{1,0:T(8,128)(2,1)S(1)}, bf16[256,256]{1,0:T(8,128)(2,1)S(1)}, u32[]{:S(2)}, u32[]{:S(2)}) collective-permute-start(bf16[256,256]{1,0:T(8,128)(2,1)S(1)} %get-tuple-element.20), channel_id=1, source_target_pairs={{0,32},{32,0},{64,96},{96,64},{1,33},{33,1},{65,97},{97,65},{2,34}... | collective-permute-start | bytes 393224 | tf_op jit(solution)/shard_map/ppermute | solution.py:93
  20.0 6.3 %collective-permute-start.7 = (bf16[256,256]{1,0:T(8,128)(2,1)S(1)}, bf16[256,256]{1,0:T(8,128)(2,1)S(1)}, u32[]{:S(2)}, u32[]{:S(2)}) collective-permute-start(bf16[256,256]{1,0:T(8,128)(2,1)S(1)} %collective-permute-done.6.refs_7_), channel_id=1, source_target_pairs={{0,4},{4,0},{8,12},{12,8},{16,20},{20,16},{24,28},{28,24},{1,5},{5... | collective-permute-start | bytes 393224 | tf_op jit(solution)/shard_map/ppermute | solution.py:67
  20.3 7.1 %collective-permute-start.11 = (bf16[256,256]{1,0:T(8,128)(2,1)S(1)}, bf16[256,256]{1,0:T(8,128)(2,1)S(1)}, u32[]{:S(2)}, u32[]{:S(2)}) collective-permute-start(bf16[256,256]{1,0:T(8,128)(2,1)S(1)} %collective-permute-done.10.refs_12_), channel_id=1, source_target_pairs={{0,28},{4,8},{8,4},{12,16},{16,12},{20,24},{24,20},{28,0},{1,29},{... | collective-permute-start | bytes 393224 | tf_op jit(solution)/shard_map/ppermute | solution.py:67
  23.0 9.8 %collective-permute-start.4 = (bf16[512,256]{1,0:T(8,128)(2,1)S(1)}, bf16[512,256]{1,0:T(8,128)(2,1)S(1)}, u32[]{:S(2)}, u32[]{:S(2)}) collective-permute-start(bf16[512,256]{1,0:T(8,128)(2,1)S(1)} %pad_maximum_fusion.1), channel_id=1, source_target_pairs={{0,32},{32,0},{64,96},{96,64},{1,33},{33,1},{65,97},{97,65},{2,34}... | collective-permute-start | bytes 786440 | tf_op jit(solution)/shard_map/ppermute | solution.py:94
  26.2 7.7 %collective-permute-start.2 = (bf16[512,256]{1,0:T(8,128)(2,1)S(1)}, bf16[512,256]{1,0:T(8,128)(2,1)S(1)}, u32[]{:S(2)}, u32[]{:S(2)}) collective-permute-start(bf16[512,256]{1,0:T(8,128)(2,1)S(1)} %pad_maximum_fusion), channel_id=1, source_target_pairs={{0,96},{32,64},{64,32},{96,0},{1,97},{33,65},{65,33},{97,1},{2,98}... | collective-permute-start | bytes 786440 | tf_op jit(solution)/shard_map/ppermute | solution.py:94
  26.3 5.1 %collective-permute-start.8 = (bf16[256,256]{1,0:T(8,128)(2,1)S(1)}, bf16[256,256]{1,0:T(8,128)(2,1)S(1)}, u32[]{:S(2)}, u32[]{:S(2)}) collective-permute-start(bf16[256,256]{1,0:T(8,128)(2,1)S(1)} %collective-permute-done.7.refs_8_), channel_id=1, source_target_pairs={{0,28},{4,8},{8,4},{12,16},{16,12},{20,24},{24,20},{28,0},{1,29},{... | collective-permute-start | bytes 393224 | tf_op jit(solution)/shard_map/ppermute | solution.py:68
  27.4 5.4 %collective-permute-start.12 = (bf16[256,256]{1,0:T(8,128)(2,1)S(1)}, bf16[256,256]{1,0:T(8,128)(2,1)S(1)}, u32[]{:S(2)}, u32[]{:S(2)}) collective-permute-start(bf16[256,256]{1,0:T(8,128)(2,1)S(1)} %collective-permute-done.11.refs_13_), channel_id=1, source_target_pairs={{0,4},{4,0},{8,12},{12,8},{16,20},{20,16},{24,28},{28,24},{1,5},{5... | collective-permute-start | bytes 393224 | tf_op jit(solution)/shard_map/ppermute | solution.py:68
  47.0 6.2 %collective-permute-start.13 = (bf16[528,128]{1,0:T(8,128)(2,1)S(1)}, bf16[528,128]{1,0:T(8,128)(2,1)S(1)}, u32[]{:S(2)}, u32[]{:S(2)}) collective-permute-start(bf16[528,128]{1,0:T(8,128)(2,1)S(1)} %get-tuple-element.17), channel_id=1, source_target_pairs={{0,32},{32,0},{64,96},{96,64},{128,160},{160,128},{192,224},{224,1... | collective-permute-start | bytes 405512 | tf_op jit(solution)/shard_map/ppermute | solution.py:236
  47.0 7.2 %collective-permute-start.14 = (bf16[528,128]{1,0:T(8,128)(2,1)S(1)}, bf16[528,128]{1,0:T(8,128)(2,1)S(1)}, u32[]{:S(2)}, u32[]{:S(2)}) collective-permute-start(bf16[528,128]{1,0:T(8,128)(2,1)S(1)} %get-tuple-element.16), channel_id=1, source_target_pairs={{0,64},{32,96},{64,0},{96,32},{128,192},{160,224},{192,128},{224,1... | collective-permute-start | bytes 405512 | tf_op jit(solution)/shard_map/ppermute | solution.py:236
  47.0 11.8 %collective-permute-start.15 = (bf16[528,128]{1,0:T(8,128)(2,1)S(1)}, bf16[528,128]{1,0:T(8,128)(2,1)S(1)}, u32[]{:S(2)}, u32[]{:S(2)}) collective-permute-start(bf16[528,128]{1,0:T(8,128)(2,1)S(1)} %get-tuple-element.15), channel_id=1, source_target_pairs={{0,96},{32,64},{64,32},{96,0},{128,224},{160,192},{192,160},{224,1... | collective-permute-start | bytes 405512 | tf_op jit(solution)/shard_map/ppermute | solution.py:236
  51.7 7.1 %collective-permute-start.16 = (bf16[528,128]{1,0:T(8,128)(2,1)S(1)}, bf16[528,128]{1,0:T(8,128)(2,1)S(1)}, u32[]{:S(2)}, u32[]{:S(2)}) collective-permute-start(bf16[528,128]{1,0:T(8,128)(2,1)S(1)} %get-tuple-element.14), channel_id=1, source_target_pairs={{0,128},{32,160},{64,192},{96,224},{128,0},{160,32},{192,64},{224,... | collective-permute-start | bytes 405512 | tf_op jit(solution)/shard_map/ppermute | solution.py:236
  51.7 7.1 %collective-permute-start.17 = (bf16[528,128]{1,0:T(8,128)(2,1)S(1)}, bf16[528,128]{1,0:T(8,128)(2,1)S(1)}, u32[]{:S(2)}, u32[]{:S(2)}) collective-permute-start(bf16[528,128]{1,0:T(8,128)(2,1)S(1)} %get-tuple-element.13), channel_id=1, source_target_pairs={{0,160},{32,128},{64,224},{96,192},{128,32},{160,0},{192,96},{224,... | collective-permute-start | bytes 405512 | tf_op jit(solution)/shard_map/ppermute | solution.py:236
  53.2 10.0 %copy-start.2 = (bf16[528,128]{1,0:T(8,128)(2,1)}, bf16[528,128]{1,0:T(8,128)(2,1)S(1)}, u32[]{:S(2)}) copy-start(bf16[528,128]{1,0:T(8,128)(2,1)S(1)} %collective-permute-done.13.refs_1_) | copy-start | bytes 405508
  53.2 7.4 %collective-permute-start.18 = (bf16[528,128]{1,0:T(8,128)(2,1)S(1)}, bf16[528,128]{1,0:T(8,128)(2,1)S(1)}, u32[]{:S(2)}, u32[]{:S(2)}) collective-permute-start(bf16[528,128]{1,0:T(8,128)(2,1)S(1)} %get-tuple-element.12), channel_id=1, source_target_pairs={{0,192},{32,224},{64,128},{96,160},{128,64},{160,96},{192,0},{224,... | collective-permute-start | bytes 405512 | tf_op jit(solution)/shard_map/ppermute | solution.py:236
  54.2 9.0 %copy-start.3 = (bf16[528,128]{1,0:T(8,128)(2,1)}, bf16[528,128]{1,0:T(8,128)(2,1)S(1)}, u32[]{:S(2)}) copy-start(bf16[528,128]{1,0:T(8,128)(2,1)S(1)} %collective-permute-done.14.refs_2_) | copy-start | bytes 405508
  54.2 9.0 %collective-permute-start.19 = (bf16[528,128]{1,0:T(8,128)(2,1)S(1)}, bf16[528,128]{1,0:T(8,128)(2,1)S(1)}, u32[]{:S(2)}, u32[]{:S(2)}) collective-permute-start(bf16[528,128]{1,0:T(8,128)(2,1)S(1)} %get-tuple-element.11), channel_id=1, source_target_pairs={{0,224},{32,192},{64,160},{96,128},{128,96},{160,64},{192,32},{224... | collective-permute-start | bytes 405512 | tf_op jit(solution)/shard_map/ppermute | solution.py:236
  58.8 4.4 %copy-start.4 = (bf16[528,128]{1,0:T(8,128)(2,1)}, bf16[528,128]{1,0:T(8,128)(2,1)S(1)}, u32[]{:S(2)}) copy-start(bf16[528,128]{1,0:T(8,128)(2,1)S(1)} %collective-permute-done.15.refs_3_) | copy-start | bytes 405508
  58.8 4.4 %copy-start.5 = (bf16[528,128]{1,0:T(8,128)(2,1)}, bf16[528,128]{1,0:T(8,128)(2,1)S(1)}, u32[]{:S(2)}) copy-start(bf16[528,128]{1,0:T(8,128)(2,1)S(1)} %collective-permute-done.16.refs_4_) | copy-start | bytes 405508
  58.8 4.4 %copy-start.6 = (bf16[528,128]{1,0:T(8,128)(2,1)}, bf16[528,128]{1,0:T(8,128)(2,1)S(1)}, u32[]{:S(2)}) copy-start(bf16[528,128]{1,0:T(8,128)(2,1)S(1)} %collective-permute-done.17.refs_5_) | copy-start | bytes 405508
  60.6 2.6 %copy-start.7 = (bf16[528,128]{1,0:T(8,128)(2,1)}, bf16[528,128]{1,0:T(8,128)(2,1)S(1)}, u32[]{:S(2)}) copy-start(bf16[528,128]{1,0:T(8,128)(2,1)S(1)} %collective-permute-done.18.refs_6_) | copy-start | bytes 405508
  63.2 0.6 copy-start.8
  67.0 9.2 %collective-permute-start.20 = (bf16[64,512]{1,0:T(8,128)(2,1)S(1)}, bf16[64,512]{1,0:T(8,128)(2,1)S(1)}, u32[]{:S(2)}, u32[]{:S(2)}) collective-permute-start(bf16[64,512]{1,0:T(8,128)(2,1)S(1)} %get-tuple-element.26), channel_id=1, source_target_pairs={{0,0},{4,8},{8,16},{12,24},{16,32},{20,40},{24,48},{28,56},{32,64}... | collective-permute-start | bytes 196616 | tf_op jit(solution)/shard_map/ppermute | solution.py:239
  70.6 13.1 %collective-permute-start.21 = (bf16[64,512]{1,0:T(8,128)(2,1)S(1)}, bf16[64,512]{1,0:T(8,128)(2,1)S(1)}, u32[]{:S(2)}, u32[]{:S(2)}) collective-permute-start(bf16[64,512]{1,0:T(8,128)(2,1)S(1)} %get-tuple-element.25), channel_id=1, source_target_pairs={{0,4},{4,12},{8,20},{12,28},{16,36},{20,44},{24,52},{28,60},{32,68... | collective-permute-start | bytes 196616 | tf_op jit(solution)/shard_map/ppermute | solution.py:242
  87.3 2.2 %collective-permute-start.22 = (bf16[2,32,5376]{2,1,0:T(8,128)(2,1)S(1)}, bf16[2,32,5376]{2,1,0:T(8,128)(2,1)S(1)}, u32[]{:S(2)}, u32[]{:S(2)}) collective-permute-start(bf16[2,32,5376]{2,1,0:T(8,128)(2,1)S(1)} %bitcast.40), channel_id=1, source_target_pairs={{0,1},{1,0},{2,3},{3,2},{4,5},{5,4},{6,7},{7,6},{8,9},{9,8},{10,11... | collective-permute-start | bytes 2064392 | tf_op jit(solution)/shard_map/ppermute | solution.py:253
  89.7 11.7 %collective-permute-start.23 = (bf16[32,5376]{1,0:T(8,128)(2,1)S(1)}, bf16[32,5376]{1,0:T(8,128)(2,1)S(1)}, u32[]{:S(2)}, u32[]{:S(2)}) collective-permute-start(bf16[32,5376]{1,0:T(8,128)(2,1)S(1)} %fusion.1), channel_id=1, source_target_pairs={{0,2},{2,0},{1,3},{3,1},{4,6},{6,4},{5,7},{7,5},{8,10},{10,8},{9,1... | collective-permute-start | bytes 1032200 | tf_op jit(solution)/shard_map/ppermute | solution.py:257

commit v2 on v1

v2 whole, which is shorter than its diff:
```python
import functools

import jax
import jax.numpy as jnp
import numpy as np
from jax import lax
from jax.experimental import pallas as pl
from jax.experimental.pallas import tpu as pltpu
from jax.sharding import Mesh
from jax.sharding import PartitionSpec as P

EPSILON = 1e-06
HD = 128
PIECE = 128
NX, NY, NZ = 2, 4, 8
GROUP = NX * NY
QUERY_FACTOR = float(168.0**-0.5 / np.log(2.0))
NEGATIVE = -1e30
FREQUENCY = (1000000.0 ** (-2.0 * np.arange(64, dtype=np.float64) / 128)).astype(np.float32)
VMEM_LIMIT = 48 * 1024 * 1024
NT = (((1,), (1,)), ((), ()))


def pairs(count, partner):
    return [(i, partner(i)) for i in range(count)]


Z_PAIRS = (pairs(NZ, lambda i: i ^ 1), pairs(NZ, lambda i: (((i + 1) ^ 1) + 7) % 8))
Y_PAIRS = (pairs(NY, lambda i: i ^ 1), pairs(NY, lambda i: i ^ 3))
X_PAIRS = pairs(NX, lambda i: i ^ 1)
BLOCK = 64


def prepare_kernel(ids_ref, q_ref, k_ref, v_ref, pos_ref, freq_ref, qg_ref, kg_ref, a_out, b_out, kv0_out, kv1_out):
    swapped = ids_ref[1] >= NZ // 2
    lane = lax.broadcasted_iota(jnp.int32, (PIECE, HD), 1)
    spread = jnp.broadcast_to(pos_ref[...].astype(jnp.float32), (PIECE, HD))
    angles = jnp.transpose(spread) * freq_ref[...]
    cosines = jnp.cos(angles)
    sines = jnp.where(lane < HD // 2, -1.0, 1.0) * jnp.sin(angles)

    def rotate(vector, gain):
        vector = vector.astype(jnp.float32)
        normed = vector * lax.rsqrt(jnp.mean(vector * vector, axis=-1, keepdims=True) + EPSILON) * gain
        return normed * cosines + pltpu.roll(normed, HD // 2, 1) * sines

    for head, out in enumerate((kv0_out, kv1_out)):
        cols = slice(head * HD, (head + 1) * HD)
        out[:, :HD] = rotate(k_ref[:, cols], kg_ref[...]).astype(jnp.bfloat16)
        out[:, HD:] = v_ref[:, cols]
    for head in range(4):
        cols = slice(head * HD, (head + 1) * HD)
        rows = rotate(q_ref[:, cols], qg_ref[...]) * QUERY_FACTOR
        first, second = rows[:BLOCK], rows[BLOCK:]
        a_out[:, cols] = jnp.where(swapped, second, first).astype(jnp.bfloat16)
        b_out[:, cols] = jnp.where(swapped, first, second).astype(jnp.bfloat16)


def prepare(ids, queries, keys, values, positions, query_gain, key_gain):
    freq = jnp.asarray(np.concatenate([FREQUENCY, FREQUENCY])[None, :])
    vmem = pl.BlockSpec(memory_space=pltpu.VMEM)
    smem = pl.BlockSpec(memory_space=pltpu.SMEM)
    block = jax.ShapeDtypeStruct((BLOCK, 4 * HD), jnp.bfloat16)
    key_value = jax.ShapeDtypeStruct((PIECE, 2 * HD), jnp.bfloat16)
    return pl.pallas_call(
        prepare_kernel,
        out_shape=(block, block, key_value, key_value),
        in_specs=[smem] + [vmem] * 7,
        out_specs=(vmem,) * 4,
    )(ids, queries, keys, values, positions[None, :], freq, query_gain[None, :], key_gain[None, :])


def gather_z(own, first):
    here, there = Z_PAIRS[first], Z_PAIRS[1 - first]
    one = lax.ppermute(own, "z", here)
    two = lax.ppermute(jnp.concatenate([own, one], axis=0), "z", there)
    three = lax.ppermute(two, "z", here)
    four = lax.ppermute(three, "z", there)
    return [own, one, two, three, four]


def z_partner(which, z):
    return z ^ 1 if which == 0 else (((z + 1) ^ 1) + 7) & 7


def z_order(first, z):
    here = functools.partial(z_partner, first)
    there = functools.partial(z_partner, 1 - first)
    two = [there(z), here(there(z))]
    near = here(z)
    three = [there(near), here(there(near))]
    far = there(z)
    far_near = here(far)
    four = [there(far_near), here(there(far_near))]
    return [z, near] + two + three + four


def folded_z(x, z, second):
    parity = (z >> 2) ^ second
    return (((z & 3) << 1) | parity) ^ (7 * x)


def fold_pairs(second, cross):
    moves = []
    for x in range(NX):
        for z in range(NZ):
            moves.append((x * NZ + z, (x ^ cross) * NZ + folded_z(x, z, second)))
    return moves


def gather_queries(a, b):
    blocks = [
        lax.ppermute(block, ("x", "z"), fold_pairs(second, cross))
        for cross in (0, 1)
        for second, block in ((0, a), (1, b))
    ]
    result = []
    for half in range(2):
        columns = slice(half * 2 * HD, (half + 1) * 2 * HD)
        own = jnp.concatenate([block[:, columns] for block in blocks], axis=0)
        near = lax.ppermute(own, "y", Y_PAIRS[half])
        far = lax.ppermute(jnp.concatenate([own, near], axis=0), "y", Y_PAIRS[1 - half])
        result += [own, near, far]
    return result


Y_STEPS = ((1, 3, 2), (3, 1, 2))


def attention_kernel(ids_ref, *refs):
    queries, pieces = refs[:6], (refs[6:11], refs[11:16])
    out_ref, q_s, k_s, vt_s, v_s = refs[16:]
    group = ids_ref[0]
    z = ids_ref[1]
    x, y = group >> 2, group & 3
    for half in range(2):
        own, near, far = queries[half * 3 : half * 3 + 3]
        first, second, third = Y_STEPS[half]
        for rel_y, ref, base in ((0, own, 0), (first, near, 0), (second, far, 0), (third, far, 2 * PIECE)):
            for rel_x in range(NX):
                rows = slice(base + rel_x * PIECE, base + (rel_x + 1) * PIECE)
                place = (x ^ rel_x) * NY + (y ^ rel_y)
                for j in range(2):
                    q_s[half, place, j] = ref[rows, j * HD : (j + 1) * HD]
        places = z_order(half, z)
        index = 0
        for piece in pieces[half]:
            for part in range(piece.shape[0] // PIECE):
                start = pl.multiple_of(places[index] * PIECE, PIECE)
                rows = slice(part * PIECE, (part + 1) * PIECE)
                k_s[half, pl.ds(start, PIECE), :] = piece[rows, :HD]
                v_s[half, pl.ds(start, PIECE), :] = piece[rows, HD:]
                index += 1
        vt_s[half] = jnp.transpose(v_s[half])

    keys = NZ * PIECE

    def one(half, step, masked):
        target = group ^ step
        outer = target >> 1
        shift = pl.multiple_of(((target ^ z) & 1) * BLOCK, BLOCK)
        rows = pl.ds(shift, BLOCK)
        query = jnp.concatenate(
            [q_s[half, source, j, rows, :] for j in range(2) for source in (outer, 7 - outer)], axis=0
        )
        scores = lax.dot_general(k_s[half], query, NT, preferred_element_type=jnp.float32)
        if masked:
            key_row = lax.broadcasted_iota(jnp.int32, (keys, 2 * PIECE), 0)
            lane = lax.broadcasted_iota(jnp.int32, (1, 2 * PIECE), 1)
            low = target * NZ + z
            block = jnp.where(lane % PIECE < BLOCK, low, 127 - low)
            last = block * BLOCK + lane % BLOCK - group * keys
            scores = jnp.where(key_row <= last, scores, NEGATIVE)
        highest = jnp.max(scores, axis=0, keepdims=True)
        weights = jnp.exp2(scores - highest)
        total = jnp.sum(weights, axis=0, keepdims=True)
        summed = jnp.dot(vt_s[half], weights.astype(jnp.bfloat16), preferred_element_type=jnp.float32)
        normal = (summed / total).astype(jnp.bfloat16)
        level = highest + jnp.log2(total)
        top = level.astype(jnp.bfloat16)
        rest = level - top.astype(jnp.float32)
        middle = rest.astype(jnp.bfloat16)
        low_part = (rest - middle.astype(jnp.float32)).astype(jnp.bfloat16)
        for j in range(2):
            head = half * 2 + j
            out_ref[step, head * HD : (head + 1) * HD, :] = normal[:, j * PIECE : (j + 1) * PIECE]
        return [part[:, j * PIECE : (j + 1) * PIECE] for j in range(2) for part in (top, middle, low_part)]

    def both(step, masked):
        rows = one(0, step, masked) + one(1, step, masked)
        block = jnp.concatenate([r.astype(jnp.float32) for r in rows] + [jnp.zeros((4, PIECE), jnp.float32)], axis=0)
        out_ref[step, 4 * HD : 4 * HD + 16, :] = block.astype(jnp.bfloat16)

    def body(step, carry):
        outer = (group ^ step) >> 1
        high = 7 - outer
        full = jnp.logical_and(outer > group, high > group)
        none = jnp.logical_and(outer < group, high < group)

        @pl.when(full)
        def _():
            both(step, False)

        @pl.when(jnp.logical_not(jnp.logical_or(full, none)))
        def _():
            both(step, True)

        @pl.when(none)
        def _():
            out_ref[step, 0 : 4 * HD, :] = jnp.zeros((4 * HD, PIECE), jnp.bfloat16)
            out_ref[step, 4 * HD : 4 * HD + 16, :] = jnp.full((16, PIECE), NEGATIVE, jnp.bfloat16)

        return carry

    lax.fori_loop(0, GROUP, body, 0)


def attention(ids, queries, pieces):
    vmem = pl.BlockSpec(memory_space=pltpu.VMEM)
    smem = pl.BlockSpec(memory_space=pltpu.SMEM)
    return pl.pallas_call(
        attention_kernel,
        out_shape=jax.ShapeDtypeStruct((GROUP, 4 * HD + 16, PIECE), jnp.bfloat16),
        in_specs=[smem] + [vmem] * 16,
        out_specs=vmem,
        scratch_shapes=[
            pltpu.VMEM((2, GROUP, 2, PIECE, HD), jnp.bfloat16),
            pltpu.VMEM((2, NZ * PIECE, HD), jnp.bfloat16),
            pltpu.VMEM((2, HD, NZ * PIECE), jnp.bfloat16),
            pltpu.VMEM((2, NZ * PIECE, HD), jnp.bfloat16),
        ],
        compiler_params=pltpu.CompilerParams(vmem_limit_bytes=VMEM_LIMIT),
    )(ids, *queries, *pieces[0], *pieces[1])


def combine_kernel(ids_ref, *refs):
    pieces, out_ref = refs[:-1], refs[-1]
    core = ids_ref[2]
    stats = [r[4 * HD : 4 * HD + 16, :].astype(jnp.float32) for r in pieces]
    quarter = PIECE // 4
    for head in range(4):
        levels = [
            s[3 * head : 3 * head + 1] + s[3 * head + 1 : 3 * head + 2] + s[3 * head + 2 : 3 * head + 3]
            for s in stats
        ]
        highest = functools.reduce(jnp.maximum, levels)
        shares = [jnp.exp2(level - highest) for level in levels]
        scale = 1.0 / functools.reduce(jnp.add, shares)
        total = None
        for share, piece in zip(shares, pieces):
            term = piece[head * HD : (head + 1) * HD, :].astype(jnp.float32) * (share * scale)
            total = term if total is None else total + term
        rows = jnp.transpose(total).astype(jnp.bfloat16)
        for k in range(4):
            own = 1 - ((k & 1) ^ core)
            start = pl.multiple_of(own * (PIECE // 2) + (k >> 1) * quarter, quarter)
            out_ref[pl.ds(start, quarter), head * HD : (head + 1) * HD] = rows[k * quarter : (k + 1) * quarter]


def combine(ids, pieces):
    vmem = pl.BlockSpec(memory_space=pltpu.VMEM)
    smem = pl.BlockSpec(memory_space=pltpu.SMEM)
    return pl.pallas_call(
        combine_kernel,
        out_shape=jax.ShapeDtypeStruct((PIECE, 4 * HD), jnp.bfloat16),
        in_specs=[smem] + [vmem] * GROUP,
        out_specs=vmem,
    )(ids, *pieces)


CHUNKS = 2


def project(rows, out_weight, w):
    chips = []
    width = out_weight.shape[1] // CHUNKS
    for chunk in range(CHUNKS):
        weight = out_weight[:, chunk * width : (chunk + 1) * width]
        product = jnp.dot(rows, weight, preferred_element_type=jnp.float32).astype(jnp.bfloat16)
        product = product.reshape(2, 2, PIECE // 4, width)
        got = lax.ppermute(product[0], "c", X_PAIRS)
        chip = product[1].astype(jnp.float32) + got.astype(jnp.float32)
        keep = lax.dynamic_index_in_dim(chip, w, 0, keepdims=False)
        give = lax.dynamic_index_in_dim(chip, 1 - w, 0, keepdims=False).astype(jnp.bfloat16)
        chips.append((keep, lax.ppermute(give, "w", X_PAIRS)))
    return jnp.concatenate([(keep + taken.astype(jnp.float32)).astype(jnp.bfloat16) for keep, taken in chips], axis=1)


def on_device(queries, keys, values, positions, query_gain, key_gain, out_weight):
    x, y, z = lax.axis_index("x"), lax.axis_index("y"), lax.axis_index("z")
    w, c = lax.axis_index("w"), lax.axis_index("c")
    ids = jnp.stack([x * NY + y, z, c]).astype(jnp.int32)
    a, b, kv0, kv1 = prepare(ids, queries, keys, values, positions, query_gain, key_gain)
    gathered = gather_queries(a, b)
    pieces = (gather_z(kv0, 0), gather_z(kv1, 1))
    partial = attention(ids, gathered, pieces)
    received = [partial[0]] + [
        lax.ppermute(partial[step], ("x", "y"), pairs(GROUP, lambda i: i ^ step)) for step in range(1, GROUP)
    ]
    return project(combine(ids, received), out_weight, w)


def solution(mesh):
    inner = Mesh(mesh.devices.reshape(NX, NY, NZ, 2, 2), ("x", "y", "z", "w", "c"))
    ctx, head = ("x", "y", "z"), ("w", "c")
    return jax.shard_map(
        on_device,
        mesh=inner,
        in_specs=(P(ctx, head), P(ctx, head), P(ctx, head), P(ctx), P(), P(), P(head, None)),
        out_specs=P(ctx + head, None),
        check_vma=False,
    )
```

time: 103 us -> 107 us (1.039)
  the two profiles are of different devices: /device:TPU:64 before, /device:TPU:1 now
where the time goes in v2:
time: 107 us; the launch traced here: 106 us
  starting transfers between devices  50.1 us (47%)
  waiting for transfers between devices  26.4 us (25%)
  Pallas kernels  17.6 us (16%)
  matrix products  4.79 us (4%)
  local copies, waits for them, and re-layouts  3.85 us (4%)
  other arithmetic  3.24 us (3%)
    ppermute x4, starting transfers between devices, gather_queries(): lax.ppermute(block, ('x', 'z'), fold_pairs(second, cross))  14.8 us
    pallas_call x1, Pallas kernels, attention(): pl.pallas_call(attention_kernel, out_shape=jax.ShapeDtypeStruct((GROUP, 4...  12.9 us
    ppermute x7, starting transfers between devices, on_device(): lax.ppermute(partial[step], ('x', 'y'), pairs(GROUP, lambda i: i ^ step))  12.7 us
    ppermute x2, waiting for transfers between devices, project(): chips.append((keep, lax.ppermute(give, 'w', X_PAIRS)))  7.61 us
    ppermute x2, starting transfers between devices, project(): got = lax.ppermute(product[0], 'c', X_PAIRS)  6.35 us
    ppermute x7, waiting for transfers between devices, on_device(): lax.ppermute(partial[step], ('x', 'y'), pairs(GROUP, lambda i: i ^ step))  5.34 us
    dot_general x2, matrix products, project(): jnp.dot(rows, weight, preferred_element_type=jnp.float32)  4.79 us
    ppermute x2, waiting for transfers between devices, gather_z(): four = lax.ppermute(three, 'z', there)  4.6 us
  transfers between devices with their start and end apart: 27, of which 12 were waited for; matrix products, arithmetic and copies ran while one was open for 2% of the time, Pallas kernels for 0%

profile of v2, /device:TPU:1, one launch (start us, length us, event | category | flops | bytes accessed | tf_op | source)
XLA Modules:
  0.0 106.4 jit_solution(12443385960376777663)
XLA Ops:
  0.0 0.6 pad_add_fusion.ids_ref
  0.6 2.5 %shard_map.82 = (bf16[64,512]{1,0:T(8,128)(2,1)}, bf16[64,512]{1,0:T(8,128)(2,1)}, bf16[128,256]{1,0:T(8,128)(2,1)}, bf16[128,256]{1,0:T(8,128)(2,1)}) custom-call(s32[3]{0:T(128)} %pad_add_fusion.ids_ref, bf16[128,512]{1,0:T(8,128)(2,1)} %q_ref.1, bf16[128,256]{1,0:T(8,128)(2,1)} %k_ref.1, bf16[128,256]{1,0:T(8,128)(2,1)} %v_ref.1, s32[1,128]{1,0:T(1,128)} %bitcast.46, ...), custom_call_target="tpu_custom_call" | custom-call | tf_op jit(solution)/shard_map/pallas_call | solution.py:65
  3.0 1.5 %collective-permute-start = (bf16[64,512]{1,0:T(8,128)(2,1)}, bf16[64,512]{1,0:T(8,128)(2,1)S(1)}, u32[]{:S(2)}, u32[]{:S(2)}) collective-permute-start(bf16[64,512]{1,0:T(8,128)(2,1)} %get-tuple-element.9), channel_id=1, source_target_pairs={{0,0},{4,8},{8,16},{12,24},{16,4},{20,12},{24,20},{28,28},{128,156... | collective-permute-start | bytes 196616 | tf_op jit(solution)/shard_map/ppermute | solution.py:113
  4.5 8.1 %collective-permute-start.2 = (bf16[64,512]{1,0:T(8,128)(2,1)}, bf16[64,512]{1,0:T(8,128)(2,1)S(1)}, u32[]{:S(2)}, u32[]{:S(2)}) collective-permute-start(bf16[64,512]{1,0:T(8,128)(2,1)} %get-tuple-element.9), channel_id=1, source_target_pairs={{0,128},{4,136},{8,144},{12,152},{16,132},{20,140},{24,148},{28,15... | collective-permute-start | bytes 196616 | tf_op jit(solution)/shard_map/ppermute | solution.py:113
  12.6 1.9 %collective-permute-start.1 = (bf16[64,512]{1,0:T(8,128)(2,1)}, bf16[64,512]{1,0:T(8,128)(2,1)S(1)}, u32[]{:S(2)}, u32[]{:S(2)}) collective-permute-start(bf16[64,512]{1,0:T(8,128)(2,1)} %get-tuple-element.10), channel_id=1, source_target_pairs={{0,4},{4,12},{8,20},{12,28},{16,0},{20,8},{24,16},{28,24},{128,152... | collective-permute-start | bytes 196616 | tf_op jit(solution)/shard_map/ppermute | solution.py:113
  14.5 3.3 %collective-permute-start.3 = (bf16[64,512]{1,0:T(8,128)(2,1)}, bf16[64,512]{1,0:T(8,128)(2,1)S(1)}, u32[]{:S(2)}, u32[]{:S(2)}) collective-permute-start(bf16[64,512]{1,0:T(8,128)(2,1)} %get-tuple-element.10), channel_id=1, source_target_pairs={{0,132},{4,140},{8,148},{12,156},{16,128},{20,136},{24,144},{28,15... | collective-permute-start | bytes 196616 | tf_op jit(solution)/shard_map/ppermute | solution.py:113
  17.9 3.4 %collective-permute-start.12 = (bf16[128,256]{1,0:T(8,128)(2,1)}, bf16[128,256]{1,0:T(8,128)(2,1)S(1)}, u32[]{:S(2)}, u32[]{:S(2)}) collective-permute-start(bf16[128,256]{1,0:T(8,128)(2,1)} %get-tuple-element.12.refs_11_), channel_id=1, source_target_pairs={{0,28},{4,8},{8,4},{12,16},{16,12},{20,24},{24,20},{28,0},{1,29},{... | collective-permute-start | bytes 196616 | tf_op jit(solution)/shard_map/ppermute | solution.py:75
  21.3 4.2 %collective-permute-done.1 = bf16[64,512]{1,0:T(8,128)(2,1)S(1)} collective-permute-done((bf16[64,512]{1,0:T(8,128)(2,1)}, bf16[64,512]{1,0:T(8,128)(2,1)S(1)}, u32[]{:S(2)}, u32[]{:S(2)}) %collective-permute-start.1) | collective-permute-done | bytes 65568 | tf_op jit(solution)/shard_map/ppermute | solution.py:113
  25.5 2.8 %collective-permute-start.6 = (bf16[256,256]{1,0:T(8,128)(2,1)S(1)}, bf16[256,256]{1,0:T(8,128)(2,1)S(1)}, u32[]{:S(2)}, u32[]{:S(2)}) collective-permute-start(bf16[256,256]{1,0:T(8,128)(2,1)S(1)} %pad_maximum_fusion.2.refs_3_), channel_id=1, source_target_pairs={{0,96},{32,64},{64,32},{96,0},{1,97},{33,65},{65,33},{97,1},{2,98}... | collective-permute-start | bytes 393224 | tf_op jit(solution)/shard_map/ppermute | solution.py:121
  28.5 0.8 pad_maximum_fusion.3
  29.3 0.1 collective-permute-start.9
  29.4 0.8 pad_maximum_fusion.4
  30.4 0.9 collective-permute-done.6.refs_4_
  31.3 0.6 collective-permute-start.7
  32.0 0.5 collective-permute-done.4.refs_1_
  32.4 1.7 %collective-permute-start.5 = (bf16[512,256]{1,0:T(8,128)(2,1)S(1)}, bf16[512,256]{1,0:T(8,128)(2,1)S(1)}, u32[]{:S(2)}, u32[]{:S(2)}) collective-permute-start(bf16[512,256]{1,0:T(8,128)(2,1)S(1)} %constant_dynamic-update-slice_fusion), channel_id=1, source_target_pairs={{0,96},{32,64},{64,32},{96,0},{1,97},{33,65},{65,33},{97,1},{2,98}... | collective-permute-start | bytes 786440 | tf_op jit(solution)/shard_map/ppermute | solution.py:122
  34.2 0.3 collective-permute-done.9.refs_8_
  34.5 2.4 %collective-permute-start.14 = (bf16[256,256]{1,0:T(8,128)(2,1)S(1)}, bf16[256,256]{1,0:T(8,128)(2,1)S(1)}, u32[]{:S(2)}, u32[]{:S(2)}) collective-permute-start(bf16[256,256]{1,0:T(8,128)(2,1)S(1)} %collective-permute-done.13.refs_13_), channel_id=1, source_target_pairs={{0,28},{4,8},{8,4},{12,16},{16,12},{20,24},{24,20},{28,0},{1,29},{... | collective-permute-start | bytes 393224 | tf_op jit(solution)/shard_map/ppermute | solution.py:77
  36.9 1.9 %collective-permute-done.10.refs_9_ = bf16[256,256]{1,0:T(8,128)(2,1)S(1)} collective-permute-done((bf16[256,256]{1,0:T(8,128)(2,1)S(1)}, bf16[256,256]{1,0:T(8,128)(2,1)S(1)}, u32[]{:S(2)}, u32[]{:S(2)}) %collective-permute-start.10) | collective-permute-done | bytes 131104 | tf_op jit(solution)/shard_map/ppermute | solution.py:77
  38.8 1.6 %collective-permute-start.11 = (bf16[256,256]{1,0:T(8,128)(2,1)S(1)}, bf16[256,256]{1,0:T(8,128)(2,1)S(1)}, u32[]{:S(2)}, u32[]{:S(2)}) collective-permute-start(bf16[256,256]{1,0:T(8,128)(2,1)S(1)} %collective-permute-done.10.refs_9_), channel_id=1, source_target_pairs={{0,28},{4,8},{8,4},{12,16},{16,12},{20,24},{24,20},{28,0},{1,29},{... | collective-permute-start | bytes 393224 | tf_op jit(solution)/shard_map/ppermute | solution.py:78
  40.4 0.2 collective-permute-start.15
  40.6 4.6 %collective-permute-done.11.refs_10_ = bf16[256,256]{1,0:T(8,128)(2,1)S(1)} collective-permute-done((bf16[256,256]{1,0:T(8,128)(2,1)S(1)}, bf16[256,256]{1,0:T(8,128)(2,1)S(1)}, u32[]{:S(2)}, u32[]{:S(2)}) %collective-permute-start.11) | collective-permute-done | bytes 131104 | tf_op jit(solution)/shard_map/ppermute | solution.py:78
  45.2 0.8 copy-done
  46.1 0.8 copy-done.1
  46.9 0.6 copy-done.2
  47.5 12.9 %shard_map.83 = bf16[8,528,128]{2,1,0:T(8,128)(2,1)S(1)} custom-call(s32[3]{0:T(128)S(1)} %copy-done.2, bf16[256,256]{1,0:T(8,128)(2,1)S(1)} %pad_maximum_fusion.1.refs_0_, bf16[256,256]{1,0:T(8,128)(2,1)S(1)} %collective-permute-done.4.refs_1_, bf16[512,256]{1,0:T(8,128)(2,1)S(1)} %collective-permute-done.5.refs_2_, ...), custom_call_target="tpu_custom_call" | custom-call | tf_op jit(solution)/shard_map/pallas_call | solution.py:221
  60.4 0.7 slice_bitcast_fusion
  61.1 1.7 %collective-permute-start.16 = (bf16[528,128]{1,0:T(8,128)(2,1)S(1)}, bf16[528,128]{1,0:T(8,128)(2,1)S(1)}, u32[]{:S(2)}, u32[]{:S(2)}) collective-permute-start(bf16[528,128]{1,0:T(8,128)(2,1)S(1)} %get-tuple-element.19), channel_id=1, source_target_pairs={{0,32},{32,0},{64,96},{96,64},{128,160},{160,128},{192,224},{224,1... | collective-permute-start | bytes 405512 | tf_op jit(solution)/shard_map/ppermute | solution.py:298
  62.9 0.8 collective-permute-start.17
  63.7 1.6 %collective-permute-start.18 = (bf16[528,128]{1,0:T(8,128)(2,1)S(1)}, bf16[528,128]{1,0:T(8,128)(2,1)S(1)}, u32[]{:S(2)}, u32[]{:S(2)}) collective-permute-start(bf16[528,128]{1,0:T(8,128)(2,1)S(1)} %get-tuple-element.17), channel_id=1, source_target_pairs={{0,96},{32,64},{64,32},{96,0},{128,224},{160,192},{192,160},{224,1... | collective-permute-start | bytes 405512 | tf_op jit(solution)/shard_map/ppermute | solution.py:298
  65.2 4.1 %collective-permute-start.19 = (bf16[528,128]{1,0:T(8,128)(2,1)S(1)}, bf16[528,128]{1,0:T(8,128)(2,1)S(1)}, u32[]{:S(2)}, u32[]{:S(2)}) collective-permute-start(bf16[528,128]{1,0:T(8,128)(2,1)S(1)} %get-tuple-element.16), channel_id=1, source_target_pairs={{0,128},{32,160},{64,192},{96,224},{128,0},{160,32},{192,64},{224,... | collective-permute-start | bytes 405512 | tf_op jit(solution)/shard_map/ppermute | solution.py:298
  69.3 2.1 %collective-permute-start.21 = (bf16[528,128]{1,0:T(8,128)(2,1)S(1)}, bf16[528,128]{1,0:T(8,128)(2,1)S(1)}, u32[]{:S(2)}, u32[]{:S(2)}) collective-permute-start(bf16[528,128]{1,0:T(8,128)(2,1)S(1)} %get-tuple-element.14), channel_id=1, source_target_pairs={{0,192},{32,224},{64,128},{96,160},{128,64},{160,96},{192,0},{224,... | collective-permute-start | bytes 405512 | tf_op jit(solution)/shard_map/ppermute | solution.py:298
  71.4 2.4 %collective-permute-start.22 = (bf16[528,128]{1,0:T(8,128)(2,1)S(1)}, bf16[528,128]{1,0:T(8,128)(2,1)S(1)}, u32[]{:S(2)}, u32[]{:S(2)}) collective-permute-start(bf16[528,128]{1,0:T(8,128)(2,1)S(1)} %get-tuple-element.13), channel_id=1, source_target_pairs={{0,224},{32,192},{64,160},{96,128},{128,96},{160,64},{192,32},{224... | collective-permute-start | bytes 405512 | tf_op jit(solution)/shard_map/ppermute | solution.py:298
  73.8 0.3 collective-permute-done.20.refs_5_
  74.1 1.9 %collective-permute-done.21.refs_6_ = bf16[528,128]{1,0:T(8,128)(2,1)S(1)} collective-permute-done((bf16[528,128]{1,0:T(8,128)(2,1)S(1)}, bf16[528,128]{1,0:T(8,128)(2,1)S(1)}, u32[]{:S(2)}, u32[]{:S(2)}) %collective-permute-start.21) | collective-permute-done | bytes 135200 | tf_op jit(solution)/shard_map/ppermute | solution.py:298
  75.9 3.2 %collective-permute-done.22.refs_7_ = bf16[528,128]{1,0:T(8,128)(2,1)S(1)} collective-permute-done((bf16[528,128]{1,0:T(8,128)(2,1)S(1)}, bf16[528,128]{1,0:T(8,128)(2,1)S(1)}, u32[]{:S(2)}, u32[]{:S(2)}) %collective-permute-start.22) | collective-permute-done | bytes 135200 | tf_op jit(solution)/shard_map/ppermute | solution.py:298
  79.2 0.6 copy-done.9
  79.8 2.3 %shard_map.84 = bf16[128,512]{1,0:T(8,128)(2,1)} custom-call(s32[3]{0:T(128)} %pad_add_fusion.ids_ref, bf16[528,128]{1,0:T(8,128)(2,1)} %get-tuple-element.20.refs_0_, bf16[528,128]{1,0:T(8,128)(2,1)} %copy-done.3, bf16[528,128]{1,0:T(8,128)(2,1)} %copy-done.4, bf16[528,128]{1,0:T(8,128)(2,1)} %copy-done.5, bf16[528,128]{1,0:T(8,128)(2,1)} %copy-done.6, ...), custom_call_target="tpu_custom_call" | custom-call | tf_op jit(solution)/shard_map/pallas_call | solution.py:263
  82.1 2.4 %convolution_convert_fusion.1 = bf16[128,2688]{1,0:T(8,128)(2,1)S(1)} fusion(bf16[128,512]{1,0:T(8,128)(2,1)} %shard_map.84, bf16[512,5376]{1,0:T(8,128)(2,1)} %param.14), kind=kOutput, calls=%fused_computation.1 | convolution fusion | flops 352665600 | bytes 3571712 | tf_op jit(solution)/shard_map/dot_general | solution.py:279
  84.5 2.4 %convolution_convert_fusion = bf16[128,2688]{1,0:T(8,128)(2,1)S(1)} fusion(bf16[128,512]{1,0:T(8,128)(2,1)S(1)} %copy-done.10, bf16[512,5376]{1,0:T(8,128)(2,1)} %param.14), kind=kOutput, calls=%fused_computation | convolution fusion | flops 352665600 | bytes 3571712 | tf_op jit(solution)/shard_map/dot_general | solution.py:279
  87.0 6.2 %collective-permute-start.23 = (bf16[2,32,2688]{2,1,0:T(8,128)(2,1)S(1)}, bf16[2,32,2688]{2,1,0:T(8,128)(2,1)S(1)}, u32[]{:S(2)}, u32[]{:S(2)}) collective-permute-start(bf16[2,32,2688]{2,1,0:T(8,128)(2,1)S(1)} %bitcast.45), channel_id=1, source_target_pairs={{0,1},{1,0},{2,3},{3,2},{4,5},{5,4},{6,7},{7,6},{8,9},{9,8},{10,11... | collective-permute-start | bytes 1032200 | tf_op jit(solution)/shard_map/ppermute | solution.py:281
  93.3 0.1 collective-permute-start.25
  93.4 1.1 %collective-permute-done.23 = bf16[2,32,2688]{2,1,0:T(8,128)(2,1)S(1)} collective-permute-done((bf16[2,32,2688]{2,1,0:T(8,128)(2,1)S(1)}, bf16[2,32,2688]{2,1,0:T(8,128)(2,1)S(1)}, u32[]{:S(2)}, u32[]{:S(2)}) %collective-permute-start.23) | collective-permute-done | bytes 344096 | tf_op jit(solution)/shard_map/ppermute | solution.py:281
  94.6 2.8 %collective-permute-start.24 = (bf16[32,2688]{1,0:T(8,128)(2,1)S(1)}, bf16[32,2688]{1,0:T(8,128)(2,1)S(1)}, u32[]{:S(2)}, u32[]{:S(2)}) collective-permute-start(bf16[32,2688]{1,0:T(8,128)(2,1)S(1)} %fusion.4), channel_id=1, source_target_pairs={{0,2},{2,0},{1,3},{3,1},{4,6},{6,4},{5,7},{7,5},{8,10},{10,8},{9,1... | collective-permute-start | bytes 516104 | tf_op jit(solution)/shard_map/ppermute | solution.py:285
  97.5 0.4 collective-permute-start.26
  97.9 3.9 %collective-permute-done.24 = bf16[32,2688]{1,0:T(8,128)(2,1)S(1)} collective-permute-done((bf16[32,2688]{1,0:T(8,128)(2,1)S(1)}, bf16[32,2688]{1,0:T(8,128)(2,1)S(1)}, u32[]{:S(2)}, u32[]{:S(2)}) %collective-permute-start.24) | collective-permute-done | bytes 172064 | tf_op jit(solution)/shard_map/ppermute | solution.py:285
  101.8 3.8 %collective-permute-done.26 = bf16[32,2688]{1,0:T(8,128)(2,1)S(1)} collective-permute-done((bf16[32,2688]{1,0:T(8,128)(2,1)S(1)}, bf16[32,2688]{1,0:T(8,128)(2,1)S(1)}, u32[]{:S(2)}, u32[]{:S(2)}) %collective-permute-start.26) | collective-permute-done | bytes 172064 | tf_op jit(solution)/shard_map/ppermute | solution.py:285
  105.6 0.8 pad_maximum_fusion
  (54 shorter events, 0.8 us)
Async XLA Ops:
  3.0 14.9 %collective-permute-start = (bf16[64,512]{1,0:T(8,128)(2,1)}, bf16[64,512]{1,0:T(8,128)(2,1)S(1)}, u32[]{:S(2)}, u32[]{:S(2)}) collective-permute-start(bf16[64,512]{1,0:T(8,128)(2,1)} %get-tuple-element.9), channel_id=1, source_target_pairs={{0,0},{4,8},{8,16},{12,24},{16,4},{20,12},{24,20},{28,28},{128,156... | collective-permute-start | bytes 196616 | tf_op jit(solution)/shard_map/ppermute | solution.py:113
  4.5 21.0 %collective-permute-start.2 = (bf16[64,512]{1,0:T(8,128)(2,1)}, bf16[64,512]{1,0:T(8,128)(2,1)S(1)}, u32[]{:S(2)}, u32[]{:S(2)}) collective-permute-start(bf16[64,512]{1,0:T(8,128)(2,1)} %get-tuple-element.9), channel_id=1, source_target_pairs={{0,128},{4,136},{8,144},{12,152},{16,132},{20,140},{24,148},{28,15... | collective-permute-start | bytes 196616 | tf_op jit(solution)/shard_map/ppermute | solution.py:113
  12.6 12.8 %collective-permute-start.1 = (bf16[64,512]{1,0:T(8,128)(2,1)}, bf16[64,512]{1,0:T(8,128)(2,1)S(1)}, u32[]{:S(2)}, u32[]{:S(2)}) collective-permute-start(bf16[64,512]{1,0:T(8,128)(2,1)} %get-tuple-element.10), channel_id=1, source_target_pairs={{0,4},{4,12},{8,20},{12,28},{16,0},{20,8},{24,16},{28,24},{128,152... | collective-permute-start | bytes 196616 | tf_op jit(solution)/shard_map/ppermute | solution.py:113
  14.5 11.0 %collective-permute-start.3 = (bf16[64,512]{1,0:T(8,128)(2,1)}, bf16[64,512]{1,0:T(8,128)(2,1)S(1)}, u32[]{:S(2)}, u32[]{:S(2)}) collective-permute-start(bf16[64,512]{1,0:T(8,128)(2,1)} %get-tuple-element.10), channel_id=1, source_target_pairs={{0,132},{4,140},{8,148},{12,156},{16,128},{20,136},{24,144},{28,15... | collective-permute-start | bytes 196616 | tf_op jit(solution)/shard_map/ppermute | solution.py:113
  17.8 10.7 %collective-permute-start.8 = (bf16[128,256]{1,0:T(8,128)(2,1)}, bf16[128,256]{1,0:T(8,128)(2,1)S(1)}, u32[]{:S(2)}, u32[]{:S(2)}) collective-permute-start(bf16[128,256]{1,0:T(8,128)(2,1)} %get-tuple-element.11.refs_6_), channel_id=1, source_target_pairs={{0,4},{4,0},{8,12},{12,8},{16,20},{20,16},{24,28},{28,24},{1,5},{5... | collective-permute-start | bytes 196616 | tf_op jit(solution)/shard_map/ppermute | solution.py:75
  17.9 11.5 %collective-permute-start.12 = (bf16[128,256]{1,0:T(8,128)(2,1)}, bf16[128,256]{1,0:T(8,128)(2,1)S(1)}, u32[]{:S(2)}, u32[]{:S(2)}) collective-permute-start(bf16[128,256]{1,0:T(8,128)(2,1)} %get-tuple-element.12.refs_11_), channel_id=1, source_target_pairs={{0,28},{4,8},{8,4},{12,16},{16,12},{20,24},{24,20},{28,0},{1,29},{... | collective-permute-start | bytes 196616 | tf_op jit(solution)/shard_map/ppermute | solution.py:75
  25.5 5.8 %collective-permute-start.6 = (bf16[256,256]{1,0:T(8,128)(2,1)S(1)}, bf16[256,256]{1,0:T(8,128)(2,1)S(1)}, u32[]{:S(2)}, u32[]{:S(2)}) collective-permute-start(bf16[256,256]{1,0:T(8,128)(2,1)S(1)} %pad_maximum_fusion.2.refs_3_), channel_id=1, source_target_pairs={{0,96},{32,64},{64,32},{96,0},{1,97},{33,65},{65,33},{97,1},{2,98}... | collective-permute-start | bytes 393224 | tf_op jit(solution)/shard_map/ppermute | solution.py:121
  28.4 4.0 %collective-permute-start.4 = (bf16[256,256]{1,0:T(8,128)(2,1)S(1)}, bf16[256,256]{1,0:T(8,128)(2,1)S(1)}, u32[]{:S(2)}, u32[]{:S(2)}) collective-permute-start(bf16[256,256]{1,0:T(8,128)(2,1)S(1)} %pad_maximum_fusion.1.refs_0_), channel_id=1, source_target_pairs={{0,32},{32,0},{64,96},{96,64},{1,33},{33,1},{65,97},{97,65},{2,34}... | collective-permute-start | bytes 393224 | tf_op jit(solution)/shard_map/ppermute | solution.py:121
  29.3 5.1 %collective-permute-start.9 = (bf16[256,256]{1,0:T(8,128)(2,1)S(1)}, bf16[256,256]{1,0:T(8,128)(2,1)S(1)}, u32[]{:S(2)}, u32[]{:S(2)}) collective-permute-start(bf16[256,256]{1,0:T(8,128)(2,1)S(1)} %pad_maximum_fusion.3), channel_id=1, source_target_pairs={{0,28},{4,8},{8,4},{12,16},{16,12},{20,24},{24,20},{28,0},{1,29},{... | collective-permute-start | bytes 393224 | tf_op jit(solution)/shard_map/ppermute | solution.py:76
  30.3 4.2 %collective-permute-start.13 = (bf16[256,256]{1,0:T(8,128)(2,1)S(1)}, bf16[256,256]{1,0:T(8,128)(2,1)S(1)}, u32[]{:S(2)}, u32[]{:S(2)}) collective-permute-start(bf16[256,256]{1,0:T(8,128)(2,1)S(1)} %pad_maximum_fusion.4), channel_id=1, source_target_pairs={{0,4},{4,0},{8,12},{12,8},{16,20},{20,16},{24,28},{28,24},{1,5},{5... | collective-permute-start | bytes 393224 | tf_op jit(solution)/shard_map/ppermute | solution.py:76
  31.3 9.3 %collective-permute-start.7 = (bf16[512,256]{1,0:T(8,128)(2,1)S(1)}, bf16[512,256]{1,0:T(8,128)(2,1)S(1)}, u32[]{:S(2)}, u32[]{:S(2)}) collective-permute-start(bf16[512,256]{1,0:T(8,128)(2,1)S(1)} %constant_dynamic-update-slice_fusion.5), channel_id=1, source_target_pairs={{0,32},{32,0},{64,96},{96,64},{1,33},{33,1},{65,97},{97,65},{2,34}... | collective-permute-start | bytes 786440 | tf_op jit(solution)/shard_map/ppermute | solution.py:122
  32.4 8.2 %collective-permute-start.5 = (bf16[512,256]{1,0:T(8,128)(2,1)S(1)}, bf16[512,256]{1,0:T(8,128)(2,1)S(1)}, u32[]{:S(2)}, u32[]{:S(2)}) collective-permute-start(bf16[512,256]{1,0:T(8,128)(2,1)S(1)} %constant_dynamic-update-slice_fusion), channel_id=1, source_target_pairs={{0,96},{32,64},{64,32},{96,0},{1,97},{33,65},{65,33},{97,1},{2,98}... | collective-permute-start | bytes 786440 | tf_op jit(solution)/shard_map/ppermute | solution.py:122
  34.5 4.3 %collective-permute-start.10 = (bf16[256,256]{1,0:T(8,128)(2,1)S(1)}, bf16[256,256]{1,0:T(8,128)(2,1)S(1)}, u32[]{:S(2)}, u32[]{:S(2)}) collective-permute-start(bf16[256,256]{1,0:T(8,128)(2,1)S(1)} %collective-permute-done.9.refs_8_), channel_id=1, source_target_pairs={{0,4},{4,0},{8,12},{12,8},{16,20},{20,16},{24,28},{28,24},{1,5},{5... | collective-permute-start | bytes 393224 | tf_op jit(solution)/shard_map/ppermute | solution.py:77
  34.5 5.9 %collective-permute-start.14 = (bf16[256,256]{1,0:T(8,128)(2,1)S(1)}, bf16[256,256]{1,0:T(8,128)(2,1)S(1)}, u32[]{:S(2)}, u32[]{:S(2)}) collective-permute-start(bf16[256,256]{1,0:T(8,128)(2,1)S(1)} %collective-permute-done.13.refs_13_), channel_id=1, source_target_pairs={{0,28},{4,8},{8,4},{12,16},{16,12},{20,24},{24,20},{28,0},{1,29},{... | collective-permute-start | bytes 393224 | tf_op jit(solution)/shard_map/ppermute | solution.py:77
  38.8 6.5 %collective-permute-start.11 = (bf16[256,256]{1,0:T(8,128)(2,1)S(1)}, bf16[256,256]{1,0:T(8,128)(2,1)S(1)}, u32[]{:S(2)}, u32[]{:S(2)}) collective-permute-start(bf16[256,256]{1,0:T(8,128)(2,1)S(1)} %collective-permute-done.10.refs_9_), channel_id=1, source_target_pairs={{0,28},{4,8},{8,4},{12,16},{16,12},{20,24},{24,20},{28,0},{1,29},{... | collective-permute-start | bytes 393224 | tf_op jit(solution)/shard_map/ppermute | solution.py:78
  40.4 4.8 %collective-permute-start.15 = (bf16[256,256]{1,0:T(8,128)(2,1)S(1)}, bf16[256,256]{1,0:T(8,128)(2,1)S(1)}, u32[]{:S(2)}, u32[]{:S(2)}) collective-permute-start(bf16[256,256]{1,0:T(8,128)(2,1)S(1)} %collective-permute-done.14.refs_14_), channel_id=1, source_target_pairs={{0,4},{4,0},{8,12},{12,8},{16,20},{20,16},{24,28},{28,24},{1,5},{5... | collective-permute-start | bytes 393224 | tf_op jit(solution)/shard_map/ppermute | solution.py:78
  45.2 0.8 copy-start
  46.1 0.8 copy-start.1
  46.9 0.6 copy-start.2
  61.1 8.2 %collective-permute-start.16 = (bf16[528,128]{1,0:T(8,128)(2,1)S(1)}, bf16[528,128]{1,0:T(8,128)(2,1)S(1)}, u32[]{:S(2)}, u32[]{:S(2)}) collective-permute-start(bf16[528,128]{1,0:T(8,128)(2,1)S(1)} %get-tuple-element.19), channel_id=1, source_target_pairs={{0,32},{32,0},{64,96},{96,64},{128,160},{160,128},{192,224},{224,1... | collective-permute-start | bytes 405512 | tf_op jit(solution)/shard_map/ppermute | solution.py:298
  62.9 8.5 %collective-permute-start.17 = (bf16[528,128]{1,0:T(8,128)(2,1)S(1)}, bf16[528,128]{1,0:T(8,128)(2,1)S(1)}, u32[]{:S(2)}, u32[]{:S(2)}) collective-permute-start(bf16[528,128]{1,0:T(8,128)(2,1)S(1)} %get-tuple-element.18), channel_id=1, source_target_pairs={{0,64},{32,96},{64,0},{96,32},{128,192},{160,224},{192,128},{224,1... | collective-permute-start | bytes 405512 | tf_op jit(solution)/shard_map/ppermute | solution.py:298
  63.7 10.1 %collective-permute-start.18 = (bf16[528,128]{1,0:T(8,128)(2,1)S(1)}, bf16[528,128]{1,0:T(8,128)(2,1)S(1)}, u32[]{:S(2)}, u32[]{:S(2)}) collective-permute-start(bf16[528,128]{1,0:T(8,128)(2,1)S(1)} %get-tuple-element.17), channel_id=1, source_target_pairs={{0,96},{32,64},{64,32},{96,0},{128,224},{160,192},{192,160},{224,1... | collective-permute-start | bytes 405512 | tf_op jit(solution)/shard_map/ppermute | solution.py:298
  65.2 8.6 %collective-permute-start.19 = (bf16[528,128]{1,0:T(8,128)(2,1)S(1)}, bf16[528,128]{1,0:T(8,128)(2,1)S(1)}, u32[]{:S(2)}, u32[]{:S(2)}) collective-permute-start(bf16[528,128]{1,0:T(8,128)(2,1)S(1)} %get-tuple-element.16), channel_id=1, source_target_pairs={{0,128},{32,160},{64,192},{96,224},{128,0},{160,32},{192,64},{224,... | collective-permute-start | bytes 405512 | tf_op jit(solution)/shard_map/ppermute | solution.py:298
  69.3 4.8 %collective-permute-start.20 = (bf16[528,128]{1,0:T(8,128)(2,1)S(1)}, bf16[528,128]{1,0:T(8,128)(2,1)S(1)}, u32[]{:S(2)}, u32[]{:S(2)}) collective-permute-start(bf16[528,128]{1,0:T(8,128)(2,1)S(1)} %get-tuple-element.15), channel_id=1, source_target_pairs={{0,160},{32,128},{64,224},{96,192},{128,32},{160,0},{192,96},{224,... | collective-permute-start | bytes 405512 | tf_op jit(solution)/shard_map/ppermute | solution.py:298
  69.3 9.8 %copy-start.3 = (bf16[528,128]{1,0:T(8,128)(2,1)}, bf16[528,128]{1,0:T(8,128)(2,1)S(1)}, u32[]{:S(2)}) copy-start(bf16[528,128]{1,0:T(8,128)(2,1)S(1)} %collective-permute-done.16.refs_1_) | copy-start | bytes 405508
  69.3 6.6 %collective-permute-start.21 = (bf16[528,128]{1,0:T(8,128)(2,1)S(1)}, bf16[528,128]{1,0:T(8,128)(2,1)S(1)}, u32[]{:S(2)}, u32[]{:S(2)}) collective-permute-start(bf16[528,128]{1,0:T(8,128)(2,1)S(1)} %get-tuple-element.14), channel_id=1, source_target_pairs={{0,192},{32,224},{64,128},{96,160},{128,64},{160,96},{192,0},{224,... | collective-permute-start | bytes 405512 | tf_op jit(solution)/shard_map/ppermute | solution.py:298
  71.4 7.8 %copy-start.4 = (bf16[528,128]{1,0:T(8,128)(2,1)}, bf16[528,128]{1,0:T(8,128)(2,1)S(1)}, u32[]{:S(2)}) copy-start(bf16[528,128]{1,0:T(8,128)(2,1)S(1)} %collective-permute-done.17.refs_2_) | copy-start | bytes 405508
  71.4 7.8 %collective-permute-start.22 = (bf16[528,128]{1,0:T(8,128)(2,1)S(1)}, bf16[528,128]{1,0:T(8,128)(2,1)S(1)}, u32[]{:S(2)}, u32[]{:S(2)}) collective-permute-start(bf16[528,128]{1,0:T(8,128)(2,1)S(1)} %get-tuple-element.13), channel_id=1, source_target_pairs={{0,224},{32,192},{64,160},{96,128},{128,96},{160,64},{192,32},{224... | collective-permute-start | bytes 405512 | tf_op jit(solution)/shard_map/ppermute | solution.py:298
  73.8 5.4 %copy-start.5 = (bf16[528,128]{1,0:T(8,128)(2,1)}, bf16[528,128]{1,0:T(8,128)(2,1)S(1)}, u32[]{:S(2)}) copy-start(bf16[528,128]{1,0:T(8,128)(2,1)S(1)} %collective-permute-done.18.refs_3_) | copy-start | bytes 405508
  73.8 5.4 %copy-start.6 = (bf16[528,128]{1,0:T(8,128)(2,1)}, bf16[528,128]{1,0:T(8,128)(2,1)S(1)}, u32[]{:S(2)}) copy-start(bf16[528,128]{1,0:T(8,128)(2,1)S(1)} %collective-permute-done.19.refs_4_) | copy-start | bytes 405508
  74.1 5.1 %copy-start.7 = (bf16[528,128]{1,0:T(8,128)(2,1)}, bf16[528,128]{1,0:T(8,128)(2,1)S(1)}, u32[]{:S(2)}) copy-start(bf16[528,128]{1,0:T(8,128)(2,1)S(1)} %collective-permute-done.20.refs_5_) | copy-start | bytes 405508
  75.9 3.2 %copy-start.8 = (bf16[528,128]{1,0:T(8,128)(2,1)}, bf16[528,128]{1,0:T(8,128)(2,1)S(1)}, u32[]{:S(2)}) copy-start(bf16[528,128]{1,0:T(8,128)(2,1)S(1)} %collective-permute-done.21.refs_6_) | copy-start | bytes 405508
  79.1 0.7 copy-start.9
  82.1 2.4 %copy-start.10 = (bf16[128,512]{1,0:T(8,128)(2,1)S(1)}, bf16[128,512]{1,0:T(8,128)(2,1)}, u32[]{:S(2)}) copy-start(bf16[128,512]{1,0:T(8,128)(2,1)} %shard_map.84) | copy-start | bytes 393220
  87.0 7.5 %collective-permute-start.23 = (bf16[2,32,2688]{2,1,0:T(8,128)(2,1)S(1)}, bf16[2,32,2688]{2,1,0:T(8,128)(2,1)S(1)}, u32[]{:S(2)}, u32[]{:S(2)}) collective-permute-start(bf16[2,32,2688]{2,1,0:T(8,128)(2,1)S(1)} %bitcast.45), channel_id=1, source_target_pairs={{0,1},{1,0},{2,3},{3,2},{4,5},{5,4},{6,7},{7,6},{8,9},{9,8},{10,11... | collective-permute-start | bytes 1032200 | tf_op jit(solution)/shard_map/ppermute | solution.py:281
  93.3 4.1 %collective-permute-start.25 = (bf16[2,32,2688]{2,1,0:T(8,128)(2,1)S(1)}, bf16[2,32,2688]{2,1,0:T(8,128)(2,1)S(1)}, u32[]{:S(2)}, u32[]{:S(2)}) collective-permute-start(bf16[2,32,2688]{2,1,0:T(8,128)(2,1)S(1)} %bitcast.44), channel_id=1, source_target_pairs={{0,1},{1,0},{2,3},{3,2},{4,5},{5,4},{6,7},{7,6},{8,9},{9,8},{10,11... | collective-permute-start | bytes 1032200 | tf_op jit(solution)/shard_map/ppermute | solution.py:281
  94.6 7.2 %collective-permute-start.24 = (bf16[32,2688]{1,0:T(8,128)(2,1)S(1)}, bf16[32,2688]{1,0:T(8,128)(2,1)S(1)}, u32[]{:S(2)}, u32[]{:S(2)}) collective-permute-start(bf16[32,2688]{1,0:T(8,128)(2,1)S(1)} %fusion.4), channel_id=1, source_target_pairs={{0,2},{2,0},{1,3},{3,1},{4,6},{6,4},{5,7},{7,5},{8,10},{10,8},{9,1... | collective-permute-start | bytes 516104 | tf_op jit(solution)/shard_map/ppermute | solution.py:285
  97.5 8.0 %collective-permute-start.26 = (bf16[32,2688]{1,0:T(8,128)(2,1)S(1)}, bf16[32,2688]{1,0:T(8,128)(2,1)S(1)}, u32[]{:S(2)}, u32[]{:S(2)}) collective-permute-start(bf16[32,2688]{1,0:T(8,128)(2,1)S(1)} %fusion.5), channel_id=1, source_target_pairs={{0,2},{2,0},{1,3},{3,1},{4,6},{6,4},{5,7},{7,5},{8,10},{10,8},{9,1... | collective-permute-start | bytes 516104 | tf_op jit(solution)/shard_map/ppermute | solution.py:285

commit v3 on v1

v3 whole, which is shorter than its diff:
```python
import functools

import jax
import jax.numpy as jnp
import numpy as np
from jax import lax
from jax.experimental import pallas as pl
from jax.experimental.pallas import tpu as pltpu
from jax.sharding import Mesh
from jax.sharding import PartitionSpec as P

EPSILON = 1e-06
HD = 128
PIECE = 128
NX, NY, NZ = 2, 4, 8
GROUP = NX * NY
QUERY_FACTOR = float(168.0**-0.5 / np.log(2.0))
NEGATIVE = -1e30
FREQUENCY = (1000000.0 ** (-2.0 * np.arange(64, dtype=np.float64) / 128)).astype(np.float32)
VMEM_LIMIT = 24 * 1024 * 1024
NT = (((1,), (1,)), ((), ()))


def pairs(count, partner):
    return [(i, partner(i)) for i in range(count)]


Z_PAIRS = (pairs(NZ, lambda i: i ^ 1), pairs(NZ, lambda i: (((i + 1) ^ 1) + 7) % 8))
Y_PAIRS = (pairs(NY, lambda i: i ^ 1), pairs(NY, lambda i: i ^ 3))
X_PAIRS = pairs(NX, lambda i: i ^ 1)
BLOCK = 64
STATS = 16
VMEM = pl.BlockSpec(memory_space=pltpu.VMEM)
SMEM = pl.BlockSpec(memory_space=pltpu.SMEM)


def rotate(vector, gain, cosines, sines):
    vector = vector.astype(jnp.float32)
    normed = vector * lax.rsqrt(jnp.mean(vector * vector, axis=-1, keepdims=True) + EPSILON) * gain
    return normed * cosines + pltpu.roll(normed, HD // 2, 1) * sines


def prepare_queries_kernel(q_ref, pos_ref, freq_ref, gain_ref, q_out, cos_out, sin_out):
    lane = lax.broadcasted_iota(jnp.int32, (PIECE, HD), 1)
    spread = jnp.broadcast_to(pos_ref[...].astype(jnp.float32), (PIECE, HD))
    angles = jnp.transpose(spread) * freq_ref[...]
    cosines = jnp.cos(angles)
    sines = jnp.where(lane < HD // 2, -1.0, 1.0) * jnp.sin(angles)
    cos_out[...] = cosines
    sin_out[...] = sines
    for head in range(4):
        cols = slice(head * HD, (head + 1) * HD)
        rows = rotate(q_ref[:, cols], gain_ref[...], cosines, sines)
        q_out[:, cols] = (rows * QUERY_FACTOR).astype(jnp.bfloat16)


def prepare_queries(queries, positions, gain):
    freq = jnp.asarray(np.concatenate([FREQUENCY, FREQUENCY])[None, :])
    table = jax.ShapeDtypeStruct((PIECE, HD), jnp.float32)
    return pl.pallas_call(
        prepare_queries_kernel,
        out_shape=(jax.ShapeDtypeStruct((PIECE, 4 * HD), jnp.bfloat16), table, table),
        in_specs=[VMEM] * 4,
        out_specs=(VMEM,) * 3,
    )(queries, positions[None, :], freq, gain[None, :])


def prepare_keys_kernel(k_ref, v_ref, cos_ref, sin_ref, gain_ref, kv0_out, kv1_out):
    for head, out in enumerate((kv0_out, kv1_out)):
        cols = slice(head * HD, (head + 1) * HD)
        rows = rotate(k_ref[:, cols], gain_ref[...], cos_ref[...], sin_ref[...])
        out[:, :HD] = rows.astype(jnp.bfloat16)
        out[:, HD:] = v_ref[:, cols]


def prepare_keys(keys, values, cosines, sines, gain):
    key_value = jax.ShapeDtypeStruct((PIECE, 2 * HD), jnp.bfloat16)
    return pl.pallas_call(
        prepare_keys_kernel,
        out_shape=(key_value, key_value),
        in_specs=[VMEM] * 5,
        out_specs=(VMEM,) * 2,
    )(keys, values, cosines, sines, gain[None, :])


def gather_z(own, first):
    here, there = Z_PAIRS[first], Z_PAIRS[1 - first]
    one = lax.ppermute(own, "z", here)
    two = lax.ppermute(jnp.concatenate([own, one], axis=0), "z", there)
    three = lax.ppermute(two, "z", here)
    four = lax.ppermute(three, "z", there)
    return [own, one, two, three, four]


def z_partner(which, z):
    return z ^ 1 if which == 0 else (((z + 1) ^ 1) + 7) & 7


def z_order(first, z):
    here = functools.partial(z_partner, first)
    there = functools.partial(z_partner, 1 - first)
    two = [there(z), here(there(z))]
    near = here(z)
    three = [there(near), here(there(near))]
    far = there(z)
    far_near = here(far)
    four = [there(far_near), here(there(far_near))]
    return [z, near] + two + three + four


def move_pairs():
    return [(x * NZ + z, x * NZ + ((((z & 3) ^ (3 * x)) << 1) | (z >> 2))) for x in range(NX) for z in range(NZ)]


def gather_xy(own):
    both = jnp.concatenate([own, lax.ppermute(own, "x", X_PAIRS)], axis=0)
    result = [both]
    for half in range(2):
        cols = both[:, half * 2 * HD : (half + 1) * 2 * HD]
        near = lax.ppermute(cols, "y", Y_PAIRS[half])
        far = lax.ppermute(jnp.concatenate([cols, near], axis=0), "y", Y_PAIRS[1 - half])
        result += [near, far]
    return result


Y_STEPS = ((1, 3, 2), (3, 1, 2))


def attention_kernel(ids_ref, *refs):
    own, pieces = refs[0], (refs[5:10], refs[10:15])
    out_ref, q_s, k_s, v_s, level_s = refs[15:]
    group, z, w = ids_ref[0], ids_ref[1], ids_ref[3]
    x, y = group >> 2, group & 3
    for half in range(2):
        near, far = refs[1 + 2 * half], refs[2 + 2 * half]
        first, second, third = Y_STEPS[half]
        for rel_y, ref, base, col in (
            (0, own, 0, half * 2 * HD),
            (first, near, 0, 0),
            (second, far, 0, 0),
            (third, far, 2 * PIECE, 0),
        ):
            for rel_x in range(NX):
                rows = slice(base + rel_x * PIECE, base + (rel_x + 1) * PIECE)
                place = (x ^ rel_x) * NY + (y ^ rel_y)
                for j in range(2):
                    q_s[half, place, j] = ref[rows, col + j * HD : col + (j + 1) * HD]
        places = z_order(half, z)
        index = 0
        for piece in pieces[half]:
            for part in range(piece.shape[0] // PIECE):
                start = pl.multiple_of(places[index] * PIECE, PIECE)
                rows = slice(part * PIECE, (part + 1) * PIECE)
                k_s[half, pl.ds(start, PIECE), :] = piece[rows, :HD]
                v_s[half, pl.ds(start, PIECE), :] = piece[rows, HD:]
                index += 1
    level_s[...] = jnp.full((PIECE, HD), NEGATIVE, jnp.float32)

    keys = NZ * PIECE
    width = 4 * PIECE

    def slot(source):
        upper = source >> 2
        end_x = ((source >> 1) & 1) ^ w
        end_y = (((source & 1) ^ upper) << 1) | ((z & 1) ^ upper)
        return group ^ ((end_x << 2) | end_y)

    def one(half, pair, masked):
        query = q_s[half, pl.ds(pair * 2, 2)].reshape(width, HD)
        scores = lax.dot_general(query, k_s[half], NT, preferred_element_type=jnp.float32)
        if masked:
            row = lax.broadcasted_iota(jnp.int32, (width, 1), 0)
            source = pair * 2 + row // (2 * PIECE)
            at_z = ((z & 1) << 2) | ((z >> 1) ^ (3 * (source >> 2)))
            last = (source * NZ + at_z) * PIECE + row % PIECE - group * keys
            column = lax.broadcasted_iota(jnp.int32, (width, keys), 1)
            scores = jnp.where(column <= last, scores, NEGATIVE)
        highest = jnp.max(scores, axis=1, keepdims=True)
        weights = jnp.exp2(scores - highest)
        total = jnp.sum(weights, axis=1, keepdims=True)
        summed = jnp.dot(weights.astype(jnp.bfloat16), v_s[half], preferred_element_type=jnp.float32)
        normal = (summed / total).astype(jnp.bfloat16)
        level = highest + jnp.log2(total)
        lane = lax.broadcasted_iota(jnp.int32, (PIECE, HD), 1)
        for r in range(2):
            step = slot(pair * 2 + r)
            for j in range(2):
                base = (r * 2 + j) * PIECE
                head = half * 2 + j
                out_ref[step, :PIECE, head * HD : (head + 1) * HD] = normal[base : base + PIECE]
                level_s[...] = jnp.where(lane == step * 4 + head, level[base : base + PIECE], level_s[...])

    def body(pair, carry):
        full = pair * 2 > group
        none = pair * 2 + 1 < group

        @pl.when(full)
        def _():
            one(0, pair, False)
            one(1, pair, False)

        @pl.when(jnp.logical_not(jnp.logical_or(full, none)))
        def _():
            one(0, pair, True)
            one(1, pair, True)

        @pl.when(none)
        def _():
            for r in range(2):
                out_ref[slot(pair * 2 + r), :PIECE, :] = jnp.zeros((PIECE, 4 * HD), jnp.bfloat16)

        return carry

    lax.fori_loop(0, GROUP // 2, body, 0)
    levels = jnp.transpose(level_s[...])
    row = lax.broadcasted_iota(jnp.int32, (STATS, PIECE), 0)
    for step in range(GROUP):
        for head in range(4):
            line = jnp.broadcast_to(levels[step * 4 + head : step * 4 + head + 1], (STATS, PIECE))
            top = line.astype(jnp.bfloat16).astype(jnp.float32)
            middle = (line - top).astype(jnp.bfloat16).astype(jnp.float32)
            rest = line - top - middle
            stats = jnp.where(row == 0, top, jnp.where(row == 1, middle, jnp.where(row == 2, rest, 0.0)))
            out_ref[step, PIECE:, head * HD : (head + 1) * HD] = stats.astype(jnp.bfloat16)


def attention(ids, queries, pieces):
    flops = 2 * 2 * 4 * GROUP * PIECE * NZ * PIECE * HD
    return pl.pallas_call(
        attention_kernel,
        out_shape=jax.ShapeDtypeStruct((GROUP, PIECE + STATS, 4 * HD), jnp.bfloat16),
        in_specs=[SMEM] + [VMEM] * 15,
        out_specs=VMEM,
        scratch_shapes=[
            pltpu.VMEM((2, GROUP, 2, PIECE, HD), jnp.bfloat16),
            pltpu.VMEM((2, NZ * PIECE, HD), jnp.bfloat16),
            pltpu.VMEM((2, NZ * PIECE, HD), jnp.bfloat16),
            pltpu.VMEM((PIECE, HD), jnp.float32),
        ],
        compiler_params=pltpu.CompilerParams(vmem_limit_bytes=VMEM_LIMIT),
        cost_estimate=pl.CostEstimate(flops=flops, bytes_accessed=2**22, transcendentals=2**22),
    )(ids, *queries, *pieces[0], *pieces[1])


def combine_kernel(ids_ref, partial, *refs):
    pieces = [partial.at[0]] + list(refs[: GROUP - 1])
    keep_out, give_out = refs[GROUP - 1 :]
    second_stays = (ids_ref[0] & 1) == 1
    stats = [piece[PIECE:, :].astype(jnp.float32) for piece in pieces]
    levels = [s[0:1] + s[1:2] + s[2:3] for s in stats]
    highest = functools.reduce(jnp.maximum, levels)
    shares = [jnp.exp2(level - highest) for level in levels]
    scale = 1.0 / functools.reduce(jnp.add, shares)
    table = jnp.concatenate([share * scale for share in shares], axis=0)
    for head in range(4):
        lanes = slice(head * HD, (head + 1) * HD)
        columns = jnp.transpose(table[:, lanes])
        totals = []
        for first in (0, BLOCK):
            rows = slice(first, first + BLOCK)
            total = None
            for s in range(GROUP):
                term = pieces[s][rows, lanes].astype(jnp.float32) * columns[rows, s : s + 1]
                total = term if total is None else total + term
            totals.append(total)
        keep_out[:, lanes] = jnp.where(second_stays, totals[1], totals[0]).astype(jnp.bfloat16)
        give_out[:, lanes] = jnp.where(second_stays, totals[0], totals[1]).astype(jnp.bfloat16)


def combine(ids, partial, received):
    block = jax.ShapeDtypeStruct((BLOCK, 4 * HD), jnp.bfloat16)
    return pl.pallas_call(
        combine_kernel,
        out_shape=(block, block),
        in_specs=[SMEM] + [VMEM] * GROUP,
        out_specs=(VMEM, VMEM),
    )(ids, partial, *received)


TILE = 768


def project_kernel(ids_ref, kept, taken, weight, other_out, mine_out, rows_s):
    core = ids_ref[2]
    quarter = PIECE // 4
    kept_high = ((ids_ref[0] ^ ids_ref[1]) & 1) == 1
    first, second = kept[...], taken[...]
    low = jnp.where(kept_high, second, first)
    high = jnp.where(kept_high, first, second)
    for k, block in enumerate((low, high)):
        for part in range(2):
            own = 1 - (part ^ core)
            start = pl.multiple_of(own * BLOCK + k * quarter, quarter)
            rows_s[pl.ds(start, quarter), :] = block[part * quarter : (part + 1) * quarter]
    rows = rows_s[...]
    for tile in range(weight.shape[1] // TILE):
        lanes = slice(tile * TILE, (tile + 1) * TILE)
        product = jnp.dot(rows, weight[:, lanes], preferred_element_type=jnp.float32).astype(jnp.bfloat16)
        other_out[:, lanes] = product[:BLOCK]
        mine_out[:, lanes] = product[BLOCK:]


def project(ids, kept, taken, out_weight):
    half = jax.ShapeDtypeStruct((BLOCK, out_weight.shape[1]), jnp.bfloat16)
    return pl.pallas_call(
        project_kernel,
        out_shape=(half, half),
        in_specs=[SMEM] + [VMEM] * 3,
        out_specs=(VMEM, VMEM),
        scratch_shapes=[pltpu.VMEM((PIECE, 4 * HD), jnp.bfloat16)],
        compiler_params=pltpu.CompilerParams(vmem_limit_bytes=VMEM_LIMIT),
        cost_estimate=pl.CostEstimate(flops=2 * PIECE * 512 * 5376, bytes_accessed=2**23, transcendentals=0),
    )(ids, kept, taken, out_weight)


def on_device(queries, keys, values, positions, query_gain, key_gain, out_weight):
    x, y, z = lax.axis_index("x"), lax.axis_index("y"), lax.axis_index("z")
    w, c = lax.axis_index("w"), lax.axis_index("c")
    ids = jnp.stack([x * NY + y, z, c, w]).astype(jnp.int32)
    query_rows, cosines, sines = prepare_queries(queries, positions, query_gain)
    moved = lax.ppermute(query_rows, ("x", "z"), move_pairs())
    kv0, kv1 = prepare_keys(keys, values, cosines, sines, key_gain)
    pieces = (gather_z(kv0, 0), gather_z(kv1, 1))
    partial = attention(ids, gather_xy(moved), pieces)
    received = [
        lax.ppermute(partial[step], ("x", "y"), pairs(GROUP, lambda i: i ^ step)) for step in range(1, GROUP)
    ]
    kept, given = combine(ids, partial, received)
    taken = lax.ppermute(given, "z", Z_PAIRS[0])
    other, mine = project(ids, kept, taken, out_weight)
    got = lax.ppermute(other, "c", X_PAIRS)
    chip = (mine.astype(jnp.float32) + got.astype(jnp.float32)).reshape(2, PIECE // 4, -1)
    keep = lax.dynamic_index_in_dim(chip, w, 0, keepdims=False)
    give = lax.dynamic_index_in_dim(chip, 1 - w, 0, keepdims=False).astype(jnp.bfloat16)
    landed = lax.ppermute(give, ("x", "w"), pairs(4, lambda i: i ^ 3))
    return (keep + landed.astype(jnp.float32)).astype(jnp.bfloat16)


def solution(mesh):
    inner = Mesh(mesh.devices.reshape(NX, NY, NZ, 2, 2), ("x", "y", "z", "w", "c"))
    ctx, head = ("x", "y", "z"), ("w", "c")
    return jax.shard_map(
        on_device,
        mesh=inner,
        in_specs=(P(ctx, head), P(ctx, head), P(ctx, head), P(ctx), P(), P(), P(head, None)),
        out_specs=P(ctx + head, None),
        check_vma=False,
    )
```

time: 103 us -> 98.2 us (0.953)
  the two profiles are of different devices: /device:TPU:64 before, /device:TPU:1 now
where the time goes in v3:
time: 98.2 us; the launch traced here: 97.8 us
  starting transfers between devices  44.7 us (46%)
  waiting for transfers between devices  28 us (29%)
  Pallas kernels  18 us (18%)
  local copies, waits for them, and re-layouts  4.24 us (4%)
  other arithmetic  2.73 us (3%)
    ppermute x7, starting transfers between devices, on_device(): lax.ppermute(partial[step], ('x', 'y'), pairs(GROUP, lambda i: i ^ step))  9.69 us
    pallas_call x1, Pallas kernels, attention(): pl.pallas_call(attention_kernel, out_shape=jax.ShapeDtypeStruct((GROUP, P...  9.46 us
    ppermute x1, waiting for transfers between devices, on_device(): landed = lax.ppermute(give, ('x', 'w'), pairs(4, lambda i: i ^ 3))  9.04 us
    ppermute x1, starting transfers between devices, on_device(): got = lax.ppermute(other, 'c', X_PAIRS)  6.87 us
    ppermute x7, waiting for transfers between devices, on_device(): lax.ppermute(partial[step], ('x', 'y'), pairs(GROUP, lambda i: i ^ step))  6.43 us
    ppermute x2, starting transfers between devices, gather_z(): one = lax.ppermute(own, 'z', here)  6.41 us
    ppermute x2, starting transfers between devices, gather_z(): four = lax.ppermute(three, 'z', there)  5.89 us
    ppermute x1, starting transfers between devices, gather_xy(): both = jnp.concatenate([own, lax.ppermute(own, 'x', X_PAIRS)], axis=0)  5.06 us
  transfers between devices with their start and end apart: 24, of which 12 were waited for; matrix products, arithmetic and copies ran while one was open for 2% of the time, Pallas kernels for 0%

profile of v3, /device:TPU:1, one launch (start us, length us, event | category | flops | bytes accessed | tf_op | source)
XLA Modules:
  0.0 97.8 jit_solution(18223316475580993062)
XLA Ops:
  0.0 2.2 %shard_map.82 = (bf16[128,512]{1,0:T(8,128)(2,1)}, f32[128,128]{1,0:T(8,128)}, f32[128,128]{1,0:T(8,128)}) custom-call(bf16[128,512]{1,0:T(8,128)(2,1)} %q_ref.1, s32[1,128]{1,0:T(1,128)} %bitcast.30, f32[1,128]{1,0:T(1,128)} %constant.36.clone.freq_ref, f32[1,128]{1,0:T(1,128)} %bitcast.31), custom_call_target="tpu_custom_call" | custom-call | tf_op jit(solution)/shard_map/pallas_call | solution.py:60
  2.2 1.8 %shard_map.83 = (bf16[128,256]{1,0:T(8,128)(2,1)}, bf16[128,256]{1,0:T(8,128)(2,1)}) custom-call(bf16[128,256]{1,0:T(8,128)(2,1)} %k_ref.1, bf16[128,256]{1,0:T(8,128)(2,1)} %v_ref.1, f32[128,128]{1,0:T(8,128)} %get-tuple-element.15.cos_ref, f32[128,128]{1,0:T(8,128)} %get-tuple-element.16.sin_ref, f32[1,128]{1,0:T(1,128)} %bitcast.32), custom_call_target="tpu_custom_call" | custom-call | tf_op jit(solution)/shard_map/pallas_call | solution.py:78
  3.9 6.4 %collective-permute-start.10 = (bf16[128,256]{1,0:T(8,128)(2,1)}, bf16[128,256]{1,0:T(8,128)(2,1)S(1)}, u32[]{:S(2)}, u32[]{:S(2)}) collective-permute-start(bf16[128,256]{1,0:T(8,128)(2,1)} %get-tuple-element.18.refs_10_), channel_id=1, source_target_pairs={{0,28},{4,8},{8,4},{12,16},{16,12},{20,24},{24,20},{28,0},{1,29},{... | collective-permute-start | bytes 196616 | tf_op jit(solution)/shard_map/ppermute | solution.py:88
  10.3 1.6 %collective-permute-start = (bf16[128,512]{1,0:T(8,128)(2,1)}, bf16[128,512]{1,0:T(8,128)(2,1)S(1)}, u32[]{:S(2)}, u32[]{:S(2)}) collective-permute-start(bf16[128,512]{1,0:T(8,128)(2,1)} %get-tuple-element.14), channel_id=1, source_target_pairs={{0,0},{4,8},{8,16},{12,24},{16,4},{20,12},{24,20},{28,28},{128,152... | collective-permute-start | bytes 393224 | tf_op jit(solution)/shard_map/ppermute | solution.py:321
  11.9 0.0 collective-permute-start.6
  11.9 0.3 collective-permute-done.10.refs_11_
  12.2 0.8 pad_maximum_fusion.3
  13.1 1.2 %collective-permute-start.11 = (bf16[256,256]{1,0:T(8,128)(2,1)S(1)}, bf16[256,256]{1,0:T(8,128)(2,1)S(1)}, u32[]{:S(2)}, u32[]{:S(2)}) collective-permute-start(bf16[256,256]{1,0:T(8,128)(2,1)S(1)} %pad_maximum_fusion.3), channel_id=1, source_target_pairs={{0,4},{4,0},{8,12},{12,8},{16,20},{20,16},{24,28},{28,24},{1,5},{5... | collective-permute-start | bytes 393224 | tf_op jit(solution)/shard_map/ppermute | solution.py:89
  14.3 5.1 %collective-permute-start.1 = (bf16[128,512]{1,0:T(8,128)(2,1)S(1)}, bf16[128,512]{1,0:T(8,128)(2,1)S(1)}, u32[]{:S(2)}, u32[]{:S(2)}) collective-permute-start(bf16[128,512]{1,0:T(8,128)(2,1)S(1)} %collective-permute-done), channel_id=1, source_target_pairs={{0,128},{128,0},{1,129},{129,1},{2,130},{130,2},{3,131},{131,3},{4... | collective-permute-start | bytes 393224 | tf_op jit(solution)/shard_map/ppermute | solution.py:116
  19.4 0.0 collective-permute-done.6.refs_6_
  19.4 0.8 pad_maximum_fusion.2
  20.2 0.7 collective-permute-start.7
  20.9 0.8 collective-permute-done.1
  21.8 2.8 %collective-permute-start.4 = (bf16[256,256]{1,0:T(8,128)(2,1)S(1)}, bf16[256,256]{1,0:T(8,128)(2,1)S(1)}, u32[]{:S(2)}, u32[]{:S(2)}) collective-permute-start(bf16[256,256]{1,0:T(8,128)(2,1)S(1)} %get-tuple-element.30), channel_id=1, source_target_pairs={{0,96},{32,64},{64,32},{96,0},{1,97},{33,65},{65,33},{97,1},{2,98}... | collective-permute-start | bytes 393224 | tf_op jit(solution)/shard_map/ppermute | solution.py:120
  24.6 0.0 collective-permute-start.2
  24.6 1.3 %collective-permute-start.12 = (bf16[256,256]{1,0:T(8,128)(2,1)S(1)}, bf16[256,256]{1,0:T(8,128)(2,1)S(1)}, u32[]{:S(2)}, u32[]{:S(2)}) collective-permute-start(bf16[256,256]{1,0:T(8,128)(2,1)S(1)} %collective-permute-done.11.refs_12_), channel_id=1, source_target_pairs={{0,28},{4,8},{8,4},{12,16},{16,12},{20,24},{24,20},{28,0},{1,29},{... | collective-permute-start | bytes 393224 | tf_op jit(solution)/shard_map/ppermute | solution.py:90
  25.9 0.0 collective-permute-done.7.refs_7_
  25.9 1.1 %collective-permute-done.4.refs_3_ = bf16[256,256]{1,0:T(8,128)(2,1)S(1)} collective-permute-done((bf16[256,256]{1,0:T(8,128)(2,1)S(1)}, bf16[256,256]{1,0:T(8,128)(2,1)S(1)}, u32[]{:S(2)}, u32[]{:S(2)}) %collective-permute-start.4) | collective-permute-done | bytes 131104 | tf_op jit(solution)/shard_map/ppermute | solution.py:120
  27.0 0.5 collective-permute-start.5
  27.5 1.2 %collective-permute-done.2.refs_1_ = bf16[256,256]{1,0:T(8,128)(2,1)S(1)} collective-permute-done((bf16[256,256]{1,0:T(8,128)(2,1)S(1)}, bf16[256,256]{1,0:T(8,128)(2,1)S(1)}, u32[]{:S(2)}, u32[]{:S(2)}) %collective-permute-start.2) | collective-permute-done | bytes 131104 | tf_op jit(solution)/shard_map/ppermute | solution.py:120
  28.7 1.1 %collective-permute-start.3 = (bf16[512,256]{1,0:T(8,128)(2,1)S(1)}, bf16[512,256]{1,0:T(8,128)(2,1)S(1)}, u32[]{:S(2)}, u32[]{:S(2)}) collective-permute-start(bf16[512,256]{1,0:T(8,128)(2,1)S(1)} %pad_maximum_fusion), channel_id=1, source_target_pairs={{0,96},{32,64},{64,32},{96,0},{1,97},{33,65},{65,33},{97,1},{2,98}... | collective-permute-start | bytes 786440 | tf_op jit(solution)/shard_map/ppermute | solution.py:121
  29.9 1.4 %collective-permute-done.12.refs_13_ = bf16[256,256]{1,0:T(8,128)(2,1)S(1)} collective-permute-done((bf16[256,256]{1,0:T(8,128)(2,1)S(1)}, bf16[256,256]{1,0:T(8,128)(2,1)S(1)}, u32[]{:S(2)}, u32[]{:S(2)}) %collective-permute-start.12) | collective-permute-done | bytes 131104 | tf_op jit(solution)/shard_map/ppermute | solution.py:90
  31.2 5.9 %collective-permute-start.9 = (bf16[256,256]{1,0:T(8,128)(2,1)S(1)}, bf16[256,256]{1,0:T(8,128)(2,1)S(1)}, u32[]{:S(2)}, u32[]{:S(2)}) collective-permute-start(bf16[256,256]{1,0:T(8,128)(2,1)S(1)} %collective-permute-done.8.refs_8_), channel_id=1, source_target_pairs={{0,28},{4,8},{8,4},{12,16},{16,12},{20,24},{24,20},{28,0},{1,29},{... | collective-permute-start | bytes 393224 | tf_op jit(solution)/shard_map/ppermute | solution.py:91
  37.1 0.1 pad_add_fusion.ids_ref
  37.2 2.6 %collective-permute-done.9.refs_9_ = bf16[256,256]{1,0:T(8,128)(2,1)S(1)} collective-permute-done((bf16[256,256]{1,0:T(8,128)(2,1)S(1)}, bf16[256,256]{1,0:T(8,128)(2,1)S(1)}, u32[]{:S(2)}, u32[]{:S(2)}) %collective-permute-start.9) | collective-permute-done | bytes 131104 | tf_op jit(solution)/shard_map/ppermute | solution.py:91
  39.8 9.5 %shard_map.84.partial = bf16[8,144,512]{2,1,0:T(8,128)(2,1)S(1)} custom-call(s32[4]{0:T(128)S(1)} %pad_add_fusion.ids_ref, bf16[256,512]{1,0:T(8,128)(2,1)S(1)} %constant_dynamic-update-slice_fusion.refs_0_, bf16[256,256]{1,0:T(8,128)(2,1)S(1)} %collective-permute-done.2.refs_1_, bf16[512,256]{1,0:T(8,128)(2,1)S(1)} %collective-permute-done.3.refs_2_, ...), custom_call_target="tpu_custom_call" | custom-call | flops 2147483648 | bytes 4194304 | tf_op jit(solution)/shard_map/pallas_call | solution.py:229
  49.3 0.1 slice_bitcast_fusion
  49.4 0.6 collective-permute-start.14
  50.0 0.3 collective-permute-start.15
  50.3 3.0 %collective-permute-start.16 = (bf16[144,512]{1,0:T(8,128)(2,1)S(1)}, bf16[144,512]{1,0:T(8,128)(2,1)S(1)}, u32[]{:S(2)}, u32[]{:S(2)}) collective-permute-start(bf16[144,512]{1,0:T(8,128)(2,1)S(1)} %get-tuple-element.27), channel_id=1, source_target_pairs={{0,96},{32,64},{64,32},{96,0},{128,224},{160,192},{192,160},{224,1... | collective-permute-start | bytes 442376 | tf_op jit(solution)/shard_map/ppermute | solution.py:326
  53.3 0.5 collective-permute-start.18
  53.8 1.6 %collective-permute-start.19 = (bf16[144,512]{1,0:T(8,128)(2,1)S(1)}, bf16[144,512]{1,0:T(8,128)(2,1)S(1)}, u32[]{:S(2)}, u32[]{:S(2)}) collective-permute-start(bf16[144,512]{1,0:T(8,128)(2,1)S(1)} %get-tuple-element.24), channel_id=1, source_target_pairs={{0,192},{32,224},{64,128},{96,160},{128,64},{160,96},{192,0},{224,... | collective-permute-start | bytes 442376 | tf_op jit(solution)/shard_map/ppermute | solution.py:326
  55.4 0.2 collective-permute-done.15.refs_1_
  55.6 3.7 %collective-permute-start.20 = (bf16[144,512]{1,0:T(8,128)(2,1)S(1)}, bf16[144,512]{1,0:T(8,128)(2,1)S(1)}, u32[]{:S(2)}, u32[]{:S(2)}) collective-permute-start(bf16[144,512]{1,0:T(8,128)(2,1)S(1)} %get-tuple-element.23), channel_id=1, source_target_pairs={{0,224},{32,192},{64,160},{96,128},{128,96},{160,64},{192,32},{224... | collective-permute-start | bytes 442376 | tf_op jit(solution)/shard_map/ppermute | solution.py:326
  59.3 1.0 %collective-permute-done.19.refs_5_ = bf16[144,512]{1,0:T(8,128)(2,1)S(1)} collective-permute-done((bf16[144,512]{1,0:T(8,128)(2,1)S(1)}, bf16[144,512]{1,0:T(8,128)(2,1)S(1)}, u32[]{:S(2)}, u32[]{:S(2)}) %collective-permute-start.19) | collective-permute-done | bytes 147488 | tf_op jit(solution)/shard_map/ppermute | solution.py:326
  60.3 5.2 %collective-permute-done.20.refs_6_ = bf16[144,512]{1,0:T(8,128)(2,1)S(1)} collective-permute-done((bf16[144,512]{1,0:T(8,128)(2,1)S(1)}, bf16[144,512]{1,0:T(8,128)(2,1)S(1)}, u32[]{:S(2)}, u32[]{:S(2)}) %collective-permute-start.20) | collective-permute-done | bytes 147488 | tf_op jit(solution)/shard_map/ppermute | solution.py:326
  65.6 0.6 copy-done.13
  66.2 3.2 %shard_map.85 = (bf16[64,512]{1,0:T(8,128)(2,1)}, bf16[64,512]{1,0:T(8,128)(2,1)}) custom-call(s32[4]{0:T(128)} %copy-done.5, bf16[8,144,512]{2,1,0:T(8,128)(2,1)} %copy-done.1, bf16[144,512]{1,0:T(8,128)(2,1)} %copy-done.7, bf16[144,512]{1,0:T(8,128)(2,1)} %copy-done.8, bf16[144,512]{1,0:T(8,128)(2,1)} %copy-done.9, bf16[144,512]{1,0:T(8,128)(2,1)} %copy-done.10, ...), custom_call_target="tpu_custom_call" | custom-call | tf_op jit(solution)/shard_map/pallas_call | solution.py:272
  69.4 3.3 %collective-permute-done.21.taken = bf16[64,512]{1,0:T(8,128)(2,1)S(1)} collective-permute-done((bf16[64,512]{1,0:T(8,128)(2,1)}, bf16[64,512]{1,0:T(8,128)(2,1)S(1)}, u32[]{:S(2)}, u32[]{:S(2)}) %collective-permute-start.21) | collective-permute-done | bytes 65568 | tf_op jit(solution)/shard_map/ppermute | solution.py:329
  72.7 2.6 %copy-done = bf16[512,5376]{1,0:T(8,128)(2,1)S(1)} copy-done((bf16[512,5376]{1,0:T(8,128)(2,1)S(1)}, bf16[512,5376]{1,0:T(8,128)(2,1)}, u32[]{:S(2)}) %copy-start) | copy-done | bytes 5505048
  75.3 0.8 copy-done.2
  76.1 1.4 %shard_map.86 = (bf16[64,5376]{1,0:T(8,128)(2,1)S(1)}, bf16[64,5376]{1,0:T(8,128)(2,1)S(1)}) custom-call(s32[4]{0:T(128)S(1)} %copy-done.6, bf16[64,512]{1,0:T(8,128)(2,1)S(1)} %copy-done.2, bf16[64,512]{1,0:T(8,128)(2,1)S(1)} %collective-permute-done.21.taken, bf16[512,5376]{1,0:T(8,128)(2,1)S(1)} %copy-done), custom_call_target="tpu_custom_call" | custom-call | flops 704643072 | bytes 8388608 | tf_op jit(solution)/shard_map/pallas_call | solution.py:305
  77.6 6.9 %collective-permute-start.22 = (bf16[64,5376]{1,0:T(8,128)(2,1)S(1)}, bf16[64,5376]{1,0:T(8,128)(2,1)S(1)}, u32[]{:S(2)}, u32[]{:S(2)}) collective-permute-start(bf16[64,5376]{1,0:T(8,128)(2,1)S(1)} %get-tuple-element.22), channel_id=1, source_target_pairs={{0,1},{1,0},{2,3},{3,2},{4,5},{5,4},{6,7},{7,6},{8,9},{9,8},{10,11... | collective-permute-start | bytes 2064392 | tf_op jit(solution)/shard_map/ppermute | solution.py:331
  84.4 1.8 %collective-permute-done.22 = bf16[64,5376]{1,0:T(8,128)(2,1)S(1)} collective-permute-done((bf16[64,5376]{1,0:T(8,128)(2,1)S(1)}, bf16[64,5376]{1,0:T(8,128)(2,1)S(1)}, u32[]{:S(2)}, u32[]{:S(2)}) %collective-permute-start.22) | collective-permute-done | bytes 688160 | tf_op jit(solution)/shard_map/ppermute | solution.py:331
  86.2 0.1 convert_add_fusion
  86.4 1.5 %collective-permute-start.23 = (bf16[32,5376]{1,0:T(8,128)(2,1)S(1)}, bf16[32,5376]{1,0:T(8,128)(2,1)S(1)}, u32[]{:S(2)}, u32[]{:S(2)}) collective-permute-start(bf16[32,5376]{1,0:T(8,128)(2,1)S(1)} %fusion.1), channel_id=1, source_target_pairs={{0,130},{2,128},{128,2},{130,0},{1,131},{3,129},{129,3},{131,1},{4... | collective-permute-start | bytes 1032200 | tf_op jit(solution)/shard_map/ppermute | solution.py:335
  87.9 9.0 %collective-permute-done.23 = bf16[32,5376]{1,0:T(8,128)(2,1)S(1)} collective-permute-done((bf16[32,5376]{1,0:T(8,128)(2,1)S(1)}, bf16[32,5376]{1,0:T(8,128)(2,1)S(1)}, u32[]{:S(2)}, u32[]{:S(2)}) %collective-permute-start.23) | collective-permute-done | bytes 344096 | tf_op jit(solution)/shard_map/ppermute | solution.py:335
  97.0 0.8 fusion
  (45 shorter events, 0.2 us)
Async XLA Ops:
  3.9 35.9 %copy-start.3 = (bf16[128,256]{1,0:T(8,128)(2,1)S(1)}, bf16[128,256]{1,0:T(8,128)(2,1)}, u32[]{:S(2)}) copy-start(bf16[128,256]{1,0:T(8,128)(2,1)} %get-tuple-element.17.refs_5_) | copy-start | bytes 196612
  3.9 35.9 %copy-start.4 = (bf16[128,256]{1,0:T(8,128)(2,1)S(1)}, bf16[128,256]{1,0:T(8,128)(2,1)}, u32[]{:S(2)}) copy-start(bf16[128,256]{1,0:T(8,128)(2,1)} %get-tuple-element.18.refs_10_) | copy-start | bytes 196612
  3.9 8.3 %collective-permute-start.10 = (bf16[128,256]{1,0:T(8,128)(2,1)}, bf16[128,256]{1,0:T(8,128)(2,1)S(1)}, u32[]{:S(2)}, u32[]{:S(2)}) collective-permute-start(bf16[128,256]{1,0:T(8,128)(2,1)} %get-tuple-element.18.refs_10_), channel_id=1, source_target_pairs={{0,28},{4,8},{8,4},{12,16},{16,12},{20,24},{24,20},{28,0},{1,29},{... | collective-permute-start | bytes 196616 | tf_op jit(solution)/shard_map/ppermute | solution.py:88
  10.3 4.0 %collective-permute-start = (bf16[128,512]{1,0:T(8,128)(2,1)}, bf16[128,512]{1,0:T(8,128)(2,1)S(1)}, u32[]{:S(2)}, u32[]{:S(2)}) collective-permute-start(bf16[128,512]{1,0:T(8,128)(2,1)} %get-tuple-element.14), channel_id=1, source_target_pairs={{0,0},{4,8},{8,16},{12,24},{16,4},{20,12},{24,20},{28,28},{128,152... | collective-permute-start | bytes 393224 | tf_op jit(solution)/shard_map/ppermute | solution.py:321
  11.9 7.5 %collective-permute-start.6 = (bf16[128,256]{1,0:T(8,128)(2,1)}, bf16[128,256]{1,0:T(8,128)(2,1)S(1)}, u32[]{:S(2)}, u32[]{:S(2)}) collective-permute-start(bf16[128,256]{1,0:T(8,128)(2,1)} %get-tuple-element.17.refs_5_), channel_id=1, source_target_pairs={{0,4},{4,0},{8,12},{12,8},{16,20},{20,16},{24,28},{28,24},{1,5},{5... | collective-permute-start | bytes 196616 | tf_op jit(solution)/shard_map/ppermute | solution.py:88
  13.1 11.5 %collective-permute-start.11 = (bf16[256,256]{1,0:T(8,128)(2,1)S(1)}, bf16[256,256]{1,0:T(8,128)(2,1)S(1)}, u32[]{:S(2)}, u32[]{:S(2)}) collective-permute-start(bf16[256,256]{1,0:T(8,128)(2,1)S(1)} %pad_maximum_fusion.3), channel_id=1, source_target_pairs={{0,4},{4,0},{8,12},{12,8},{16,20},{20,16},{24,28},{28,24},{1,5},{5... | collective-permute-start | bytes 393224 | tf_op jit(solution)/shard_map/ppermute | solution.py:89
  14.3 7.4 %collective-permute-start.1 = (bf16[128,512]{1,0:T(8,128)(2,1)S(1)}, bf16[128,512]{1,0:T(8,128)(2,1)S(1)}, u32[]{:S(2)}, u32[]{:S(2)}) collective-permute-start(bf16[128,512]{1,0:T(8,128)(2,1)S(1)} %collective-permute-done), channel_id=1, source_target_pairs={{0,128},{128,0},{1,129},{129,1},{2,130},{130,2},{3,131},{131,3},{4... | collective-permute-start | bytes 393224 | tf_op jit(solution)/shard_map/ppermute | solution.py:116
  20.2 5.7 %collective-permute-start.7 = (bf16[256,256]{1,0:T(8,128)(2,1)S(1)}, bf16[256,256]{1,0:T(8,128)(2,1)S(1)}, u32[]{:S(2)}, u32[]{:S(2)}) collective-permute-start(bf16[256,256]{1,0:T(8,128)(2,1)S(1)} %pad_maximum_fusion.2), channel_id=1, source_target_pairs={{0,28},{4,8},{8,4},{12,16},{16,12},{20,24},{24,20},{28,0},{1,29},{... | collective-permute-start | bytes 393224 | tf_op jit(solution)/shard_map/ppermute | solution.py:89
  21.8 5.2 %collective-permute-start.4 = (bf16[256,256]{1,0:T(8,128)(2,1)S(1)}, bf16[256,256]{1,0:T(8,128)(2,1)S(1)}, u32[]{:S(2)}, u32[]{:S(2)}) collective-permute-start(bf16[256,256]{1,0:T(8,128)(2,1)S(1)} %get-tuple-element.30), channel_id=1, source_target_pairs={{0,96},{32,64},{64,32},{96,0},{1,97},{33,65},{65,33},{97,1},{2,98}... | collective-permute-start | bytes 393224 | tf_op jit(solution)/shard_map/ppermute | solution.py:120
  24.6 4.1 %collective-permute-start.2 = (bf16[256,256]{1,0:T(8,128)(2,1)S(1)}, bf16[256,256]{1,0:T(8,128)(2,1)S(1)}, u32[]{:S(2)}, u32[]{:S(2)}) collective-permute-start(bf16[256,256]{1,0:T(8,128)(2,1)S(1)} %get-tuple-element.31), channel_id=1, source_target_pairs={{0,32},{32,0},{64,96},{96,64},{1,33},{33,1},{65,97},{97,65},{2,34}... | collective-permute-start | bytes 393224 | tf_op jit(solution)/shard_map/ppermute | solution.py:120
  24.6 6.6 %collective-permute-start.12 = (bf16[256,256]{1,0:T(8,128)(2,1)S(1)}, bf16[256,256]{1,0:T(8,128)(2,1)S(1)}, u32[]{:S(2)}, u32[]{:S(2)}) collective-permute-start(bf16[256,256]{1,0:T(8,128)(2,1)S(1)} %collective-permute-done.11.refs_12_), channel_id=1, source_target_pairs={{0,28},{4,8},{8,4},{12,16},{16,12},{20,24},{24,20},{28,0},{1,29},{... | collective-permute-start | bytes 393224 | tf_op jit(solution)/shard_map/ppermute | solution.py:90
  25.9 5.4 %collective-permute-start.8 = (bf16[256,256]{1,0:T(8,128)(2,1)S(1)}, bf16[256,256]{1,0:T(8,128)(2,1)S(1)}, u32[]{:S(2)}, u32[]{:S(2)}) collective-permute-start(bf16[256,256]{1,0:T(8,128)(2,1)S(1)} %collective-permute-done.7.refs_7_), channel_id=1, source_target_pairs={{0,4},{4,0},{8,12},{12,8},{16,20},{20,16},{24,28},{28,24},{1,5},{5... | collective-permute-start | bytes 393224 | tf_op jit(solution)/shard_map/ppermute | solution.py:90
  27.0 12.8 %collective-permute-start.5 = (bf16[512,256]{1,0:T(8,128)(2,1)S(1)}, bf16[512,256]{1,0:T(8,128)(2,1)S(1)}, u32[]{:S(2)}, u32[]{:S(2)}) collective-permute-start(bf16[512,256]{1,0:T(8,128)(2,1)S(1)} %pad_maximum_fusion.1), channel_id=1, source_target_pairs={{0,32},{32,0},{64,96},{96,64},{1,33},{33,1},{65,97},{97,65},{2,34}... | collective-permute-start | bytes 786440 | tf_op jit(solution)/shard_map/ppermute | solution.py:121
  28.7 11.1 %collective-permute-start.3 = (bf16[512,256]{1,0:T(8,128)(2,1)S(1)}, bf16[512,256]{1,0:T(8,128)(2,1)S(1)}, u32[]{:S(2)}, u32[]{:S(2)}) collective-permute-start(bf16[512,256]{1,0:T(8,128)(2,1)S(1)} %pad_maximum_fusion), channel_id=1, source_target_pairs={{0,96},{32,64},{64,32},{96,0},{1,97},{33,65},{65,33},{97,1},{2,98}... | collective-permute-start | bytes 786440 | tf_op jit(solution)/shard_map/ppermute | solution.py:121
  31.2 6.0 %collective-permute-start.13 = (bf16[256,256]{1,0:T(8,128)(2,1)S(1)}, bf16[256,256]{1,0:T(8,128)(2,1)S(1)}, u32[]{:S(2)}, u32[]{:S(2)}) collective-permute-start(bf16[256,256]{1,0:T(8,128)(2,1)S(1)} %collective-permute-done.12.refs_13_), channel_id=1, source_target_pairs={{0,4},{4,0},{8,12},{12,8},{16,20},{20,16},{24,28},{28,24},{1,5},{5... | collective-permute-start | bytes 393224 | tf_op jit(solution)/shard_map/ppermute | solution.py:91
  31.2 8.5 %collective-permute-start.9 = (bf16[256,256]{1,0:T(8,128)(2,1)S(1)}, bf16[256,256]{1,0:T(8,128)(2,1)S(1)}, u32[]{:S(2)}, u32[]{:S(2)}) collective-permute-start(bf16[256,256]{1,0:T(8,128)(2,1)S(1)} %collective-permute-done.8.refs_8_), channel_id=1, source_target_pairs={{0,28},{4,8},{8,4},{12,16},{16,12},{20,24},{24,20},{28,0},{1,29},{... | collective-permute-start | bytes 393224 | tf_op jit(solution)/shard_map/ppermute | solution.py:91
  37.2 12.1 %copy-start.5 = (s32[4]{0:T(128)}, s32[4]{0:T(128)S(1)}, u32[]{:S(2)}) copy-start(s32[4]{0:T(128)S(1)} %pad_add_fusion.ids_ref) | copy-start | bytes 52
  49.3 16.3 %copy-start.1 = (bf16[8,144,512]{2,1,0:T(8,128)(2,1)}, bf16[8,144,512]{2,1,0:T(8,128)(2,1)S(1)}, u32[]{:S(2)}) copy-start(bf16[8,144,512]{2,1,0:T(8,128)(2,1)S(1)} %shard_map.84.partial) | copy-start | bytes 3538948
  49.4 23.4 %copy-start.6 = (s32[4]{0:T(128)S(1)}, s32[4]{0:T(128)}, u32[]{:S(2)}) copy-start(s32[4]{0:T(128)} %copy-done.5) | copy-start | bytes 52
  49.4 4.5 %collective-permute-start.14 = (bf16[144,512]{1,0:T(8,128)(2,1)S(1)}, bf16[144,512]{1,0:T(8,128)(2,1)S(1)}, u32[]{:S(2)}, u32[]{:S(2)}) collective-permute-start(bf16[144,512]{1,0:T(8,128)(2,1)S(1)} %get-tuple-element.29), channel_id=1, source_target_pairs={{0,32},{32,0},{64,96},{96,64},{128,160},{160,128},{192,224},{224,1... | collective-permute-start | bytes 442376 | tf_op jit(solution)/shard_map/ppermute | solution.py:326
  50.0 5.6 %collective-permute-start.15 = (bf16[144,512]{1,0:T(8,128)(2,1)S(1)}, bf16[144,512]{1,0:T(8,128)(2,1)S(1)}, u32[]{:S(2)}, u32[]{:S(2)}) collective-permute-start(bf16[144,512]{1,0:T(8,128)(2,1)S(1)} %get-tuple-element.28), channel_id=1, source_target_pairs={{0,64},{32,96},{64,0},{96,32},{128,192},{160,224},{192,128},{224,1... | collective-permute-start | bytes 442376 | tf_op jit(solution)/shard_map/ppermute | solution.py:326
  50.3 9.0 %collective-permute-start.16 = (bf16[144,512]{1,0:T(8,128)(2,1)S(1)}, bf16[144,512]{1,0:T(8,128)(2,1)S(1)}, u32[]{:S(2)}, u32[]{:S(2)}) collective-permute-start(bf16[144,512]{1,0:T(8,128)(2,1)S(1)} %get-tuple-element.27), channel_id=1, source_target_pairs={{0,96},{32,64},{64,32},{96,0},{128,224},{160,192},{192,160},{224,1... | collective-permute-start | bytes 442376 | tf_op jit(solution)/shard_map/ppermute | solution.py:326
  53.3 6.0 %collective-permute-start.17 = (bf16[144,512]{1,0:T(8,128)(2,1)S(1)}, bf16[144,512]{1,0:T(8,128)(2,1)S(1)}, u32[]{:S(2)}, u32[]{:S(2)}) collective-permute-start(bf16[144,512]{1,0:T(8,128)(2,1)S(1)} %get-tuple-element.26), channel_id=1, source_target_pairs={{0,128},{32,160},{64,192},{96,224},{128,0},{160,32},{192,64},{224,... | collective-permute-start | bytes 442376 | tf_op jit(solution)/shard_map/ppermute | solution.py:326
  53.3 6.0 %collective-permute-start.18 = (bf16[144,512]{1,0:T(8,128)(2,1)S(1)}, bf16[144,512]{1,0:T(8,128)(2,1)S(1)}, u32[]{:S(2)}, u32[]{:S(2)}) collective-permute-start(bf16[144,512]{1,0:T(8,128)(2,1)S(1)} %get-tuple-element.25), channel_id=1, source_target_pairs={{0,160},{32,128},{64,224},{96,192},{128,32},{160,0},{192,96},{224,... | collective-permute-start | bytes 442376 | tf_op jit(solution)/shard_map/ppermute | solution.py:326
  53.8 11.7 %copy-start.7 = (bf16[144,512]{1,0:T(8,128)(2,1)}, bf16[144,512]{1,0:T(8,128)(2,1)S(1)}, u32[]{:S(2)}) copy-start(bf16[144,512]{1,0:T(8,128)(2,1)S(1)} %collective-permute-done.14.refs_0_) | copy-start | bytes 442372
  53.8 6.5 %collective-permute-start.19 = (bf16[144,512]{1,0:T(8,128)(2,1)S(1)}, bf16[144,512]{1,0:T(8,128)(2,1)S(1)}, u32[]{:S(2)}, u32[]{:S(2)}) collective-permute-start(bf16[144,512]{1,0:T(8,128)(2,1)S(1)} %get-tuple-element.24), channel_id=1, source_target_pairs={{0,192},{32,224},{64,128},{96,160},{128,64},{160,96},{192,0},{224,... | collective-permute-start | bytes 442376 | tf_op jit(solution)/shard_map/ppermute | solution.py:326
  55.6 9.9 %copy-start.8 = (bf16[144,512]{1,0:T(8,128)(2,1)}, bf16[144,512]{1,0:T(8,128)(2,1)S(1)}, u32[]{:S(2)}) copy-start(bf16[144,512]{1,0:T(8,128)(2,1)S(1)} %collective-permute-done.15.refs_1_) | copy-start | bytes 442372
  55.6 9.9 %collective-permute-start.20 = (bf16[144,512]{1,0:T(8,128)(2,1)S(1)}, bf16[144,512]{1,0:T(8,128)(2,1)S(1)}, u32[]{:S(2)}, u32[]{:S(2)}) collective-permute-start(bf16[144,512]{1,0:T(8,128)(2,1)S(1)} %get-tuple-element.23), channel_id=1, source_target_pairs={{0,224},{32,192},{64,160},{96,128},{128,96},{160,64},{192,32},{224... | collective-permute-start | bytes 442376 | tf_op jit(solution)/shard_map/ppermute | solution.py:326
  59.3 6.3 %copy-start.9 = (bf16[144,512]{1,0:T(8,128)(2,1)}, bf16[144,512]{1,0:T(8,128)(2,1)S(1)}, u32[]{:S(2)}) copy-start(bf16[144,512]{1,0:T(8,128)(2,1)S(1)} %collective-permute-done.16.refs_2_) | copy-start | bytes 442372
  59.3 6.3 %copy-start.10 = (bf16[144,512]{1,0:T(8,128)(2,1)}, bf16[144,512]{1,0:T(8,128)(2,1)S(1)}, u32[]{:S(2)}) copy-start(bf16[144,512]{1,0:T(8,128)(2,1)S(1)} %collective-permute-done.17.refs_3_) | copy-start | bytes 442372
  59.3 6.3 %copy-start.11 = (bf16[144,512]{1,0:T(8,128)(2,1)}, bf16[144,512]{1,0:T(8,128)(2,1)S(1)}, u32[]{:S(2)}) copy-start(bf16[144,512]{1,0:T(8,128)(2,1)S(1)} %collective-permute-done.18.refs_4_) | copy-start | bytes 442372
  60.3 5.2 %copy-start.12 = (bf16[144,512]{1,0:T(8,128)(2,1)}, bf16[144,512]{1,0:T(8,128)(2,1)S(1)}, u32[]{:S(2)}) copy-start(bf16[144,512]{1,0:T(8,128)(2,1)S(1)} %collective-permute-done.19.refs_5_) | copy-start | bytes 442372
  65.6 0.6 copy-start.13
  69.4 3.3 %collective-permute-start.21 = (bf16[64,512]{1,0:T(8,128)(2,1)}, bf16[64,512]{1,0:T(8,128)(2,1)S(1)}, u32[]{:S(2)}, u32[]{:S(2)}) collective-permute-start(bf16[64,512]{1,0:T(8,128)(2,1)} %get-tuple-element.20), channel_id=1, source_target_pairs={{0,4},{4,0},{8,12},{12,8},{16,20},{20,16},{24,28},{28,24},{1,5},{5... | collective-permute-start | bytes 196616 | tf_op jit(solution)/shard_map/ppermute | solution.py:329
  72.7 2.6 %copy-start = (bf16[512,5376]{1,0:T(8,128)(2,1)S(1)}, bf16[512,5376]{1,0:T(8,128)(2,1)}, u32[]{:S(2)}) copy-start(bf16[512,5376]{1,0:T(8,128)(2,1)} %weight.1) | copy-start | bytes 16515076
  75.3 0.8 copy-start.2
  77.6 8.6 %collective-permute-start.22 = (bf16[64,5376]{1,0:T(8,128)(2,1)S(1)}, bf16[64,5376]{1,0:T(8,128)(2,1)S(1)}, u32[]{:S(2)}, u32[]{:S(2)}) collective-permute-start(bf16[64,5376]{1,0:T(8,128)(2,1)S(1)} %get-tuple-element.22), channel_id=1, source_target_pairs={{0,1},{1,0},{2,3},{3,2},{4,5},{5,4},{6,7},{7,6},{8,9},{9,8},{10,11... | collective-permute-start | bytes 2064392 | tf_op jit(solution)/shard_map/ppermute | solution.py:331
  86.4 10.6 %collective-permute-start.23 = (bf16[32,5376]{1,0:T(8,128)(2,1)S(1)}, bf16[32,5376]{1,0:T(8,128)(2,1)S(1)}, u32[]{:S(2)}, u32[]{:S(2)}) collective-permute-start(bf16[32,5376]{1,0:T(8,128)(2,1)S(1)} %fusion.1), channel_id=1, source_target_pairs={{0,130},{2,128},{128,2},{130,0},{1,131},{3,129},{129,3},{131,1},{4... | collective-permute-start | bytes 1032200 | tf_op jit(solution)/shard_map/ppermute | solution.py:335

commit v4 on v3

--- a/solution.py
+++ b/solution.py
@@ -25,8 +25,22 @@
     return [(i, partner(i)) for i in range(count)]
 
 
-Z_PAIRS = (pairs(NZ, lambda i: i ^ 1), pairs(NZ, lambda i: (((i + 1) ^ 1) + 7) % 8))
-Y_PAIRS = (pairs(NY, lambda i: i ^ 1), pairs(NY, lambda i: i ^ 3))
+def z_partner(which, z):
+    return z ^ 1 if which == 0 else (((z + 1) ^ 1) + 7) & 7
+
+
+def y_partner(which, y):
+    return y ^ (1, 3)[which]
+
+
+def by_core(count, partner):
+    return tuple(
+        [(i * 2 + core, partner(core ^ turn, i) * 2 + core) for i in range(count) for core in range(2)] for turn in range(2)
+    )
+
+
+Z_PAIRS = by_core(NZ, z_partner)
+Y_PAIRS = by_core(NY, y_partner)
 X_PAIRS = pairs(NX, lambda i: i ^ 1)
 BLOCK = 64
 STATS = 16
@@ -65,46 +79,46 @@
     )(queries, positions[None, :], freq, gain[None, :])
 
 
-def prepare_keys_kernel(k_ref, v_ref, cos_ref, sin_ref, gain_ref, kv0_out, kv1_out):
-    for head, out in enumerate((kv0_out, kv1_out)):
+def prepare_keys_kernel(k_ref, v_ref, cos_ref, sin_ref, gain_ref, out):
+    for head in range(2):
         cols = slice(head * HD, (head + 1) * HD)
         rows = rotate(k_ref[:, cols], gain_ref[...], cos_ref[...], sin_ref[...])
-        out[:, :HD] = rows.astype(jnp.bfloat16)
-        out[:, HD:] = v_ref[:, cols]
+        out[:, cols] = rows.astype(jnp.bfloat16)
+    out[:, 2 * HD :] = v_ref[...]
 
 
 def prepare_keys(keys, values, cosines, sines, gain):
-    key_value = jax.ShapeDtypeStruct((PIECE, 2 * HD), jnp.bfloat16)
     return pl.pallas_call(
         prepare_keys_kernel,
-        out_shape=(key_value, key_value),
+        out_shape=jax.ShapeDtypeStruct((PIECE, 4 * HD), jnp.bfloat16),
         in_specs=[VMEM] * 5,
-        out_specs=(VMEM,) * 2,
+        out_specs=VMEM,
     )(keys, values, cosines, sines, gain[None, :])
 
 
-def gather_z(own, first):
-    here, there = Z_PAIRS[first], Z_PAIRS[1 - first]
-    one = lax.ppermute(own, "z", here)
-    two = lax.ppermute(jnp.concatenate([own, one], axis=0), "z", there)
-    three = lax.ppermute(two, "z", here)
-    four = lax.ppermute(three, "z", there)
+def gather_z(own):
+    here, there = Z_PAIRS
+    one = lax.ppermute(own, ("z", "c"), here)
+    two = lax.ppermute(jnp.concatenate([own, one], axis=0), ("z", "c"), there)
+    three = lax.ppermute(two, ("z", "c"), here)
+    four = lax.ppermute(three, ("z", "c"), there)
     return [own, one, two, three, four]
 
 
-def z_partner(which, z):
-    return z ^ 1 if which == 0 else (((z + 1) ^ 1) + 7) & 7
-
-
-def z_order(first, z):
-    here = functools.partial(z_partner, first)
-    there = functools.partial(z_partner, 1 - first)
-    two = [there(z), here(there(z))]
-    near = here(z)
+def z_order(core, z):
+    def step(which, place):
+        return jnp.where(which == 0, z_partner(0, place), z_partner(1, place))
+
+    def here(place):
+        return step(core, place)
+
+    def there(place):
+        return step(1 - core, place)
+
+    far, near = there(z), here(z)
+    two = [far, here(far)]
     three = [there(near), here(there(near))]
-    far = there(z)
-    far_near = here(far)
-    four = [there(far_near), here(there(far_near))]
+    four = [there(here(far)), here(there(here(far)))]
     return [z, near] + two + three + four
 
 
@@ -114,46 +128,34 @@
 
 def gather_xy(own):
     both = jnp.concatenate([own, lax.ppermute(own, "x", X_PAIRS)], axis=0)
-    result = [both]
-    for half in range(2):
-        cols = both[:, half * 2 * HD : (half + 1) * 2 * HD]
-        near = lax.ppermute(cols, "y", Y_PAIRS[half])
-        far = lax.ppermute(jnp.concatenate([cols, near], axis=0), "y", Y_PAIRS[1 - half])
-        result += [near, far]
-    return result
-
-
-Y_STEPS = ((1, 3, 2), (3, 1, 2))
+    near = lax.ppermute(both, ("y", "c"), Y_PAIRS[0])
+    far = lax.ppermute(jnp.concatenate([both, near], axis=0), ("y", "c"), Y_PAIRS[1])
+    return both, near, far
 
 
 def attention_kernel(ids_ref, *refs):
-    own, pieces = refs[0], (refs[5:10], refs[10:15])
-    out_ref, q_s, k_s, v_s, level_s = refs[15:]
-    group, z, w = ids_ref[0], ids_ref[1], ids_ref[3]
+    own, near, far = refs[:3]
+    pieces = refs[3:8]
+    out_ref, q_s, k_s, v_s, level_s = refs[8:]
+    group, z, core, w = ids_ref[0], ids_ref[1], ids_ref[2], ids_ref[3]
     x, y = group >> 2, group & 3
-    for half in range(2):
-        near, far = refs[1 + 2 * half], refs[2 + 2 * half]
-        first, second, third = Y_STEPS[half]
-        for rel_y, ref, base, col in (
-            (0, own, 0, half * 2 * HD),
-            (first, near, 0, 0),
-            (second, far, 0, 0),
-            (third, far, 2 * PIECE, 0),
-        ):
-            for rel_x in range(NX):
-                rows = slice(base + rel_x * PIECE, base + (rel_x + 1) * PIECE)
-                place = (x ^ rel_x) * NY + (y ^ rel_y)
-                for j in range(2):
-                    q_s[half, place, j] = ref[rows, col + j * HD : col + (j + 1) * HD]
-        places = z_order(half, z)
-        index = 0
-        for piece in pieces[half]:
-            for part in range(piece.shape[0] // PIECE):
-                start = pl.multiple_of(places[index] * PIECE, PIECE)
-                rows = slice(part * PIECE, (part + 1) * PIECE)
-                k_s[half, pl.ds(start, PIECE), :] = piece[rows, :HD]
-                v_s[half, pl.ds(start, PIECE), :] = piece[rows, HD:]
-                index += 1
+    first = 1 + 2 * core
+    for rel_y, ref, base in ((0, own, 0), (first, near, 0), (4 - first, far, 0), (2, far, 2 * PIECE)):
+        for rel_x in range(NX):
+            rows = slice(base + rel_x * PIECE, base + (rel_x + 1) * PIECE)
+            place = (x ^ rel_x) * NY + (y ^ rel_y)
+            for head in range(4):
+                q_s[head // 2, place, head % 2] = ref[rows, head * HD : (head + 1) * HD]
+    places = z_order(core, z)
+    index = 0
+    for piece in pieces:
+        for part in range(piece.shape[0] // PIECE):
+            start = pl.multiple_of(places[index] * PIECE, PIECE)
+            rows = slice(part * PIECE, (part + 1) * PIECE)
+            for half in range(2):
+                k_s[half, pl.ds(start, PIECE), :] = piece[rows, half * HD : (half + 1) * HD]
+                v_s[half, pl.ds(start, PIECE), :] = piece[rows, (2 + half) * HD : (3 + half) * HD]
+            index += 1
     level_s[...] = jnp.full((PIECE, HD), NEGATIVE, jnp.float32)
 
     keys = NZ * PIECE
@@ -229,7 +231,7 @@
     return pl.pallas_call(
         attention_kernel,
         out_shape=jax.ShapeDtypeStruct((GROUP, PIECE + STATS, 4 * HD), jnp.bfloat16),
-        in_specs=[SMEM] + [VMEM] * 15,
+        in_specs=[SMEM] + [VMEM] * 8,
         out_specs=VMEM,
         scratch_shapes=[
             pltpu.VMEM((2, GROUP, 2, PIECE, HD), jnp.bfloat16),
@@ -239,7 +241,7 @@
         ],
         compiler_params=pltpu.CompilerParams(vmem_limit_bytes=VMEM_LIMIT),
         cost_estimate=pl.CostEstimate(flops=flops, bytes_accessed=2**22, transcendentals=2**22),
-    )(ids, *queries, *pieces[0], *pieces[1])
+    )(ids, *queries, *pieces)
 
 
 def combine_kernel(ids_ref, partial, *refs):
@@ -277,40 +279,12 @@
     )(ids, partial, *received)
 
 
-TILE = 768
-
-
-def project_kernel(ids_ref, kept, taken, weight, other_out, mine_out, rows_s):
-    core = ids_ref[2]
-    quarter = PIECE // 4
-    kept_high = ((ids_ref[0] ^ ids_ref[1]) & 1) == 1
-    first, second = kept[...], taken[...]
-    low = jnp.where(kept_high, second, first)
-    high = jnp.where(kept_high, first, second)
-    for k, block in enumerate((low, high)):
-        for part in range(2):
-            own = 1 - (part ^ core)
-            start = pl.multiple_of(own * BLOCK + k * quarter, quarter)
-            rows_s[pl.ds(start, quarter), :] = block[part * quarter : (part + 1) * quarter]
-    rows = rows_s[...]
-    for tile in range(weight.shape[1] // TILE):
-        lanes = slice(tile * TILE, (tile + 1) * TILE)
-        product = jnp.dot(rows, weight[:, lanes], preferred_element_type=jnp.float32).astype(jnp.bfloat16)
-        other_out[:, lanes] = product[:BLOCK]
-        mine_out[:, lanes] = product[BLOCK:]
-
-
-def project(ids, kept, taken, out_weight):
-    half = jax.ShapeDtypeStruct((BLOCK, out_weight.shape[1]), jnp.bfloat16)
-    return pl.pallas_call(
-        project_kernel,
-        out_shape=(half, half),
-        in_specs=[SMEM] + [VMEM] * 3,
-        out_specs=(VMEM, VMEM),
-        scratch_shapes=[pltpu.VMEM((PIECE, 4 * HD), jnp.bfloat16)],
-        compiler_params=pltpu.CompilerParams(vmem_limit_bytes=VMEM_LIMIT),
-        cost_estimate=pl.CostEstimate(flops=2 * PIECE * 512 * 5376, bytes_accessed=2**23, transcendentals=0),
-    )(ids, kept, taken, out_weight)
+def project(block, out_weight, c):
+    product = jnp.dot(block, out_weight, preferred_element_type=jnp.float32).astype(jnp.bfloat16)
+    product = product.reshape(2, PIECE // 4, -1)
+    mine = lax.dynamic_index_in_dim(product, c, 0, keepdims=False)
+    other = lax.dynamic_index_in_dim(product, 1 - c, 0, keepdims=False)
+    return mine.astype(jnp.float32) + lax.ppermute(other, "c", X_PAIRS).astype(jnp.float32)
 
 
 def on_device(queries, keys, values, positions, query_gain, key_gain, out_weight):
@@ -319,19 +293,17 @@
     ids = jnp.stack([x * NY + y, z, c, w]).astype(jnp.int32)
     query_rows, cosines, sines = prepare_queries(queries, positions, query_gain)
     moved = lax.ppermute(query_rows, ("x", "z"), move_pairs())
-    kv0, kv1 = prepare_keys(keys, values, cosines, sines, key_gain)
-    pieces = (gather_z(kv0, 0), gather_z(kv1, 1))
+    pieces = gather_z(prepare_keys(keys, values, cosines, sines, key_gain))
     partial = attention(ids, gather_xy(moved), pieces)
     received = [
         lax.ppermute(partial[step], ("x", "y"), pairs(GROUP, lambda i: i ^ step)) for step in range(1, GROUP)
     ]
     kept, given = combine(ids, partial, received)
-    taken = lax.ppermute(given, "z", Z_PAIRS[0])
-    other, mine = project(ids, kept, taken, out_weight)
-    got = lax.ppermute(other, "c", X_PAIRS)
-    chip = (mine.astype(jnp.float32) + got.astype(jnp.float32)).reshape(2, PIECE // 4, -1)
-    keep = lax.dynamic_index_in_dim(chip, w, 0, keepdims=False)
-    give = lax.dynamic_index_in_dim(chip, 1 - w, 0, keepdims=False).astype(jnp.bfloat16)
+    taken = lax.ppermute(given, "z", pairs(NZ, lambda i: i ^ 1))
+    sums = [project(block, out_weight, c) for block in (kept, taken)]
+    own_kept = ((y ^ z) & 1) == w
+    keep = jnp.where(own_kept, sums[0], sums[1])
+    give = jnp.where(own_kept, sums[1], sums[0]).astype(jnp.bfloat16)
     landed = lax.ppermute(give, ("x", "w"), pairs(4, lambda i: i ^ 3))
     return (keep + landed.astype(jnp.float32)).astype(jnp.bfloat16)
 

time: 98.2 us -> 94.4 us (0.961)
  matrix products: 0 us -> 7.32 us
  starting transfers between devices: 44.7 us -> 38.2 us
  local copies, waits for them, and re-layouts: 4.24 us -> 1.74 us
  Pallas kernels: 18 us -> 16.5 us
    dot_general x0 -> x2, matrix products: none -> 7.32 us  [project(): jnp.dot(block, out_weight, preferred_element_type=jnp.float32)]
    ppermute x14 -> x9, starting transfers between devices: 26.8 us -> 23.8 us  [the longest x1 6.41 us: gather_z(): one = lax.ppermute(own, ('z', 'c'), here)]
    unnamed x29 -> x21, local copies, waits for them, and re-layouts: 4.09 us -> 1.6 us
    ppermute x1, starting transfers between devices: 5.06 us -> 2.68 us  [gather_xy(): both = jnp.concatenate([own, lax.ppermute(own, 'x', X_PAIRS)], axis=0)]
    ppermute x7, waiting for transfers between devices: 6.43 us -> 8.11 us  [on_device(): lax.ppermute(partial[step], ('x', 'y'), pairs(GROUP, lambda i: i ^ step))]
    pallas_call x2 -> x1, Pallas kernels: 3.18 us -> 1.78 us  [prepare_keys(): pl.pallas_call(prepare_keys_kernel, out_shape=jax.ShapeDtypeStruct((PIECE...]
    ppermute x14 -> x9, waiting for transfers between devices: 11.7 us -> 10.6 us  [the longest x1 5.44 us: gather_z(): four = lax.ppermute(three, ('z', 'c'), there)]
    ppermute x7, starting transfers between devices: 9.69 us -> 8.67 us  [on_device(): lax.ppermute(partial[step], ('x', 'y'), pairs(GROUP, lambda i: i ^ step))]
  transfers between devices with their start and end apart: 24 -> 19, of which waited for: 12 -> 9; matrix products, arithmetic and copies ran while one was open for 2% -> 9% of each run, Pallas kernels for 0% -> 2%
where the time goes in v4:
time: 94.4 us; the launch traced here: 94.1 us
  starting transfers between devices  38.2 us (40%)
  waiting for transfers between devices  28 us (30%)
  Pallas kernels  16.5 us (17%)
  matrix products  7.32 us (8%)
  other arithmetic  2.15 us (2%)
  local copies, waits for them, and re-layouts  1.74 us (2%)
    pallas_call x1, Pallas kernels, attention(): pl.pallas_call(attention_kernel, out_shape=jax.ShapeDtypeStruct((GROUP, P...  9.45 us
    ppermute x1, waiting for transfers between devices, on_device(): landed = lax.ppermute(give, ('x', 'w'), pairs(4, lambda i: i ^ 3))  9.28 us
    ppermute x7, starting transfers between devices, on_device(): lax.ppermute(partial[step], ('x', 'y'), pairs(GROUP, lambda i: i ^ step))  8.67 us
    ppermute x7, waiting for transfers between devices, on_device(): lax.ppermute(partial[step], ('x', 'y'), pairs(GROUP, lambda i: i ^ step))  8.11 us
    dot_general x2, matrix products, project(): jnp.dot(block, out_weight, preferred_element_type=jnp.float32)  7.32 us
    ppermute x1, starting transfers between devices, gather_z(): one = lax.ppermute(own, ('z', 'c'), here)  6.41 us
    ppermute x1, waiting for transfers between devices, gather_z(): four = lax.ppermute(three, ('z', 'c'), there)  5.44 us
    ppermute x2, starting transfers between devices, project(): lax.ppermute(other, 'c', X_PAIRS).astype(jnp.float32)  5.07 us
  transfers between devices with their start and end apart: 19, of which 9 were waited for; matrix products, arithmetic and copies ran while one was open for 9% of the time, Pallas kernels for 2%

profile of v4, /device:TPU:1, one launch (start us, length us, event | category | flops | bytes accessed | tf_op | source)
XLA Modules:
  0.0 94.1 jit_solution(9413105005864131051)
XLA Ops:
  0.0 2.2 %shard_map.82 = (bf16[128,512]{1,0:T(8,128)(2,1)}, f32[128,128]{1,0:T(8,128)}, f32[128,128]{1,0:T(8,128)}) custom-call(bf16[128,512]{1,0:T(8,128)(2,1)} %q_ref.1, s32[1,128]{1,0:T(1,128)} %bitcast.45, f32[1,128]{1,0:T(1,128)} %constant.40.clone.freq_ref, f32[1,128]{1,0:T(1,128)} %bitcast.46), custom_call_target="tpu_custom_call" | custom-call | tf_op jit(solution)/shard_map/pallas_call | solution.py:74
  2.2 1.6 %collective-permute-start = (bf16[128,512]{1,0:T(8,128)(2,1)}, bf16[128,512]{1,0:T(8,128)(2,1)S(1)}, u32[]{:S(2)}, u32[]{:S(2)}) collective-permute-start(bf16[128,512]{1,0:T(8,128)(2,1)} %get-tuple-element.10), channel_id=1, source_target_pairs={{0,0},{4,8},{8,16},{12,24},{16,4},{20,12},{24,20},{28,28},{128,152... | collective-permute-start | bytes 393224 | tf_op jit(solution)/shard_map/ppermute | solution.py:295
  3.7 1.8 %shard_map.83.refs_3_ = bf16[128,512]{1,0:T(8,128)(2,1)} custom-call(bf16[128,256]{1,0:T(8,128)(2,1)} %k_ref.1, bf16[128,256]{1,0:T(8,128)(2,1)} %v_ref.1, f32[128,128]{1,0:T(8,128)} %get-tuple-element.11.cos_ref, f32[128,128]{1,0:T(8,128)} %get-tuple-element.12.sin_ref, f32[1,128]{1,0:T(1,128)} %bitcast.47), custom_call_target="tpu_custom_call" | custom-call | tf_op jit(solution)/shard_map/pallas_call | solution.py:91
  5.5 6.4 %collective-permute-start.4 = (bf16[128,512]{1,0:T(8,128)(2,1)}, bf16[128,512]{1,0:T(8,128)(2,1)S(1)}, u32[]{:S(2)}, u32[]{:S(2)}) collective-permute-start(bf16[128,512]{1,0:T(8,128)(2,1)} %shard_map.83.refs_3_), channel_id=1, source_target_pairs={{0,4},{1,29},{4,0},{5,9},{8,12},{9,5},{12,8},{13,17},{16,20},{17,1... | collective-permute-start | bytes 393224 | tf_op jit(solution)/shard_map/ppermute | solution.py:101
  11.9 0.0 collective-permute-done
  11.9 2.7 %collective-permute-start.1 = (bf16[128,512]{1,0:T(8,128)(2,1)S(1)}, bf16[128,512]{1,0:T(8,128)(2,1)S(1)}, u32[]{:S(2)}, u32[]{:S(2)}) collective-permute-start(bf16[128,512]{1,0:T(8,128)(2,1)S(1)} %collective-permute-done), channel_id=1, source_target_pairs={{0,128},{128,0},{1,129},{129,1},{2,130},{130,2},{3,131},{131,3},{4... | collective-permute-start | bytes 393224 | tf_op jit(solution)/shard_map/ppermute | solution.py:130
  14.6 0.0 collective-permute-done.4.refs_4_
  14.6 0.9 pad_maximum_fusion.1
  15.5 3.9 %collective-permute-start.5 = (bf16[256,512]{1,0:T(8,128)(2,1)S(1)}, bf16[256,512]{1,0:T(8,128)(2,1)S(1)}, u32[]{:S(2)}, u32[]{:S(2)}) collective-permute-start(bf16[256,512]{1,0:T(8,128)(2,1)S(1)} %pad_maximum_fusion.1), channel_id=1, source_target_pairs={{0,28},{1,5},{4,8},{5,1},{8,4},{9,13},{12,16},{13,9},{16,12},{17,2... | collective-permute-start | bytes 786440 | tf_op jit(solution)/shard_map/ppermute | solution.py:102
  19.4 0.0 collective-permute-done.1
  19.4 2.8 %collective-permute-start.2 = (bf16[256,512]{1,0:T(8,128)(2,1)S(1)}, bf16[256,512]{1,0:T(8,128)(2,1)S(1)}, u32[]{:S(2)}, u32[]{:S(2)}) collective-permute-start(bf16[256,512]{1,0:T(8,128)(2,1)S(1)} %constant_dynamic-update-slice_fusion.refs_0_), channel_id=1, source_target_pairs={{0,32},{1,97},{32,0},{33,65},{64,96},{65,33},{96,64},{97,1},{2,34}... | collective-permute-start | bytes 786440 | tf_op jit(solution)/shard_map/ppermute | solution.py:131
  22.2 1.2 %collective-permute-done.5.refs_5_ = bf16[256,512]{1,0:T(8,128)(2,1)S(1)} collective-permute-done((bf16[256,512]{1,0:T(8,128)(2,1)S(1)}, bf16[256,512]{1,0:T(8,128)(2,1)S(1)}, u32[]{:S(2)}, u32[]{:S(2)}) %collective-permute-start.5) | collective-permute-done | bytes 262176 | tf_op jit(solution)/shard_map/ppermute | solution.py:102
  23.4 4.3 %collective-permute-start.6 = (bf16[256,512]{1,0:T(8,128)(2,1)S(1)}, bf16[256,512]{1,0:T(8,128)(2,1)S(1)}, u32[]{:S(2)}, u32[]{:S(2)}) collective-permute-start(bf16[256,512]{1,0:T(8,128)(2,1)S(1)} %collective-permute-done.5.refs_5_), channel_id=1, source_target_pairs={{0,4},{1,29},{4,0},{5,9},{8,12},{9,5},{12,8},{13,17},{16,20},{17,1... | collective-permute-start | bytes 786440 | tf_op jit(solution)/shard_map/ppermute | solution.py:103
  27.7 0.0 collective-permute-done.2.refs_1_
  27.7 1.4 %collective-permute-start.3 = (bf16[512,512]{1,0:T(8,128)(2,1)S(1)}, bf16[512,512]{1,0:T(8,128)(2,1)S(1)}, u32[]{:S(2)}, u32[]{:S(2)}) collective-permute-start(bf16[512,512]{1,0:T(8,128)(2,1)S(1)} %pad_maximum_fusion), channel_id=1, source_target_pairs={{0,96},{1,33},{32,64},{33,1},{64,32},{65,97},{96,0},{97,65},{2,98}... | collective-permute-start | bytes 1572872 | tf_op jit(solution)/shard_map/ppermute | solution.py:132
  29.1 2.3 %collective-permute-done.6.refs_6_ = bf16[256,512]{1,0:T(8,128)(2,1)S(1)} collective-permute-done((bf16[256,512]{1,0:T(8,128)(2,1)S(1)}, bf16[256,512]{1,0:T(8,128)(2,1)S(1)}, u32[]{:S(2)}, u32[]{:S(2)}) %collective-permute-start.6) | collective-permute-done | bytes 262176 | tf_op jit(solution)/shard_map/ppermute | solution.py:103
  31.5 0.0 collective-permute-start.7
  31.5 0.1 pad_add_fusion.ids_ref
  31.5 5.4 %collective-permute-done.7.refs_7_ = bf16[256,512]{1,0:T(8,128)(2,1)S(1)} collective-permute-done((bf16[256,512]{1,0:T(8,128)(2,1)S(1)}, bf16[256,512]{1,0:T(8,128)(2,1)S(1)}, u32[]{:S(2)}, u32[]{:S(2)}) %collective-permute-start.7) | collective-permute-done | bytes 262176 | tf_op jit(solution)/shard_map/ppermute | solution.py:104
  37.0 0.0 collective-permute-done.3.refs_2_
  37.0 0.9 copy-done.1
  37.9 9.4 %shard_map.84.partial = bf16[8,144,512]{2,1,0:T(8,128)(2,1)S(1)} custom-call(s32[4]{0:T(128)S(1)} %pad_add_fusion.ids_ref, bf16[256,512]{1,0:T(8,128)(2,1)S(1)} %constant_dynamic-update-slice_fusion.refs_0_, bf16[256,512]{1,0:T(8,128)(2,1)S(1)} %collective-permute-done.2.refs_1_, bf16[512,512]{1,0:T(8,128)(2,1)S(1)} %collective-permute-done.3.refs_2_, ...), custom_call_target="tpu_custom_call" | custom-call | flops 2147483648 | bytes 4194304 | tf_op jit(solution)/shard_map/pallas_call | solution.py:231
  47.4 0.1 slice_bitcast_fusion
  47.4 0.1 collective-permute-start.14
  47.5 4.0 %collective-permute-start.13 = (bf16[144,512]{1,0:T(8,128)(2,1)S(1)}, bf16[144,512]{1,0:T(8,128)(2,1)S(1)}, u32[]{:S(2)}, u32[]{:S(2)}) collective-permute-start(bf16[144,512]{1,0:T(8,128)(2,1)S(1)} %get-tuple-element.16), channel_id=1, source_target_pairs={{0,192},{32,224},{64,128},{96,160},{128,64},{160,96},{192,0},{224,... | collective-permute-start | bytes 442376 | tf_op jit(solution)/shard_map/ppermute | solution.py:299
  51.5 1.3 %collective-permute-start.11 = (bf16[144,512]{1,0:T(8,128)(2,1)S(1)}, bf16[144,512]{1,0:T(8,128)(2,1)S(1)}, u32[]{:S(2)}, u32[]{:S(2)}) collective-permute-start(bf16[144,512]{1,0:T(8,128)(2,1)S(1)} %get-tuple-element.18), channel_id=1, source_target_pairs={{0,128},{32,160},{64,192},{96,224},{128,0},{160,32},{192,64},{224,... | collective-permute-start | bytes 442376 | tf_op jit(solution)/shard_map/ppermute | solution.py:299
  52.9 0.8 collective-permute-start.10
  53.6 2.3 %collective-permute-start.9 = (bf16[144,512]{1,0:T(8,128)(2,1)S(1)}, bf16[144,512]{1,0:T(8,128)(2,1)S(1)}, u32[]{:S(2)}, u32[]{:S(2)}) collective-permute-start(bf16[144,512]{1,0:T(8,128)(2,1)S(1)} %get-tuple-element.20), channel_id=1, source_target_pairs={{0,64},{32,96},{64,0},{96,32},{128,192},{160,224},{192,128},{224,1... | collective-permute-start | bytes 442376 | tf_op jit(solution)/shard_map/ppermute | solution.py:299
  55.9 0.0 collective-permute-done.13.refs_5_
  56.0 0.2 collective-permute-start.8
  56.1 2.2 %collective-permute-done.12.refs_4_ = bf16[144,512]{1,0:T(8,128)(2,1)S(1)} collective-permute-done((bf16[144,512]{1,0:T(8,128)(2,1)S(1)}, bf16[144,512]{1,0:T(8,128)(2,1)S(1)}, u32[]{:S(2)}, u32[]{:S(2)}) %collective-permute-start.12) | collective-permute-done | bytes 147488 | tf_op jit(solution)/shard_map/ppermute | solution.py:299
  58.4 1.9 %collective-permute-done.11.refs_3_ = bf16[144,512]{1,0:T(8,128)(2,1)S(1)} collective-permute-done((bf16[144,512]{1,0:T(8,128)(2,1)S(1)}, bf16[144,512]{1,0:T(8,128)(2,1)S(1)}, u32[]{:S(2)}, u32[]{:S(2)}) %collective-permute-start.11) | collective-permute-done | bytes 147488 | tf_op jit(solution)/shard_map/ppermute | solution.py:299
  60.3 2.9 %collective-permute-done.10.refs_2_ = bf16[144,512]{1,0:T(8,128)(2,1)S(1)} collective-permute-done((bf16[144,512]{1,0:T(8,128)(2,1)S(1)}, bf16[144,512]{1,0:T(8,128)(2,1)S(1)}, u32[]{:S(2)}, u32[]{:S(2)}) %collective-permute-start.10) | collective-permute-done | bytes 147488 | tf_op jit(solution)/shard_map/ppermute | solution.py:299
  63.3 1.0 %collective-permute-done.8.refs_0_ = bf16[144,512]{1,0:T(8,128)(2,1)S(1)} collective-permute-done((bf16[144,512]{1,0:T(8,128)(2,1)S(1)}, bf16[144,512]{1,0:T(8,128)(2,1)S(1)}, u32[]{:S(2)}, u32[]{:S(2)}) %collective-permute-start.8) | collective-permute-done | bytes 147488 | tf_op jit(solution)/shard_map/ppermute | solution.py:299
  64.3 0.0 copy-start.9
  64.3 0.7 copy-done.9
  65.0 3.1 %shard_map.85 = (bf16[64,512]{1,0:T(8,128)(2,1)}, bf16[64,512]{1,0:T(8,128)(2,1)}) custom-call(s32[4]{0:T(128)} %copy-done.2, bf16[8,144,512]{2,1,0:T(8,128)(2,1)} %copy-done, bf16[144,512]{1,0:T(8,128)(2,1)} %copy-done.9, bf16[144,512]{1,0:T(8,128)(2,1)} %copy-done.8, bf16[144,512]{1,0:T(8,128)(2,1)} %copy-done.7, bf16[144,512]{1,0:T(8,128)(2,1)} %copy-done.6, ...), custom_call_target="tpu_custom_call" | custom-call | tf_op jit(solution)/shard_map/pallas_call | solution.py:274
  68.1 0.0 collective-permute-start.16
  68.1 3.7 %convolution_convert_fusion.1 = bf16[64,5376]{1,0:T(8,128)(2,1)S(1)} fusion(bf16[64,512]{1,0:T(8,128)(2,1)} %get-tuple-element.13, bf16[512,5376]{1,0:T(8,128)(2,1)} %param.14), kind=kOutput, calls=%fused_computation.1 | convolution fusion | flops 352665600 | bytes 6258688 | tf_op jit(solution)/shard_map/dot_general | solution.py:283
  71.8 5.0 %collective-permute-start.15 = (bf16[32,5376]{1,0:T(8,128)(2,1)S(1)}, bf16[32,5376]{1,0:T(8,128)(2,1)S(1)}, u32[]{:S(2)}, u32[]{:S(2)}) collective-permute-start(bf16[32,5376]{1,0:T(8,128)(2,1)S(1)} %dynamic-slice_bitcast_fusion.1), channel_id=1, source_target_pairs={{0,1},{1,0},{2,3},{3,2},{4,5},{5,4},{6,7},{7,6},{8,9},{9,8},{10,11... | collective-permute-start | bytes 1032200 | tf_op jit(solution)/shard_map/ppermute | solution.py:287
  76.8 3.6 %convolution_convert_fusion = bf16[64,5376]{1,0:T(8,128)(2,1)S(1)} fusion(bf16[64,512]{1,0:T(8,128)(2,1)S(1)} %collective-permute-done.16, bf16[512,5376]{1,0:T(8,128)(2,1)} %param.14), kind=kOutput, calls=%fused_computation | convolution fusion | flops 352665600 | bytes 6258688 | tf_op jit(solution)/shard_map/dot_general | solution.py:283
  80.5 0.1 collective-permute-start.17
  80.6 0.0 collective-permute-done.15
  80.6 1.6 %collective-permute-done.17 = bf16[32,5376]{1,0:T(8,128)(2,1)S(1)} collective-permute-done((bf16[32,5376]{1,0:T(8,128)(2,1)S(1)}, bf16[32,5376]{1,0:T(8,128)(2,1)S(1)}, u32[]{:S(2)}, u32[]{:S(2)}) %collective-permute-start.17) | collective-permute-done | bytes 344096 | tf_op jit(solution)/shard_map/ppermute | solution.py:287
  82.2 0.2 select_convert_fusion
  82.4 1.5 %collective-permute-start.18 = (bf16[32,5376]{1,0:T(8,128)(2,1)S(1)}, bf16[32,5376]{1,0:T(8,128)(2,1)S(1)}, u32[]{:S(2)}, u32[]{:S(2)}) collective-permute-start(bf16[32,5376]{1,0:T(8,128)(2,1)S(1)} %select_convert_fusion), channel_id=1, source_target_pairs={{0,130},{2,128},{128,2},{130,0},{1,131},{3,129},{129,3},{131,1},{4... | collective-permute-start | bytes 1032200 | tf_op jit(solution)/shard_map/ppermute | solution.py:307
  83.9 9.3 %collective-permute-done.18 = bf16[32,5376]{1,0:T(8,128)(2,1)S(1)} collective-permute-done((bf16[32,5376]{1,0:T(8,128)(2,1)S(1)}, bf16[32,5376]{1,0:T(8,128)(2,1)S(1)}, u32[]{:S(2)}, u32[]{:S(2)}) %collective-permute-start.18) | collective-permute-done | bytes 344096 | tf_op jit(solution)/shard_map/ppermute | solution.py:307
  93.2 0.9 %add_convert_fusion = bf16[32,5376]{1,0:T(8,128)(2,1)} fusion(bf16[32,5376]{1,0:T(8,128)(2,1)S(1)} %collective-permute-done.18, bf16[32,5376]{1,0:T(8,128)(2,1)S(1)} %collective-permute-done.15, bf16[32,5376]{1,0:T(8,128)(2,1)S(1)} %collective-permute-done.17, pred[]{:T(512)S(6)} %eq.3, bf16[2,32,5376]{2,1,0:T(8,128)(2,1)S(1)} %bitcast.44, s32[]{:T(128)S(6)} %select_n.22, ...), kind=kLoop, calls=%fused_computation.4 | loop fusion | flops 1720320 | bytes 2064389 | tf_op jit(solution)/shard_map/convert_element_type | solution.py:308
  (26 shorter events, 0.2 us)
Async XLA Ops:
  2.2 9.7 %collective-permute-start = (bf16[128,512]{1,0:T(8,128)(2,1)}, bf16[128,512]{1,0:T(8,128)(2,1)S(1)}, u32[]{:S(2)}, u32[]{:S(2)}) collective-permute-start(bf16[128,512]{1,0:T(8,128)(2,1)} %get-tuple-element.10), channel_id=1, source_target_pairs={{0,0},{4,8},{8,16},{12,24},{16,4},{20,12},{24,20},{28,28},{128,152... | collective-permute-start | bytes 393224 | tf_op jit(solution)/shard_map/ppermute | solution.py:295
  5.5 9.1 %collective-permute-start.4 = (bf16[128,512]{1,0:T(8,128)(2,1)}, bf16[128,512]{1,0:T(8,128)(2,1)S(1)}, u32[]{:S(2)}, u32[]{:S(2)}) collective-permute-start(bf16[128,512]{1,0:T(8,128)(2,1)} %shard_map.83.refs_3_), channel_id=1, source_target_pairs={{0,4},{1,29},{4,0},{5,9},{8,12},{9,5},{12,8},{13,17},{16,20},{17,1... | collective-permute-start | bytes 393224 | tf_op jit(solution)/shard_map/ppermute | solution.py:101
  11.9 7.5 %collective-permute-start.1 = (bf16[128,512]{1,0:T(8,128)(2,1)S(1)}, bf16[128,512]{1,0:T(8,128)(2,1)S(1)}, u32[]{:S(2)}, u32[]{:S(2)}) collective-permute-start(bf16[128,512]{1,0:T(8,128)(2,1)S(1)} %collective-permute-done), channel_id=1, source_target_pairs={{0,128},{128,0},{1,129},{129,1},{2,130},{130,2},{3,131},{131,3},{4... | collective-permute-start | bytes 393224 | tf_op jit(solution)/shard_map/ppermute | solution.py:130
  15.5 7.9 %collective-permute-start.5 = (bf16[256,512]{1,0:T(8,128)(2,1)S(1)}, bf16[256,512]{1,0:T(8,128)(2,1)S(1)}, u32[]{:S(2)}, u32[]{:S(2)}) collective-permute-start(bf16[256,512]{1,0:T(8,128)(2,1)S(1)} %pad_maximum_fusion.1), channel_id=1, source_target_pairs={{0,28},{1,5},{4,8},{5,1},{8,4},{9,13},{12,16},{13,9},{16,12},{17,2... | collective-permute-start | bytes 786440 | tf_op jit(solution)/shard_map/ppermute | solution.py:102
  19.4 8.3 %collective-permute-start.2 = (bf16[256,512]{1,0:T(8,128)(2,1)S(1)}, bf16[256,512]{1,0:T(8,128)(2,1)S(1)}, u32[]{:S(2)}, u32[]{:S(2)}) collective-permute-start(bf16[256,512]{1,0:T(8,128)(2,1)S(1)} %constant_dynamic-update-slice_fusion.refs_0_), channel_id=1, source_target_pairs={{0,32},{1,97},{32,0},{33,65},{64,96},{65,33},{96,64},{97,1},{2,34}... | collective-permute-start | bytes 786440 | tf_op jit(solution)/shard_map/ppermute | solution.py:131
  23.4 8.0 %collective-permute-start.6 = (bf16[256,512]{1,0:T(8,128)(2,1)S(1)}, bf16[256,512]{1,0:T(8,128)(2,1)S(1)}, u32[]{:S(2)}, u32[]{:S(2)}) collective-permute-start(bf16[256,512]{1,0:T(8,128)(2,1)S(1)} %collective-permute-done.5.refs_5_), channel_id=1, source_target_pairs={{0,4},{1,29},{4,0},{5,9},{8,12},{9,5},{12,8},{13,17},{16,20},{17,1... | collective-permute-start | bytes 786440 | tf_op jit(solution)/shard_map/ppermute | solution.py:103
  27.7 9.2 %collective-permute-start.3 = (bf16[512,512]{1,0:T(8,128)(2,1)S(1)}, bf16[512,512]{1,0:T(8,128)(2,1)S(1)}, u32[]{:S(2)}, u32[]{:S(2)}) collective-permute-start(bf16[512,512]{1,0:T(8,128)(2,1)S(1)} %pad_maximum_fusion), channel_id=1, source_target_pairs={{0,96},{1,33},{32,64},{33,1},{64,32},{65,97},{96,0},{97,65},{2,98}... | collective-permute-start | bytes 1572872 | tf_op jit(solution)/shard_map/ppermute | solution.py:132
  31.5 5.5 %collective-permute-start.7 = (bf16[256,512]{1,0:T(8,128)(2,1)S(1)}, bf16[256,512]{1,0:T(8,128)(2,1)S(1)}, u32[]{:S(2)}, u32[]{:S(2)}) collective-permute-start(bf16[256,512]{1,0:T(8,128)(2,1)S(1)} %collective-permute-done.6.refs_6_), channel_id=1, source_target_pairs={{0,28},{1,5},{4,8},{5,1},{8,4},{9,13},{12,16},{13,9},{16,12},{17,2... | collective-permute-start | bytes 786440 | tf_op jit(solution)/shard_map/ppermute | solution.py:104
  31.5 32.7 %copy-start.2 = (s32[4]{0:T(128)}, s32[4]{0:T(128)S(1)}, u32[]{:S(2)}) copy-start(s32[4]{0:T(128)S(1)} %pad_add_fusion.ids_ref) | copy-start | bytes 52
  37.0 0.9 copy-start.1
  47.3 16.9 %copy-start = (bf16[8,144,512]{2,1,0:T(8,128)(2,1)}, bf16[8,144,512]{2,1,0:T(8,128)(2,1)S(1)}, u32[]{:S(2)}) copy-start(bf16[8,144,512]{2,1,0:T(8,128)(2,1)S(1)} %shard_map.84.partial) | copy-start | bytes 3538948
  47.4 6.2 %collective-permute-start.14 = (bf16[144,512]{1,0:T(8,128)(2,1)S(1)}, bf16[144,512]{1,0:T(8,128)(2,1)S(1)}, u32[]{:S(2)}, u32[]{:S(2)}) collective-permute-start(bf16[144,512]{1,0:T(8,128)(2,1)S(1)} %get-tuple-element.15), channel_id=1, source_target_pairs={{0,224},{32,192},{64,160},{96,128},{128,96},{160,64},{192,32},{224... | collective-permute-start | bytes 442376 | tf_op jit(solution)/shard_map/ppermute | solution.py:299
  47.5 8.4 %collective-permute-start.13 = (bf16[144,512]{1,0:T(8,128)(2,1)S(1)}, bf16[144,512]{1,0:T(8,128)(2,1)S(1)}, u32[]{:S(2)}, u32[]{:S(2)}) collective-permute-start(bf16[144,512]{1,0:T(8,128)(2,1)S(1)} %get-tuple-element.16), channel_id=1, source_target_pairs={{0,192},{32,224},{64,128},{96,160},{128,64},{160,96},{192,0},{224,... | collective-permute-start | bytes 442376 | tf_op jit(solution)/shard_map/ppermute | solution.py:299
  51.5 6.9 %collective-permute-start.12 = (bf16[144,512]{1,0:T(8,128)(2,1)S(1)}, bf16[144,512]{1,0:T(8,128)(2,1)S(1)}, u32[]{:S(2)}, u32[]{:S(2)}) collective-permute-start(bf16[144,512]{1,0:T(8,128)(2,1)S(1)} %get-tuple-element.17), channel_id=1, source_target_pairs={{0,160},{32,128},{64,224},{96,192},{128,32},{160,0},{192,96},{224,... | collective-permute-start | bytes 442376 | tf_op jit(solution)/shard_map/ppermute | solution.py:299
  51.5 8.8 %collective-permute-start.11 = (bf16[144,512]{1,0:T(8,128)(2,1)S(1)}, bf16[144,512]{1,0:T(8,128)(2,1)S(1)}, u32[]{:S(2)}, u32[]{:S(2)}) collective-permute-start(bf16[144,512]{1,0:T(8,128)(2,1)S(1)} %get-tuple-element.18), channel_id=1, source_target_pairs={{0,128},{32,160},{64,192},{96,224},{128,0},{160,32},{192,64},{224,... | collective-permute-start | bytes 442376 | tf_op jit(solution)/shard_map/ppermute | solution.py:299
  52.9 10.4 %collective-permute-start.10 = (bf16[144,512]{1,0:T(8,128)(2,1)S(1)}, bf16[144,512]{1,0:T(8,128)(2,1)S(1)}, u32[]{:S(2)}, u32[]{:S(2)}) collective-permute-start(bf16[144,512]{1,0:T(8,128)(2,1)S(1)} %get-tuple-element.19), channel_id=1, source_target_pairs={{0,96},{32,64},{64,32},{96,0},{128,224},{160,192},{192,160},{224,1... | collective-permute-start | bytes 442376 | tf_op jit(solution)/shard_map/ppermute | solution.py:299
  53.6 10.6 %copy-start.3 = (bf16[144,512]{1,0:T(8,128)(2,1)}, bf16[144,512]{1,0:T(8,128)(2,1)S(1)}, u32[]{:S(2)}) copy-start(bf16[144,512]{1,0:T(8,128)(2,1)S(1)} %collective-permute-done.14.refs_6_) | copy-start | bytes 442372
  53.6 9.6 %collective-permute-start.9 = (bf16[144,512]{1,0:T(8,128)(2,1)S(1)}, bf16[144,512]{1,0:T(8,128)(2,1)S(1)}, u32[]{:S(2)}, u32[]{:S(2)}) collective-permute-start(bf16[144,512]{1,0:T(8,128)(2,1)S(1)} %get-tuple-element.20), channel_id=1, source_target_pairs={{0,64},{32,96},{64,0},{96,32},{128,192},{160,224},{192,128},{224,1... | collective-permute-start | bytes 442376 | tf_op jit(solution)/shard_map/ppermute | solution.py:299
  56.0 8.3 %copy-start.4 = (bf16[144,512]{1,0:T(8,128)(2,1)}, bf16[144,512]{1,0:T(8,128)(2,1)S(1)}, u32[]{:S(2)}) copy-start(bf16[144,512]{1,0:T(8,128)(2,1)S(1)} %collective-permute-done.13.refs_5_) | copy-start | bytes 442372
  56.0 8.3 %collective-permute-start.8 = (bf16[144,512]{1,0:T(8,128)(2,1)S(1)}, bf16[144,512]{1,0:T(8,128)(2,1)S(1)}, u32[]{:S(2)}, u32[]{:S(2)}) collective-permute-start(bf16[144,512]{1,0:T(8,128)(2,1)S(1)} %get-tuple-element.21), channel_id=1, source_target_pairs={{0,32},{32,0},{64,96},{96,64},{128,160},{160,128},{192,224},{224,1... | collective-permute-start | bytes 442376 | tf_op jit(solution)/shard_map/ppermute | solution.py:299
  58.4 5.9 %copy-start.5 = (bf16[144,512]{1,0:T(8,128)(2,1)}, bf16[144,512]{1,0:T(8,128)(2,1)S(1)}, u32[]{:S(2)}) copy-start(bf16[144,512]{1,0:T(8,128)(2,1)S(1)} %collective-permute-done.12.refs_4_) | copy-start | bytes 442372
  60.3 4.0 %copy-start.6 = (bf16[144,512]{1,0:T(8,128)(2,1)}, bf16[144,512]{1,0:T(8,128)(2,1)S(1)}, u32[]{:S(2)}) copy-start(bf16[144,512]{1,0:T(8,128)(2,1)S(1)} %collective-permute-done.11.refs_3_) | copy-start | bytes 442372
  63.2 1.0 %copy-start.7 = (bf16[144,512]{1,0:T(8,128)(2,1)}, bf16[144,512]{1,0:T(8,128)(2,1)S(1)}, u32[]{:S(2)}) copy-start(bf16[144,512]{1,0:T(8,128)(2,1)S(1)} %collective-permute-done.10.refs_2_) | copy-start | bytes 442372
  63.2 1.0 %copy-start.8 = (bf16[144,512]{1,0:T(8,128)(2,1)}, bf16[144,512]{1,0:T(8,128)(2,1)S(1)}, u32[]{:S(2)}) copy-start(bf16[144,512]{1,0:T(8,128)(2,1)S(1)} %collective-permute-done.9.refs_1_) | copy-start | bytes 442372
  64.3 0.7 copy-start.9
  68.1 8.7 %collective-permute-start.16 = (bf16[64,512]{1,0:T(8,128)(2,1)}, bf16[64,512]{1,0:T(8,128)(2,1)S(1)}, u32[]{:S(2)}, u32[]{:S(2)}) collective-permute-start(bf16[64,512]{1,0:T(8,128)(2,1)} %get-tuple-element.14), channel_id=1, source_target_pairs={{0,4},{4,0},{8,12},{12,8},{16,20},{20,16},{24,28},{28,24},{1,5},{5... | collective-permute-start | bytes 196616 | tf_op jit(solution)/shard_map/ppermute | solution.py:302
  71.8 8.8 %collective-permute-start.15 = (bf16[32,5376]{1,0:T(8,128)(2,1)S(1)}, bf16[32,5376]{1,0:T(8,128)(2,1)S(1)}, u32[]{:S(2)}, u32[]{:S(2)}) collective-permute-start(bf16[32,5376]{1,0:T(8,128)(2,1)S(1)} %dynamic-slice_bitcast_fusion.1), channel_id=1, source_target_pairs={{0,1},{1,0},{2,3},{3,2},{4,5},{5,4},{6,7},{7,6},{8,9},{9,8},{10,11... | collective-permute-start | bytes 1032200 | tf_op jit(solution)/shard_map/ppermute | solution.py:287
  80.5 1.7 %collective-permute-start.17 = (bf16[32,5376]{1,0:T(8,128)(2,1)S(1)}, bf16[32,5376]{1,0:T(8,128)(2,1)S(1)}, u32[]{:S(2)}, u32[]{:S(2)}) collective-permute-start(bf16[32,5376]{1,0:T(8,128)(2,1)S(1)} %dynamic-slice_bitcast_fusion), channel_id=1, source_target_pairs={{0,1},{1,0},{2,3},{3,2},{4,5},{5,4},{6,7},{7,6},{8,9},{9,8},{10,11... | collective-permute-start | bytes 1032200 | tf_op jit(solution)/shard_map/ppermute | solution.py:287
  82.4 10.8 %collective-permute-start.18 = (bf16[32,5376]{1,0:T(8,128)(2,1)S(1)}, bf16[32,5376]{1,0:T(8,128)(2,1)S(1)}, u32[]{:S(2)}, u32[]{:S(2)}) collective-permute-start(bf16[32,5376]{1,0:T(8,128)(2,1)S(1)} %select_convert_fusion), channel_id=1, source_target_pairs={{0,130},{2,128},{128,2},{130,0},{1,131},{3,129},{129,3},{131,1},{4... | collective-permute-start | bytes 1032200 | tf_op jit(solution)/shard_map/ppermute | solution.py:307

commit v5 on v4

--- a/solution.py
+++ b/solution.py
@@ -17,7 +17,8 @@
 QUERY_FACTOR = float(168.0**-0.5 / np.log(2.0))
 NEGATIVE = -1e30
 FREQUENCY = (1000000.0 ** (-2.0 * np.arange(64, dtype=np.float64) / 128)).astype(np.float32)
-VMEM_LIMIT = 24 * 1024 * 1024
+VMEM_LIMIT = 16 * 1024 * 1024
+SMALL = pltpu.CompilerParams(vmem_limit_bytes=8 * 1024 * 1024)
 NT = (((1,), (1,)), ((), ()))
 
 
@@ -54,7 +55,7 @@
     return normed * cosines + pltpu.roll(normed, HD // 2, 1) * sines
 
 
-def prepare_queries_kernel(q_ref, pos_ref, freq_ref, gain_ref, q_out, cos_out, sin_out):
+def prepare_keys_kernel(k_ref, v_ref, pos_ref, freq_ref, gain_ref, out, cos_out, sin_out):
     lane = lax.broadcasted_iota(jnp.int32, (PIECE, HD), 1)
     spread = jnp.broadcast_to(pos_ref[...].astype(jnp.float32), (PIECE, HD))
     angles = jnp.transpose(spread) * freq_ref[...]
@@ -62,38 +63,38 @@
     sines = jnp.where(lane < HD // 2, -1.0, 1.0) * jnp.sin(angles)
     cos_out[...] = cosines
     sin_out[...] = sines
+    for head in range(2):
+        cols = slice(head * HD, (head + 1) * HD)
+        rows = rotate(k_ref[:, cols], gain_ref[...], cosines, sines)
+        out[:, cols] = rows.astype(jnp.bfloat16)
+    out[:, 2 * HD :] = v_ref[...]
+
+
+def prepare_keys(keys, values, positions, gain):
+    freq = jnp.asarray(np.concatenate([FREQUENCY, FREQUENCY])[None, :])
+    table = jax.ShapeDtypeStruct((PIECE, HD), jnp.float32)
+    return pl.pallas_call(
+        prepare_keys_kernel,
+        out_shape=(jax.ShapeDtypeStruct((PIECE, 4 * HD), jnp.bfloat16), table, table),
+        in_specs=[VMEM] * 5,
+        out_specs=(VMEM,) * 3,
+    )(keys, values, positions[None, :], freq, gain[None, :])
+
+
+def prepare_queries_kernel(q_ref, cos_ref, sin_ref, gain_ref, out):
     for head in range(4):
         cols = slice(head * HD, (head + 1) * HD)
-        rows = rotate(q_ref[:, cols], gain_ref[...], cosines, sines)
-        q_out[:, cols] = (rows * QUERY_FACTOR).astype(jnp.bfloat16)
-
-
-def prepare_queries(queries, positions, gain):
-    freq = jnp.asarray(np.concatenate([FREQUENCY, FREQUENCY])[None, :])
-    table = jax.ShapeDtypeStruct((PIECE, HD), jnp.float32)
+        rows = rotate(q_ref[:, cols], gain_ref[...], cos_ref[...], sin_ref[...])
+        out[:, cols] = (rows * QUERY_FACTOR).astype(jnp.bfloat16)
+
+
+def prepare_queries(queries, cosines, sines, gain):
     return pl.pallas_call(
         prepare_queries_kernel,
-        out_shape=(jax.ShapeDtypeStruct((PIECE, 4 * HD), jnp.bfloat16), table, table),
+        out_shape=jax.ShapeDtypeStruct((PIECE, 4 * HD), jnp.bfloat16),
         in_specs=[VMEM] * 4,
-        out_specs=(VMEM,) * 3,
-    )(queries, positions[None, :], freq, gain[None, :])
-
-
-def prepare_keys_kernel(k_ref, v_ref, cos_ref, sin_ref, gain_ref, out):
-    for head in range(2):
-        cols = slice(head * HD, (head + 1) * HD)
-        rows = rotate(k_ref[:, cols], gain_ref[...], cos_ref[...], sin_ref[...])
-        out[:, cols] = rows.astype(jnp.bfloat16)
-    out[:, 2 * HD :] = v_ref[...]
-
-
-def prepare_keys(keys, values, cosines, sines, gain):
-    return pl.pallas_call(
-        prepare_keys_kernel,
-        out_shape=jax.ShapeDtypeStruct((PIECE, 4 * HD), jnp.bfloat16),
-        in_specs=[VMEM] * 5,
         out_specs=VMEM,
-    )(keys, values, cosines, sines, gain[None, :])
+    )(queries, cosines, sines, gain[None, :])
 
 
 def gather_z(own):
@@ -131,6 +132,23 @@
     near = lax.ppermute(both, ("y", "c"), Y_PAIRS[0])
     far = lax.ppermute(jnp.concatenate([both, near], axis=0), ("y", "c"), Y_PAIRS[1])
     return both, near, far
+
+
+def turned(step):
+    return (4 * (step & 1)) ^ ((step >> 1) & 1) ^ (3 * ((step >> 2) & 1))
+
+
+def position(core, step):
+    back = (2 * (step & 1)) ^ (6 * ((step >> 1) & 1)) ^ ((step >> 2) & 1)
+    return jnp.where(core == 0, step, back)
+
+
+def exchange(partial):
+    received = []
+    for k in range(1, GROUP):
+        moves = [(g * 2 + c, (g ^ (turned(k) if c else k)) * 2 + c) for g in range(GROUP) for c in range(2)]
+        received.append(lax.ppermute(partial[k], ("x", "y", "c"), moves))
+    return received
 
 
 def attention_kernel(ids_ref, *refs):
@@ -165,7 +183,7 @@
         upper = source >> 2
         end_x = ((source >> 1) & 1) ^ w
         end_y = (((source & 1) ^ upper) << 1) | ((z & 1) ^ upper)
-        return group ^ ((end_x << 2) | end_y)
+        return position(core, group ^ ((end_x << 2) | end_y))
 
     def one(half, pair, masked):
         query = q_s[half, pl.ds(pair * 2, 2)].reshape(width, HD)
@@ -276,34 +294,61 @@
         out_shape=(block, block),
         in_specs=[SMEM] + [VMEM] * GROUP,
         out_specs=(VMEM, VMEM),
+        compiler_params=SMALL,
     )(ids, partial, *received)
 
 
-def project(block, out_weight, c):
-    product = jnp.dot(block, out_weight, preferred_element_type=jnp.float32).astype(jnp.bfloat16)
-    product = product.reshape(2, PIECE // 4, -1)
-    mine = lax.dynamic_index_in_dim(product, c, 0, keepdims=False)
-    other = lax.dynamic_index_in_dim(product, 1 - c, 0, keepdims=False)
-    return mine.astype(jnp.float32) + lax.ppermute(other, "c", X_PAIRS).astype(jnp.float32)
+TILE = 768
+
+
+def project_kernel(ids_ref, kept, taken, weight, other_out, mine_out, rows_s):
+    core = ids_ref[2]
+    quarter = PIECE // 4
+    kept_high = ((ids_ref[0] ^ ids_ref[1]) & 1) == 1
+    first, second = kept[...], taken[...]
+    low = jnp.where(kept_high, second, first)
+    high = jnp.where(kept_high, first, second)
+    for k, block in enumerate((low, high)):
+        for part in range(2):
+            own = 1 - (part ^ core)
+            start = pl.multiple_of(own * BLOCK + k * quarter, quarter)
+            rows_s[pl.ds(start, quarter), :] = block[part * quarter : (part + 1) * quarter]
+    rows = rows_s[...]
+    for tile in range(weight.shape[1] // TILE):
+        lanes = slice(tile * TILE, (tile + 1) * TILE)
+        product = jnp.dot(rows, weight[:, lanes], preferred_element_type=jnp.float32).astype(jnp.bfloat16)
+        other_out[:, lanes] = product[:BLOCK]
+        mine_out[:, lanes] = product[BLOCK:]
+
+
+def project(ids, kept, taken, out_weight):
+    half = jax.ShapeDtypeStruct((BLOCK, out_weight.shape[1]), jnp.bfloat16)
+    return pl.pallas_call(
+        project_kernel,
+        out_shape=(half, half),
+        in_specs=[SMEM] + [VMEM] * 3,
+        out_specs=(VMEM, VMEM),
+        scratch_shapes=[pltpu.VMEM((PIECE, 4 * HD), jnp.bfloat16)],
+        compiler_params=pltpu.CompilerParams(vmem_limit_bytes=VMEM_LIMIT),
+        cost_estimate=pl.CostEstimate(flops=2 * PIECE * 512 * 5376, bytes_accessed=2**23, transcendentals=0),
+    )(ids, kept, taken, out_weight)
 
 
 def on_device(queries, keys, values, positions, query_gain, key_gain, out_weight):
     x, y, z = lax.axis_index("x"), lax.axis_index("y"), lax.axis_index("z")
     w, c = lax.axis_index("w"), lax.axis_index("c")
     ids = jnp.stack([x * NY + y, z, c, w]).astype(jnp.int32)
-    query_rows, cosines, sines = prepare_queries(queries, positions, query_gain)
-    moved = lax.ppermute(query_rows, ("x", "z"), move_pairs())
-    pieces = gather_z(prepare_keys(keys, values, cosines, sines, key_gain))
+    key_rows, cosines, sines = prepare_keys(keys, values, positions, key_gain)
+    moved = lax.ppermute(prepare_queries(queries, cosines, sines, query_gain), ("x", "z"), move_pairs())
+    pieces = gather_z(key_rows)
     partial = attention(ids, gather_xy(moved), pieces)
-    received = [
-        lax.ppermute(partial[step], ("x", "y"), pairs(GROUP, lambda i: i ^ step)) for step in range(1, GROUP)
-    ]
-    kept, given = combine(ids, partial, received)
+    kept, given = combine(ids, partial, exchange(partial))
     taken = lax.ppermute(given, "z", pairs(NZ, lambda i: i ^ 1))
-    sums = [project(block, out_weight, c) for block in (kept, taken)]
-    own_kept = ((y ^ z) & 1) == w
-    keep = jnp.where(own_kept, sums[0], sums[1])
-    give = jnp.where(own_kept, sums[1], sums[0]).astype(jnp.bfloat16)
+    other, mine = project(ids, kept, taken, out_weight)
+    got = lax.ppermute(other, "c", X_PAIRS)
+    chip = (mine.astype(jnp.float32) + got.astype(jnp.float32)).reshape(2, PIECE // 4, -1)
+    keep = lax.dynamic_index_in_dim(chip, w, 0, keepdims=False)
+    give = lax.dynamic_index_in_dim(chip, 1 - w, 0, keepdims=False).astype(jnp.bfloat16)
     landed = lax.ppermute(give, ("x", "w"), pairs(4, lambda i: i ^ 3))
     return (keep + landed.astype(jnp.float32)).astype(jnp.bfloat16)
 

time: 94.4 us -> 90 us (0.953)
  matrix products: 7.32 us -> 0 us
  starting transfers between devices: 38.2 us -> 43.9 us
  local copies, waits for them, and re-layouts: 1.74 us -> 0.15 us
    dot_general x2 -> x0, matrix products: 7.32 us -> none  [project(): jnp.dot(block, out_weight, preferred_element_type=jnp.float32)]
    ppermute x1, waiting for transfers between devices: 0.01 us -> 2.2 us  [on_device(): taken = lax.ppermute(given, 'z', pairs(NZ, lambda i: i ^ 1))]
    ppermute x1, starting transfers between devices: 2.68 us -> 4.46 us  [gather_xy(): both = jnp.concatenate([own, lax.ppermute(own, 'x', X_PAIRS)], axis=0)]
    ppermute x10 -> x9, starting transfers between devices: 15.3 us -> 17.1 us  [the longest x7 9.11 us: exchange(): received.append(lax.ppermute(partial[k], ('x', 'y', 'c'), moves))]
    pallas_call x1, Pallas kernels: 3.13 us -> 1.4 us  [combine(): pl.pallas_call(combine_kernel, out_shape=(block, block), in_specs=[SMEM]...]
    ppermute x10 -> x9, waiting for transfers between devices: 9.74 us -> 8.15 us  [the longest x7 6.38 us: exchange(): received.append(lax.ppermute(partial[k], ('x', 'y', 'c'), moves))]
    unnamed x21 -> x7, local copies, waits for them, and re-layouts: 1.6 us -> 0.02 us
    pallas_call x2 -> x3, Pallas kernels: 3.95 us -> 5.32 us  [the longest x1 1.96 us: prepare_queries(): pl.pallas_call(prepare_queries_kernel, out_shape=jax.ShapeDtypeStruct((PI...]
  transfers between devices with their start and end apart: 19 -> 18, of which waited for: 9 -> 9; matrix products, arithmetic and copies ran while one was open for 9% -> 1% of each run, Pallas kernels for 2% -> 0%
where the time goes in v5:
time: 90 us; the launch traced here: 89.8 us
  starting transfers between devices  43.9 us (49%)
  waiting for transfers between devices  27.5 us (31%)
  Pallas kernels  16.2 us (18%)
  other arithmetic  1.96 us (2%)
    pallas_call x1, Pallas kernels, attention(): pl.pallas_call(attention_kernel, out_shape=jax.ShapeDtypeStruct((GROUP, P...  9.45 us
    ppermute x7, starting transfers between devices, exchange(): received.append(lax.ppermute(partial[k], ('x', 'y', 'c'), moves))  9.11 us
    ppermute x1, waiting for transfers between devices, on_device(): landed = lax.ppermute(give, ('x', 'w'), pairs(4, lambda i: i ^ 3))  8.2 us
    ppermute x1, starting transfers between devices, gather_z(): one = lax.ppermute(own, ('z', 'c'), here)  6.41 us
    ppermute x1, starting transfers between devices, on_device(): got = lax.ppermute(other, 'c', X_PAIRS)  6.4 us
    ppermute x7, waiting for transfers between devices, exchange(): received.append(lax.ppermute(partial[k], ('x', 'y', 'c'), moves))  6.38 us
    ppermute x1, waiting for transfers between devices, gather_z(): four = lax.ppermute(three, ('z', 'c'), there)  5.43 us
    ppermute x1, starting transfers between devices, gather_xy(): both = jnp.concatenate([own, lax.ppermute(own, 'x', X_PAIRS)], axis=0)  4.46 us
  transfers between devices with their start and end apart: 18, of which 9 were waited for; matrix products, arithmetic and copies ran while one was open for 1% of the time, Pallas kernels for 0%

profile of v5, /device:TPU:1, one launch (start us, length us, event | category | flops | bytes accessed | tf_op | source)
XLA Modules:
  0.0 89.8 jit_solution(10028488068435507572)
XLA Ops:
  0.0 1.9 %shard_map.82 = (bf16[128,512]{1,0:T(8,128)(2,1)}, f32[128,128]{1,0:T(8,128)}, f32[128,128]{1,0:T(8,128)}) custom-call(bf16[128,256]{1,0:T(8,128)(2,1)} %k_ref.1, bf16[128,256]{1,0:T(8,128)(2,1)} %v_ref.1, s32[1,128]{1,0:T(1,128)} %bitcast.32, f32[1,128]{1,0:T(1,128)} %constant.36.clone.freq_ref, f32[1,128]{1,0:T(1,128)} %bitcast.33), custom_call_target="tpu_custom_call" | custom-call | tf_op jit(solution)/shard_map/pallas_call | solution.py:76
  1.9 2.0 %shard_map.83 = bf16[128,512]{1,0:T(8,128)(2,1)} custom-call(bf16[128,512]{1,0:T(8,128)(2,1)} %q_ref.1, f32[128,128]{1,0:T(8,128)} %get-tuple-element.12.cos_ref, f32[128,128]{1,0:T(8,128)} %get-tuple-element.13.sin_ref, f32[1,128]{1,0:T(1,128)} %bitcast.34), custom_call_target="tpu_custom_call" | custom-call | tf_op jit(solution)/shard_map/pallas_call | solution.py:92
  3.9 1.6 %collective-permute-start = (bf16[128,512]{1,0:T(8,128)(2,1)}, bf16[128,512]{1,0:T(8,128)(2,1)S(1)}, u32[]{:S(2)}, u32[]{:S(2)}) collective-permute-start(bf16[128,512]{1,0:T(8,128)(2,1)} %shard_map.83), channel_id=1, source_target_pairs={{0,0},{4,8},{8,16},{12,24},{16,4},{20,12},{24,20},{28,28},{128,152... | collective-permute-start | bytes 393224 | tf_op jit(solution)/shard_map/ppermute | solution.py:342
  5.4 6.4 %collective-permute-start.4 = (bf16[128,512]{1,0:T(8,128)(2,1)}, bf16[128,512]{1,0:T(8,128)(2,1)S(1)}, u32[]{:S(2)}, u32[]{:S(2)}) collective-permute-start(bf16[128,512]{1,0:T(8,128)(2,1)} %get-tuple-element.14.refs_3_), channel_id=1, source_target_pairs={{0,4},{1,29},{4,0},{5,9},{8,12},{9,5},{12,8},{13,17},{16,20},{17,1... | collective-permute-start | bytes 393224 | tf_op jit(solution)/shard_map/ppermute | solution.py:102
  11.8 0.0 collective-permute-done
  11.9 4.5 %collective-permute-start.1 = (bf16[128,512]{1,0:T(8,128)(2,1)S(1)}, bf16[128,512]{1,0:T(8,128)(2,1)S(1)}, u32[]{:S(2)}, u32[]{:S(2)}) collective-permute-start(bf16[128,512]{1,0:T(8,128)(2,1)S(1)} %collective-permute-done), channel_id=1, source_target_pairs={{0,128},{128,0},{1,129},{129,1},{2,130},{130,2},{3,131},{131,3},{4... | collective-permute-start | bytes 393224 | tf_op jit(solution)/shard_map/ppermute | solution.py:131
  16.3 0.0 collective-permute-done.4.refs_4_
  16.3 0.9 %pad_maximum_fusion.1 = bf16[256,512]{1,0:T(8,128)(2,1)S(1)} fusion(bf16[128,512]{1,0:T(8,128)(2,1)S(1)} %collective-permute-done.4.refs_4_, bf16[128,512]{1,0:T(8,128)(2,1)} %get-tuple-element.14.refs_3_), kind=kLoop, calls=%fused_computation.6 | loop fusion | flops 524288 | bytes 524288 | tf_op jit(solution)/shard_map/concatenate | solution.py:103
  17.2 3.9 %collective-permute-start.5 = (bf16[256,512]{1,0:T(8,128)(2,1)S(1)}, bf16[256,512]{1,0:T(8,128)(2,1)S(1)}, u32[]{:S(2)}, u32[]{:S(2)}) collective-permute-start(bf16[256,512]{1,0:T(8,128)(2,1)S(1)} %pad_maximum_fusion.1), channel_id=1, source_target_pairs={{0,28},{1,5},{4,8},{5,1},{8,4},{9,13},{12,16},{13,9},{16,12},{17,2... | collective-permute-start | bytes 786440 | tf_op jit(solution)/shard_map/ppermute | solution.py:103
  21.1 0.0 collective-permute-done.1
  21.1 2.8 %collective-permute-start.2 = (bf16[256,512]{1,0:T(8,128)(2,1)S(1)}, bf16[256,512]{1,0:T(8,128)(2,1)S(1)}, u32[]{:S(2)}, u32[]{:S(2)}) collective-permute-start(bf16[256,512]{1,0:T(8,128)(2,1)S(1)} %constant_dynamic-update-slice_fusion.refs_0_), channel_id=1, source_target_pairs={{0,32},{1,97},{32,0},{33,65},{64,96},{65,33},{96,64},{97,1},{2,34}... | collective-permute-start | bytes 786440 | tf_op jit(solution)/shard_map/ppermute | solution.py:132
  24.0 1.2 %collective-permute-done.5.refs_5_ = bf16[256,512]{1,0:T(8,128)(2,1)S(1)} collective-permute-done((bf16[256,512]{1,0:T(8,128)(2,1)S(1)}, bf16[256,512]{1,0:T(8,128)(2,1)S(1)}, u32[]{:S(2)}, u32[]{:S(2)}) %collective-permute-start.5) | collective-permute-done | bytes 262176 | tf_op jit(solution)/shard_map/ppermute | solution.py:103
  25.2 4.3 %collective-permute-start.6 = (bf16[256,512]{1,0:T(8,128)(2,1)S(1)}, bf16[256,512]{1,0:T(8,128)(2,1)S(1)}, u32[]{:S(2)}, u32[]{:S(2)}) collective-permute-start(bf16[256,512]{1,0:T(8,128)(2,1)S(1)} %collective-permute-done.5.refs_5_), channel_id=1, source_target_pairs={{0,4},{1,29},{4,0},{5,9},{8,12},{9,5},{12,8},{13,17},{16,20},{17,1... | collective-permute-start | bytes 786440 | tf_op jit(solution)/shard_map/ppermute | solution.py:104
  29.4 0.0 collective-permute-done.2.refs_1_
  29.5 1.4 %collective-permute-start.3 = (bf16[512,512]{1,0:T(8,128)(2,1)S(1)}, bf16[512,512]{1,0:T(8,128)(2,1)S(1)}, u32[]{:S(2)}, u32[]{:S(2)}) collective-permute-start(bf16[512,512]{1,0:T(8,128)(2,1)S(1)} %pad_maximum_fusion), channel_id=1, source_target_pairs={{0,96},{1,33},{32,64},{33,1},{64,32},{65,97},{96,0},{97,65},{2,98}... | collective-permute-start | bytes 1572872 | tf_op jit(solution)/shard_map/ppermute | solution.py:133
  30.8 2.3 %collective-permute-done.6.refs_6_ = bf16[256,512]{1,0:T(8,128)(2,1)S(1)} collective-permute-done((bf16[256,512]{1,0:T(8,128)(2,1)S(1)}, bf16[256,512]{1,0:T(8,128)(2,1)S(1)}, u32[]{:S(2)}, u32[]{:S(2)}) %collective-permute-start.6) | collective-permute-done | bytes 262176 | tf_op jit(solution)/shard_map/ppermute | solution.py:104
  33.2 0.0 collective-permute-start.7
  33.2 0.1 pad_add_fusion.ids_ref
  33.3 5.4 %collective-permute-done.7.refs_7_ = bf16[256,512]{1,0:T(8,128)(2,1)S(1)} collective-permute-done((bf16[256,512]{1,0:T(8,128)(2,1)S(1)}, bf16[256,512]{1,0:T(8,128)(2,1)S(1)}, u32[]{:S(2)}, u32[]{:S(2)}) %collective-permute-start.7) | collective-permute-done | bytes 262176 | tf_op jit(solution)/shard_map/ppermute | solution.py:105
  38.7 0.0 collective-permute-done.3.refs_2_
  38.7 0.0 copy-done
  38.7 9.5 %shard_map.84.partial = bf16[8,144,512]{2,1,0:T(8,128)(2,1)S(1)} custom-call(s32[4]{0:T(128)S(1)} %pad_add_fusion.ids_ref, bf16[256,512]{1,0:T(8,128)(2,1)S(1)} %constant_dynamic-update-slice_fusion.refs_0_, bf16[256,512]{1,0:T(8,128)(2,1)S(1)} %collective-permute-done.2.refs_1_, bf16[512,512]{1,0:T(8,128)(2,1)S(1)} %collective-permute-done.3.refs_2_, ...), custom_call_target="tpu_custom_call" | custom-call | flops 2147483648 | bytes 4194304 | tf_op jit(solution)/shard_map/pallas_call | solution.py:249
  48.2 0.1 slice_bitcast_fusion
  48.2 0.1 collective-permute-start.10
  48.3 0.9 collective-permute-start.11
  49.2 4.0 %collective-permute-start.12 = (bf16[144,512]{1,0:T(8,128)(2,1)S(1)}, bf16[144,512]{1,0:T(8,128)(2,1)S(1)}, u32[]{:S(2)}, u32[]{:S(2)}) collective-permute-start(bf16[144,512]{1,0:T(8,128)(2,1)S(1)} %get-tuple-element.21), channel_id=1, source_target_pairs={{0,160},{1,225},{32,128},{33,193},{64,224},{65,161},{96,192},{97,1... | collective-permute-start | bytes 442376 | tf_op jit(solution)/shard_map/ppermute | solution.py:150
  53.2 0.0 collective-permute-start.13
  53.2 1.8 %collective-permute-start.14 = (bf16[144,512]{1,0:T(8,128)(2,1)S(1)}, bf16[144,512]{1,0:T(8,128)(2,1)S(1)}, u32[]{:S(2)}, u32[]{:S(2)}) collective-permute-start(bf16[144,512]{1,0:T(8,128)(2,1)S(1)} %get-tuple-element.19), channel_id=1, source_target_pairs={{0,224},{1,193},{32,192},{33,225},{64,160},{65,129},{96,128},{97,1... | collective-permute-start | bytes 442376 | tf_op jit(solution)/shard_map/ppermute | solution.py:150
  55.0 0.0 collective-permute-done.10.refs_2_
  55.0 2.4 %collective-permute-start.8 = (bf16[144,512]{1,0:T(8,128)(2,1)S(1)}, bf16[144,512]{1,0:T(8,128)(2,1)S(1)}, u32[]{:S(2)}, u32[]{:S(2)}) collective-permute-start(bf16[144,512]{1,0:T(8,128)(2,1)S(1)} %get-tuple-element.25), channel_id=1, source_target_pairs={{0,32},{1,129},{32,0},{33,161},{64,96},{65,193},{96,64},{97,225},{... | collective-permute-start | bytes 442376 | tf_op jit(solution)/shard_map/ppermute | solution.py:150
  57.4 0.0 collective-permute-done.11.refs_3_
  57.4 0.0 collective-permute-start.9
  57.4 0.0 collective-permute-done.12.refs_4_
  57.4 2.2 %collective-permute-done.13.refs_5_ = bf16[144,512]{1,0:T(8,128)(2,1)S(1)} collective-permute-done((bf16[144,512]{1,0:T(8,128)(2,1)S(1)}, bf16[144,512]{1,0:T(8,128)(2,1)S(1)}, u32[]{:S(2)}, u32[]{:S(2)}) %collective-permute-start.13) | collective-permute-done | bytes 147488 | tf_op jit(solution)/shard_map/ppermute | solution.py:150
  59.6 1.6 %collective-permute-done.14.refs_6_ = bf16[144,512]{1,0:T(8,128)(2,1)S(1)} collective-permute-done((bf16[144,512]{1,0:T(8,128)(2,1)S(1)}, bf16[144,512]{1,0:T(8,128)(2,1)S(1)}, u32[]{:S(2)}, u32[]{:S(2)}) %collective-permute-start.14) | collective-permute-done | bytes 147488 | tf_op jit(solution)/shard_map/ppermute | solution.py:150
  61.2 2.6 %collective-permute-done.8.refs_0_ = bf16[144,512]{1,0:T(8,128)(2,1)S(1)} collective-permute-done((bf16[144,512]{1,0:T(8,128)(2,1)S(1)}, bf16[144,512]{1,0:T(8,128)(2,1)S(1)}, u32[]{:S(2)}, u32[]{:S(2)}) %collective-permute-start.8) | collective-permute-done | bytes 147488 | tf_op jit(solution)/shard_map/ppermute | solution.py:150
  63.7 0.0 collective-permute-done.9.refs_1_
  63.7 1.4 %shard_map.85 = (bf16[64,512]{1,0:T(8,128)(2,1)S(1)}, bf16[64,512]{1,0:T(8,128)(2,1)S(1)}) custom-call(s32[4]{0:T(128)S(1)} %pad_add_fusion.ids_ref, bf16[8,144,512]{2,1,0:T(8,128)(2,1)S(1)} %shard_map.84.partial, bf16[144,512]{1,0:T(8,128)(2,1)S(1)} %collective-permute-done.8.refs_0_, bf16[144,512]{1,0:T(8,128)(2,1)S(1)} %collective-permute-done.9.refs_1_, ...), custom_call_target="tpu_custom_call" | custom-call | tf_op jit(solution)/shard_map/pallas_call | solution.py:292
  65.2 1.3 %collective-permute-start.15 = (bf16[64,512]{1,0:T(8,128)(2,1)S(1)}, bf16[64,512]{1,0:T(8,128)(2,1)S(1)}, u32[]{:S(2)}, u32[]{:S(2)}) collective-permute-start(bf16[64,512]{1,0:T(8,128)(2,1)S(1)} %get-tuple-element.16), channel_id=1, source_target_pairs={{0,4},{4,0},{8,12},{12,8},{16,20},{20,16},{24,28},{28,24},{1,5},{5... | collective-permute-start | bytes 196616 | tf_op jit(solution)/shard_map/ppermute | solution.py:346
  66.5 2.2 %collective-permute-done.15.taken = bf16[64,512]{1,0:T(8,128)(2,1)S(1)} collective-permute-done((bf16[64,512]{1,0:T(8,128)(2,1)S(1)}, bf16[64,512]{1,0:T(8,128)(2,1)S(1)}, u32[]{:S(2)}, u32[]{:S(2)}) %collective-permute-start.15) | collective-permute-done | bytes 65568 | tf_op jit(solution)/shard_map/ppermute | solution.py:346
  68.7 0.0 slice-done
  68.7 1.4 %shard_map.86 = (bf16[64,5376]{1,0:T(8,128)(2,1)S(1)}, bf16[64,5376]{1,0:T(8,128)(2,1)S(1)}) custom-call(s32[4]{0:T(128)S(1)} %pad_add_fusion.ids_ref, bf16[64,512]{1,0:T(8,128)(2,1)S(1)} %get-tuple-element.15.kept, bf16[64,512]{1,0:T(8,128)(2,1)S(1)} %collective-permute-done.15.taken, bf16[512,5376]{1,0:T(8,128)(2,1)S(1)} %bitcast.29), custom_call_target="tpu_custom_call" | custom-call | flops 704643072 | bytes 8388608 | tf_op jit(solution)/shard_map/pallas_call | solution.py:326
  70.1 6.4 %collective-permute-start.16 = (bf16[64,5376]{1,0:T(8,128)(2,1)S(1)}, bf16[64,5376]{1,0:T(8,128)(2,1)S(1)}, u32[]{:S(2)}, u32[]{:S(2)}) collective-permute-start(bf16[64,5376]{1,0:T(8,128)(2,1)S(1)} %get-tuple-element.18), channel_id=1, source_target_pairs={{0,1},{1,0},{2,3},{3,2},{4,5},{5,4},{6,7},{7,6},{8,9},{9,8},{10,11... | collective-permute-start | bytes 2064392 | tf_op jit(solution)/shard_map/ppermute | solution.py:348
  76.5 1.8 %collective-permute-done.16 = bf16[64,5376]{1,0:T(8,128)(2,1)S(1)} collective-permute-done((bf16[64,5376]{1,0:T(8,128)(2,1)S(1)}, bf16[64,5376]{1,0:T(8,128)(2,1)S(1)}, u32[]{:S(2)}, u32[]{:S(2)}) %collective-permute-start.16) | collective-permute-done | bytes 688160 | tf_op jit(solution)/shard_map/ppermute | solution.py:348
  78.3 0.1 convert_add_fusion
  78.5 2.4 %collective-permute-start.17 = (bf16[32,5376]{1,0:T(8,128)(2,1)S(1)}, bf16[32,5376]{1,0:T(8,128)(2,1)S(1)}, u32[]{:S(2)}, u32[]{:S(2)}) collective-permute-start(bf16[32,5376]{1,0:T(8,128)(2,1)S(1)} %fusion.1), channel_id=1, source_target_pairs={{0,130},{2,128},{128,2},{130,0},{1,131},{3,129},{129,3},{131,1},{4... | collective-permute-start | bytes 1032200 | tf_op jit(solution)/shard_map/ppermute | solution.py:352
  80.8 8.2 %collective-permute-done.17 = bf16[32,5376]{1,0:T(8,128)(2,1)S(1)} collective-permute-done((bf16[32,5376]{1,0:T(8,128)(2,1)S(1)}, bf16[32,5376]{1,0:T(8,128)(2,1)S(1)}, u32[]{:S(2)}, u32[]{:S(2)}) %collective-permute-start.17) | collective-permute-done | bytes 344096 | tf_op jit(solution)/shard_map/ppermute | solution.py:352
  89.0 0.8 fusion
  (9 shorter events, 0.1 us)
Async XLA Ops:
  1.9 36.8 %copy-start = (bf16[128,512]{1,0:T(8,128)(2,1)S(1)}, bf16[128,512]{1,0:T(8,128)(2,1)}, u32[]{:S(2)}) copy-start(bf16[128,512]{1,0:T(8,128)(2,1)} %get-tuple-element.14.refs_3_) | copy-start | bytes 393220
  3.9 8.0 %collective-permute-start = (bf16[128,512]{1,0:T(8,128)(2,1)}, bf16[128,512]{1,0:T(8,128)(2,1)S(1)}, u32[]{:S(2)}, u32[]{:S(2)}) collective-permute-start(bf16[128,512]{1,0:T(8,128)(2,1)} %shard_map.83), channel_id=1, source_target_pairs={{0,0},{4,8},{8,16},{12,24},{16,4},{20,12},{24,20},{28,28},{128,152... | collective-permute-start | bytes 393224 | tf_op jit(solution)/shard_map/ppermute | solution.py:342
  5.4 10.9 %collective-permute-start.4 = (bf16[128,512]{1,0:T(8,128)(2,1)}, bf16[128,512]{1,0:T(8,128)(2,1)S(1)}, u32[]{:S(2)}, u32[]{:S(2)}) collective-permute-start(bf16[128,512]{1,0:T(8,128)(2,1)} %get-tuple-element.14.refs_3_), channel_id=1, source_target_pairs={{0,4},{1,29},{4,0},{5,9},{8,12},{9,5},{12,8},{13,17},{16,20},{17,1... | collective-permute-start | bytes 393224 | tf_op jit(solution)/shard_map/ppermute | solution.py:102
  11.9 9.3 %collective-permute-start.1 = (bf16[128,512]{1,0:T(8,128)(2,1)S(1)}, bf16[128,512]{1,0:T(8,128)(2,1)S(1)}, u32[]{:S(2)}, u32[]{:S(2)}) collective-permute-start(bf16[128,512]{1,0:T(8,128)(2,1)S(1)} %collective-permute-done), channel_id=1, source_target_pairs={{0,128},{128,0},{1,129},{129,1},{2,130},{130,2},{3,131},{131,3},{4... | collective-permute-start | bytes 393224 | tf_op jit(solution)/shard_map/ppermute | solution.py:131
  17.2 7.9 %collective-permute-start.5 = (bf16[256,512]{1,0:T(8,128)(2,1)S(1)}, bf16[256,512]{1,0:T(8,128)(2,1)S(1)}, u32[]{:S(2)}, u32[]{:S(2)}) collective-permute-start(bf16[256,512]{1,0:T(8,128)(2,1)S(1)} %pad_maximum_fusion.1), channel_id=1, source_target_pairs={{0,28},{1,5},{4,8},{5,1},{8,4},{9,13},{12,16},{13,9},{16,12},{17,2... | collective-permute-start | bytes 786440 | tf_op jit(solution)/shard_map/ppermute | solution.py:103
  21.1 8.3 %collective-permute-start.2 = (bf16[256,512]{1,0:T(8,128)(2,1)S(1)}, bf16[256,512]{1,0:T(8,128)(2,1)S(1)}, u32[]{:S(2)}, u32[]{:S(2)}) collective-permute-start(bf16[256,512]{1,0:T(8,128)(2,1)S(1)} %constant_dynamic-update-slice_fusion.refs_0_), channel_id=1, source_target_pairs={{0,32},{1,97},{32,0},{33,65},{64,96},{65,33},{96,64},{97,1},{2,34}... | collective-permute-start | bytes 786440 | tf_op jit(solution)/shard_map/ppermute | solution.py:132
  25.2 8.0 %collective-permute-start.6 = (bf16[256,512]{1,0:T(8,128)(2,1)S(1)}, bf16[256,512]{1,0:T(8,128)(2,1)S(1)}, u32[]{:S(2)}, u32[]{:S(2)}) collective-permute-start(bf16[256,512]{1,0:T(8,128)(2,1)S(1)} %collective-permute-done.5.refs_5_), channel_id=1, source_target_pairs={{0,4},{1,29},{4,0},{5,9},{8,12},{9,5},{12,8},{13,17},{16,20},{17,1... | collective-permute-start | bytes 786440 | tf_op jit(solution)/shard_map/ppermute | solution.py:104
  29.5 9.2 %collective-permute-start.3 = (bf16[512,512]{1,0:T(8,128)(2,1)S(1)}, bf16[512,512]{1,0:T(8,128)(2,1)S(1)}, u32[]{:S(2)}, u32[]{:S(2)}) collective-permute-start(bf16[512,512]{1,0:T(8,128)(2,1)S(1)} %pad_maximum_fusion), channel_id=1, source_target_pairs={{0,96},{1,33},{32,64},{33,1},{64,32},{65,97},{96,0},{97,65},{2,98}... | collective-permute-start | bytes 1572872 | tf_op jit(solution)/shard_map/ppermute | solution.py:133
  33.2 5.5 %collective-permute-start.7 = (bf16[256,512]{1,0:T(8,128)(2,1)S(1)}, bf16[256,512]{1,0:T(8,128)(2,1)S(1)}, u32[]{:S(2)}, u32[]{:S(2)}) collective-permute-start(bf16[256,512]{1,0:T(8,128)(2,1)S(1)} %collective-permute-done.6.refs_6_), channel_id=1, source_target_pairs={{0,28},{1,5},{4,8},{5,1},{8,4},{9,13},{12,16},{13,9},{16,12},{17,2... | collective-permute-start | bytes 786440 | tf_op jit(solution)/shard_map/ppermute | solution.py:105
  33.2 35.5 %slice-start = ((s8[5505024]{0:T(1024)(128)(4,1)}), s8[4194304]{0:T(1024)(128)(4,1)S(1)}, s32[]{:S(2)}) async-start(s8[5505024]{0:T(1024)(128)(4,1)} %bitcast.28), calls=%async_computation | async-start | bytes 8388608
  33.3 35.4 %slice-start.1 = ((s8[5505024]{0:T(1024)(128)(4,1)}), s8[1310720]{0:T(1024)(128)(4,1)S(1)}, s32[]{:S(2)}) async-start(s8[5505024]{0:T(1024)(128)(4,1)} %bitcast.28), calls=%async_computation.1 | async-start | bytes 2621440
  48.2 6.7 %collective-permute-start.10 = (bf16[144,512]{1,0:T(8,128)(2,1)S(1)}, bf16[144,512]{1,0:T(8,128)(2,1)S(1)}, u32[]{:S(2)}, u32[]{:S(2)}) collective-permute-start(bf16[144,512]{1,0:T(8,128)(2,1)S(1)} %get-tuple-element.23), channel_id=1, source_target_pairs={{0,96},{1,161},{32,64},{33,129},{64,32},{65,225},{96,0},{97,193},{... | collective-permute-start | bytes 442376 | tf_op jit(solution)/shard_map/ppermute | solution.py:150
  48.3 9.0 %collective-permute-start.11 = (bf16[144,512]{1,0:T(8,128)(2,1)S(1)}, bf16[144,512]{1,0:T(8,128)(2,1)S(1)}, u32[]{:S(2)}, u32[]{:S(2)}) collective-permute-start(bf16[144,512]{1,0:T(8,128)(2,1)S(1)} %get-tuple-element.22), channel_id=1, source_target_pairs={{0,128},{1,97},{32,160},{33,65},{64,192},{65,33},{96,224},{97,1},{... | collective-permute-start | bytes 442376 | tf_op jit(solution)/shard_map/ppermute | solution.py:150
  49.2 8.2 %collective-permute-start.12 = (bf16[144,512]{1,0:T(8,128)(2,1)S(1)}, bf16[144,512]{1,0:T(8,128)(2,1)S(1)}, u32[]{:S(2)}, u32[]{:S(2)}) collective-permute-start(bf16[144,512]{1,0:T(8,128)(2,1)S(1)} %get-tuple-element.21), channel_id=1, source_target_pairs={{0,160},{1,225},{32,128},{33,193},{64,224},{65,161},{96,192},{97,1... | collective-permute-start | bytes 442376 | tf_op jit(solution)/shard_map/ppermute | solution.py:150
  53.2 6.4 %collective-permute-start.13 = (bf16[144,512]{1,0:T(8,128)(2,1)S(1)}, bf16[144,512]{1,0:T(8,128)(2,1)S(1)}, u32[]{:S(2)}, u32[]{:S(2)}) collective-permute-start(bf16[144,512]{1,0:T(8,128)(2,1)S(1)} %get-tuple-element.20), channel_id=1, source_target_pairs={{0,192},{1,65},{32,224},{33,97},{64,128},{65,1},{96,160},{97,33},{... | collective-permute-start | bytes 442376 | tf_op jit(solution)/shard_map/ppermute | solution.py:150
  53.2 8.0 %collective-permute-start.14 = (bf16[144,512]{1,0:T(8,128)(2,1)S(1)}, bf16[144,512]{1,0:T(8,128)(2,1)S(1)}, u32[]{:S(2)}, u32[]{:S(2)}) collective-permute-start(bf16[144,512]{1,0:T(8,128)(2,1)S(1)} %get-tuple-element.19), channel_id=1, source_target_pairs={{0,224},{1,193},{32,192},{33,225},{64,160},{65,129},{96,128},{97,1... | collective-permute-start | bytes 442376 | tf_op jit(solution)/shard_map/ppermute | solution.py:150
  55.0 8.8 %collective-permute-start.8 = (bf16[144,512]{1,0:T(8,128)(2,1)S(1)}, bf16[144,512]{1,0:T(8,128)(2,1)S(1)}, u32[]{:S(2)}, u32[]{:S(2)}) collective-permute-start(bf16[144,512]{1,0:T(8,128)(2,1)S(1)} %get-tuple-element.25), channel_id=1, source_target_pairs={{0,32},{1,129},{32,0},{33,161},{64,96},{65,193},{96,64},{97,225},{... | collective-permute-start | bytes 442376 | tf_op jit(solution)/shard_map/ppermute | solution.py:150
  57.4 6.4 %collective-permute-start.9 = (bf16[144,512]{1,0:T(8,128)(2,1)S(1)}, bf16[144,512]{1,0:T(8,128)(2,1)S(1)}, u32[]{:S(2)}, u32[]{:S(2)}) collective-permute-start(bf16[144,512]{1,0:T(8,128)(2,1)S(1)} %get-tuple-element.24), channel_id=1, source_target_pairs={{0,64},{1,33},{32,96},{33,1},{64,0},{65,97},{96,32},{97,65},{128,1... | collective-permute-start | bytes 442376 | tf_op jit(solution)/shard_map/ppermute | solution.py:150
  65.2 3.5 %collective-permute-start.15 = (bf16[64,512]{1,0:T(8,128)(2,1)S(1)}, bf16[64,512]{1,0:T(8,128)(2,1)S(1)}, u32[]{:S(2)}, u32[]{:S(2)}) collective-permute-start(bf16[64,512]{1,0:T(8,128)(2,1)S(1)} %get-tuple-element.16), channel_id=1, source_target_pairs={{0,4},{4,0},{8,12},{12,8},{16,20},{20,16},{24,28},{28,24},{1,5},{5... | collective-permute-start | bytes 196616 | tf_op jit(solution)/shard_map/ppermute | solution.py:346
  70.1 8.2 %collective-permute-start.16 = (bf16[64,5376]{1,0:T(8,128)(2,1)S(1)}, bf16[64,5376]{1,0:T(8,128)(2,1)S(1)}, u32[]{:S(2)}, u32[]{:S(2)}) collective-permute-start(bf16[64,5376]{1,0:T(8,128)(2,1)S(1)} %get-tuple-element.18), channel_id=1, source_target_pairs={{0,1},{1,0},{2,3},{3,2},{4,5},{5,4},{6,7},{7,6},{8,9},{9,8},{10,11... | collective-permute-start | bytes 2064392 | tf_op jit(solution)/shard_map/ppermute | solution.py:348
  78.5 10.6 %collective-permute-start.17 = (bf16[32,5376]{1,0:T(8,128)(2,1)S(1)}, bf16[32,5376]{1,0:T(8,128)(2,1)S(1)}, u32[]{:S(2)}, u32[]{:S(2)}) collective-permute-start(bf16[32,5376]{1,0:T(8,128)(2,1)S(1)} %fusion.1), channel_id=1, source_target_pairs={{0,130},{2,128},{128,2},{130,0},{1,131},{3,129},{129,3},{131,1},{4... | collective-permute-start | bytes 1032200 | tf_op jit(solution)/shard_map/ppermute | solution.py:352

commit v6 on v5

--- a/solution.py
+++ b/solution.py
@@ -185,7 +185,7 @@
         end_y = (((source & 1) ^ upper) << 1) | ((z & 1) ^ upper)
         return position(core, group ^ ((end_x << 2) | end_y))
 
-    def one(half, pair, masked):
+    def score(half, pair, masked):
         query = q_s[half, pl.ds(pair * 2, 2)].reshape(width, HD)
         scores = lax.dot_general(query, k_s[half], NT, preferred_element_type=jnp.float32)
         if masked:
@@ -195,6 +195,9 @@
             last = (source * NZ + at_z) * PIECE + row % PIECE - group * keys
             column = lax.broadcasted_iota(jnp.int32, (width, keys), 1)
             scores = jnp.where(column <= last, scores, NEGATIVE)
+        return scores
+
+    def finish(half, pair, scores):
         highest = jnp.max(scores, axis=1, keepdims=True)
         weights = jnp.exp2(scores - highest)
         total = jnp.sum(weights, axis=1, keepdims=True)
@@ -210,19 +213,24 @@
                 out_ref[step, :PIECE, head * HD : (head + 1) * HD] = normal[base : base + PIECE]
                 level_s[...] = jnp.where(lane == step * 4 + head, level[base : base + PIECE], level_s[...])
 
+    def run(tiles):
+        scores = score(*tiles[0])
+        for index, tile in enumerate(tiles):
+            following = score(*tiles[index + 1]) if index + 1 < len(tiles) else None
+            finish(tile[0], tile[1], scores)
+            scores = following
+
     def body(pair, carry):
         full = pair * 2 > group
         none = pair * 2 + 1 < group
 
         @pl.when(full)
         def _():
-            one(0, pair, False)
-            one(1, pair, False)
+            run([(0, pair, False), (1, pair, False)])
 
         @pl.when(jnp.logical_not(jnp.logical_or(full, none)))
         def _():
-            one(0, pair, True)
-            one(1, pair, True)
+            run([(0, pair, True), (1, pair, True)])
 
         @pl.when(none)
         def _():
@@ -231,7 +239,14 @@
 
         return carry
 
-    lax.fori_loop(0, GROUP // 2, body, 0)
+    @pl.when(group < 2)
+    def _():
+        run([(half, pair, pair == 0) for pair in range(GROUP // 2) for half in range(2)])
+
+    @pl.when(group >= 2)
+    def _():
+        lax.fori_loop(0, GROUP // 2, body, 0)
+
     levels = jnp.transpose(level_s[...])
     row = lax.broadcasted_iota(jnp.int32, (STATS, PIECE), 0)
     for step in range(GROUP):
@@ -257,7 +272,7 @@
             pltpu.VMEM((2, NZ * PIECE, HD), jnp.bfloat16),
             pltpu.VMEM((PIECE, HD), jnp.float32),
         ],
-        compiler_params=pltpu.CompilerParams(vmem_limit_bytes=VMEM_LIMIT),
+        compiler_params=pltpu.CompilerParams(vmem_limit_bytes=36 * 1024 * 1024),
         cost_estimate=pl.CostEstimate(flops=flops, bytes_accessed=2**22, transcendentals=2**22),
     )(ids, *queries, *pieces)
 
@@ -298,10 +313,14 @@
     )(ids, partial, *received)
 
 
-TILE = 768
-
-
-def project_kernel(ids_ref, kept, taken, weight, other_out, mine_out, rows_s):
+TILE = 896
+
+
+CHUNKS = 3
+
+
+def project_kernel(ids_ref, kept, taken, weight, *refs):
+    others, mines, rows_s = refs[:CHUNKS], refs[CHUNKS : 2 * CHUNKS], refs[-1]
     core = ids_ref[2]
     quarter = PIECE // 4
     kept_high = ((ids_ref[0] ^ ids_ref[1]) & 1) == 1
@@ -314,20 +333,24 @@
             start = pl.multiple_of(own * BLOCK + k * quarter, quarter)
             rows_s[pl.ds(start, quarter), :] = block[part * quarter : (part + 1) * quarter]
     rows = rows_s[...]
-    for tile in range(weight.shape[1] // TILE):
-        lanes = slice(tile * TILE, (tile + 1) * TILE)
-        product = jnp.dot(rows, weight[:, lanes], preferred_element_type=jnp.float32).astype(jnp.bfloat16)
-        other_out[:, lanes] = product[:BLOCK]
-        mine_out[:, lanes] = product[BLOCK:]
+    tiles = weight.shape[1] // CHUNKS // TILE
+    for chunk in range(CHUNKS):
+        for tile in range(tiles):
+            lanes = slice(tile * TILE, (tile + 1) * TILE)
+            start = (chunk * tiles + tile) * TILE
+            product = jnp.dot(rows, weight[:, start : start + TILE], preferred_element_type=jnp.float32)
+            product = product.astype(jnp.bfloat16)
+            others[chunk][:, lanes] = product[:BLOCK]
+            mines[chunk][:, lanes] = product[BLOCK:]
 
 
 def project(ids, kept, taken, out_weight):
-    half = jax.ShapeDtypeStruct((BLOCK, out_weight.shape[1]), jnp.bfloat16)
+    half = jax.ShapeDtypeStruct((BLOCK, out_weight.shape[1] // CHUNKS), jnp.bfloat16)
     return pl.pallas_call(
         project_kernel,
-        out_shape=(half, half),
+        out_shape=(half,) * (2 * CHUNKS),
         in_specs=[SMEM] + [VMEM] * 3,
-        out_specs=(VMEM, VMEM),
+        out_specs=(VMEM,) * (2 * CHUNKS),
         scratch_shapes=[pltpu.VMEM((PIECE, 4 * HD), jnp.bfloat16)],
         compiler_params=pltpu.CompilerParams(vmem_limit_bytes=VMEM_LIMIT),
         cost_estimate=pl.CostEstimate(flops=2 * PIECE * 512 * 5376, bytes_accessed=2**23, transcendentals=0),
@@ -344,13 +367,16 @@
     partial = attention(ids, gather_xy(moved), pieces)
     kept, given = combine(ids, partial, exchange(partial))
     taken = lax.ppermute(given, "z", pairs(NZ, lambda i: i ^ 1))
-    other, mine = project(ids, kept, taken, out_weight)
-    got = lax.ppermute(other, "c", X_PAIRS)
-    chip = (mine.astype(jnp.float32) + got.astype(jnp.float32)).reshape(2, PIECE // 4, -1)
-    keep = lax.dynamic_index_in_dim(chip, w, 0, keepdims=False)
-    give = lax.dynamic_index_in_dim(chip, 1 - w, 0, keepdims=False).astype(jnp.bfloat16)
-    landed = lax.ppermute(give, ("x", "w"), pairs(4, lambda i: i ^ 3))
-    return (keep + landed.astype(jnp.float32)).astype(jnp.bfloat16)
+    products = project(ids, kept, taken, out_weight)
+    result = []
+    for other, mine in zip(products[:CHUNKS], products[CHUNKS:]):
+        got = lax.ppermute(other, "c", X_PAIRS)
+        chip = (mine.astype(jnp.float32) + got.astype(jnp.float32)).reshape(2, PIECE // 4, -1)
+        keep = lax.dynamic_index_in_dim(chip, w, 0, keepdims=False)
+        give = lax.dynamic_index_in_dim(chip, 1 - w, 0, keepdims=False).astype(jnp.bfloat16)
+        landed = lax.ppermute(give, ("x", "w"), pairs(4, lambda i: i ^ 3))
+        result.append((keep + landed.astype(jnp.float32)).astype(jnp.bfloat16))
+    return jnp.concatenate(result, axis=1)
 
 
 def solution(mesh):

time: 90 us -> 88.2 us (0.980)
  starting transfers between devices: 43.9 us -> 46.7 us
  waiting for transfers between devices: 27.5 us -> 25.1 us
  Pallas kernels: 16.2 us -> 14 us
    ppermute x1 -> x3, starting transfers between devices: 2.38 us -> 6.34 us  [on_device(): landed = lax.ppermute(give, ('x', 'w'), pairs(4, lambda i: i ^ 3))]
    ppermute x1 -> x3, waiting for transfers between devices: 8.2 us -> 4.8 us  [on_device(): landed = lax.ppermute(give, ('x', 'w'), pairs(4, lambda i: i ^ 3))]
    pallas_call x1, Pallas kernels: 9.45 us -> 7.13 us  [attention(): pl.pallas_call(attention_kernel, out_shape=jax.ShapeDtypeStruct((GROUP, P...]
    ppermute x7, waiting for transfers between devices: 6.38 us -> 7.63 us  [exchange(): received.append(lax.ppermute(partial[k], ('x', 'y', 'c'), moves))]
    ppermute x1, starting transfers between devices: 1.29 us -> 0.09 us  [on_device(): taken = lax.ppermute(given, 'z', pairs(NZ, lambda i: i ^ 1))]
    ppermute x1 -> x3, waiting for transfers between devices: 1.77 us -> 0.61 us  [on_device(): got = lax.ppermute(other, 'c', X_PAIRS)]
    ppermute x1 -> x3, starting transfers between devices: 6.4 us -> 6.39 us  [on_device(): got = lax.ppermute(other, 'c', X_PAIRS)]
  transfers between devices with their start and end apart: 18 -> 22, of which waited for: 9 -> 11; matrix products, arithmetic and copies ran while one was open for 1% -> 1% of each run, Pallas kernels for 0% -> 0%
where the time goes in v6:
time: 88.2 us; the launch traced here: 88.1 us
  starting transfers between devices  46.7 us (53%)
  waiting for transfers between devices  25.1 us (28%)
  Pallas kernels  14 us (16%)
  other arithmetic  2 us (2%)
    ppermute x7, starting transfers between devices, exchange(): received.append(lax.ppermute(partial[k], ('x', 'y', 'c'), moves))  9.12 us
    ppermute x7, waiting for transfers between devices, exchange(): received.append(lax.ppermute(partial[k], ('x', 'y', 'c'), moves))  7.63 us
    pallas_call x1, Pallas kernels, attention(): pl.pallas_call(attention_kernel, out_shape=jax.ShapeDtypeStruct((GROUP, P...  7.13 us
    ppermute x1, starting transfers between devices, gather_z(): one = lax.ppermute(own, ('z', 'c'), here)  6.41 us
    ppermute x3, starting transfers between devices, on_device(): got = lax.ppermute(other, 'c', X_PAIRS)  6.39 us
    ppermute x3, starting transfers between devices, on_device(): landed = lax.ppermute(give, ('x', 'w'), pairs(4, lambda i: i ^ 3))  6.34 us
    ppermute x1, waiting for transfers between devices, gather_z(): four = lax.ppermute(three, ('z', 'c'), there)  5.43 us
    ppermute x3, waiting for transfers between devices, on_device(): landed = lax.ppermute(give, ('x', 'w'), pairs(4, lambda i: i ^ 3))  4.8 us
  transfers between devices with their start and end apart: 22, of which 11 were waited for; matrix products, arithmetic and copies ran while one was open for 1% of the time, Pallas kernels for 0%

profile of v6, /device:TPU:1, one launch (start us, length us, event | category | flops | bytes accessed | tf_op | source)
XLA Modules:
  0.0 88.1 jit_solution(8462965143667269189)
XLA Ops:
  0.0 1.9 %shard_map.82 = (bf16[128,512]{1,0:T(8,128)(2,1)}, f32[128,128]{1,0:T(8,128)}, f32[128,128]{1,0:T(8,128)}) custom-call(bf16[128,256]{1,0:T(8,128)(2,1)} %k_ref.1, bf16[128,256]{1,0:T(8,128)(2,1)} %v_ref.1, s32[1,128]{1,0:T(1,128)} %bitcast.50, f32[1,128]{1,0:T(1,128)} %constant.44.clone.freq_ref, f32[1,128]{1,0:T(1,128)} %bitcast.51), custom_call_target="tpu_custom_call" | custom-call | tf_op jit(solution)/shard_map/pallas_call | solution.py:76
  1.9 2.0 %shard_map.83 = bf16[128,512]{1,0:T(8,128)(2,1)} custom-call(bf16[128,512]{1,0:T(8,128)(2,1)} %q_ref.1, f32[128,128]{1,0:T(8,128)} %get-tuple-element.16.cos_ref, f32[128,128]{1,0:T(8,128)} %get-tuple-element.17.sin_ref, f32[1,128]{1,0:T(1,128)} %bitcast.52), custom_call_target="tpu_custom_call" | custom-call | tf_op jit(solution)/shard_map/pallas_call | solution.py:92
  3.9 1.6 %collective-permute-start = (bf16[128,512]{1,0:T(8,128)(2,1)}, bf16[128,512]{1,0:T(8,128)(2,1)S(1)}, u32[]{:S(2)}, u32[]{:S(2)}) collective-permute-start(bf16[128,512]{1,0:T(8,128)(2,1)} %shard_map.83), channel_id=1, source_target_pairs={{0,0},{4,8},{8,16},{12,24},{16,4},{20,12},{24,20},{28,28},{128,152... | collective-permute-start | bytes 393224 | tf_op jit(solution)/shard_map/ppermute | solution.py:365
  5.4 6.4 %collective-permute-start.4 = (bf16[128,512]{1,0:T(8,128)(2,1)}, bf16[128,512]{1,0:T(8,128)(2,1)S(1)}, u32[]{:S(2)}, u32[]{:S(2)}) collective-permute-start(bf16[128,512]{1,0:T(8,128)(2,1)} %get-tuple-element.18.refs_3_), channel_id=1, source_target_pairs={{0,4},{1,29},{4,0},{5,9},{8,12},{9,5},{12,8},{13,17},{16,20},{17,1... | collective-permute-start | bytes 393224 | tf_op jit(solution)/shard_map/ppermute | solution.py:102
  11.8 0.0 collective-permute-done
  11.9 4.5 %collective-permute-start.1 = (bf16[128,512]{1,0:T(8,128)(2,1)S(1)}, bf16[128,512]{1,0:T(8,128)(2,1)S(1)}, u32[]{:S(2)}, u32[]{:S(2)}) collective-permute-start(bf16[128,512]{1,0:T(8,128)(2,1)S(1)} %collective-permute-done), channel_id=1, source_target_pairs={{0,128},{128,0},{1,129},{129,1},{2,130},{130,2},{3,131},{131,3},{4... | collective-permute-start | bytes 393224 | tf_op jit(solution)/shard_map/ppermute | solution.py:131
  16.3 0.0 collective-permute-done.4.refs_4_
  16.3 0.9 %pad_maximum_fusion.2 = bf16[256,512]{1,0:T(8,128)(2,1)S(1)} fusion(bf16[128,512]{1,0:T(8,128)(2,1)S(1)} %collective-permute-done.4.refs_4_, bf16[128,512]{1,0:T(8,128)(2,1)} %get-tuple-element.18.refs_3_), kind=kLoop, calls=%fused_computation.5 | loop fusion | flops 524288 | bytes 524288 | tf_op jit(solution)/shard_map/concatenate | solution.py:103
  17.2 3.9 %collective-permute-start.5 = (bf16[256,512]{1,0:T(8,128)(2,1)S(1)}, bf16[256,512]{1,0:T(8,128)(2,1)S(1)}, u32[]{:S(2)}, u32[]{:S(2)}) collective-permute-start(bf16[256,512]{1,0:T(8,128)(2,1)S(1)} %pad_maximum_fusion.2), channel_id=1, source_target_pairs={{0,28},{1,5},{4,8},{5,1},{8,4},{9,13},{12,16},{13,9},{16,12},{17,2... | collective-permute-start | bytes 786440 | tf_op jit(solution)/shard_map/ppermute | solution.py:103
  21.1 0.0 collective-permute-done.1
  21.1 2.8 %collective-permute-start.2 = (bf16[256,512]{1,0:T(8,128)(2,1)S(1)}, bf16[256,512]{1,0:T(8,128)(2,1)S(1)}, u32[]{:S(2)}, u32[]{:S(2)}) collective-permute-start(bf16[256,512]{1,0:T(8,128)(2,1)S(1)} %constant_dynamic-update-slice_fusion.refs_0_), channel_id=1, source_target_pairs={{0,32},{1,97},{32,0},{33,65},{64,96},{65,33},{96,64},{97,1},{2,34}... | collective-permute-start | bytes 786440 | tf_op jit(solution)/shard_map/ppermute | solution.py:132
  24.0 1.2 %collective-permute-done.5.refs_5_ = bf16[256,512]{1,0:T(8,128)(2,1)S(1)} collective-permute-done((bf16[256,512]{1,0:T(8,128)(2,1)S(1)}, bf16[256,512]{1,0:T(8,128)(2,1)S(1)}, u32[]{:S(2)}, u32[]{:S(2)}) %collective-permute-start.5) | collective-permute-done | bytes 262176 | tf_op jit(solution)/shard_map/ppermute | solution.py:103
  25.2 4.3 %collective-permute-start.6 = (bf16[256,512]{1,0:T(8,128)(2,1)S(1)}, bf16[256,512]{1,0:T(8,128)(2,1)S(1)}, u32[]{:S(2)}, u32[]{:S(2)}) collective-permute-start(bf16[256,512]{1,0:T(8,128)(2,1)S(1)} %collective-permute-done.5.refs_5_), channel_id=1, source_target_pairs={{0,4},{1,29},{4,0},{5,9},{8,12},{9,5},{12,8},{13,17},{16,20},{17,1... | collective-permute-start | bytes 786440 | tf_op jit(solution)/shard_map/ppermute | solution.py:104
  29.4 0.0 collective-permute-done.2.refs_1_
  29.5 1.4 %collective-permute-start.3 = (bf16[512,512]{1,0:T(8,128)(2,1)S(1)}, bf16[512,512]{1,0:T(8,128)(2,1)S(1)}, u32[]{:S(2)}, u32[]{:S(2)}) collective-permute-start(bf16[512,512]{1,0:T(8,128)(2,1)S(1)} %pad_maximum_fusion), channel_id=1, source_target_pairs={{0,96},{1,33},{32,64},{33,1},{64,32},{65,97},{96,0},{97,65},{2,98}... | collective-permute-start | bytes 1572872 | tf_op jit(solution)/shard_map/ppermute | solution.py:133
  30.8 2.3 %collective-permute-done.6.refs_6_ = bf16[256,512]{1,0:T(8,128)(2,1)S(1)} collective-permute-done((bf16[256,512]{1,0:T(8,128)(2,1)S(1)}, bf16[256,512]{1,0:T(8,128)(2,1)S(1)}, u32[]{:S(2)}, u32[]{:S(2)}) %collective-permute-start.6) | collective-permute-done | bytes 262176 | tf_op jit(solution)/shard_map/ppermute | solution.py:104
  33.2 0.0 collective-permute-start.7
  33.2 0.1 pad_add_fusion.ids_ref
  33.3 5.4 %collective-permute-done.7.refs_7_ = bf16[256,512]{1,0:T(8,128)(2,1)S(1)} collective-permute-done((bf16[256,512]{1,0:T(8,128)(2,1)S(1)}, bf16[256,512]{1,0:T(8,128)(2,1)S(1)}, u32[]{:S(2)}, u32[]{:S(2)}) %collective-permute-start.7) | collective-permute-done | bytes 262176 | tf_op jit(solution)/shard_map/ppermute | solution.py:105
  38.7 7.1 %shard_map.84.partial = bf16[8,144,512]{2,1,0:T(8,128)(2,1)S(1)} custom-call(s32[4]{0:T(128)S(1)} %pad_add_fusion.ids_ref, bf16[256,512]{1,0:T(8,128)(2,1)S(1)} %constant_dynamic-update-slice_fusion.refs_0_, bf16[256,512]{1,0:T(8,128)(2,1)S(1)} %collective-permute-done.2.refs_1_, bf16[512,512]{1,0:T(8,128)(2,1)S(1)} %collective-permute-done.3.refs_2_, ...), custom_call_target="tpu_custom_call" | custom-call | flops 2147483648 | bytes 4194304 | tf_op jit(solution)/shard_map/pallas_call | solution.py:264
  45.8 0.1 slice_bitcast_fusion
  45.9 0.6 collective-permute-start.10
  46.5 2.0 %collective-permute-start.11 = (bf16[144,512]{1,0:T(8,128)(2,1)S(1)}, bf16[144,512]{1,0:T(8,128)(2,1)S(1)}, u32[]{:S(2)}, u32[]{:S(2)}) collective-permute-start(bf16[144,512]{1,0:T(8,128)(2,1)S(1)} %get-tuple-element.30), channel_id=1, source_target_pairs={{0,128},{1,97},{32,160},{33,65},{64,192},{65,33},{96,224},{97,1},{... | collective-permute-start | bytes 442376 | tf_op jit(solution)/shard_map/ppermute | solution.py:150
  48.5 2.4 %collective-permute-start.12 = (bf16[144,512]{1,0:T(8,128)(2,1)S(1)}, bf16[144,512]{1,0:T(8,128)(2,1)S(1)}, u32[]{:S(2)}, u32[]{:S(2)}) collective-permute-start(bf16[144,512]{1,0:T(8,128)(2,1)S(1)} %get-tuple-element.29), channel_id=1, source_target_pairs={{0,160},{1,225},{32,128},{33,193},{64,224},{65,161},{96,192},{97,1... | collective-permute-start | bytes 442376 | tf_op jit(solution)/shard_map/ppermute | solution.py:150
  50.9 1.1 %collective-permute-start.13 = (bf16[144,512]{1,0:T(8,128)(2,1)S(1)}, bf16[144,512]{1,0:T(8,128)(2,1)S(1)}, u32[]{:S(2)}, u32[]{:S(2)}) collective-permute-start(bf16[144,512]{1,0:T(8,128)(2,1)S(1)} %get-tuple-element.28), channel_id=1, source_target_pairs={{0,192},{1,65},{32,224},{33,97},{64,128},{65,1},{96,160},{97,33},{... | collective-permute-start | bytes 442376 | tf_op jit(solution)/shard_map/ppermute | solution.py:150
  51.9 1.1 %collective-permute-start.14 = (bf16[144,512]{1,0:T(8,128)(2,1)S(1)}, bf16[144,512]{1,0:T(8,128)(2,1)S(1)}, u32[]{:S(2)}, u32[]{:S(2)}) collective-permute-start(bf16[144,512]{1,0:T(8,128)(2,1)S(1)} %get-tuple-element.27), channel_id=1, source_target_pairs={{0,224},{1,193},{32,192},{33,225},{64,160},{65,129},{96,128},{97,1... | collective-permute-start | bytes 442376 | tf_op jit(solution)/shard_map/ppermute | solution.py:150
  53.0 0.0 collective-permute-done.10.refs_2_
  53.0 2.0 %collective-permute-start.8 = (bf16[144,512]{1,0:T(8,128)(2,1)S(1)}, bf16[144,512]{1,0:T(8,128)(2,1)S(1)}, u32[]{:S(2)}, u32[]{:S(2)}) collective-permute-start(bf16[144,512]{1,0:T(8,128)(2,1)S(1)} %get-tuple-element.33), channel_id=1, source_target_pairs={{0,32},{1,129},{32,0},{33,161},{64,96},{65,193},{96,64},{97,225},{... | collective-permute-start | bytes 442376 | tf_op jit(solution)/shard_map/ppermute | solution.py:150
  55.0 0.0 collective-permute-done.11.refs_3_
  55.0 1.4 %collective-permute-done.13.refs_5_ = bf16[144,512]{1,0:T(8,128)(2,1)S(1)} collective-permute-done((bf16[144,512]{1,0:T(8,128)(2,1)S(1)}, bf16[144,512]{1,0:T(8,128)(2,1)S(1)}, u32[]{:S(2)}, u32[]{:S(2)}) %collective-permute-start.13) | collective-permute-done | bytes 147488 | tf_op jit(solution)/shard_map/ppermute | solution.py:150
  56.4 3.8 %collective-permute-done.14.refs_6_ = bf16[144,512]{1,0:T(8,128)(2,1)S(1)} collective-permute-done((bf16[144,512]{1,0:T(8,128)(2,1)S(1)}, bf16[144,512]{1,0:T(8,128)(2,1)S(1)}, u32[]{:S(2)}, u32[]{:S(2)}) %collective-permute-start.14) | collective-permute-done | bytes 147488 | tf_op jit(solution)/shard_map/ppermute | solution.py:150
  60.3 2.4 %collective-permute-done.8.refs_0_ = bf16[144,512]{1,0:T(8,128)(2,1)S(1)} collective-permute-done((bf16[144,512]{1,0:T(8,128)(2,1)S(1)}, bf16[144,512]{1,0:T(8,128)(2,1)S(1)}, u32[]{:S(2)}, u32[]{:S(2)}) %collective-permute-start.8) | collective-permute-done | bytes 147488 | tf_op jit(solution)/shard_map/ppermute | solution.py:150
  62.7 0.0 collective-permute-done.9.refs_1_
  62.7 1.4 %shard_map.85 = (bf16[64,512]{1,0:T(8,128)(2,1)S(1)}, bf16[64,512]{1,0:T(8,128)(2,1)S(1)}) custom-call(s32[4]{0:T(128)S(1)} %pad_add_fusion.ids_ref, bf16[8,144,512]{2,1,0:T(8,128)(2,1)S(1)} %shard_map.84.partial, bf16[144,512]{1,0:T(8,128)(2,1)S(1)} %collective-permute-done.8.refs_0_, bf16[144,512]{1,0:T(8,128)(2,1)S(1)} %collective-permute-done.9.refs_1_, ...), custom_call_target="tpu_custom_call" | custom-call | tf_op jit(solution)/shard_map/pallas_call | solution.py:307
  64.1 0.1 collective-permute-start.15
  64.2 3.1 %collective-permute-done.15.taken = bf16[64,512]{1,0:T(8,128)(2,1)S(1)} collective-permute-done((bf16[64,512]{1,0:T(8,128)(2,1)S(1)}, bf16[64,512]{1,0:T(8,128)(2,1)S(1)}, u32[]{:S(2)}, u32[]{:S(2)}) %collective-permute-start.15) | collective-permute-done | bytes 65568 | tf_op jit(solution)/shard_map/ppermute | solution.py:369
  67.3 1.5 %shard_map.86 = (bf16[64,1792]{1,0:T(8,128)(2,1)S(1)}, bf16[64,1792]{1,0:T(8,128)(2,1)S(1)}, bf16[64,1792]{1,0:T(8,128)(2,1)S(1)}, bf16[64,1792]{1,0:T(8,128)(2,...) custom-call(s32[4]{0:T(128)S(1)} %pad_add_fusion.ids_ref, ...), custom_call_target="tpu_custom_call" | custom-call | flops 704643072 | bytes 8388608 | tf_op jit(solution)/shard_map/pallas_call | solution.py:349
  68.8 5.9 %collective-permute-start.16 = (bf16[64,1792]{1,0:T(8,128)(2,1)S(1)}, bf16[64,1792]{1,0:T(8,128)(2,1)S(1)}, u32[]{:S(2)}, u32[]{:S(2)}) collective-permute-start(bf16[64,1792]{1,0:T(8,128)(2,1)S(1)} %get-tuple-element.22), channel_id=1, source_target_pairs={{0,1},{1,0},{2,3},{3,2},{4,5},{5,4},{6,7},{7,6},{8,9},{9,8},{10,11... | collective-permute-start | bytes 688136 | tf_op jit(solution)/shard_map/ppermute | solution.py:373
  74.7 0.1 collective-permute-start.18
  74.8 0.4 collective-permute-start.20
  75.2 0.6 collective-permute-done.16
  75.9 3.5 %collective-permute-start.17 = (bf16[32,1792]{1,0:T(8,128)(2,1)S(1)}, bf16[32,1792]{1,0:T(8,128)(2,1)S(1)}, u32[]{:S(2)}, u32[]{:S(2)}) collective-permute-start(bf16[32,1792]{1,0:T(8,128)(2,1)S(1)} %fusion.3), channel_id=1, source_target_pairs={{0,130},{2,128},{128,2},{130,0},{1,131},{3,129},{129,3},{131,1},{4... | collective-permute-start | bytes 344072 | tf_op jit(solution)/shard_map/ppermute | solution.py:377
  79.5 0.3 collective-permute-start.19
  79.9 2.6 %collective-permute-start.21 = (bf16[32,1792]{1,0:T(8,128)(2,1)S(1)}, bf16[32,1792]{1,0:T(8,128)(2,1)S(1)}, u32[]{:S(2)}, u32[]{:S(2)}) collective-permute-start(bf16[32,1792]{1,0:T(8,128)(2,1)S(1)} %fusion.5), channel_id=1, source_target_pairs={{0,130},{2,128},{128,2},{130,0},{1,131},{3,129},{129,3},{131,1},{4... | collective-permute-start | bytes 344072 | tf_op jit(solution)/shard_map/ppermute | solution.py:377
  82.4 0.2 collective-permute-done.17
  82.7 2.2 %collective-permute-done.19 = bf16[32,1792]{1,0:T(8,128)(2,1)S(1)} collective-permute-done((bf16[32,1792]{1,0:T(8,128)(2,1)S(1)}, bf16[32,1792]{1,0:T(8,128)(2,1)S(1)}, u32[]{:S(2)}, u32[]{:S(2)}) %collective-permute-start.19) | collective-permute-done | bytes 114720 | tf_op jit(solution)/shard_map/ppermute | solution.py:377
  84.9 2.4 %collective-permute-done.21 = bf16[32,1792]{1,0:T(8,128)(2,1)S(1)} collective-permute-done((bf16[32,1792]{1,0:T(8,128)(2,1)S(1)}, bf16[32,1792]{1,0:T(8,128)(2,1)S(1)}, u32[]{:S(2)}, u32[]{:S(2)}) %collective-permute-start.21) | collective-permute-done | bytes 114720 | tf_op jit(solution)/shard_map/ppermute | solution.py:377
  87.3 0.8 pad_maximum_fusion.1
  (24 shorter events, 0.4 us)
Async XLA Ops:
  1.9 36.8 %copy-start = (bf16[128,512]{1,0:T(8,128)(2,1)S(1)}, bf16[128,512]{1,0:T(8,128)(2,1)}, u32[]{:S(2)}) copy-start(bf16[128,512]{1,0:T(8,128)(2,1)} %get-tuple-element.18.refs_3_) | copy-start | bytes 393220
  3.9 8.0 %collective-permute-start = (bf16[128,512]{1,0:T(8,128)(2,1)}, bf16[128,512]{1,0:T(8,128)(2,1)S(1)}, u32[]{:S(2)}, u32[]{:S(2)}) collective-permute-start(bf16[128,512]{1,0:T(8,128)(2,1)} %shard_map.83), channel_id=1, source_target_pairs={{0,0},{4,8},{8,16},{12,24},{16,4},{20,12},{24,20},{28,28},{128,152... | collective-permute-start | bytes 393224 | tf_op jit(solution)/shard_map/ppermute | solution.py:365
  5.4 10.9 %collective-permute-start.4 = (bf16[128,512]{1,0:T(8,128)(2,1)}, bf16[128,512]{1,0:T(8,128)(2,1)S(1)}, u32[]{:S(2)}, u32[]{:S(2)}) collective-permute-start(bf16[128,512]{1,0:T(8,128)(2,1)} %get-tuple-element.18.refs_3_), channel_id=1, source_target_pairs={{0,4},{1,29},{4,0},{5,9},{8,12},{9,5},{12,8},{13,17},{16,20},{17,1... | collective-permute-start | bytes 393224 | tf_op jit(solution)/shard_map/ppermute | solution.py:102
  11.9 9.3 %collective-permute-start.1 = (bf16[128,512]{1,0:T(8,128)(2,1)S(1)}, bf16[128,512]{1,0:T(8,128)(2,1)S(1)}, u32[]{:S(2)}, u32[]{:S(2)}) collective-permute-start(bf16[128,512]{1,0:T(8,128)(2,1)S(1)} %collective-permute-done), channel_id=1, source_target_pairs={{0,128},{128,0},{1,129},{129,1},{2,130},{130,2},{3,131},{131,3},{4... | collective-permute-start | bytes 393224 | tf_op jit(solution)/shard_map/ppermute | solution.py:131
  17.2 7.9 %collective-permute-start.5 = (bf16[256,512]{1,0:T(8,128)(2,1)S(1)}, bf16[256,512]{1,0:T(8,128)(2,1)S(1)}, u32[]{:S(2)}, u32[]{:S(2)}) collective-permute-start(bf16[256,512]{1,0:T(8,128)(2,1)S(1)} %pad_maximum_fusion.2), channel_id=1, source_target_pairs={{0,28},{1,5},{4,8},{5,1},{8,4},{9,13},{12,16},{13,9},{16,12},{17,2... | collective-permute-start | bytes 786440 | tf_op jit(solution)/shard_map/ppermute | solution.py:103
  21.1 8.3 %collective-permute-start.2 = (bf16[256,512]{1,0:T(8,128)(2,1)S(1)}, bf16[256,512]{1,0:T(8,128)(2,1)S(1)}, u32[]{:S(2)}, u32[]{:S(2)}) collective-permute-start(bf16[256,512]{1,0:T(8,128)(2,1)S(1)} %constant_dynamic-update-slice_fusion.refs_0_), channel_id=1, source_target_pairs={{0,32},{1,97},{32,0},{33,65},{64,96},{65,33},{96,64},{97,1},{2,34}... | collective-permute-start | bytes 786440 | tf_op jit(solution)/shard_map/ppermute | solution.py:132
  25.2 8.0 %collective-permute-start.6 = (bf16[256,512]{1,0:T(8,128)(2,1)S(1)}, bf16[256,512]{1,0:T(8,128)(2,1)S(1)}, u32[]{:S(2)}, u32[]{:S(2)}) collective-permute-start(bf16[256,512]{1,0:T(8,128)(2,1)S(1)} %collective-permute-done.5.refs_5_), channel_id=1, source_target_pairs={{0,4},{1,29},{4,0},{5,9},{8,12},{9,5},{12,8},{13,17},{16,20},{17,1... | collective-permute-start | bytes 786440 | tf_op jit(solution)/shard_map/ppermute | solution.py:104
  29.5 9.2 %collective-permute-start.3 = (bf16[512,512]{1,0:T(8,128)(2,1)S(1)}, bf16[512,512]{1,0:T(8,128)(2,1)S(1)}, u32[]{:S(2)}, u32[]{:S(2)}) collective-permute-start(bf16[512,512]{1,0:T(8,128)(2,1)S(1)} %pad_maximum_fusion), channel_id=1, source_target_pairs={{0,96},{1,33},{32,64},{33,1},{64,32},{65,97},{96,0},{97,65},{2,98}... | collective-permute-start | bytes 1572872 | tf_op jit(solution)/shard_map/ppermute | solution.py:133
  33.2 5.5 %collective-permute-start.7 = (bf16[256,512]{1,0:T(8,128)(2,1)S(1)}, bf16[256,512]{1,0:T(8,128)(2,1)S(1)}, u32[]{:S(2)}, u32[]{:S(2)}) collective-permute-start(bf16[256,512]{1,0:T(8,128)(2,1)S(1)} %collective-permute-done.6.refs_6_), channel_id=1, source_target_pairs={{0,28},{1,5},{4,8},{5,1},{8,4},{9,13},{12,16},{13,9},{16,12},{17,2... | collective-permute-start | bytes 786440 | tf_op jit(solution)/shard_map/ppermute | solution.py:105
  33.2 34.1 %slice-start = ((s8[5505024]{0:T(1024)(128)(4,1)}), s8[4194304]{0:T(1024)(128)(4,1)S(1)}, s32[]{:S(2)}) async-start(s8[5505024]{0:T(1024)(128)(4,1)} %bitcast.42), calls=%async_computation | async-start | bytes 8388608
  33.3 34.0 %slice-start.1 = ((s8[5505024]{0:T(1024)(128)(4,1)}), s8[1310720]{0:T(1024)(128)(4,1)S(1)}, s32[]{:S(2)}) async-start(s8[5505024]{0:T(1024)(128)(4,1)} %bitcast.42), calls=%async_computation.1 | async-start | bytes 2621440
  45.9 7.1 %collective-permute-start.10 = (bf16[144,512]{1,0:T(8,128)(2,1)S(1)}, bf16[144,512]{1,0:T(8,128)(2,1)S(1)}, u32[]{:S(2)}, u32[]{:S(2)}) collective-permute-start(bf16[144,512]{1,0:T(8,128)(2,1)S(1)} %get-tuple-element.31), channel_id=1, source_target_pairs={{0,96},{1,161},{32,64},{33,129},{64,32},{65,225},{96,0},{97,193},{... | collective-permute-start | bytes 442376 | tf_op jit(solution)/shard_map/ppermute | solution.py:150
  46.5 8.6 %collective-permute-start.11 = (bf16[144,512]{1,0:T(8,128)(2,1)S(1)}, bf16[144,512]{1,0:T(8,128)(2,1)S(1)}, u32[]{:S(2)}, u32[]{:S(2)}) collective-permute-start(bf16[144,512]{1,0:T(8,128)(2,1)S(1)} %get-tuple-element.30), channel_id=1, source_target_pairs={{0,128},{1,97},{32,160},{33,65},{64,192},{65,33},{96,224},{97,1},{... | collective-permute-start | bytes 442376 | tf_op jit(solution)/shard_map/ppermute | solution.py:150
  48.5 6.6 %collective-permute-start.12 = (bf16[144,512]{1,0:T(8,128)(2,1)S(1)}, bf16[144,512]{1,0:T(8,128)(2,1)S(1)}, u32[]{:S(2)}, u32[]{:S(2)}) collective-permute-start(bf16[144,512]{1,0:T(8,128)(2,1)S(1)} %get-tuple-element.29), channel_id=1, source_target_pairs={{0,160},{1,225},{32,128},{33,193},{64,224},{65,161},{96,192},{97,1... | collective-permute-start | bytes 442376 | tf_op jit(solution)/shard_map/ppermute | solution.py:150
  50.9 5.6 %collective-permute-start.13 = (bf16[144,512]{1,0:T(8,128)(2,1)S(1)}, bf16[144,512]{1,0:T(8,128)(2,1)S(1)}, u32[]{:S(2)}, u32[]{:S(2)}) collective-permute-start(bf16[144,512]{1,0:T(8,128)(2,1)S(1)} %get-tuple-element.28), channel_id=1, source_target_pairs={{0,192},{1,65},{32,224},{33,97},{64,128},{65,1},{96,160},{97,33},{... | collective-permute-start | bytes 442376 | tf_op jit(solution)/shard_map/ppermute | solution.py:150
  51.9 8.3 %collective-permute-start.14 = (bf16[144,512]{1,0:T(8,128)(2,1)S(1)}, bf16[144,512]{1,0:T(8,128)(2,1)S(1)}, u32[]{:S(2)}, u32[]{:S(2)}) collective-permute-start(bf16[144,512]{1,0:T(8,128)(2,1)S(1)} %get-tuple-element.27), channel_id=1, source_target_pairs={{0,224},{1,193},{32,192},{33,225},{64,160},{65,129},{96,128},{97,1... | collective-permute-start | bytes 442376 | tf_op jit(solution)/shard_map/ppermute | solution.py:150
  53.0 9.6 %collective-permute-start.8 = (bf16[144,512]{1,0:T(8,128)(2,1)S(1)}, bf16[144,512]{1,0:T(8,128)(2,1)S(1)}, u32[]{:S(2)}, u32[]{:S(2)}) collective-permute-start(bf16[144,512]{1,0:T(8,128)(2,1)S(1)} %get-tuple-element.33), channel_id=1, source_target_pairs={{0,32},{1,129},{32,0},{33,161},{64,96},{65,193},{96,64},{97,225},{... | collective-permute-start | bytes 442376 | tf_op jit(solution)/shard_map/ppermute | solution.py:150
  55.0 7.6 %collective-permute-start.9 = (bf16[144,512]{1,0:T(8,128)(2,1)S(1)}, bf16[144,512]{1,0:T(8,128)(2,1)S(1)}, u32[]{:S(2)}, u32[]{:S(2)}) collective-permute-start(bf16[144,512]{1,0:T(8,128)(2,1)S(1)} %get-tuple-element.32), channel_id=1, source_target_pairs={{0,64},{1,33},{32,96},{33,1},{64,0},{65,97},{96,32},{97,65},{128,1... | collective-permute-start | bytes 442376 | tf_op jit(solution)/shard_map/ppermute | solution.py:150
  64.1 3.2 %collective-permute-start.15 = (bf16[64,512]{1,0:T(8,128)(2,1)S(1)}, bf16[64,512]{1,0:T(8,128)(2,1)S(1)}, u32[]{:S(2)}, u32[]{:S(2)}) collective-permute-start(bf16[64,512]{1,0:T(8,128)(2,1)S(1)} %get-tuple-element.20), channel_id=1, source_target_pairs={{0,4},{4,0},{8,12},{12,8},{16,20},{20,16},{24,28},{28,24},{1,5},{5... | collective-permute-start | bytes 196616 | tf_op jit(solution)/shard_map/ppermute | solution.py:369
  68.8 7.0 %collective-permute-start.16 = (bf16[64,1792]{1,0:T(8,128)(2,1)S(1)}, bf16[64,1792]{1,0:T(8,128)(2,1)S(1)}, u32[]{:S(2)}, u32[]{:S(2)}) collective-permute-start(bf16[64,1792]{1,0:T(8,128)(2,1)S(1)} %get-tuple-element.22), channel_id=1, source_target_pairs={{0,1},{1,0},{2,3},{3,2},{4,5},{5,4},{6,7},{7,6},{8,9},{9,8},{10,11... | collective-permute-start | bytes 688136 | tf_op jit(solution)/shard_map/ppermute | solution.py:373
  74.7 4.7 %collective-permute-start.18 = (bf16[64,1792]{1,0:T(8,128)(2,1)S(1)}, bf16[64,1792]{1,0:T(8,128)(2,1)S(1)}, u32[]{:S(2)}, u32[]{:S(2)}) collective-permute-start(bf16[64,1792]{1,0:T(8,128)(2,1)S(1)} %get-tuple-element.24), channel_id=1, source_target_pairs={{0,1},{1,0},{2,3},{3,2},{4,5},{5,4},{6,7},{7,6},{8,9},{9,8},{10,11... | collective-permute-start | bytes 688136 | tf_op jit(solution)/shard_map/ppermute | solution.py:373
  74.8 5.0 %collective-permute-start.20 = (bf16[64,1792]{1,0:T(8,128)(2,1)S(1)}, bf16[64,1792]{1,0:T(8,128)(2,1)S(1)}, u32[]{:S(2)}, u32[]{:S(2)}) collective-permute-start(bf16[64,1792]{1,0:T(8,128)(2,1)S(1)} %get-tuple-element.26), channel_id=1, source_target_pairs={{0,1},{1,0},{2,3},{3,2},{4,5},{5,4},{6,7},{7,6},{8,9},{9,8},{10,11... | collective-permute-start | bytes 688136 | tf_op jit(solution)/shard_map/ppermute | solution.py:373
  75.9 6.7 %collective-permute-start.17 = (bf16[32,1792]{1,0:T(8,128)(2,1)S(1)}, bf16[32,1792]{1,0:T(8,128)(2,1)S(1)}, u32[]{:S(2)}, u32[]{:S(2)}) collective-permute-start(bf16[32,1792]{1,0:T(8,128)(2,1)S(1)} %fusion.3), channel_id=1, source_target_pairs={{0,130},{2,128},{128,2},{130,0},{1,131},{3,129},{129,3},{131,1},{4... | collective-permute-start | bytes 344072 | tf_op jit(solution)/shard_map/ppermute | solution.py:377
  79.5 5.3 %collective-permute-start.19 = (bf16[32,1792]{1,0:T(8,128)(2,1)S(1)}, bf16[32,1792]{1,0:T(8,128)(2,1)S(1)}, u32[]{:S(2)}, u32[]{:S(2)}) collective-permute-start(bf16[32,1792]{1,0:T(8,128)(2,1)S(1)} %fusion.4), channel_id=1, source_target_pairs={{0,130},{2,128},{128,2},{130,0},{1,131},{3,129},{129,3},{131,1},{4... | collective-permute-start | bytes 344072 | tf_op jit(solution)/shard_map/ppermute | solution.py:377
  79.9 7.4 %collective-permute-start.21 = (bf16[32,1792]{1,0:T(8,128)(2,1)S(1)}, bf16[32,1792]{1,0:T(8,128)(2,1)S(1)}, u32[]{:S(2)}, u32[]{:S(2)}) collective-permute-start(bf16[32,1792]{1,0:T(8,128)(2,1)S(1)} %fusion.5), channel_id=1, source_target_pairs={{0,130},{2,128},{128,2},{130,0},{1,131},{3,129},{129,3},{131,1},{4... | collective-permute-start | bytes 344072 | tf_op jit(solution)/shard_map/ppermute | solution.py:377

commit v7 on v6

--- a/solution.py
+++ b/solution.py
@@ -55,46 +55,32 @@
     return normed * cosines + pltpu.roll(normed, HD // 2, 1) * sines
 
 
-def prepare_keys_kernel(k_ref, v_ref, pos_ref, freq_ref, gain_ref, out, cos_out, sin_out):
+def prepare_kernel(q_ref, k_ref, v_ref, pos_ref, freq_ref, q_gain, k_gain, q_out, kv_out):
     lane = lax.broadcasted_iota(jnp.int32, (PIECE, HD), 1)
     spread = jnp.broadcast_to(pos_ref[...].astype(jnp.float32), (PIECE, HD))
     angles = jnp.transpose(spread) * freq_ref[...]
     cosines = jnp.cos(angles)
     sines = jnp.where(lane < HD // 2, -1.0, 1.0) * jnp.sin(angles)
-    cos_out[...] = cosines
-    sin_out[...] = sines
+    for head in range(4):
+        cols = slice(head * HD, (head + 1) * HD)
+        rows = rotate(q_ref[:, cols], q_gain[...], cosines, sines)
+        q_out[:, cols] = (rows * QUERY_FACTOR).astype(jnp.bfloat16)
     for head in range(2):
         cols = slice(head * HD, (head + 1) * HD)
-        rows = rotate(k_ref[:, cols], gain_ref[...], cosines, sines)
-        out[:, cols] = rows.astype(jnp.bfloat16)
-    out[:, 2 * HD :] = v_ref[...]
-
-
-def prepare_keys(keys, values, positions, gain):
+        rows = rotate(k_ref[:, cols], k_gain[...], cosines, sines)
+        kv_out[:, cols] = rows.astype(jnp.bfloat16)
+    kv_out[:, 2 * HD :] = v_ref[...]
+
+
+def prepare(queries, keys, values, positions, query_gain, key_gain):
     freq = jnp.asarray(np.concatenate([FREQUENCY, FREQUENCY])[None, :])
-    table = jax.ShapeDtypeStruct((PIECE, HD), jnp.float32)
+    piece = jax.ShapeDtypeStruct((PIECE, 4 * HD), jnp.bfloat16)
     return pl.pallas_call(
-        prepare_keys_kernel,
-        out_shape=(jax.ShapeDtypeStruct((PIECE, 4 * HD), jnp.bfloat16), table, table),
-        in_specs=[VMEM] * 5,
-        out_specs=(VMEM,) * 3,
-    )(keys, values, positions[None, :], freq, gain[None, :])
-
-
-def prepare_queries_kernel(q_ref, cos_ref, sin_ref, gain_ref, out):
-    for head in range(4):
-        cols = slice(head * HD, (head + 1) * HD)
-        rows = rotate(q_ref[:, cols], gain_ref[...], cos_ref[...], sin_ref[...])
-        out[:, cols] = (rows * QUERY_FACTOR).astype(jnp.bfloat16)
-
-
-def prepare_queries(queries, cosines, sines, gain):
-    return pl.pallas_call(
-        prepare_queries_kernel,
-        out_shape=jax.ShapeDtypeStruct((PIECE, 4 * HD), jnp.bfloat16),
-        in_specs=[VMEM] * 4,
-        out_specs=VMEM,
-    )(queries, cosines, sines, gain[None, :])
+        prepare_kernel,
+        out_shape=(piece, piece),
+        in_specs=[VMEM] * 7,
+        out_specs=(VMEM,) * 2,
+    )(queries, keys, values, positions[None, :], freq, query_gain[None, :], key_gain[None, :])
 
 
 def gather_z(own):
@@ -361,8 +347,8 @@
     x, y, z = lax.axis_index("x"), lax.axis_index("y"), lax.axis_index("z")
     w, c = lax.axis_index("w"), lax.axis_index("c")
     ids = jnp.stack([x * NY + y, z, c, w]).astype(jnp.int32)
-    key_rows, cosines, sines = prepare_keys(keys, values, positions, key_gain)
-    moved = lax.ppermute(prepare_queries(queries, cosines, sines, query_gain), ("x", "z"), move_pairs())
+    query_rows, key_rows = prepare(queries, keys, values, positions, query_gain, key_gain)
+    moved = lax.ppermute(query_rows, ("x", "z"), move_pairs())
     pieces = gather_z(key_rows)
     partial = attention(ids, gather_xy(moved), pieces)
     kept, given = combine(ids, partial, exchange(partial))

time: 88.2 us -> 87 us (0.986)
  Pallas kernels: 14 us -> 12.6 us
    pallas_call x2 -> x1, Pallas kernels: 3.89 us -> 2.45 us  [prepare(): pl.pallas_call(prepare_kernel, out_shape=(piece, piece), in_specs=[VMEM]...]
  transfers between devices with their start and end apart: 22 -> 22, of which waited for: 11 -> 11; matrix products, arithmetic and copies ran while one was open for 1% -> 2% of each run, Pallas kernels for 0% -> 0%
where the time goes in v7:
time: 87 us; the launch traced here: 86.8 us
  starting transfers between devices  46.8 us (54%)
  waiting for transfers between devices  25.1 us (29%)
  Pallas kernels  12.6 us (14%)
  other arithmetic  2 us (2%)
    ppermute x7, starting transfers between devices, exchange(): received.append(lax.ppermute(partial[k], ('x', 'y', 'c'), moves))  9.11 us
    ppermute x7, waiting for transfers between devices, exchange(): received.append(lax.ppermute(partial[k], ('x', 'y', 'c'), moves))  7.63 us
    pallas_call x1, Pallas kernels, attention(): pl.pallas_call(attention_kernel, out_shape=jax.ShapeDtypeStruct((GROUP, P...  7.13 us
    ppermute x1, starting transfers between devices, gather_z(): one = lax.ppermute(own, ('z', 'c'), here)  6.41 us
    ppermute x3, starting transfers between devices, on_device(): got = lax.ppermute(other, 'c', X_PAIRS)  6.4 us
    ppermute x3, starting transfers between devices, on_device(): landed = lax.ppermute(give, ('x', 'w'), pairs(4, lambda i: i ^ 3))  6.34 us
    ppermute x1, waiting for transfers between devices, gather_z(): four = lax.ppermute(three, ('z', 'c'), there)  5.43 us
    ppermute x3, waiting for transfers between devices, on_device(): landed = lax.ppermute(give, ('x', 'w'), pairs(4, lambda i: i ^ 3))  4.8 us
  transfers between devices with their start and end apart: 22, of which 11 were waited for; matrix products, arithmetic and copies ran while one was open for 2% of the time, Pallas kernels for 0%

profile of v7, /device:TPU:1, one launch (start us, length us, event | category | flops | bytes accessed | tf_op | source)
XLA Modules:
  0.0 86.8 jit_solution(7389308952968343772)
XLA Ops:
  0.0 2.4 %shard_map.82 = (bf16[128,512]{1,0:T(8,128)(2,1)}, bf16[128,512]{1,0:T(8,128)(2,1)}) custom-call(bf16[128,512]{1,0:T(8,128)(2,1)} %q_ref.1, bf16[128,256]{1,0:T(8,128)(2,1)} %k_ref.1, bf16[128,256]{1,0:T(8,128)(2,1)} %v_ref.1, s32[1,128]{1,0:T(1,128)} %bitcast.50, f32[1,128]{1,0:T(1,128)} %constant.44.clone.freq_ref, f32[1,128]{1,0:T(1,128)} %bitcast.51, ...), custom_call_target="tpu_custom_call" | custom-call | tf_op jit(solution)/shard_map/pallas_call | solution.py:78
  2.4 1.7 %collective-permute-start = (bf16[128,512]{1,0:T(8,128)(2,1)}, bf16[128,512]{1,0:T(8,128)(2,1)S(1)}, u32[]{:S(2)}, u32[]{:S(2)}) collective-permute-start(bf16[128,512]{1,0:T(8,128)(2,1)} %get-tuple-element.15), channel_id=1, source_target_pairs={{0,0},{4,8},{8,16},{12,24},{16,4},{20,12},{24,20},{28,28},{128,152... | collective-permute-start | bytes 393224 | tf_op jit(solution)/shard_map/ppermute | solution.py:351
  4.1 6.4 %collective-permute-start.4 = (bf16[128,512]{1,0:T(8,128)(2,1)}, bf16[128,512]{1,0:T(8,128)(2,1)S(1)}, u32[]{:S(2)}, u32[]{:S(2)}) collective-permute-start(bf16[128,512]{1,0:T(8,128)(2,1)} %get-tuple-element.16.refs_3_), channel_id=1, source_target_pairs={{0,4},{1,29},{4,0},{5,9},{8,12},{9,5},{12,8},{13,17},{16,20},{17,1... | collective-permute-start | bytes 393224 | tf_op jit(solution)/shard_map/ppermute | solution.py:88
  10.5 0.0 collective-permute-done
  10.5 4.5 %collective-permute-start.1 = (bf16[128,512]{1,0:T(8,128)(2,1)S(1)}, bf16[128,512]{1,0:T(8,128)(2,1)S(1)}, u32[]{:S(2)}, u32[]{:S(2)}) collective-permute-start(bf16[128,512]{1,0:T(8,128)(2,1)S(1)} %collective-permute-done), channel_id=1, source_target_pairs={{0,128},{128,0},{1,129},{129,1},{2,130},{130,2},{3,131},{131,3},{4... | collective-permute-start | bytes 393224 | tf_op jit(solution)/shard_map/ppermute | solution.py:117
  15.0 0.0 collective-permute-done.4.refs_4_
  15.0 0.9 %pad_maximum_fusion.2 = bf16[256,512]{1,0:T(8,128)(2,1)S(1)} fusion(bf16[128,512]{1,0:T(8,128)(2,1)S(1)} %collective-permute-done.4.refs_4_, bf16[128,512]{1,0:T(8,128)(2,1)} %get-tuple-element.16.refs_3_), kind=kLoop, calls=%fused_computation.5 | loop fusion | flops 524288 | bytes 524288 | tf_op jit(solution)/shard_map/concatenate | solution.py:89
  15.9 3.9 %collective-permute-start.5 = (bf16[256,512]{1,0:T(8,128)(2,1)S(1)}, bf16[256,512]{1,0:T(8,128)(2,1)S(1)}, u32[]{:S(2)}, u32[]{:S(2)}) collective-permute-start(bf16[256,512]{1,0:T(8,128)(2,1)S(1)} %pad_maximum_fusion.2), channel_id=1, source_target_pairs={{0,28},{1,5},{4,8},{5,1},{8,4},{9,13},{12,16},{13,9},{16,12},{17,2... | collective-permute-start | bytes 786440 | tf_op jit(solution)/shard_map/ppermute | solution.py:89
  19.8 0.0 collective-permute-done.1
  19.8 2.8 %collective-permute-start.2 = (bf16[256,512]{1,0:T(8,128)(2,1)S(1)}, bf16[256,512]{1,0:T(8,128)(2,1)S(1)}, u32[]{:S(2)}, u32[]{:S(2)}) collective-permute-start(bf16[256,512]{1,0:T(8,128)(2,1)S(1)} %constant_dynamic-update-slice_fusion.refs_0_), channel_id=1, source_target_pairs={{0,32},{1,97},{32,0},{33,65},{64,96},{65,33},{96,64},{97,1},{2,34}... | collective-permute-start | bytes 786440 | tf_op jit(solution)/shard_map/ppermute | solution.py:118
  22.7 1.2 %collective-permute-done.5.refs_5_ = bf16[256,512]{1,0:T(8,128)(2,1)S(1)} collective-permute-done((bf16[256,512]{1,0:T(8,128)(2,1)S(1)}, bf16[256,512]{1,0:T(8,128)(2,1)S(1)}, u32[]{:S(2)}, u32[]{:S(2)}) %collective-permute-start.5) | collective-permute-done | bytes 262176 | tf_op jit(solution)/shard_map/ppermute | solution.py:89
  23.8 4.3 %collective-permute-start.6 = (bf16[256,512]{1,0:T(8,128)(2,1)S(1)}, bf16[256,512]{1,0:T(8,128)(2,1)S(1)}, u32[]{:S(2)}, u32[]{:S(2)}) collective-permute-start(bf16[256,512]{1,0:T(8,128)(2,1)S(1)} %collective-permute-done.5.refs_5_), channel_id=1, source_target_pairs={{0,4},{1,29},{4,0},{5,9},{8,12},{9,5},{12,8},{13,17},{16,20},{17,1... | collective-permute-start | bytes 786440 | tf_op jit(solution)/shard_map/ppermute | solution.py:90
  28.2 1.4 %collective-permute-start.3 = (bf16[512,512]{1,0:T(8,128)(2,1)S(1)}, bf16[512,512]{1,0:T(8,128)(2,1)S(1)}, u32[]{:S(2)}, u32[]{:S(2)}) collective-permute-start(bf16[512,512]{1,0:T(8,128)(2,1)S(1)} %pad_maximum_fusion), channel_id=1, source_target_pairs={{0,96},{1,33},{32,64},{33,1},{64,32},{65,97},{96,0},{97,65},{2,98}... | collective-permute-start | bytes 1572872 | tf_op jit(solution)/shard_map/ppermute | solution.py:119
  29.5 2.3 %collective-permute-done.6.refs_6_ = bf16[256,512]{1,0:T(8,128)(2,1)S(1)} collective-permute-done((bf16[256,512]{1,0:T(8,128)(2,1)S(1)}, bf16[256,512]{1,0:T(8,128)(2,1)S(1)}, u32[]{:S(2)}, u32[]{:S(2)}) %collective-permute-start.6) | collective-permute-done | bytes 262176 | tf_op jit(solution)/shard_map/ppermute | solution.py:90
  31.9 0.1 pad_add_fusion.ids_ref
  32.0 5.4 %collective-permute-done.7.refs_7_ = bf16[256,512]{1,0:T(8,128)(2,1)S(1)} collective-permute-done((bf16[256,512]{1,0:T(8,128)(2,1)S(1)}, bf16[256,512]{1,0:T(8,128)(2,1)S(1)}, u32[]{:S(2)}, u32[]{:S(2)}) %collective-permute-start.7) | collective-permute-done | bytes 262176 | tf_op jit(solution)/shard_map/ppermute | solution.py:91
  37.4 0.0 collective-permute-done.3.refs_2_
  37.4 7.1 %shard_map.83.partial = bf16[8,144,512]{2,1,0:T(8,128)(2,1)S(1)} custom-call(s32[4]{0:T(128)S(1)} %pad_add_fusion.ids_ref, bf16[256,512]{1,0:T(8,128)(2,1)S(1)} %constant_dynamic-update-slice_fusion.refs_0_, bf16[256,512]{1,0:T(8,128)(2,1)S(1)} %collective-permute-done.2.refs_1_, bf16[512,512]{1,0:T(8,128)(2,1)S(1)} %collective-permute-done.3.refs_2_, ...), custom_call_target="tpu_custom_call" | custom-call | flops 2147483648 | bytes 4194304 | tf_op jit(solution)/shard_map/pallas_call | solution.py:250
  44.5 0.1 slice_bitcast_fusion
  44.6 0.6 collective-permute-start.10
  45.2 2.0 %collective-permute-start.11 = (bf16[144,512]{1,0:T(8,128)(2,1)S(1)}, bf16[144,512]{1,0:T(8,128)(2,1)S(1)}, u32[]{:S(2)}, u32[]{:S(2)}) collective-permute-start(bf16[144,512]{1,0:T(8,128)(2,1)S(1)} %get-tuple-element.28), channel_id=1, source_target_pairs={{0,128},{1,97},{32,160},{33,65},{64,192},{65,33},{96,224},{97,1},{... | collective-permute-start | bytes 442376 | tf_op jit(solution)/shard_map/ppermute | solution.py:136
  47.2 2.4 %collective-permute-start.12 = (bf16[144,512]{1,0:T(8,128)(2,1)S(1)}, bf16[144,512]{1,0:T(8,128)(2,1)S(1)}, u32[]{:S(2)}, u32[]{:S(2)}) collective-permute-start(bf16[144,512]{1,0:T(8,128)(2,1)S(1)} %get-tuple-element.27), channel_id=1, source_target_pairs={{0,160},{1,225},{32,128},{33,193},{64,224},{65,161},{96,192},{97,1... | collective-permute-start | bytes 442376 | tf_op jit(solution)/shard_map/ppermute | solution.py:136
  49.6 1.1 %collective-permute-start.13 = (bf16[144,512]{1,0:T(8,128)(2,1)S(1)}, bf16[144,512]{1,0:T(8,128)(2,1)S(1)}, u32[]{:S(2)}, u32[]{:S(2)}) collective-permute-start(bf16[144,512]{1,0:T(8,128)(2,1)S(1)} %get-tuple-element.26), channel_id=1, source_target_pairs={{0,192},{1,65},{32,224},{33,97},{64,128},{65,1},{96,160},{97,33},{... | collective-permute-start | bytes 442376 | tf_op jit(solution)/shard_map/ppermute | solution.py:136
  50.6 1.1 %collective-permute-start.14 = (bf16[144,512]{1,0:T(8,128)(2,1)S(1)}, bf16[144,512]{1,0:T(8,128)(2,1)S(1)}, u32[]{:S(2)}, u32[]{:S(2)}) collective-permute-start(bf16[144,512]{1,0:T(8,128)(2,1)S(1)} %get-tuple-element.25), channel_id=1, source_target_pairs={{0,224},{1,193},{32,192},{33,225},{64,160},{65,129},{96,128},{97,1... | collective-permute-start | bytes 442376 | tf_op jit(solution)/shard_map/ppermute | solution.py:136
  51.7 0.0 collective-permute-done.10.refs_2_
  51.7 2.0 %collective-permute-start.8 = (bf16[144,512]{1,0:T(8,128)(2,1)S(1)}, bf16[144,512]{1,0:T(8,128)(2,1)S(1)}, u32[]{:S(2)}, u32[]{:S(2)}) collective-permute-start(bf16[144,512]{1,0:T(8,128)(2,1)S(1)} %get-tuple-element.31), channel_id=1, source_target_pairs={{0,32},{1,129},{32,0},{33,161},{64,96},{65,193},{96,64},{97,225},{... | collective-permute-start | bytes 442376 | tf_op jit(solution)/shard_map/ppermute | solution.py:136
  53.7 0.0 collective-permute-start.9
  53.7 0.0 collective-permute-done.12.refs_4_
  53.7 1.4 %collective-permute-done.13.refs_5_ = bf16[144,512]{1,0:T(8,128)(2,1)S(1)} collective-permute-done((bf16[144,512]{1,0:T(8,128)(2,1)S(1)}, bf16[144,512]{1,0:T(8,128)(2,1)S(1)}, u32[]{:S(2)}, u32[]{:S(2)}) %collective-permute-start.13) | collective-permute-done | bytes 147488 | tf_op jit(solution)/shard_map/ppermute | solution.py:136
  55.1 3.8 %collective-permute-done.14.refs_6_ = bf16[144,512]{1,0:T(8,128)(2,1)S(1)} collective-permute-done((bf16[144,512]{1,0:T(8,128)(2,1)S(1)}, bf16[144,512]{1,0:T(8,128)(2,1)S(1)}, u32[]{:S(2)}, u32[]{:S(2)}) %collective-permute-start.14) | collective-permute-done | bytes 147488 | tf_op jit(solution)/shard_map/ppermute | solution.py:136
  59.0 2.4 %collective-permute-done.8.refs_0_ = bf16[144,512]{1,0:T(8,128)(2,1)S(1)} collective-permute-done((bf16[144,512]{1,0:T(8,128)(2,1)S(1)}, bf16[144,512]{1,0:T(8,128)(2,1)S(1)}, u32[]{:S(2)}, u32[]{:S(2)}) %collective-permute-start.8) | collective-permute-done | bytes 147488 | tf_op jit(solution)/shard_map/ppermute | solution.py:136
  61.4 0.0 collective-permute-done.9.refs_1_
  61.4 1.5 %shard_map.84 = (bf16[64,512]{1,0:T(8,128)(2,1)S(1)}, bf16[64,512]{1,0:T(8,128)(2,1)S(1)}) custom-call(s32[4]{0:T(128)S(1)} %pad_add_fusion.ids_ref, bf16[8,144,512]{2,1,0:T(8,128)(2,1)S(1)} %shard_map.83.partial, bf16[144,512]{1,0:T(8,128)(2,1)S(1)} %collective-permute-done.8.refs_0_, bf16[144,512]{1,0:T(8,128)(2,1)S(1)} %collective-permute-done.9.refs_1_, ...), custom_call_target="tpu_custom_call" | custom-call | tf_op jit(solution)/shard_map/pallas_call | solution.py:293
  62.8 0.1 collective-permute-start.15
  62.9 3.1 %collective-permute-done.15.taken = bf16[64,512]{1,0:T(8,128)(2,1)S(1)} collective-permute-done((bf16[64,512]{1,0:T(8,128)(2,1)S(1)}, bf16[64,512]{1,0:T(8,128)(2,1)S(1)}, u32[]{:S(2)}, u32[]{:S(2)}) %collective-permute-start.15) | collective-permute-done | bytes 65568 | tf_op jit(solution)/shard_map/ppermute | solution.py:355
  66.0 1.5 %shard_map.85 = (bf16[64,1792]{1,0:T(8,128)(2,1)S(1)}, bf16[64,1792]{1,0:T(8,128)(2,1)S(1)}, bf16[64,1792]{1,0:T(8,128)(2,1)S(1)}, bf16[64,1792]{1,0:T(8,128)(2,...) custom-call(s32[4]{0:T(128)S(1)} %pad_add_fusion.ids_ref, ...), custom_call_target="tpu_custom_call" | custom-call | flops 704643072 | bytes 8388608 | tf_op jit(solution)/shard_map/pallas_call | solution.py:335
  67.6 5.9 %collective-permute-start.16 = (bf16[64,1792]{1,0:T(8,128)(2,1)S(1)}, bf16[64,1792]{1,0:T(8,128)(2,1)S(1)}, u32[]{:S(2)}, u32[]{:S(2)}) collective-permute-start(bf16[64,1792]{1,0:T(8,128)(2,1)S(1)} %get-tuple-element.20), channel_id=1, source_target_pairs={{0,1},{1,0},{2,3},{3,2},{4,5},{5,4},{6,7},{7,6},{8,9},{9,8},{10,11... | collective-permute-start | bytes 688136 | tf_op jit(solution)/shard_map/ppermute | solution.py:359
  73.5 0.1 collective-permute-start.18
  73.6 0.4 collective-permute-start.20
  74.0 0.6 collective-permute-done.16
  74.7 3.5 %collective-permute-start.17 = (bf16[32,1792]{1,0:T(8,128)(2,1)S(1)}, bf16[32,1792]{1,0:T(8,128)(2,1)S(1)}, u32[]{:S(2)}, u32[]{:S(2)}) collective-permute-start(bf16[32,1792]{1,0:T(8,128)(2,1)S(1)} %fusion.3), channel_id=1, source_target_pairs={{0,130},{2,128},{128,2},{130,0},{1,131},{3,129},{129,3},{131,1},{4... | collective-permute-start | bytes 344072 | tf_op jit(solution)/shard_map/ppermute | solution.py:363
  78.2 0.0 collective-permute-done.18
  78.2 0.3 collective-permute-start.19
  78.6 2.6 %collective-permute-start.21 = (bf16[32,1792]{1,0:T(8,128)(2,1)S(1)}, bf16[32,1792]{1,0:T(8,128)(2,1)S(1)}, u32[]{:S(2)}, u32[]{:S(2)}) collective-permute-start(bf16[32,1792]{1,0:T(8,128)(2,1)S(1)} %fusion.5), channel_id=1, source_target_pairs={{0,130},{2,128},{128,2},{130,0},{1,131},{3,129},{129,3},{131,1},{4... | collective-permute-start | bytes 344072 | tf_op jit(solution)/shard_map/ppermute | solution.py:363
  81.2 0.2 collective-permute-done.17
  81.4 2.2 %collective-permute-done.19 = bf16[32,1792]{1,0:T(8,128)(2,1)S(1)} collective-permute-done((bf16[32,1792]{1,0:T(8,128)(2,1)S(1)}, bf16[32,1792]{1,0:T(8,128)(2,1)S(1)}, u32[]{:S(2)}, u32[]{:S(2)}) %collective-permute-start.19) | collective-permute-done | bytes 114720 | tf_op jit(solution)/shard_map/ppermute | solution.py:363
  83.6 2.4 %collective-permute-done.21 = bf16[32,1792]{1,0:T(8,128)(2,1)S(1)} collective-permute-done((bf16[32,1792]{1,0:T(8,128)(2,1)S(1)}, bf16[32,1792]{1,0:T(8,128)(2,1)S(1)}, u32[]{:S(2)}, u32[]{:S(2)}) %collective-permute-start.21) | collective-permute-done | bytes 114720 | tf_op jit(solution)/shard_map/ppermute | solution.py:363
  86.1 0.8 pad_maximum_fusion.1
  (23 shorter events, 0.4 us)
Async XLA Ops:
  2.4 34.9 %copy-start = (bf16[128,512]{1,0:T(8,128)(2,1)S(1)}, bf16[128,512]{1,0:T(8,128)(2,1)}, u32[]{:S(2)}) copy-start(bf16[128,512]{1,0:T(8,128)(2,1)} %get-tuple-element.16.refs_3_) | copy-start | bytes 393220
  2.4 8.1 %collective-permute-start = (bf16[128,512]{1,0:T(8,128)(2,1)}, bf16[128,512]{1,0:T(8,128)(2,1)S(1)}, u32[]{:S(2)}, u32[]{:S(2)}) collective-permute-start(bf16[128,512]{1,0:T(8,128)(2,1)} %get-tuple-element.15), channel_id=1, source_target_pairs={{0,0},{4,8},{8,16},{12,24},{16,4},{20,12},{24,20},{28,28},{128,152... | collective-permute-start | bytes 393224 | tf_op jit(solution)/shard_map/ppermute | solution.py:351
  4.1 10.9 %collective-permute-start.4 = (bf16[128,512]{1,0:T(8,128)(2,1)}, bf16[128,512]{1,0:T(8,128)(2,1)S(1)}, u32[]{:S(2)}, u32[]{:S(2)}) collective-permute-start(bf16[128,512]{1,0:T(8,128)(2,1)} %get-tuple-element.16.refs_3_), channel_id=1, source_target_pairs={{0,4},{1,29},{4,0},{5,9},{8,12},{9,5},{12,8},{13,17},{16,20},{17,1... | collective-permute-start | bytes 393224 | tf_op jit(solution)/shard_map/ppermute | solution.py:88
  10.5 9.3 %collective-permute-start.1 = (bf16[128,512]{1,0:T(8,128)(2,1)S(1)}, bf16[128,512]{1,0:T(8,128)(2,1)S(1)}, u32[]{:S(2)}, u32[]{:S(2)}) collective-permute-start(bf16[128,512]{1,0:T(8,128)(2,1)S(1)} %collective-permute-done), channel_id=1, source_target_pairs={{0,128},{128,0},{1,129},{129,1},{2,130},{130,2},{3,131},{131,3},{4... | collective-permute-start | bytes 393224 | tf_op jit(solution)/shard_map/ppermute | solution.py:117
  15.9 7.9 %collective-permute-start.5 = (bf16[256,512]{1,0:T(8,128)(2,1)S(1)}, bf16[256,512]{1,0:T(8,128)(2,1)S(1)}, u32[]{:S(2)}, u32[]{:S(2)}) collective-permute-start(bf16[256,512]{1,0:T(8,128)(2,1)S(1)} %pad_maximum_fusion.2), channel_id=1, source_target_pairs={{0,28},{1,5},{4,8},{5,1},{8,4},{9,13},{12,16},{13,9},{16,12},{17,2... | collective-permute-start | bytes 786440 | tf_op jit(solution)/shard_map/ppermute | solution.py:89
  19.8 8.3 %collective-permute-start.2 = (bf16[256,512]{1,0:T(8,128)(2,1)S(1)}, bf16[256,512]{1,0:T(8,128)(2,1)S(1)}, u32[]{:S(2)}, u32[]{:S(2)}) collective-permute-start(bf16[256,512]{1,0:T(8,128)(2,1)S(1)} %constant_dynamic-update-slice_fusion.refs_0_), channel_id=1, source_target_pairs={{0,32},{1,97},{32,0},{33,65},{64,96},{65,33},{96,64},{97,1},{2,34}... | collective-permute-start | bytes 786440 | tf_op jit(solution)/shard_map/ppermute | solution.py:118
  23.8 8.0 %collective-permute-start.6 = (bf16[256,512]{1,0:T(8,128)(2,1)S(1)}, bf16[256,512]{1,0:T(8,128)(2,1)S(1)}, u32[]{:S(2)}, u32[]{:S(2)}) collective-permute-start(bf16[256,512]{1,0:T(8,128)(2,1)S(1)} %collective-permute-done.5.refs_5_), channel_id=1, source_target_pairs={{0,4},{1,29},{4,0},{5,9},{8,12},{9,5},{12,8},{13,17},{16,20},{17,1... | collective-permute-start | bytes 786440 | tf_op jit(solution)/shard_map/ppermute | solution.py:90
  28.2 9.2 %collective-permute-start.3 = (bf16[512,512]{1,0:T(8,128)(2,1)S(1)}, bf16[512,512]{1,0:T(8,128)(2,1)S(1)}, u32[]{:S(2)}, u32[]{:S(2)}) collective-permute-start(bf16[512,512]{1,0:T(8,128)(2,1)S(1)} %pad_maximum_fusion), channel_id=1, source_target_pairs={{0,96},{1,33},{32,64},{33,1},{64,32},{65,97},{96,0},{97,65},{2,98}... | collective-permute-start | bytes 1572872 | tf_op jit(solution)/shard_map/ppermute | solution.py:119
  31.9 5.5 %collective-permute-start.7 = (bf16[256,512]{1,0:T(8,128)(2,1)S(1)}, bf16[256,512]{1,0:T(8,128)(2,1)S(1)}, u32[]{:S(2)}, u32[]{:S(2)}) collective-permute-start(bf16[256,512]{1,0:T(8,128)(2,1)S(1)} %collective-permute-done.6.refs_6_), channel_id=1, source_target_pairs={{0,28},{1,5},{4,8},{5,1},{8,4},{9,13},{12,16},{13,9},{16,12},{17,2... | collective-permute-start | bytes 786440 | tf_op jit(solution)/shard_map/ppermute | solution.py:91
  31.9 34.2 %slice-start = ((s8[5505024]{0:T(1024)(128)(4,1)}), s8[4194304]{0:T(1024)(128)(4,1)S(1)}, s32[]{:S(2)}) async-start(s8[5505024]{0:T(1024)(128)(4,1)} %bitcast.42), calls=%async_computation | async-start | bytes 8388608
  32.0 34.1 %slice-start.1 = ((s8[5505024]{0:T(1024)(128)(4,1)}), s8[1310720]{0:T(1024)(128)(4,1)S(1)}, s32[]{:S(2)}) async-start(s8[5505024]{0:T(1024)(128)(4,1)} %bitcast.42), calls=%async_computation.1 | async-start | bytes 2621440
  44.6 7.1 %collective-permute-start.10 = (bf16[144,512]{1,0:T(8,128)(2,1)S(1)}, bf16[144,512]{1,0:T(8,128)(2,1)S(1)}, u32[]{:S(2)}, u32[]{:S(2)}) collective-permute-start(bf16[144,512]{1,0:T(8,128)(2,1)S(1)} %get-tuple-element.29), channel_id=1, source_target_pairs={{0,96},{1,161},{32,64},{33,129},{64,32},{65,225},{96,0},{97,193},{... | collective-permute-start | bytes 442376 | tf_op jit(solution)/shard_map/ppermute | solution.py:136
  45.2 8.6 %collective-permute-start.11 = (bf16[144,512]{1,0:T(8,128)(2,1)S(1)}, bf16[144,512]{1,0:T(8,128)(2,1)S(1)}, u32[]{:S(2)}, u32[]{:S(2)}) collective-permute-start(bf16[144,512]{1,0:T(8,128)(2,1)S(1)} %get-tuple-element.28), channel_id=1, source_target_pairs={{0,128},{1,97},{32,160},{33,65},{64,192},{65,33},{96,224},{97,1},{... | collective-permute-start | bytes 442376 | tf_op jit(solution)/shard_map/ppermute | solution.py:136
  47.2 6.6 %collective-permute-start.12 = (bf16[144,512]{1,0:T(8,128)(2,1)S(1)}, bf16[144,512]{1,0:T(8,128)(2,1)S(1)}, u32[]{:S(2)}, u32[]{:S(2)}) collective-permute-start(bf16[144,512]{1,0:T(8,128)(2,1)S(1)} %get-tuple-element.27), channel_id=1, source_target_pairs={{0,160},{1,225},{32,128},{33,193},{64,224},{65,161},{96,192},{97,1... | collective-permute-start | bytes 442376 | tf_op jit(solution)/shard_map/ppermute | solution.py:136
  49.6 5.6 %collective-permute-start.13 = (bf16[144,512]{1,0:T(8,128)(2,1)S(1)}, bf16[144,512]{1,0:T(8,128)(2,1)S(1)}, u32[]{:S(2)}, u32[]{:S(2)}) collective-permute-start(bf16[144,512]{1,0:T(8,128)(2,1)S(1)} %get-tuple-element.26), channel_id=1, source_target_pairs={{0,192},{1,65},{32,224},{33,97},{64,128},{65,1},{96,160},{97,33},{... | collective-permute-start | bytes 442376 | tf_op jit(solution)/shard_map/ppermute | solution.py:136
  50.6 8.3 %collective-permute-start.14 = (bf16[144,512]{1,0:T(8,128)(2,1)S(1)}, bf16[144,512]{1,0:T(8,128)(2,1)S(1)}, u32[]{:S(2)}, u32[]{:S(2)}) collective-permute-start(bf16[144,512]{1,0:T(8,128)(2,1)S(1)} %get-tuple-element.25), channel_id=1, source_target_pairs={{0,224},{1,193},{32,192},{33,225},{64,160},{65,129},{96,128},{97,1... | collective-permute-start | bytes 442376 | tf_op jit(solution)/shard_map/ppermute | solution.py:136
  51.7 9.6 %collective-permute-start.8 = (bf16[144,512]{1,0:T(8,128)(2,1)S(1)}, bf16[144,512]{1,0:T(8,128)(2,1)S(1)}, u32[]{:S(2)}, u32[]{:S(2)}) collective-permute-start(bf16[144,512]{1,0:T(8,128)(2,1)S(1)} %get-tuple-element.31), channel_id=1, source_target_pairs={{0,32},{1,129},{32,0},{33,161},{64,96},{65,193},{96,64},{97,225},{... | collective-permute-start | bytes 442376 | tf_op jit(solution)/shard_map/ppermute | solution.py:136
  53.7 7.6 %collective-permute-start.9 = (bf16[144,512]{1,0:T(8,128)(2,1)S(1)}, bf16[144,512]{1,0:T(8,128)(2,1)S(1)}, u32[]{:S(2)}, u32[]{:S(2)}) collective-permute-start(bf16[144,512]{1,0:T(8,128)(2,1)S(1)} %get-tuple-element.30), channel_id=1, source_target_pairs={{0,64},{1,33},{32,96},{33,1},{64,0},{65,97},{96,32},{97,65},{128,1... | collective-permute-start | bytes 442376 | tf_op jit(solution)/shard_map/ppermute | solution.py:136
  62.8 3.2 %collective-permute-start.15 = (bf16[64,512]{1,0:T(8,128)(2,1)S(1)}, bf16[64,512]{1,0:T(8,128)(2,1)S(1)}, u32[]{:S(2)}, u32[]{:S(2)}) collective-permute-start(bf16[64,512]{1,0:T(8,128)(2,1)S(1)} %get-tuple-element.18), channel_id=1, source_target_pairs={{0,4},{4,0},{8,12},{12,8},{16,20},{20,16},{24,28},{28,24},{1,5},{5... | collective-permute-start | bytes 196616 | tf_op jit(solution)/shard_map/ppermute | solution.py:355
  67.6 7.0 %collective-permute-start.16 = (bf16[64,1792]{1,0:T(8,128)(2,1)S(1)}, bf16[64,1792]{1,0:T(8,128)(2,1)S(1)}, u32[]{:S(2)}, u32[]{:S(2)}) collective-permute-start(bf16[64,1792]{1,0:T(8,128)(2,1)S(1)} %get-tuple-element.20), channel_id=1, source_target_pairs={{0,1},{1,0},{2,3},{3,2},{4,5},{5,4},{6,7},{7,6},{8,9},{9,8},{10,11... | collective-permute-start | bytes 688136 | tf_op jit(solution)/shard_map/ppermute | solution.py:359
  73.5 4.7 %collective-permute-start.18 = (bf16[64,1792]{1,0:T(8,128)(2,1)S(1)}, bf16[64,1792]{1,0:T(8,128)(2,1)S(1)}, u32[]{:S(2)}, u32[]{:S(2)}) collective-permute-start(bf16[64,1792]{1,0:T(8,128)(2,1)S(1)} %get-tuple-element.22), channel_id=1, source_target_pairs={{0,1},{1,0},{2,3},{3,2},{4,5},{5,4},{6,7},{7,6},{8,9},{9,8},{10,11... | collective-permute-start | bytes 688136 | tf_op jit(solution)/shard_map/ppermute | solution.py:359
  73.6 5.0 %collective-permute-start.20 = (bf16[64,1792]{1,0:T(8,128)(2,1)S(1)}, bf16[64,1792]{1,0:T(8,128)(2,1)S(1)}, u32[]{:S(2)}, u32[]{:S(2)}) collective-permute-start(bf16[64,1792]{1,0:T(8,128)(2,1)S(1)} %get-tuple-element.24), channel_id=1, source_target_pairs={{0,1},{1,0},{2,3},{3,2},{4,5},{5,4},{6,7},{7,6},{8,9},{9,8},{10,11... | collective-permute-start | bytes 688136 | tf_op jit(solution)/shard_map/ppermute | solution.py:359
  74.7 6.7 %collective-permute-start.17 = (bf16[32,1792]{1,0:T(8,128)(2,1)S(1)}, bf16[32,1792]{1,0:T(8,128)(2,1)S(1)}, u32[]{:S(2)}, u32[]{:S(2)}) collective-permute-start(bf16[32,1792]{1,0:T(8,128)(2,1)S(1)} %fusion.3), channel_id=1, source_target_pairs={{0,130},{2,128},{128,2},{130,0},{1,131},{3,129},{129,3},{131,1},{4... | collective-permute-start | bytes 344072 | tf_op jit(solution)/shard_map/ppermute | solution.py:363
  78.2 5.3 %collective-permute-start.19 = (bf16[32,1792]{1,0:T(8,128)(2,1)S(1)}, bf16[32,1792]{1,0:T(8,128)(2,1)S(1)}, u32[]{:S(2)}, u32[]{:S(2)}) collective-permute-start(bf16[32,1792]{1,0:T(8,128)(2,1)S(1)} %fusion.4), channel_id=1, source_target_pairs={{0,130},{2,128},{128,2},{130,0},{1,131},{3,129},{129,3},{131,1},{4... | collective-permute-start | bytes 344072 | tf_op jit(solution)/shard_map/ppermute | solution.py:363
  78.6 7.4 %collective-permute-start.21 = (bf16[32,1792]{1,0:T(8,128)(2,1)S(1)}, bf16[32,1792]{1,0:T(8,128)(2,1)S(1)}, u32[]{:S(2)}, u32[]{:S(2)}) collective-permute-start(bf16[32,1792]{1,0:T(8,128)(2,1)S(1)} %fusion.5), channel_id=1, source_target_pairs={{0,130},{2,128},{128,2},{130,0},{1,131},{3,129},{129,3},{131,1},{4... | collective-permute-start | bytes 344072 | tf_op jit(solution)/shard_map/ppermute | solution.py:363

commit v8 on v7

--- a/solution.py
+++ b/solution.py
@@ -120,21 +120,10 @@
     return both, near, far
 
 
-def turned(step):
-    return (4 * (step & 1)) ^ ((step >> 1) & 1) ^ (3 * ((step >> 2) & 1))
-
-
-def position(core, step):
-    back = (2 * (step & 1)) ^ (6 * ((step >> 1) & 1)) ^ ((step >> 2) & 1)
-    return jnp.where(core == 0, step, back)
-
-
 def exchange(partial):
-    received = []
-    for k in range(1, GROUP):
-        moves = [(g * 2 + c, (g ^ (turned(k) if c else k)) * 2 + c) for g in range(GROUP) for c in range(2)]
-        received.append(lax.ppermute(partial[k], ("x", "y", "c"), moves))
-    return received
+    return [
+        lax.ppermute(partial[step], ("x", "y"), pairs(GROUP, lambda i: i ^ step)) for step in range(1, GROUP)
+    ]
 
 
 def attention_kernel(ids_ref, *refs):
@@ -169,7 +158,7 @@
         upper = source >> 2
         end_x = ((source >> 1) & 1) ^ w
         end_y = (((source & 1) ^ upper) << 1) | ((z & 1) ^ upper)
-        return position(core, group ^ ((end_x << 2) | end_y))
+        return group ^ ((end_x << 2) | end_y)
 
     def score(half, pair, masked):
         query = q_s[half, pl.ds(pair * 2, 2)].reshape(width, HD)

time: 87 us -> 86.2 us (level)
  starting transfers between devices: 46.8 us -> 44.1 us
  waiting for transfers between devices: 25.1 us -> 27.1 us
    ppermute x3, starting transfers between devices: 6.4 us -> 4.45 us  [on_device(): got = lax.ppermute(other, 'c', X_PAIRS)]
    ppermute x3, starting transfers between devices: 6.34 us -> 4.84 us  [on_device(): landed = lax.ppermute(give, ('x', 'w'), pairs(4, lambda i: i ^ 3))]
    ppermute x7, waiting for transfers between devices: 7.63 us -> 8.8 us  [exchange(): lax.ppermute(partial[step], ('x', 'y'), pairs(GROUP, lambda i: i ^ step))]
where the time goes in v8:
time: 86.2 us; the launch traced here: 86.1 us
  starting transfers between devices  44.1 us (51%)
  waiting for transfers between devices  27.1 us (31%)
  Pallas kernels  12.6 us (15%)
  other arithmetic  2 us (2%)
    ppermute x7, starting transfers between devices, exchange(): lax.ppermute(partial[step], ('x', 'y'), pairs(GROUP, lambda i: i ^ step))  9.88 us
    ppermute x7, waiting for transfers between devices, exchange(): lax.ppermute(partial[step], ('x', 'y'), pairs(GROUP, lambda i: i ^ step))  8.8 us
    pallas_call x1, Pallas kernels, attention(): pl.pallas_call(attention_kernel, out_shape=jax.ShapeDtypeStruct((GROUP, P...  7.13 us
    ppermute x1, starting transfers between devices, gather_z(): one = lax.ppermute(own, ('z', 'c'), here)  6.41 us
    ppermute x3, waiting for transfers between devices, on_device(): landed = lax.ppermute(give, ('x', 'w'), pairs(4, lambda i: i ^ 3))  5.58 us
    ppermute x1, waiting for transfers between devices, gather_z(): four = lax.ppermute(three, ('z', 'c'), there)  5.43 us
    ppermute x3, starting transfers between devices, on_device(): landed = lax.ppermute(give, ('x', 'w'), pairs(4, lambda i: i ^ 3))  4.84 us
    ppermute x1, starting transfers between devices, gather_xy(): both = jnp.concatenate([own, lax.ppermute(own, 'x', X_PAIRS)], axis=0)  4.46 us
  transfers between devices with their start and end apart: 22, of which 11 were waited for; matrix products, arithmetic and copies ran while one was open for 2% of the time, Pallas kernels for 0%

profile of v8, /device:TPU:1, one launch (start us, length us, event | category | flops | bytes accessed | tf_op | source)
XLA Modules:
  0.0 86.1 jit_solution(15032432153114848580)
XLA Ops:
  0.0 2.4 %shard_map.82 = (bf16[128,512]{1,0:T(8,128)(2,1)}, bf16[128,512]{1,0:T(8,128)(2,1)}) custom-call(bf16[128,512]{1,0:T(8,128)(2,1)} %q_ref.1, bf16[128,256]{1,0:T(8,128)(2,1)} %k_ref.1, bf16[128,256]{1,0:T(8,128)(2,1)} %v_ref.1, s32[1,128]{1,0:T(1,128)} %bitcast.50, f32[1,128]{1,0:T(1,128)} %constant.44.clone.freq_ref, f32[1,128]{1,0:T(1,128)} %bitcast.51, ...), custom_call_target="tpu_custom_call" | custom-call | tf_op jit(solution)/shard_map/pallas_call | solution.py:78
  2.4 1.7 %collective-permute-start = (bf16[128,512]{1,0:T(8,128)(2,1)}, bf16[128,512]{1,0:T(8,128)(2,1)S(1)}, u32[]{:S(2)}, u32[]{:S(2)}) collective-permute-start(bf16[128,512]{1,0:T(8,128)(2,1)} %get-tuple-element.15), channel_id=1, source_target_pairs={{0,0},{4,8},{8,16},{12,24},{16,4},{20,12},{24,20},{28,28},{128,152... | collective-permute-start | bytes 393224 | tf_op jit(solution)/shard_map/ppermute | solution.py:340
  4.1 6.4 %collective-permute-start.4 = (bf16[128,512]{1,0:T(8,128)(2,1)}, bf16[128,512]{1,0:T(8,128)(2,1)S(1)}, u32[]{:S(2)}, u32[]{:S(2)}) collective-permute-start(bf16[128,512]{1,0:T(8,128)(2,1)} %get-tuple-element.16.refs_3_), channel_id=1, source_target_pairs={{0,4},{1,29},{4,0},{5,9},{8,12},{9,5},{12,8},{13,17},{16,20},{17,1... | collective-permute-start | bytes 393224 | tf_op jit(solution)/shard_map/ppermute | solution.py:88
  10.5 0.0 collective-permute-done
  10.5 4.5 %collective-permute-start.1 = (bf16[128,512]{1,0:T(8,128)(2,1)S(1)}, bf16[128,512]{1,0:T(8,128)(2,1)S(1)}, u32[]{:S(2)}, u32[]{:S(2)}) collective-permute-start(bf16[128,512]{1,0:T(8,128)(2,1)S(1)} %collective-permute-done), channel_id=1, source_target_pairs={{0,128},{128,0},{1,129},{129,1},{2,130},{130,2},{3,131},{131,3},{4... | collective-permute-start | bytes 393224 | tf_op jit(solution)/shard_map/ppermute | solution.py:117
  15.0 0.0 collective-permute-done.4.refs_4_
  15.0 0.9 %pad_maximum_fusion.2 = bf16[256,512]{1,0:T(8,128)(2,1)S(1)} fusion(bf16[128,512]{1,0:T(8,128)(2,1)S(1)} %collective-permute-done.4.refs_4_, bf16[128,512]{1,0:T(8,128)(2,1)} %get-tuple-element.16.refs_3_), kind=kLoop, calls=%fused_computation.5 | loop fusion | flops 524288 | bytes 524288 | tf_op jit(solution)/shard_map/concatenate | solution.py:89
  15.9 3.9 %collective-permute-start.5 = (bf16[256,512]{1,0:T(8,128)(2,1)S(1)}, bf16[256,512]{1,0:T(8,128)(2,1)S(1)}, u32[]{:S(2)}, u32[]{:S(2)}) collective-permute-start(bf16[256,512]{1,0:T(8,128)(2,1)S(1)} %pad_maximum_fusion.2), channel_id=1, source_target_pairs={{0,28},{1,5},{4,8},{5,1},{8,4},{9,13},{12,16},{13,9},{16,12},{17,2... | collective-permute-start | bytes 786440 | tf_op jit(solution)/shard_map/ppermute | solution.py:89
  19.8 0.0 collective-permute-done.1
  19.8 2.8 %collective-permute-start.2 = (bf16[256,512]{1,0:T(8,128)(2,1)S(1)}, bf16[256,512]{1,0:T(8,128)(2,1)S(1)}, u32[]{:S(2)}, u32[]{:S(2)}) collective-permute-start(bf16[256,512]{1,0:T(8,128)(2,1)S(1)} %constant_dynamic-update-slice_fusion.refs_0_), channel_id=1, source_target_pairs={{0,32},{1,97},{32,0},{33,65},{64,96},{65,33},{96,64},{97,1},{2,34}... | collective-permute-start | bytes 786440 | tf_op jit(solution)/shard_map/ppermute | solution.py:118
  22.7 1.2 %collective-permute-done.5.refs_5_ = bf16[256,512]{1,0:T(8,128)(2,1)S(1)} collective-permute-done((bf16[256,512]{1,0:T(8,128)(2,1)S(1)}, bf16[256,512]{1,0:T(8,128)(2,1)S(1)}, u32[]{:S(2)}, u32[]{:S(2)}) %collective-permute-start.5) | collective-permute-done | bytes 262176 | tf_op jit(solution)/shard_map/ppermute | solution.py:89
  23.8 4.3 %collective-permute-start.6 = (bf16[256,512]{1,0:T(8,128)(2,1)S(1)}, bf16[256,512]{1,0:T(8,128)(2,1)S(1)}, u32[]{:S(2)}, u32[]{:S(2)}) collective-permute-start(bf16[256,512]{1,0:T(8,128)(2,1)S(1)} %collective-permute-done.5.refs_5_), channel_id=1, source_target_pairs={{0,4},{1,29},{4,0},{5,9},{8,12},{9,5},{12,8},{13,17},{16,20},{17,1... | collective-permute-start | bytes 786440 | tf_op jit(solution)/shard_map/ppermute | solution.py:90
  28.1 0.0 collective-permute-done.2.refs_1_
  28.2 1.4 %collective-permute-start.3 = (bf16[512,512]{1,0:T(8,128)(2,1)S(1)}, bf16[512,512]{1,0:T(8,128)(2,1)S(1)}, u32[]{:S(2)}, u32[]{:S(2)}) collective-permute-start(bf16[512,512]{1,0:T(8,128)(2,1)S(1)} %pad_maximum_fusion), channel_id=1, source_target_pairs={{0,96},{1,33},{32,64},{33,1},{64,32},{65,97},{96,0},{97,65},{2,98}... | collective-permute-start | bytes 1572872 | tf_op jit(solution)/shard_map/ppermute | solution.py:119
  29.5 2.3 %collective-permute-done.6.refs_6_ = bf16[256,512]{1,0:T(8,128)(2,1)S(1)} collective-permute-done((bf16[256,512]{1,0:T(8,128)(2,1)S(1)}, bf16[256,512]{1,0:T(8,128)(2,1)S(1)}, u32[]{:S(2)}, u32[]{:S(2)}) %collective-permute-start.6) | collective-permute-done | bytes 262176 | tf_op jit(solution)/shard_map/ppermute | solution.py:90
  31.9 0.0 collective-permute-start.7
  31.9 0.1 pad_add_fusion.ids_ref
  32.0 5.4 %collective-permute-done.7.refs_7_ = bf16[256,512]{1,0:T(8,128)(2,1)S(1)} collective-permute-done((bf16[256,512]{1,0:T(8,128)(2,1)S(1)}, bf16[256,512]{1,0:T(8,128)(2,1)S(1)}, u32[]{:S(2)}, u32[]{:S(2)}) %collective-permute-start.7) | collective-permute-done | bytes 262176 | tf_op jit(solution)/shard_map/ppermute | solution.py:91
  37.4 0.0 collective-permute-done.3.refs_2_
  37.4 7.1 %shard_map.83.partial = bf16[8,144,512]{2,1,0:T(8,128)(2,1)S(1)} custom-call(s32[4]{0:T(128)S(1)} %pad_add_fusion.ids_ref, bf16[256,512]{1,0:T(8,128)(2,1)S(1)} %constant_dynamic-update-slice_fusion.refs_0_, bf16[256,512]{1,0:T(8,128)(2,1)S(1)} %collective-permute-done.2.refs_1_, bf16[512,512]{1,0:T(8,128)(2,1)S(1)} %collective-permute-done.3.refs_2_, ...), custom_call_target="tpu_custom_call" | custom-call | flops 2147483648 | bytes 4194304 | tf_op jit(solution)/shard_map/pallas_call | solution.py:239
  44.5 0.1 slice_bitcast_fusion
  44.6 2.5 %collective-permute-start.10 = (bf16[144,512]{1,0:T(8,128)(2,1)S(1)}, bf16[144,512]{1,0:T(8,128)(2,1)S(1)}, u32[]{:S(2)}, u32[]{:S(2)}) collective-permute-start(bf16[144,512]{1,0:T(8,128)(2,1)S(1)} %get-tuple-element.29), channel_id=1, source_target_pairs={{0,96},{32,64},{64,32},{96,0},{128,224},{160,192},{192,160},{224,1... | collective-permute-start | bytes 442376 | tf_op jit(solution)/shard_map/ppermute | solution.py:125
  47.1 0.0 collective-permute-start.11
  47.1 1.0 %collective-permute-start.12 = (bf16[144,512]{1,0:T(8,128)(2,1)S(1)}, bf16[144,512]{1,0:T(8,128)(2,1)S(1)}, u32[]{:S(2)}, u32[]{:S(2)}) collective-permute-start(bf16[144,512]{1,0:T(8,128)(2,1)S(1)} %get-tuple-element.27), channel_id=1, source_target_pairs={{0,160},{32,128},{64,224},{96,192},{128,32},{160,0},{192,96},{224,... | collective-permute-start | bytes 442376 | tf_op jit(solution)/shard_map/ppermute | solution.py:125
  48.1 1.3 %collective-permute-start.13 = (bf16[144,512]{1,0:T(8,128)(2,1)S(1)}, bf16[144,512]{1,0:T(8,128)(2,1)S(1)}, u32[]{:S(2)}, u32[]{:S(2)}) collective-permute-start(bf16[144,512]{1,0:T(8,128)(2,1)S(1)} %get-tuple-element.26), channel_id=1, source_target_pairs={{0,192},{32,224},{64,128},{96,160},{128,64},{160,96},{192,0},{224,... | collective-permute-start | bytes 442376 | tf_op jit(solution)/shard_map/ppermute | solution.py:125
  49.5 3.6 %collective-permute-start.14 = (bf16[144,512]{1,0:T(8,128)(2,1)S(1)}, bf16[144,512]{1,0:T(8,128)(2,1)S(1)}, u32[]{:S(2)}, u32[]{:S(2)}) collective-permute-start(bf16[144,512]{1,0:T(8,128)(2,1)S(1)} %get-tuple-element.25), channel_id=1, source_target_pairs={{0,224},{32,192},{64,160},{96,128},{128,96},{160,64},{192,32},{224... | collective-permute-start | bytes 442376 | tf_op jit(solution)/shard_map/ppermute | solution.py:125
  53.0 1.5 %collective-permute-start.9 = (bf16[144,512]{1,0:T(8,128)(2,1)S(1)}, bf16[144,512]{1,0:T(8,128)(2,1)S(1)}, u32[]{:S(2)}, u32[]{:S(2)}) collective-permute-start(bf16[144,512]{1,0:T(8,128)(2,1)S(1)} %get-tuple-element.30), channel_id=1, source_target_pairs={{0,64},{32,96},{64,0},{96,32},{128,192},{160,224},{192,128},{224,1... | collective-permute-start | bytes 442376 | tf_op jit(solution)/shard_map/ppermute | solution.py:125
  54.5 0.0 collective-permute-done.12.refs_4_
  54.5 0.9 %collective-permute-done.13.refs_5_ = bf16[144,512]{1,0:T(8,128)(2,1)S(1)} collective-permute-done((bf16[144,512]{1,0:T(8,128)(2,1)S(1)}, bf16[144,512]{1,0:T(8,128)(2,1)S(1)}, u32[]{:S(2)}, u32[]{:S(2)}) %collective-permute-start.13) | collective-permute-done | bytes 147488 | tf_op jit(solution)/shard_map/ppermute | solution.py:125
  55.4 5.2 %collective-permute-done.14.refs_6_ = bf16[144,512]{1,0:T(8,128)(2,1)S(1)} collective-permute-done((bf16[144,512]{1,0:T(8,128)(2,1)S(1)}, bf16[144,512]{1,0:T(8,128)(2,1)S(1)}, u32[]{:S(2)}, u32[]{:S(2)}) %collective-permute-start.14) | collective-permute-done | bytes 147488 | tf_op jit(solution)/shard_map/ppermute | solution.py:125
  60.7 2.6 %collective-permute-done.9.refs_1_ = bf16[144,512]{1,0:T(8,128)(2,1)S(1)} collective-permute-done((bf16[144,512]{1,0:T(8,128)(2,1)S(1)}, bf16[144,512]{1,0:T(8,128)(2,1)S(1)}, u32[]{:S(2)}, u32[]{:S(2)}) %collective-permute-start.9) | collective-permute-done | bytes 147488 | tf_op jit(solution)/shard_map/ppermute | solution.py:125
  63.3 1.5 %shard_map.84 = (bf16[64,512]{1,0:T(8,128)(2,1)S(1)}, bf16[64,512]{1,0:T(8,128)(2,1)S(1)}) custom-call(s32[4]{0:T(128)S(1)} %pad_add_fusion.ids_ref, bf16[8,144,512]{2,1,0:T(8,128)(2,1)S(1)} %shard_map.83.partial, bf16[144,512]{1,0:T(8,128)(2,1)S(1)} %collective-permute-done.8.refs_0_, bf16[144,512]{1,0:T(8,128)(2,1)S(1)} %collective-permute-done.9.refs_1_, ...), custom_call_target="tpu_custom_call" | custom-call | tf_op jit(solution)/shard_map/pallas_call | solution.py:282
  64.8 0.1 collective-permute-start.15
  64.9 3.1 %collective-permute-done.15.taken = bf16[64,512]{1,0:T(8,128)(2,1)S(1)} collective-permute-done((bf16[64,512]{1,0:T(8,128)(2,1)S(1)}, bf16[64,512]{1,0:T(8,128)(2,1)S(1)}, u32[]{:S(2)}, u32[]{:S(2)}) %collective-permute-start.15) | collective-permute-done | bytes 65568 | tf_op jit(solution)/shard_map/ppermute | solution.py:344
  68.0 1.5 %shard_map.85 = (bf16[64,1792]{1,0:T(8,128)(2,1)S(1)}, bf16[64,1792]{1,0:T(8,128)(2,1)S(1)}, bf16[64,1792]{1,0:T(8,128)(2,1)S(1)}, bf16[64,1792]{1,0:T(8,128)(2,...) custom-call(s32[4]{0:T(128)S(1)} %pad_add_fusion.ids_ref, ...), custom_call_target="tpu_custom_call" | custom-call | flops 704643072 | bytes 8388608 | tf_op jit(solution)/shard_map/pallas_call | solution.py:324
  69.5 3.9 %collective-permute-start.16 = (bf16[64,1792]{1,0:T(8,128)(2,1)S(1)}, bf16[64,1792]{1,0:T(8,128)(2,1)S(1)}, u32[]{:S(2)}, u32[]{:S(2)}) collective-permute-start(bf16[64,1792]{1,0:T(8,128)(2,1)S(1)} %get-tuple-element.20), channel_id=1, source_target_pairs={{0,1},{1,0},{2,3},{3,2},{4,5},{5,4},{6,7},{7,6},{8,9},{9,8},{10,11... | collective-permute-start | bytes 688136 | tf_op jit(solution)/shard_map/ppermute | solution.py:348
  73.4 0.1 collective-permute-start.18
  73.6 0.4 collective-permute-start.20
  74.0 0.6 collective-permute-done.16
  74.6 2.0 %collective-permute-start.17 = (bf16[32,1792]{1,0:T(8,128)(2,1)S(1)}, bf16[32,1792]{1,0:T(8,128)(2,1)S(1)}, u32[]{:S(2)}, u32[]{:S(2)}) collective-permute-start(bf16[32,1792]{1,0:T(8,128)(2,1)S(1)} %fusion.3), channel_id=1, source_target_pairs={{0,130},{2,128},{128,2},{130,0},{1,131},{3,129},{129,3},{131,1},{4... | collective-permute-start | bytes 344072 | tf_op jit(solution)/shard_map/ppermute | solution.py:352
  76.6 0.0 collective-permute-done.18
  76.7 0.9 %collective-permute-start.19 = (bf16[32,1792]{1,0:T(8,128)(2,1)S(1)}, bf16[32,1792]{1,0:T(8,128)(2,1)S(1)}, u32[]{:S(2)}, u32[]{:S(2)}) collective-permute-start(bf16[32,1792]{1,0:T(8,128)(2,1)S(1)} %fusion.4), channel_id=1, source_target_pairs={{0,130},{2,128},{128,2},{130,0},{1,131},{3,129},{129,3},{131,1},{4... | collective-permute-start | bytes 344072 | tf_op jit(solution)/shard_map/ppermute | solution.py:352
  77.6 0.0 collective-permute-done.20
  77.7 2.0 %collective-permute-start.21 = (bf16[32,1792]{1,0:T(8,128)(2,1)S(1)}, bf16[32,1792]{1,0:T(8,128)(2,1)S(1)}, u32[]{:S(2)}, u32[]{:S(2)}) collective-permute-start(bf16[32,1792]{1,0:T(8,128)(2,1)S(1)} %fusion.5), channel_id=1, source_target_pairs={{0,130},{2,128},{128,2},{130,0},{1,131},{3,129},{129,3},{131,1},{4... | collective-permute-start | bytes 344072 | tf_op jit(solution)/shard_map/ppermute | solution.py:352
  79.7 0.6 collective-permute-done.17
  80.3 2.5 %collective-permute-done.19 = bf16[32,1792]{1,0:T(8,128)(2,1)S(1)} collective-permute-done((bf16[32,1792]{1,0:T(8,128)(2,1)S(1)}, bf16[32,1792]{1,0:T(8,128)(2,1)S(1)}, u32[]{:S(2)}, u32[]{:S(2)}) %collective-permute-start.19) | collective-permute-done | bytes 114720 | tf_op jit(solution)/shard_map/ppermute | solution.py:352
  82.9 2.4 %collective-permute-done.21 = bf16[32,1792]{1,0:T(8,128)(2,1)S(1)} collective-permute-done((bf16[32,1792]{1,0:T(8,128)(2,1)S(1)}, bf16[32,1792]{1,0:T(8,128)(2,1)S(1)}, u32[]{:S(2)}, u32[]{:S(2)}) %collective-permute-start.21) | collective-permute-done | bytes 114720 | tf_op jit(solution)/shard_map/ppermute | solution.py:352
  85.3 0.8 pad_maximum_fusion.1
  (23 shorter events, 0.4 us)
Async XLA Ops:
  2.4 34.9 %copy-start = (bf16[128,512]{1,0:T(8,128)(2,1)S(1)}, bf16[128,512]{1,0:T(8,128)(2,1)}, u32[]{:S(2)}) copy-start(bf16[128,512]{1,0:T(8,128)(2,1)} %get-tuple-element.16.refs_3_) | copy-start | bytes 393220
  2.4 8.1 %collective-permute-start = (bf16[128,512]{1,0:T(8,128)(2,1)}, bf16[128,512]{1,0:T(8,128)(2,1)S(1)}, u32[]{:S(2)}, u32[]{:S(2)}) collective-permute-start(bf16[128,512]{1,0:T(8,128)(2,1)} %get-tuple-element.15), channel_id=1, source_target_pairs={{0,0},{4,8},{8,16},{12,24},{16,4},{20,12},{24,20},{28,28},{128,152... | collective-permute-start | bytes 393224 | tf_op jit(solution)/shard_map/ppermute | solution.py:340
  4.1 10.9 %collective-permute-start.4 = (bf16[128,512]{1,0:T(8,128)(2,1)}, bf16[128,512]{1,0:T(8,128)(2,1)S(1)}, u32[]{:S(2)}, u32[]{:S(2)}) collective-permute-start(bf16[128,512]{1,0:T(8,128)(2,1)} %get-tuple-element.16.refs_3_), channel_id=1, source_target_pairs={{0,4},{1,29},{4,0},{5,9},{8,12},{9,5},{12,8},{13,17},{16,20},{17,1... | collective-permute-start | bytes 393224 | tf_op jit(solution)/shard_map/ppermute | solution.py:88
  10.5 9.3 %collective-permute-start.1 = (bf16[128,512]{1,0:T(8,128)(2,1)S(1)}, bf16[128,512]{1,0:T(8,128)(2,1)S(1)}, u32[]{:S(2)}, u32[]{:S(2)}) collective-permute-start(bf16[128,512]{1,0:T(8,128)(2,1)S(1)} %collective-permute-done), channel_id=1, source_target_pairs={{0,128},{128,0},{1,129},{129,1},{2,130},{130,2},{3,131},{131,3},{4... | collective-permute-start | bytes 393224 | tf_op jit(solution)/shard_map/ppermute | solution.py:117
  15.9 7.9 %collective-permute-start.5 = (bf16[256,512]{1,0:T(8,128)(2,1)S(1)}, bf16[256,512]{1,0:T(8,128)(2,1)S(1)}, u32[]{:S(2)}, u32[]{:S(2)}) collective-permute-start(bf16[256,512]{1,0:T(8,128)(2,1)S(1)} %pad_maximum_fusion.2), channel_id=1, source_target_pairs={{0,28},{1,5},{4,8},{5,1},{8,4},{9,13},{12,16},{13,9},{16,12},{17,2... | collective-permute-start | bytes 786440 | tf_op jit(solution)/shard_map/ppermute | solution.py:89
  19.8 8.3 %collective-permute-start.2 = (bf16[256,512]{1,0:T(8,128)(2,1)S(1)}, bf16[256,512]{1,0:T(8,128)(2,1)S(1)}, u32[]{:S(2)}, u32[]{:S(2)}) collective-permute-start(bf16[256,512]{1,0:T(8,128)(2,1)S(1)} %constant_dynamic-update-slice_fusion.refs_0_), channel_id=1, source_target_pairs={{0,32},{1,97},{32,0},{33,65},{64,96},{65,33},{96,64},{97,1},{2,34}... | collective-permute-start | bytes 786440 | tf_op jit(solution)/shard_map/ppermute | solution.py:118
  23.8 8.0 %collective-permute-start.6 = (bf16[256,512]{1,0:T(8,128)(2,1)S(1)}, bf16[256,512]{1,0:T(8,128)(2,1)S(1)}, u32[]{:S(2)}, u32[]{:S(2)}) collective-permute-start(bf16[256,512]{1,0:T(8,128)(2,1)S(1)} %collective-permute-done.5.refs_5_), channel_id=1, source_target_pairs={{0,4},{1,29},{4,0},{5,9},{8,12},{9,5},{12,8},{13,17},{16,20},{17,1... | collective-permute-start | bytes 786440 | tf_op jit(solution)/shard_map/ppermute | solution.py:90
  28.2 9.2 %collective-permute-start.3 = (bf16[512,512]{1,0:T(8,128)(2,1)S(1)}, bf16[512,512]{1,0:T(8,128)(2,1)S(1)}, u32[]{:S(2)}, u32[]{:S(2)}) collective-permute-start(bf16[512,512]{1,0:T(8,128)(2,1)S(1)} %pad_maximum_fusion), channel_id=1, source_target_pairs={{0,96},{1,33},{32,64},{33,1},{64,32},{65,97},{96,0},{97,65},{2,98}... | collective-permute-start | bytes 1572872 | tf_op jit(solution)/shard_map/ppermute | solution.py:119
  31.9 5.5 %collective-permute-start.7 = (bf16[256,512]{1,0:T(8,128)(2,1)S(1)}, bf16[256,512]{1,0:T(8,128)(2,1)S(1)}, u32[]{:S(2)}, u32[]{:S(2)}) collective-permute-start(bf16[256,512]{1,0:T(8,128)(2,1)S(1)} %collective-permute-done.6.refs_6_), channel_id=1, source_target_pairs={{0,28},{1,5},{4,8},{5,1},{8,4},{9,13},{12,16},{13,9},{16,12},{17,2... | collective-permute-start | bytes 786440 | tf_op jit(solution)/shard_map/ppermute | solution.py:91
  31.9 36.1 %slice-start = ((s8[5505024]{0:T(1024)(128)(4,1)}), s8[4194304]{0:T(1024)(128)(4,1)S(1)}, s32[]{:S(2)}) async-start(s8[5505024]{0:T(1024)(128)(4,1)} %bitcast.42), calls=%async_computation | async-start | bytes 8388608
  32.0 36.0 %slice-start.1 = ((s8[5505024]{0:T(1024)(128)(4,1)}), s8[1310720]{0:T(1024)(128)(4,1)S(1)}, s32[]{:S(2)}) async-start(s8[5505024]{0:T(1024)(128)(4,1)} %bitcast.42), calls=%async_computation.1 | async-start | bytes 2621440
  44.6 8.4 %collective-permute-start.10 = (bf16[144,512]{1,0:T(8,128)(2,1)S(1)}, bf16[144,512]{1,0:T(8,128)(2,1)S(1)}, u32[]{:S(2)}, u32[]{:S(2)}) collective-permute-start(bf16[144,512]{1,0:T(8,128)(2,1)S(1)} %get-tuple-element.29), channel_id=1, source_target_pairs={{0,96},{32,64},{64,32},{96,0},{128,224},{160,192},{192,160},{224,1... | collective-permute-start | bytes 442376 | tf_op jit(solution)/shard_map/ppermute | solution.py:125
  47.1 6.0 %collective-permute-start.11 = (bf16[144,512]{1,0:T(8,128)(2,1)S(1)}, bf16[144,512]{1,0:T(8,128)(2,1)S(1)}, u32[]{:S(2)}, u32[]{:S(2)}) collective-permute-start(bf16[144,512]{1,0:T(8,128)(2,1)S(1)} %get-tuple-element.28), channel_id=1, source_target_pairs={{0,128},{32,160},{64,192},{96,224},{128,0},{160,32},{192,64},{224,... | collective-permute-start | bytes 442376 | tf_op jit(solution)/shard_map/ppermute | solution.py:125
  47.1 7.4 %collective-permute-start.12 = (bf16[144,512]{1,0:T(8,128)(2,1)S(1)}, bf16[144,512]{1,0:T(8,128)(2,1)S(1)}, u32[]{:S(2)}, u32[]{:S(2)}) collective-permute-start(bf16[144,512]{1,0:T(8,128)(2,1)S(1)} %get-tuple-element.27), channel_id=1, source_target_pairs={{0,160},{32,128},{64,224},{96,192},{128,32},{160,0},{192,96},{224,... | collective-permute-start | bytes 442376 | tf_op jit(solution)/shard_map/ppermute | solution.py:125
  48.1 7.3 %collective-permute-start.13 = (bf16[144,512]{1,0:T(8,128)(2,1)S(1)}, bf16[144,512]{1,0:T(8,128)(2,1)S(1)}, u32[]{:S(2)}, u32[]{:S(2)}) collective-permute-start(bf16[144,512]{1,0:T(8,128)(2,1)S(1)} %get-tuple-element.26), channel_id=1, source_target_pairs={{0,192},{32,224},{64,128},{96,160},{128,64},{160,96},{192,0},{224,... | collective-permute-start | bytes 442376 | tf_op jit(solution)/shard_map/ppermute | solution.py:125
  49.5 11.2 %collective-permute-start.14 = (bf16[144,512]{1,0:T(8,128)(2,1)S(1)}, bf16[144,512]{1,0:T(8,128)(2,1)S(1)}, u32[]{:S(2)}, u32[]{:S(2)}) collective-permute-start(bf16[144,512]{1,0:T(8,128)(2,1)S(1)} %get-tuple-element.25), channel_id=1, source_target_pairs={{0,224},{32,192},{64,160},{96,128},{128,96},{160,64},{192,32},{224... | collective-permute-start | bytes 442376 | tf_op jit(solution)/shard_map/ppermute | solution.py:125
  53.0 7.7 %collective-permute-start.8 = (bf16[144,512]{1,0:T(8,128)(2,1)S(1)}, bf16[144,512]{1,0:T(8,128)(2,1)S(1)}, u32[]{:S(2)}, u32[]{:S(2)}) collective-permute-start(bf16[144,512]{1,0:T(8,128)(2,1)S(1)} %get-tuple-element.31), channel_id=1, source_target_pairs={{0,32},{32,0},{64,96},{96,64},{128,160},{160,128},{192,224},{224,1... | collective-permute-start | bytes 442376 | tf_op jit(solution)/shard_map/ppermute | solution.py:125
  53.0 10.3 %collective-permute-start.9 = (bf16[144,512]{1,0:T(8,128)(2,1)S(1)}, bf16[144,512]{1,0:T(8,128)(2,1)S(1)}, u32[]{:S(2)}, u32[]{:S(2)}) collective-permute-start(bf16[144,512]{1,0:T(8,128)(2,1)S(1)} %get-tuple-element.30), channel_id=1, source_target_pairs={{0,64},{32,96},{64,0},{96,32},{128,192},{160,224},{192,128},{224,1... | collective-permute-start | bytes 442376 | tf_op jit(solution)/shard_map/ppermute | solution.py:125
  64.8 3.2 %collective-permute-start.15 = (bf16[64,512]{1,0:T(8,128)(2,1)S(1)}, bf16[64,512]{1,0:T(8,128)(2,1)S(1)}, u32[]{:S(2)}, u32[]{:S(2)}) collective-permute-start(bf16[64,512]{1,0:T(8,128)(2,1)S(1)} %get-tuple-element.18), channel_id=1, source_target_pairs={{0,4},{4,0},{8,12},{12,8},{16,20},{20,16},{24,28},{28,24},{1,5},{5... | collective-permute-start | bytes 196616 | tf_op jit(solution)/shard_map/ppermute | solution.py:344
  69.5 5.1 %collective-permute-start.16 = (bf16[64,1792]{1,0:T(8,128)(2,1)S(1)}, bf16[64,1792]{1,0:T(8,128)(2,1)S(1)}, u32[]{:S(2)}, u32[]{:S(2)}) collective-permute-start(bf16[64,1792]{1,0:T(8,128)(2,1)S(1)} %get-tuple-element.20), channel_id=1, source_target_pairs={{0,1},{1,0},{2,3},{3,2},{4,5},{5,4},{6,7},{7,6},{8,9},{9,8},{10,11... | collective-permute-start | bytes 688136 | tf_op jit(solution)/shard_map/ppermute | solution.py:348
  73.4 3.2 %collective-permute-start.18 = (bf16[64,1792]{1,0:T(8,128)(2,1)S(1)}, bf16[64,1792]{1,0:T(8,128)(2,1)S(1)}, u32[]{:S(2)}, u32[]{:S(2)}) collective-permute-start(bf16[64,1792]{1,0:T(8,128)(2,1)S(1)} %get-tuple-element.22), channel_id=1, source_target_pairs={{0,1},{1,0},{2,3},{3,2},{4,5},{5,4},{6,7},{7,6},{8,9},{9,8},{10,11... | collective-permute-start | bytes 688136 | tf_op jit(solution)/shard_map/ppermute | solution.py:348
  73.6 4.0 %collective-permute-start.20 = (bf16[64,1792]{1,0:T(8,128)(2,1)S(1)}, bf16[64,1792]{1,0:T(8,128)(2,1)S(1)}, u32[]{:S(2)}, u32[]{:S(2)}) collective-permute-start(bf16[64,1792]{1,0:T(8,128)(2,1)S(1)} %get-tuple-element.24), channel_id=1, source_target_pairs={{0,1},{1,0},{2,3},{3,2},{4,5},{5,4},{6,7},{7,6},{8,9},{9,8},{10,11... | collective-permute-start | bytes 688136 | tf_op jit(solution)/shard_map/ppermute | solution.py:348
  74.6 5.7 %collective-permute-start.17 = (bf16[32,1792]{1,0:T(8,128)(2,1)S(1)}, bf16[32,1792]{1,0:T(8,128)(2,1)S(1)}, u32[]{:S(2)}, u32[]{:S(2)}) collective-permute-start(bf16[32,1792]{1,0:T(8,128)(2,1)S(1)} %fusion.3), channel_id=1, source_target_pairs={{0,130},{2,128},{128,2},{130,0},{1,131},{3,129},{129,3},{131,1},{4... | collective-permute-start | bytes 344072 | tf_op jit(solution)/shard_map/ppermute | solution.py:352
  76.7 6.1 %collective-permute-start.19 = (bf16[32,1792]{1,0:T(8,128)(2,1)S(1)}, bf16[32,1792]{1,0:T(8,128)(2,1)S(1)}, u32[]{:S(2)}, u32[]{:S(2)}) collective-permute-start(bf16[32,1792]{1,0:T(8,128)(2,1)S(1)} %fusion.4), channel_id=1, source_target_pairs={{0,130},{2,128},{128,2},{130,0},{1,131},{3,129},{129,3},{131,1},{4... | collective-permute-start | bytes 344072 | tf_op jit(solution)/shard_map/ppermute | solution.py:352
  77.7 7.6 %collective-permute-start.21 = (bf16[32,1792]{1,0:T(8,128)(2,1)S(1)}, bf16[32,1792]{1,0:T(8,128)(2,1)S(1)}, u32[]{:S(2)}, u32[]{:S(2)}) collective-permute-start(bf16[32,1792]{1,0:T(8,128)(2,1)S(1)} %fusion.5), channel_id=1, source_target_pairs={{0,130},{2,128},{128,2},{130,0},{1,131},{3,129},{129,3},{131,1},{4... | collective-permute-start | bytes 344072 | tf_op jit(solution)/shard_map/ppermute | solution.py:352

commit v9 on v8

--- a/solution.py
+++ b/solution.py
@@ -57,10 +57,16 @@
 
 def prepare_kernel(q_ref, k_ref, v_ref, pos_ref, freq_ref, q_gain, k_gain, q_out, kv_out):
     lane = lax.broadcasted_iota(jnp.int32, (PIECE, HD), 1)
-    spread = jnp.broadcast_to(pos_ref[...].astype(jnp.float32), (PIECE, HD))
-    angles = jnp.transpose(spread) * freq_ref[...]
-    cosines = jnp.cos(angles)
-    sines = jnp.where(lane < HD // 2, -1.0, 1.0) * jnp.sin(angles)
+    spread = jnp.transpose(jnp.broadcast_to(pos_ref[...].astype(jnp.float32), (PIECE, HD)))
+    left = lane[:BLOCK] < HD // 2
+    angles = jnp.where(left, spread[:BLOCK], spread[BLOCK:]) * freq_ref[...]
+
+    def unpack(packed):
+        turned = pltpu.roll(packed, HD // 2, 1)
+        return jnp.concatenate([jnp.where(left, packed, turned), jnp.where(left, turned, packed)], axis=0)
+
+    cosines = unpack(jnp.cos(angles))
+    sines = jnp.where(lane < HD // 2, -1.0, 1.0) * unpack(jnp.sin(angles))
     for head in range(4):
         cols = slice(head * HD, (head + 1) * HD)
         rows = rotate(q_ref[:, cols], q_gain[...], cosines, sines)

time: 86.2 us -> 86.1 us (level)
  no operation moved by 1% of the time
where the time goes in v9:
time: 86.1 us; the launch traced here: 86 us
  starting transfers between devices  44.1 us (51%)
  waiting for transfers between devices  27.1 us (31%)
  Pallas kernels  12.5 us (15%)
  other arithmetic  2 us (2%)
    ppermute x7, starting transfers between devices, exchange(): lax.ppermute(partial[step], ('x', 'y'), pairs(GROUP, lambda i: i ^ step))  9.88 us
    ppermute x7, waiting for transfers between devices, exchange(): lax.ppermute(partial[step], ('x', 'y'), pairs(GROUP, lambda i: i ^ step))  8.81 us
    pallas_call x1, Pallas kernels, attention(): pl.pallas_call(attention_kernel, out_shape=jax.ShapeDtypeStruct((GROUP, P...  7.13 us
    ppermute x1, starting transfers between devices, gather_z(): one = lax.ppermute(own, ('z', 'c'), here)  6.41 us
    ppermute x3, waiting for transfers between devices, on_device(): landed = lax.ppermute(give, ('x', 'w'), pairs(4, lambda i: i ^ 3))  5.59 us
    ppermute x1, waiting for transfers between devices, gather_z(): four = lax.ppermute(three, ('z', 'c'), there)  5.43 us
    ppermute x3, starting transfers between devices, on_device(): landed = lax.ppermute(give, ('x', 'w'), pairs(4, lambda i: i ^ 3))  4.83 us
    ppermute x1, starting transfers between devices, gather_xy(): both = jnp.concatenate([own, lax.ppermute(own, 'x', X_PAIRS)], axis=0)  4.46 us
  transfers between devices with their start and end apart: 22, of which 11 were waited for; matrix products, arithmetic and copies ran while one was open for 2% of the time, Pallas kernels for 0%

profile of v9, /device:TPU:1, one launch (start us, length us, event | category | flops | bytes accessed | tf_op | source)
XLA Modules:
  0.0 86.0 jit_solution(11352149638467387533)
XLA Ops:
  0.0 2.4 %shard_map.82 = (bf16[128,512]{1,0:T(8,128)(2,1)}, bf16[128,512]{1,0:T(8,128)(2,1)}) custom-call(bf16[128,512]{1,0:T(8,128)(2,1)} %q_ref.1, bf16[128,256]{1,0:T(8,128)(2,1)} %k_ref.1, bf16[128,256]{1,0:T(8,128)(2,1)} %v_ref.1, s32[1,128]{1,0:T(1,128)} %bitcast.50, f32[1,128]{1,0:T(1,128)} %constant.44.clone.freq_ref, f32[1,128]{1,0:T(1,128)} %bitcast.51, ...), custom_call_target="tpu_custom_call" | custom-call | tf_op jit(solution)/shard_map/pallas_call | solution.py:84
  2.4 1.7 %collective-permute-start = (bf16[128,512]{1,0:T(8,128)(2,1)}, bf16[128,512]{1,0:T(8,128)(2,1)S(1)}, u32[]{:S(2)}, u32[]{:S(2)}) collective-permute-start(bf16[128,512]{1,0:T(8,128)(2,1)} %get-tuple-element.15), channel_id=1, source_target_pairs={{0,0},{4,8},{8,16},{12,24},{16,4},{20,12},{24,20},{28,28},{128,152... | collective-permute-start | bytes 393224 | tf_op jit(solution)/shard_map/ppermute | solution.py:346
  4.1 6.4 %collective-permute-start.4 = (bf16[128,512]{1,0:T(8,128)(2,1)}, bf16[128,512]{1,0:T(8,128)(2,1)S(1)}, u32[]{:S(2)}, u32[]{:S(2)}) collective-permute-start(bf16[128,512]{1,0:T(8,128)(2,1)} %get-tuple-element.16.refs_3_), channel_id=1, source_target_pairs={{0,4},{1,29},{4,0},{5,9},{8,12},{9,5},{12,8},{13,17},{16,20},{17,1... | collective-permute-start | bytes 393224 | tf_op jit(solution)/shard_map/ppermute | solution.py:94
  10.5 0.0 collective-permute-done
  10.5 4.5 %collective-permute-start.1 = (bf16[128,512]{1,0:T(8,128)(2,1)S(1)}, bf16[128,512]{1,0:T(8,128)(2,1)S(1)}, u32[]{:S(2)}, u32[]{:S(2)}) collective-permute-start(bf16[128,512]{1,0:T(8,128)(2,1)S(1)} %collective-permute-done), channel_id=1, source_target_pairs={{0,128},{128,0},{1,129},{129,1},{2,130},{130,2},{3,131},{131,3},{4... | collective-permute-start | bytes 393224 | tf_op jit(solution)/shard_map/ppermute | solution.py:123
  14.9 0.0 collective-permute-done.4.refs_4_
  14.9 0.9 %pad_maximum_fusion.2 = bf16[256,512]{1,0:T(8,128)(2,1)S(1)} fusion(bf16[128,512]{1,0:T(8,128)(2,1)S(1)} %collective-permute-done.4.refs_4_, bf16[128,512]{1,0:T(8,128)(2,1)} %get-tuple-element.16.refs_3_), kind=kLoop, calls=%fused_computation.5 | loop fusion | flops 524288 | bytes 524288 | tf_op jit(solution)/shard_map/concatenate | solution.py:95
  15.9 3.9 %collective-permute-start.5 = (bf16[256,512]{1,0:T(8,128)(2,1)S(1)}, bf16[256,512]{1,0:T(8,128)(2,1)S(1)}, u32[]{:S(2)}, u32[]{:S(2)}) collective-permute-start(bf16[256,512]{1,0:T(8,128)(2,1)S(1)} %pad_maximum_fusion.2), channel_id=1, source_target_pairs={{0,28},{1,5},{4,8},{5,1},{8,4},{9,13},{12,16},{13,9},{16,12},{17,2... | collective-permute-start | bytes 786440 | tf_op jit(solution)/shard_map/ppermute | solution.py:95
  19.7 0.0 collective-permute-done.1
  19.8 2.8 %collective-permute-start.2 = (bf16[256,512]{1,0:T(8,128)(2,1)S(1)}, bf16[256,512]{1,0:T(8,128)(2,1)S(1)}, u32[]{:S(2)}, u32[]{:S(2)}) collective-permute-start(bf16[256,512]{1,0:T(8,128)(2,1)S(1)} %constant_dynamic-update-slice_fusion.refs_0_), channel_id=1, source_target_pairs={{0,32},{1,97},{32,0},{33,65},{64,96},{65,33},{96,64},{97,1},{2,34}... | collective-permute-start | bytes 786440 | tf_op jit(solution)/shard_map/ppermute | solution.py:124
  22.6 1.2 %collective-permute-done.5.refs_5_ = bf16[256,512]{1,0:T(8,128)(2,1)S(1)} collective-permute-done((bf16[256,512]{1,0:T(8,128)(2,1)S(1)}, bf16[256,512]{1,0:T(8,128)(2,1)S(1)}, u32[]{:S(2)}, u32[]{:S(2)}) %collective-permute-start.5) | collective-permute-done | bytes 262176 | tf_op jit(solution)/shard_map/ppermute | solution.py:95
  23.8 4.3 %collective-permute-start.6 = (bf16[256,512]{1,0:T(8,128)(2,1)S(1)}, bf16[256,512]{1,0:T(8,128)(2,1)S(1)}, u32[]{:S(2)}, u32[]{:S(2)}) collective-permute-start(bf16[256,512]{1,0:T(8,128)(2,1)S(1)} %collective-permute-done.5.refs_5_), channel_id=1, source_target_pairs={{0,4},{1,29},{4,0},{5,9},{8,12},{9,5},{12,8},{13,17},{16,20},{17,1... | collective-permute-start | bytes 786440 | tf_op jit(solution)/shard_map/ppermute | solution.py:96
  28.0 0.0 collective-permute-done.2.refs_1_
  28.1 1.4 %collective-permute-start.3 = (bf16[512,512]{1,0:T(8,128)(2,1)S(1)}, bf16[512,512]{1,0:T(8,128)(2,1)S(1)}, u32[]{:S(2)}, u32[]{:S(2)}) collective-permute-start(bf16[512,512]{1,0:T(8,128)(2,1)S(1)} %pad_maximum_fusion), channel_id=1, source_target_pairs={{0,96},{1,33},{32,64},{33,1},{64,32},{65,97},{96,0},{97,65},{2,98}... | collective-permute-start | bytes 1572872 | tf_op jit(solution)/shard_map/ppermute | solution.py:125
  29.5 2.3 %collective-permute-done.6.refs_6_ = bf16[256,512]{1,0:T(8,128)(2,1)S(1)} collective-permute-done((bf16[256,512]{1,0:T(8,128)(2,1)S(1)}, bf16[256,512]{1,0:T(8,128)(2,1)S(1)}, u32[]{:S(2)}, u32[]{:S(2)}) %collective-permute-start.6) | collective-permute-done | bytes 262176 | tf_op jit(solution)/shard_map/ppermute | solution.py:96
  31.8 0.0 collective-permute-start.7
  31.8 0.1 pad_add_fusion.ids_ref
  31.9 5.4 %collective-permute-done.7.refs_7_ = bf16[256,512]{1,0:T(8,128)(2,1)S(1)} collective-permute-done((bf16[256,512]{1,0:T(8,128)(2,1)S(1)}, bf16[256,512]{1,0:T(8,128)(2,1)S(1)}, u32[]{:S(2)}, u32[]{:S(2)}) %collective-permute-start.7) | collective-permute-done | bytes 262176 | tf_op jit(solution)/shard_map/ppermute | solution.py:97
  37.3 7.1 %shard_map.83.partial = bf16[8,144,512]{2,1,0:T(8,128)(2,1)S(1)} custom-call(s32[4]{0:T(128)S(1)} %pad_add_fusion.ids_ref, bf16[256,512]{1,0:T(8,128)(2,1)S(1)} %constant_dynamic-update-slice_fusion.refs_0_, bf16[256,512]{1,0:T(8,128)(2,1)S(1)} %collective-permute-done.2.refs_1_, bf16[512,512]{1,0:T(8,128)(2,1)S(1)} %collective-permute-done.3.refs_2_, ...), custom_call_target="tpu_custom_call" | custom-call | flops 2147483648 | bytes 4194304 | tf_op jit(solution)/shard_map/pallas_call | solution.py:245
  44.5 0.1 slice_bitcast_fusion
  44.5 2.5 %collective-permute-start.10 = (bf16[144,512]{1,0:T(8,128)(2,1)S(1)}, bf16[144,512]{1,0:T(8,128)(2,1)S(1)}, u32[]{:S(2)}, u32[]{:S(2)}) collective-permute-start(bf16[144,512]{1,0:T(8,128)(2,1)S(1)} %get-tuple-element.29), channel_id=1, source_target_pairs={{0,96},{32,64},{64,32},{96,0},{128,224},{160,192},{192,160},{224,1... | collective-permute-start | bytes 442376 | tf_op jit(solution)/shard_map/ppermute | solution.py:131
  47.0 0.0 collective-permute-start.11
  47.0 1.0 %collective-permute-start.12 = (bf16[144,512]{1,0:T(8,128)(2,1)S(1)}, bf16[144,512]{1,0:T(8,128)(2,1)S(1)}, u32[]{:S(2)}, u32[]{:S(2)}) collective-permute-start(bf16[144,512]{1,0:T(8,128)(2,1)S(1)} %get-tuple-element.27), channel_id=1, source_target_pairs={{0,160},{32,128},{64,224},{96,192},{128,32},{160,0},{192,96},{224,... | collective-permute-start | bytes 442376 | tf_op jit(solution)/shard_map/ppermute | solution.py:131
  48.0 1.3 %collective-permute-start.13 = (bf16[144,512]{1,0:T(8,128)(2,1)S(1)}, bf16[144,512]{1,0:T(8,128)(2,1)S(1)}, u32[]{:S(2)}, u32[]{:S(2)}) collective-permute-start(bf16[144,512]{1,0:T(8,128)(2,1)S(1)} %get-tuple-element.26), channel_id=1, source_target_pairs={{0,192},{32,224},{64,128},{96,160},{128,64},{160,96},{192,0},{224,... | collective-permute-start | bytes 442376 | tf_op jit(solution)/shard_map/ppermute | solution.py:131
  49.4 3.6 %collective-permute-start.14 = (bf16[144,512]{1,0:T(8,128)(2,1)S(1)}, bf16[144,512]{1,0:T(8,128)(2,1)S(1)}, u32[]{:S(2)}, u32[]{:S(2)}) collective-permute-start(bf16[144,512]{1,0:T(8,128)(2,1)S(1)} %get-tuple-element.25), channel_id=1, source_target_pairs={{0,224},{32,192},{64,160},{96,128},{128,96},{160,64},{192,32},{224... | collective-permute-start | bytes 442376 | tf_op jit(solution)/shard_map/ppermute | solution.py:131
  52.9 0.0 collective-permute-done.10.refs_2_
  52.9 0.0 collective-permute-start.8
  52.9 0.0 collective-permute-done.11.refs_3_
  53.0 1.5 %collective-permute-start.9 = (bf16[144,512]{1,0:T(8,128)(2,1)S(1)}, bf16[144,512]{1,0:T(8,128)(2,1)S(1)}, u32[]{:S(2)}, u32[]{:S(2)}) collective-permute-start(bf16[144,512]{1,0:T(8,128)(2,1)S(1)} %get-tuple-element.30), channel_id=1, source_target_pairs={{0,64},{32,96},{64,0},{96,32},{128,192},{160,224},{192,128},{224,1... | collective-permute-start | bytes 442376 | tf_op jit(solution)/shard_map/ppermute | solution.py:131
  54.4 0.9 %collective-permute-done.13.refs_5_ = bf16[144,512]{1,0:T(8,128)(2,1)S(1)} collective-permute-done((bf16[144,512]{1,0:T(8,128)(2,1)S(1)}, bf16[144,512]{1,0:T(8,128)(2,1)S(1)}, u32[]{:S(2)}, u32[]{:S(2)}) %collective-permute-start.13) | collective-permute-done | bytes 147488 | tf_op jit(solution)/shard_map/ppermute | solution.py:131
  55.4 5.2 %collective-permute-done.14.refs_6_ = bf16[144,512]{1,0:T(8,128)(2,1)S(1)} collective-permute-done((bf16[144,512]{1,0:T(8,128)(2,1)S(1)}, bf16[144,512]{1,0:T(8,128)(2,1)S(1)}, u32[]{:S(2)}, u32[]{:S(2)}) %collective-permute-start.14) | collective-permute-done | bytes 147488 | tf_op jit(solution)/shard_map/ppermute | solution.py:131
  60.6 2.6 %collective-permute-done.9.refs_1_ = bf16[144,512]{1,0:T(8,128)(2,1)S(1)} collective-permute-done((bf16[144,512]{1,0:T(8,128)(2,1)S(1)}, bf16[144,512]{1,0:T(8,128)(2,1)S(1)}, u32[]{:S(2)}, u32[]{:S(2)}) %collective-permute-start.9) | collective-permute-done | bytes 147488 | tf_op jit(solution)/shard_map/ppermute | solution.py:131
  63.2 1.5 %shard_map.84 = (bf16[64,512]{1,0:T(8,128)(2,1)S(1)}, bf16[64,512]{1,0:T(8,128)(2,1)S(1)}) custom-call(s32[4]{0:T(128)S(1)} %pad_add_fusion.ids_ref, bf16[8,144,512]{2,1,0:T(8,128)(2,1)S(1)} %shard_map.83.partial, bf16[144,512]{1,0:T(8,128)(2,1)S(1)} %collective-permute-done.8.refs_0_, bf16[144,512]{1,0:T(8,128)(2,1)S(1)} %collective-permute-done.9.refs_1_, ...), custom_call_target="tpu_custom_call" | custom-call | tf_op jit(solution)/shard_map/pallas_call | solution.py:288
  64.7 0.1 collective-permute-start.15
  64.8 3.1 %collective-permute-done.15.taken = bf16[64,512]{1,0:T(8,128)(2,1)S(1)} collective-permute-done((bf16[64,512]{1,0:T(8,128)(2,1)S(1)}, bf16[64,512]{1,0:T(8,128)(2,1)S(1)}, u32[]{:S(2)}, u32[]{:S(2)}) %collective-permute-start.15) | collective-permute-done | bytes 65568 | tf_op jit(solution)/shard_map/ppermute | solution.py:350
  67.9 1.5 %shard_map.85 = (bf16[64,1792]{1,0:T(8,128)(2,1)S(1)}, bf16[64,1792]{1,0:T(8,128)(2,1)S(1)}, bf16[64,1792]{1,0:T(8,128)(2,1)S(1)}, bf16[64,1792]{1,0:T(8,128)(2,...) custom-call(s32[4]{0:T(128)S(1)} %pad_add_fusion.ids_ref, ...), custom_call_target="tpu_custom_call" | custom-call | flops 704643072 | bytes 8388608 | tf_op jit(solution)/shard_map/pallas_call | solution.py:330
  69.4 3.9 %collective-permute-start.16 = (bf16[64,1792]{1,0:T(8,128)(2,1)S(1)}, bf16[64,1792]{1,0:T(8,128)(2,1)S(1)}, u32[]{:S(2)}, u32[]{:S(2)}) collective-permute-start(bf16[64,1792]{1,0:T(8,128)(2,1)S(1)} %get-tuple-element.20), channel_id=1, source_target_pairs={{0,1},{1,0},{2,3},{3,2},{4,5},{5,4},{6,7},{7,6},{8,9},{9,8},{10,11... | collective-permute-start | bytes 688136 | tf_op jit(solution)/shard_map/ppermute | solution.py:354
  73.4 0.1 collective-permute-start.18
  73.5 0.4 collective-permute-start.20
  73.9 0.6 collective-permute-done.16
  74.6 2.0 %collective-permute-start.17 = (bf16[32,1792]{1,0:T(8,128)(2,1)S(1)}, bf16[32,1792]{1,0:T(8,128)(2,1)S(1)}, u32[]{:S(2)}, u32[]{:S(2)}) collective-permute-start(bf16[32,1792]{1,0:T(8,128)(2,1)S(1)} %fusion.3), channel_id=1, source_target_pairs={{0,130},{2,128},{128,2},{130,0},{1,131},{3,129},{129,3},{131,1},{4... | collective-permute-start | bytes 344072 | tf_op jit(solution)/shard_map/ppermute | solution.py:358
  76.6 0.0 collective-permute-done.18
  76.6 0.9 %collective-permute-start.19 = (bf16[32,1792]{1,0:T(8,128)(2,1)S(1)}, bf16[32,1792]{1,0:T(8,128)(2,1)S(1)}, u32[]{:S(2)}, u32[]{:S(2)}) collective-permute-start(bf16[32,1792]{1,0:T(8,128)(2,1)S(1)} %fusion.4), channel_id=1, source_target_pairs={{0,130},{2,128},{128,2},{130,0},{1,131},{3,129},{129,3},{131,1},{4... | collective-permute-start | bytes 344072 | tf_op jit(solution)/shard_map/ppermute | solution.py:358
  77.6 2.0 %collective-permute-start.21 = (bf16[32,1792]{1,0:T(8,128)(2,1)S(1)}, bf16[32,1792]{1,0:T(8,128)(2,1)S(1)}, u32[]{:S(2)}, u32[]{:S(2)}) collective-permute-start(bf16[32,1792]{1,0:T(8,128)(2,1)S(1)} %fusion.5), channel_id=1, source_target_pairs={{0,130},{2,128},{128,2},{130,0},{1,131},{3,129},{129,3},{131,1},{4... | collective-permute-start | bytes 344072 | tf_op jit(solution)/shard_map/ppermute | solution.py:358
  79.6 0.7 collective-permute-done.17
  80.3 2.5 %collective-permute-done.19 = bf16[32,1792]{1,0:T(8,128)(2,1)S(1)} collective-permute-done((bf16[32,1792]{1,0:T(8,128)(2,1)S(1)}, bf16[32,1792]{1,0:T(8,128)(2,1)S(1)}, u32[]{:S(2)}, u32[]{:S(2)}) %collective-permute-start.19) | collective-permute-done | bytes 114720 | tf_op jit(solution)/shard_map/ppermute | solution.py:358
  82.8 2.4 %collective-permute-done.21 = bf16[32,1792]{1,0:T(8,128)(2,1)S(1)} collective-permute-done((bf16[32,1792]{1,0:T(8,128)(2,1)S(1)}, bf16[32,1792]{1,0:T(8,128)(2,1)S(1)}, u32[]{:S(2)}, u32[]{:S(2)}) %collective-permute-start.21) | collective-permute-done | bytes 114720 | tf_op jit(solution)/shard_map/ppermute | solution.py:358
  85.2 0.8 pad_maximum_fusion.1
  (23 shorter events, 0.4 us)
Async XLA Ops:
  2.4 34.9 %copy-start = (bf16[128,512]{1,0:T(8,128)(2,1)S(1)}, bf16[128,512]{1,0:T(8,128)(2,1)}, u32[]{:S(2)}) copy-start(bf16[128,512]{1,0:T(8,128)(2,1)} %get-tuple-element.16.refs_3_) | copy-start | bytes 393220
  2.4 8.1 %collective-permute-start = (bf16[128,512]{1,0:T(8,128)(2,1)}, bf16[128,512]{1,0:T(8,128)(2,1)S(1)}, u32[]{:S(2)}, u32[]{:S(2)}) collective-permute-start(bf16[128,512]{1,0:T(8,128)(2,1)} %get-tuple-element.15), channel_id=1, source_target_pairs={{0,0},{4,8},{8,16},{12,24},{16,4},{20,12},{24,20},{28,28},{128,152... | collective-permute-start | bytes 393224 | tf_op jit(solution)/shard_map/ppermute | solution.py:346
  4.1 10.9 %collective-permute-start.4 = (bf16[128,512]{1,0:T(8,128)(2,1)}, bf16[128,512]{1,0:T(8,128)(2,1)S(1)}, u32[]{:S(2)}, u32[]{:S(2)}) collective-permute-start(bf16[128,512]{1,0:T(8,128)(2,1)} %get-tuple-element.16.refs_3_), channel_id=1, source_target_pairs={{0,4},{1,29},{4,0},{5,9},{8,12},{9,5},{12,8},{13,17},{16,20},{17,1... | collective-permute-start | bytes 393224 | tf_op jit(solution)/shard_map/ppermute | solution.py:94
  10.5 9.3 %collective-permute-start.1 = (bf16[128,512]{1,0:T(8,128)(2,1)S(1)}, bf16[128,512]{1,0:T(8,128)(2,1)S(1)}, u32[]{:S(2)}, u32[]{:S(2)}) collective-permute-start(bf16[128,512]{1,0:T(8,128)(2,1)S(1)} %collective-permute-done), channel_id=1, source_target_pairs={{0,128},{128,0},{1,129},{129,1},{2,130},{130,2},{3,131},{131,3},{4... | collective-permute-start | bytes 393224 | tf_op jit(solution)/shard_map/ppermute | solution.py:123
  15.9 7.9 %collective-permute-start.5 = (bf16[256,512]{1,0:T(8,128)(2,1)S(1)}, bf16[256,512]{1,0:T(8,128)(2,1)S(1)}, u32[]{:S(2)}, u32[]{:S(2)}) collective-permute-start(bf16[256,512]{1,0:T(8,128)(2,1)S(1)} %pad_maximum_fusion.2), channel_id=1, source_target_pairs={{0,28},{1,5},{4,8},{5,1},{8,4},{9,13},{12,16},{13,9},{16,12},{17,2... | collective-permute-start | bytes 786440 | tf_op jit(solution)/shard_map/ppermute | solution.py:95
  19.8 8.3 %collective-permute-start.2 = (bf16[256,512]{1,0:T(8,128)(2,1)S(1)}, bf16[256,512]{1,0:T(8,128)(2,1)S(1)}, u32[]{:S(2)}, u32[]{:S(2)}) collective-permute-start(bf16[256,512]{1,0:T(8,128)(2,1)S(1)} %constant_dynamic-update-slice_fusion.refs_0_), channel_id=1, source_target_pairs={{0,32},{1,97},{32,0},{33,65},{64,96},{65,33},{96,64},{97,1},{2,34}... | collective-permute-start | bytes 786440 | tf_op jit(solution)/shard_map/ppermute | solution.py:124
  23.8 8.0 %collective-permute-start.6 = (bf16[256,512]{1,0:T(8,128)(2,1)S(1)}, bf16[256,512]{1,0:T(8,128)(2,1)S(1)}, u32[]{:S(2)}, u32[]{:S(2)}) collective-permute-start(bf16[256,512]{1,0:T(8,128)(2,1)S(1)} %collective-permute-done.5.refs_5_), channel_id=1, source_target_pairs={{0,4},{1,29},{4,0},{5,9},{8,12},{9,5},{12,8},{13,17},{16,20},{17,1... | collective-permute-start | bytes 786440 | tf_op jit(solution)/shard_map/ppermute | solution.py:96
  28.1 9.2 %collective-permute-start.3 = (bf16[512,512]{1,0:T(8,128)(2,1)S(1)}, bf16[512,512]{1,0:T(8,128)(2,1)S(1)}, u32[]{:S(2)}, u32[]{:S(2)}) collective-permute-start(bf16[512,512]{1,0:T(8,128)(2,1)S(1)} %pad_maximum_fusion), channel_id=1, source_target_pairs={{0,96},{1,33},{32,64},{33,1},{64,32},{65,97},{96,0},{97,65},{2,98}... | collective-permute-start | bytes 1572872 | tf_op jit(solution)/shard_map/ppermute | solution.py:125
  31.8 5.5 %collective-permute-start.7 = (bf16[256,512]{1,0:T(8,128)(2,1)S(1)}, bf16[256,512]{1,0:T(8,128)(2,1)S(1)}, u32[]{:S(2)}, u32[]{:S(2)}) collective-permute-start(bf16[256,512]{1,0:T(8,128)(2,1)S(1)} %collective-permute-done.6.refs_6_), channel_id=1, source_target_pairs={{0,28},{1,5},{4,8},{5,1},{8,4},{9,13},{12,16},{13,9},{16,12},{17,2... | collective-permute-start | bytes 786440 | tf_op jit(solution)/shard_map/ppermute | solution.py:97
  31.8 36.1 %slice-start = ((s8[5505024]{0:T(1024)(128)(4,1)}), s8[4194304]{0:T(1024)(128)(4,1)S(1)}, s32[]{:S(2)}) async-start(s8[5505024]{0:T(1024)(128)(4,1)} %bitcast.42), calls=%async_computation | async-start | bytes 8388608
  31.9 36.0 %slice-start.1 = ((s8[5505024]{0:T(1024)(128)(4,1)}), s8[1310720]{0:T(1024)(128)(4,1)S(1)}, s32[]{:S(2)}) async-start(s8[5505024]{0:T(1024)(128)(4,1)} %bitcast.42), calls=%async_computation.1 | async-start | bytes 2621440
  44.5 8.4 %collective-permute-start.10 = (bf16[144,512]{1,0:T(8,128)(2,1)S(1)}, bf16[144,512]{1,0:T(8,128)(2,1)S(1)}, u32[]{:S(2)}, u32[]{:S(2)}) collective-permute-start(bf16[144,512]{1,0:T(8,128)(2,1)S(1)} %get-tuple-element.29), channel_id=1, source_target_pairs={{0,96},{32,64},{64,32},{96,0},{128,224},{160,192},{192,160},{224,1... | collective-permute-start | bytes 442376 | tf_op jit(solution)/shard_map/ppermute | solution.py:131
  47.0 6.0 %collective-permute-start.11 = (bf16[144,512]{1,0:T(8,128)(2,1)S(1)}, bf16[144,512]{1,0:T(8,128)(2,1)S(1)}, u32[]{:S(2)}, u32[]{:S(2)}) collective-permute-start(bf16[144,512]{1,0:T(8,128)(2,1)S(1)} %get-tuple-element.28), channel_id=1, source_target_pairs={{0,128},{32,160},{64,192},{96,224},{128,0},{160,32},{192,64},{224,... | collective-permute-start | bytes 442376 | tf_op jit(solution)/shard_map/ppermute | solution.py:131
  47.0 7.4 %collective-permute-start.12 = (bf16[144,512]{1,0:T(8,128)(2,1)S(1)}, bf16[144,512]{1,0:T(8,128)(2,1)S(1)}, u32[]{:S(2)}, u32[]{:S(2)}) collective-permute-start(bf16[144,512]{1,0:T(8,128)(2,1)S(1)} %get-tuple-element.27), channel_id=1, source_target_pairs={{0,160},{32,128},{64,224},{96,192},{128,32},{160,0},{192,96},{224,... | collective-permute-start | bytes 442376 | tf_op jit(solution)/shard_map/ppermute | solution.py:131
  48.0 7.3 %collective-permute-start.13 = (bf16[144,512]{1,0:T(8,128)(2,1)S(1)}, bf16[144,512]{1,0:T(8,128)(2,1)S(1)}, u32[]{:S(2)}, u32[]{:S(2)}) collective-permute-start(bf16[144,512]{1,0:T(8,128)(2,1)S(1)} %get-tuple-element.26), channel_id=1, source_target_pairs={{0,192},{32,224},{64,128},{96,160},{128,64},{160,96},{192,0},{224,... | collective-permute-start | bytes 442376 | tf_op jit(solution)/shard_map/ppermute | solution.py:131
  49.4 11.2 %collective-permute-start.14 = (bf16[144,512]{1,0:T(8,128)(2,1)S(1)}, bf16[144,512]{1,0:T(8,128)(2,1)S(1)}, u32[]{:S(2)}, u32[]{:S(2)}) collective-permute-start(bf16[144,512]{1,0:T(8,128)(2,1)S(1)} %get-tuple-element.25), channel_id=1, source_target_pairs={{0,224},{32,192},{64,160},{96,128},{128,96},{160,64},{192,32},{224... | collective-permute-start | bytes 442376 | tf_op jit(solution)/shard_map/ppermute | solution.py:131
  52.9 7.7 %collective-permute-start.8 = (bf16[144,512]{1,0:T(8,128)(2,1)S(1)}, bf16[144,512]{1,0:T(8,128)(2,1)S(1)}, u32[]{:S(2)}, u32[]{:S(2)}) collective-permute-start(bf16[144,512]{1,0:T(8,128)(2,1)S(1)} %get-tuple-element.31), channel_id=1, source_target_pairs={{0,32},{32,0},{64,96},{96,64},{128,160},{160,128},{192,224},{224,1... | collective-permute-start | bytes 442376 | tf_op jit(solution)/shard_map/ppermute | solution.py:131
  53.0 10.3 %collective-permute-start.9 = (bf16[144,512]{1,0:T(8,128)(2,1)S(1)}, bf16[144,512]{1,0:T(8,128)(2,1)S(1)}, u32[]{:S(2)}, u32[]{:S(2)}) collective-permute-start(bf16[144,512]{1,0:T(8,128)(2,1)S(1)} %get-tuple-element.30), channel_id=1, source_target_pairs={{0,64},{32,96},{64,0},{96,32},{128,192},{160,224},{192,128},{224,1... | collective-permute-start | bytes 442376 | tf_op jit(solution)/shard_map/ppermute | solution.py:131
  64.7 3.2 %collective-permute-start.15 = (bf16[64,512]{1,0:T(8,128)(2,1)S(1)}, bf16[64,512]{1,0:T(8,128)(2,1)S(1)}, u32[]{:S(2)}, u32[]{:S(2)}) collective-permute-start(bf16[64,512]{1,0:T(8,128)(2,1)S(1)} %get-tuple-element.18), channel_id=1, source_target_pairs={{0,4},{4,0},{8,12},{12,8},{16,20},{20,16},{24,28},{28,24},{1,5},{5... | collective-permute-start | bytes 196616 | tf_op jit(solution)/shard_map/ppermute | solution.py:350
  69.4 5.1 %collective-permute-start.16 = (bf16[64,1792]{1,0:T(8,128)(2,1)S(1)}, bf16[64,1792]{1,0:T(8,128)(2,1)S(1)}, u32[]{:S(2)}, u32[]{:S(2)}) collective-permute-start(bf16[64,1792]{1,0:T(8,128)(2,1)S(1)} %get-tuple-element.20), channel_id=1, source_target_pairs={{0,1},{1,0},{2,3},{3,2},{4,5},{5,4},{6,7},{7,6},{8,9},{9,8},{10,11... | collective-permute-start | bytes 688136 | tf_op jit(solution)/shard_map/ppermute | solution.py:354
  73.4 3.2 %collective-permute-start.18 = (bf16[64,1792]{1,0:T(8,128)(2,1)S(1)}, bf16[64,1792]{1,0:T(8,128)(2,1)S(1)}, u32[]{:S(2)}, u32[]{:S(2)}) collective-permute-start(bf16[64,1792]{1,0:T(8,128)(2,1)S(1)} %get-tuple-element.22), channel_id=1, source_target_pairs={{0,1},{1,0},{2,3},{3,2},{4,5},{5,4},{6,7},{7,6},{8,9},{9,8},{10,11... | collective-permute-start | bytes 688136 | tf_op jit(solution)/shard_map/ppermute | solution.py:354
  73.5 4.0 %collective-permute-start.20 = (bf16[64,1792]{1,0:T(8,128)(2,1)S(1)}, bf16[64,1792]{1,0:T(8,128)(2,1)S(1)}, u32[]{:S(2)}, u32[]{:S(2)}) collective-permute-start(bf16[64,1792]{1,0:T(8,128)(2,1)S(1)} %get-tuple-element.24), channel_id=1, source_target_pairs={{0,1},{1,0},{2,3},{3,2},{4,5},{5,4},{6,7},{7,6},{8,9},{9,8},{10,11... | collective-permute-start | bytes 688136 | tf_op jit(solution)/shard_map/ppermute | solution.py:354
  74.6 5.7 %collective-permute-start.17 = (bf16[32,1792]{1,0:T(8,128)(2,1)S(1)}, bf16[32,1792]{1,0:T(8,128)(2,1)S(1)}, u32[]{:S(2)}, u32[]{:S(2)}) collective-permute-start(bf16[32,1792]{1,0:T(8,128)(2,1)S(1)} %fusion.3), channel_id=1, source_target_pairs={{0,130},{2,128},{128,2},{130,0},{1,131},{3,129},{129,3},{131,1},{4... | collective-permute-start | bytes 344072 | tf_op jit(solution)/shard_map/ppermute | solution.py:358
  76.6 6.1 %collective-permute-start.19 = (bf16[32,1792]{1,0:T(8,128)(2,1)S(1)}, bf16[32,1792]{1,0:T(8,128)(2,1)S(1)}, u32[]{:S(2)}, u32[]{:S(2)}) collective-permute-start(bf16[32,1792]{1,0:T(8,128)(2,1)S(1)} %fusion.4), channel_id=1, source_target_pairs={{0,130},{2,128},{128,2},{130,0},{1,131},{3,129},{129,3},{131,1},{4... | collective-permute-start | bytes 344072 | tf_op jit(solution)/shard_map/ppermute | solution.py:358
  77.6 7.6 %collective-permute-start.21 = (bf16[32,1792]{1,0:T(8,128)(2,1)S(1)}, bf16[32,1792]{1,0:T(8,128)(2,1)S(1)}, u32[]{:S(2)}, u32[]{:S(2)}) collective-permute-start(bf16[32,1792]{1,0:T(8,128)(2,1)S(1)} %fusion.5), channel_id=1, source_target_pairs={{0,130},{2,128},{128,2},{130,0},{1,131},{3,129},{129,3},{131,1},{4... | collective-permute-start | bytes 344072 | tf_op jit(solution)/shard_map/ppermute | solution.py:358
